TPU v7x, 32 devices: a whole 2x2x4 slice. The times are simulated.
32 devices in a mesh: gz: 2 (over core), row: 4 (over y, x), col: 4 (over z).
Axes of the slice: x: 2, y: 2, z: 4, core: 2. Of those that a mesh axis runs over, the one named last changes fastest.
Arguments:
- right_side: float32 [4, 16, 16384], P(None, 'col', 'row'), may hold values from -6 to 6
- layer_sums: float32 [2, 4, 16, 16384], P('gz', None, 'col', 'row'), may hold values from -6 to 6
- lower_blocks: float32 [6, 16, 256, 256], P(None, 'col', 'row'), may hold values from -0.1875 to 0.1875
- upper_blocks: float32 [6, 16, 256, 256], P(None, 'col', 'row'), may hold values from -0.1875 to 0.1875
- lower_inverse: float32 [4, 16, 256, 256], P(None, 'col'), may hold values from -1 to 2, as said below
- upper_diagonal_inverses: float32 [4, 16, 256, 256], P(None, 'col'), may hold values from -1 to 2
- pattern: int32 [6, 16], P(None, 'col'), may hold values 0 or 1
- parents: int32 [3, 16], replicated, may hold values from 0 to 15
Outputs:
- forward_solution: float32 [4, 16, 16384], P(None, 'col')
- solution: float32 [4, 16, 16384], P(None, 'col')
Inputs may be any that keep to these rules, and one draw needn't show every extreme that they name: `lower_inverse`: inverses of the diagonal blocks of L.
All inputs are finite; a program needn't handle non-finite values. No bound on the sum of `pattern` on one device may be relied on, other than what follows from the above.
Results may differ from a plain program's by a relative error of at most 0.00013.
Values sent between devices are 32-bit elements; how exact they have to be, the bound alone decides.
No kernel may reach another device: no remote copies, remote signals or barrier semaphores. Data moves between devices by JAX's collectives and lax.ppermute only.
A program may use at most 128 MiB of HBM per device.

v0:
```python
import jax
import jax.numpy as jnp
from jax import lax
from jax.sharding import PartitionSpec as P

WIDTH = 256
COLUMNS = 64


def place_of(height, distance):
    return height * (height - 1) // 2 + distance - 1


def solve_nodes(pieces, inverse):
    full_rows = lax.all_gather(pieces, "row", axis=1, tiled=True)
    return jnp.einsum("jvw,jwk->jvk", inverse, full_rows, precision=lax.Precision.HIGHEST)


def body(
    right_side,
    layer_sums,
    lower_blocks,
    upper_blocks,
    lower_inverse,
    upper_diagonal_inverses,
    pattern,
    parents,
):
    per_column = right_side.shape[1]
    part_rows = lower_blocks.shape[2]
    node_count = parents.shape[1]
    grid_column = lax.axis_index("col")
    present = pattern.astype(jnp.float32)
    node_range = jnp.arange(node_count, dtype=jnp.int32)
    picker_masks = {}
    for height in range(1, 4):
        current = lax.dynamic_slice_in_dim(
            parents[height - 1], grid_column * per_column, per_column, 0
        )
        for distance in range(1, height + 1):
            if distance > 1:
                lookup = parents[height - distance]
                current = jnp.sum(
                    jnp.where(current[:, None] == node_range[None, :], lookup[None, :], 0), axis=1
                )
            picker_masks[height, distance] = (current[:, None] == node_range[None, :]).astype(
                jnp.float32
            )
    shaped_right = right_side.reshape(4, per_column, part_rows, COLUMNS)
    own_columns = COLUMNS // lax.axis_size("gz")
    subtree_total = lax.psum_scatter(
        layer_sums[0].reshape(4, per_column, part_rows, COLUMNS),
        "gz",
        scatter_dimension=3,
        tiled=True,
    )
    own_right = lax.dynamic_slice_in_dim(
        shaped_right, lax.axis_index("gz") * own_columns, own_columns, 3
    )
    initial = own_right - subtree_total
    forward = [None] * 4
    received = [jnp.zeros((per_column, part_rows, own_columns), jnp.float32) for height in range(4)]
    for height in (3, 2, 1, 0):
        incoming = received[height]
        solved = solve_nodes(initial[height] - incoming, lower_inverse[height])
        forward[height] = solved
        summand_terms = []
        for distance in range(1, height + 1):
            block_place = place_of(height, distance)
            product = jnp.einsum(
                "jvw,jwk->jvk", lower_blocks[block_place], solved, precision=lax.Precision.HIGHEST
            )
            product = product * present[block_place][:, None, None]
            summand_terms.append(
                jnp.einsum(
                    "ja,jvk->avk",
                    picker_masks[height, distance],
                    product,
                    precision=lax.Precision.HIGHEST,
                )
            )
        if height > 0:
            gathered = lax.psum_scatter(
                jnp.stack(summand_terms, 1), "col", scatter_dimension=0, tiled=True
            )
            for distance in range(1, height + 1):
                received[height - distance] = (
                    received[height - distance] + gathered[:, distance - 1]
                )
    backward = [None] * 4
    whole_levels = [None] * 3
    row_start = lax.axis_index("row") * part_rows
    for height in range(4):
        remaining_right = lax.dynamic_slice_in_dim(forward[height], row_start, part_rows, 1)
        for distance in range(1, height + 1):
            block_place = place_of(height, distance)
            chosen = jnp.einsum(
                "ja,awk->jwk",
                picker_masks[height, distance],
                whole_levels[height - distance],
                precision=lax.Precision.HIGHEST,
            )
            update = jnp.einsum(
                "jvw,jwk->jvk", upper_blocks[block_place], chosen, precision=lax.Precision.HIGHEST
            )
            remaining_right = remaining_right - update * present[block_place][:, None, None]
        solved = solve_nodes(remaining_right, upper_diagonal_inverses[height])
        backward[height] = solved
        if height < 3:
            whole_levels[height] = lax.all_gather(solved, "col", axis=0, tiled=True)
    forward_all = jnp.stack(forward)
    backward_sweep_levels = jnp.stack(backward)
    forward_all, backward_sweep_levels = (
        lax.all_gather(forward_all, "gz", axis=3, tiled=True),
        lax.all_gather(backward_sweep_levels, "gz", axis=3, tiled=True),
    )
    return (
        forward_all.reshape(4, per_column, WIDTH * COLUMNS),
        backward_sweep_levels.reshape(4, per_column, WIDTH * COLUMNS),
    )


def solution(mesh):
    in_specs = (
        P(None, "col", "row"),
        P("gz", None, "col", "row"),
        P(None, "col", "row", None),
        P(None, "col", "row", None),
        P(None, "col", None, None),
        P(None, "col", None, None),
        P(None, "col"),
        P(),
    )
    out_specs = (P(None, "col", None), P(None, "col", None))
    return jax.shard_map(body, mesh=mesh, in_specs=in_specs, out_specs=out_specs, check_vma=False)
```

profile of v0, /device:TPU:0, one launch (start us, length us, event | category | flops | bytes accessed | tf_op | source)
XLA Modules:
  0.0 304.1 jit_solution(16849978489420073043)
XLA Ops:
  11.2 10.1 %reduce-scatter.9.cloned.1.call-done = f32[32,1024]{1,0:T(8,128)} async-done(((f32[64,1024]{1,0:T(8,128)}), f32[32,1024]{1,0:T(8,128)}) %reduce-scatter.9.cloned.1.call-update) | async-done | bytes 131088
  22.9 10.6 %all-gather = f32[1,4,256,32]{3,1,0,2:T(4,128)S(1)} all-gather(f32[1,4,64,32]{3,1,0,2:T(4,128)S(1)} %copy.85), channel_id=2, replica_groups=mesh['gz'=2,'row'=4,'col'=4] {'row'}, dimensions={2}, use_global_device_ids=true | all-gather | bytes 163840 | tf_op jit(solution)/shard_map/all_gather | solution.py:15
  33.7 2.3 fusion.28
  40.8 42.6 %all-reduce.5.cloned.1.call-done = f32[16,3,64,32]{2,3,0,1:T(8,128)} async-done(((f32[16,3,64,32]{2,3,0,1:T(8,128)}), f32[16,3,64,32]{2,3,0,1:T(8,128)}) %all-reduce.5.cloned.1.call-update) | async-done | bytes 393232
  84.5 10.0 %all_gather.40 = f32[4,256,32]{2,0,1:T(4,128)S(1)} all-gather(f32[4,64,32]{2,0,1:T(4,128)S(1)} %copy.93), channel_id=1, replica_groups=mesh['gz'=2,'row'=4,'col'=4] {'row'}, dimensions={1}, use_global_device_ids=true | all-gather | bytes 163840 | tf_op jit(solution)/shard_map/all_gather | solution.py:15
  94.5 2.3 fusion.26
  99.7 37.0 %all-reduce.7.cloned.1.call-done = f32[16,2,64,32]{2,3,0,1:T(8,128)} async-done(((f32[16,2,64,32]{2,3,0,1:T(8,128)}), f32[16,2,64,32]{2,3,0,1:T(8,128)}) %all-reduce.7.cloned.1.call-update) | async-done | bytes 262160
  137.8 10.0 %all_gather.41 = f32[4,256,32]{2,0,1:T(4,128)S(1)} all-gather(f32[4,64,32]{2,0,1:T(4,128)S(1)} %copy.101), channel_id=1, replica_groups=mesh['gz'=2,'row'=4,'col'=4] {'row'}, dimensions={1}, use_global_device_ids=true | all-gather | bytes 163840 | tf_op jit(solution)/shard_map/all_gather | solution.py:15
  147.8 2.3 fusion.24
  152.0 19.2 %reduce-scatter.7.cloned.1.call-done = f32[4,1,64,32]{2,3,1,0:T(8,128)} async-done(((f32[16,1,64,32]{2,3,1,0:T(8,128)}), f32[4,1,64,32]{2,3,1,0:T(8,128)}) %reduce-scatter.7.cloned.1.call-update) | async-done | bytes 32784 | tf_op jit(solution)/shard_map/reduce_scatter | solution.py:83
  172.3 10.7 %all_gather.42 = f32[4,256,32]{2,0,1:T(4,128)S(1)} all-gather(f32[4,64,32]{2,0,1:T(4,128)S(1)} %copy.106), channel_id=1, replica_groups=mesh['gz'=2,'row'=4,'col'=4] {'row'}, dimensions={1}, use_global_device_ids=true | all-gather | bytes 163840 | tf_op jit(solution)/shard_map/all_gather | solution.py:15
  183.0 2.3 fusion.22
  185.5 10.2 %all_gather.44 = f32[4,256,32]{2,0,1:T(4,128)S(1)} all-gather(f32[4,64,32]{2,0,1:T(4,128)S(1)} %copy.109), channel_id=1, replica_groups=mesh['gz'=2,'row'=4,'col'=4] {'row'}, dimensions={1}, use_global_device_ids=true | all-gather | bytes 163840 | tf_op jit(solution)/shard_map/all_gather | solution.py:15
  195.7 2.4 fusion.20
  198.1 15.2 %all_gather.45 = f32[16,256,32]{1,2,0:T(8,128)S(1)} all-gather(f32[4,256,32]{1,2,0:T(8,128)S(1)} %bitcast.203), channel_id=1, replica_groups=mesh['gz'=2,'row'=4,'col'=4] {'col'}, dimensions={0}, use_global_device_ids=true | all-gather | bytes 655360 | tf_op jit(solution)/shard_map/all_gather | solution.py:110
  215.0 9.4 %all_gather.46 = f32[4,256,32]{2,0,1:T(4,128)S(1)} all-gather(f32[4,64,32]{2,0,1:T(4,128)S(1)} %copy.113), channel_id=1, replica_groups=mesh['gz'=2,'row'=4,'col'=4] {'row'}, dimensions={1}, use_global_device_ids=true | all-gather | bytes 163840 | tf_op jit(solution)/shard_map/all_gather | solution.py:15
  224.4 2.3 fusion.18
  226.7 14.7 %all_gather.47 = f32[16,256,32]{1,2,0:T(8,128)S(1)} all-gather(f32[4,256,32]{1,2,0:T(8,128)S(1)} %bitcast.205), channel_id=1, replica_groups=mesh['gz'=2,'row'=4,'col'=4] {'col'}, dimensions={0}, use_global_device_ids=true | all-gather | bytes 655360 | tf_op jit(solution)/shard_map/all_gather | solution.py:110
  243.5 9.8 %all_gather.48 = f32[4,256,32]{2,0,1:T(4,128)S(1)} all-gather(f32[4,64,32]{2,0,1:T(4,128)S(1)} %copy.119), channel_id=1, replica_groups=mesh['gz'=2,'row'=4,'col'=4] {'row'}, dimensions={1}, use_global_device_ids=true | all-gather | bytes 163840 | tf_op jit(solution)/shard_map/all_gather | solution.py:15
  253.3 2.3 fusion.16
  255.6 14.7 %all_gather.49 = f32[16,256,32]{1,2,0:T(8,128)S(1)} all-gather(f32[4,256,32]{1,2,0:T(8,128)S(1)} %bitcast.207), channel_id=1, replica_groups=mesh['gz'=2,'row'=4,'col'=4] {'col'}, dimensions={0}, use_global_device_ids=true | all-gather | bytes 655360 | tf_op jit(solution)/shard_map/all_gather | solution.py:110
  273.6 9.5 %all_gather.50 = f32[4,256,32]{2,0,1:T(4,128)S(1)} all-gather(f32[4,64,32]{2,0,1:T(4,128)S(1)} %copy.127), channel_id=1, replica_groups=mesh['gz'=2,'row'=4,'col'=4] {'row'}, dimensions={1}, use_global_device_ids=true | all-gather | bytes 163840 | tf_op jit(solution)/shard_map/all_gather | solution.py:15
  283.1 2.3 convolution_bitcast_fusion.6
  290.0 3.6 %all-gather.6.cloned.1.call-done = f32[4,4,256,64]{2,3,1,0:T(8,128)} async-done(((f32[4,4,256,32]{2,3,1,0:T(8,128)}), f32[4,4,256,64]{2,3,1,0:T(8,128)}) %all-gather.6.cloned.1.call-update) | async-done | bytes 1048592 | tf_op jit(solution)/shard_map/all_gather | solution.py:115
  (97 shorter events, 32.9 us)
Async XLA Ops:
  7.2 2.9 copy-start.4
  7.2 2.9 copy-start.3
  7.2 2.9 copy-start.2
  7.2 14.0 %reduce-scatter.9.cloned.1.call-start = ((), (), s32[]{:S(2)}) async-start(), calls=%async_computation.5 | async-start | bytes 393216
  10.0 73.4 %all-reduce.5.cloned.1.call-start = ((), (), s32[]{:S(2)}) async-start(), calls=%async_computation.6 | async-start | bytes 1572864
  22.7 13.2 %copy-start = (f32[6,4,64,256]{3,2,1,0:T(8,128)S(1)}, f32[6,4,64,256]{3,2,1,0:T(8,128)}, u32[]{:S(2)}) copy-start(f32[6,4,64,256]{3,2,1,0:T(8,128)} %param.10) | copy-start | bytes 4718596
  38.4 1.2 copy-start.5
  39.5 97.1 %all-reduce.7.cloned.1.call-start = ((), (), s32[]{:S(2)}) async-start(), calls=%async_computation.7 | async-start | bytes 1048576
  99.5 71.8 %reduce-scatter.7.cloned.1.call-start = ((), (), s32[]{:S(2)}) async-start(), calls=%async_computation.2 | async-start | bytes 327680 | tf_op jit(solution)/shard_map/reduce_scatter | solution.py:83
  151.7 134.6 %all-gather.4.cloned.1.call-start = ((), (), s32[]{:S(2)}) async-start(), calls=%async_computation.3 | async-start | bytes 1572864 | tf_op jit(solution)/shard_map/all_gather | solution.py:114
  195.7 18.9 %copy-start.1 = (f32[6,4,64,256]{3,2,1,0:T(8,128)S(1)}, f32[6,4,64,256]{3,2,1,0:T(8,128)}, u32[]{:S(2)}) copy-start(f32[6,4,64,256]{3,2,1,0:T(8,128)} %param.11) | copy-start | bytes 4718596
  271.7 21.8 %all-gather.6.cloned.1.call-start = ((), (), s32[]{:S(2)}) async-start(), calls=%async_computation.4 | async-start | bytes 1572864 | tf_op jit(solution)/shard_map/all_gather | solution.py:115
Sparse Core Ops, SparseCore 0:
  10.8 10.3 reduce-scatter.8
  39.6 43.7 all-reduce.4
  99.6 37.0 all-reduce.6
  151.8 19.3 reduce-scatter.6
  271.9 6.9 all-gather.3
  286.4 7.1 all-gather.5
where the time goes:
time: 305 us; the launch traced here: 304 us
  blocking collectives  125 us (41%)
  waiting for transfers between devices  113 us (37%)
  matrix products  29 us (10%)
  local copies, waits for them, and re-layouts  19.8 us (6%)
  between operations  15.3 us (5%)
    unnamed x9, waiting for transfers between devices  89.7 us
    all_gather x8, blocking collectives, solve_nodes(): full_rows = lax.all_gather(pieces, 'row', axis=1, tiled=True)  80.2 us
    all_gather x3, blocking collectives, body(): whole_levels[height] = lax.all_gather(solved, 'col', axis=0, tiled=True)  44.5 us
    reduce_scatter x1, waiting for transfers between devices, body(): lax.psum_scatter(jnp.stack(summand_terms, 1), 'col', scatter_dimension=0,...  19.2 us
    dot_general x8, matrix products, solve_nodes(): jnp.einsum('jvw,jwk->jvk', inverse, full_rows, precision=lax.Precision.HI...  18.7 us
  transfers between devices with their start and end apart: 6, of which 5 were waited for; matrix products, arithmetic and copies ran while one was open for 3% of the time, Pallas kernels for 0%

commit v1 on v0

v1 whole, which is shorter than its diff:
```python
import functools

import jax
import jax.numpy as jnp
from jax import lax
from jax.experimental import pallas as pl
from jax.experimental.pallas import tpu as pltpu
from jax.sharding import PartitionSpec as P

WIDTH = 256
COLUMNS = 64
F32 = jnp.float32
BF16 = jnp.bfloat16


def place_of(height, distance):
    return height * (height - 1) // 2 + distance - 1


def partner_of(index, step, count):
    assert count & (count - 1) == 0
    return index ^ step


def exchange(value, axis, step):
    count = lax.axis_size(axis)
    return lax.ppermute(value, axis, [(i, partner_of(i, step, count)) for i in range(count)])


def split(value):
    high = value.astype(BF16)
    return high, (value - high.astype(F32)).astype(BF16)


def dot(left, right):
    return jnp.dot(left, right, preferred_element_type=F32)


def product(left, right_high, right_both):
    high, low = split(left)
    lanes = right_high.shape[1]
    both = dot(high, right_both)
    return both[:, :lanes] + both[:, lanes:] + dot(low, right_high)


def forward_kernel(height, sizes, *refs):
    nodes, part, own, row_count, col_count = sizes
    lanes = nodes * own
    pieces = refs[:row_count]
    parents, pattern, inverse, blocks = refs[row_count : row_count + 4]
    refs = refs[row_count + 4 :]
    pending_in = refs[: height] if height < 3 else ()
    refs = refs[len(pending_in) :]
    solved_ref = refs[0]
    sends = refs[1 : 1 + (col_count if height else 0)]
    refs = refs[1 + len(sends) :]
    pending_out = refs[: max(height - 1, 0)]
    refs = refs[len(pending_out) :]
    full, urgent = refs
    row = lax.axis_index("row")
    col = lax.axis_index("col")
    for step in range(row_count):
        start = partner_of(row, step, row_count) * part
        full[pl.ds(pl.multiple_of(start, part), part), :] = pieces[step][...]
    lane = lax.broadcasted_iota(jnp.int32, (1, lanes), 1) // own
    high, low = split(full[...])
    both = jnp.concatenate([high, low], axis=1)
    solved = jnp.zeros_like(full)
    for node in range(nodes):
        solved = jnp.where(lane == node, product(inverse[0, node], high, both), solved)
    solved_ref[...] = solved
    if height == 0:
        return
    high, low = split(solved)
    both = jnp.concatenate([high, low], axis=1)
    targets = []
    for level in range(height):
        target = urgent if level == height - 1 else pending_out[level]
        target[...] = pending_in[level][...] if pending_in else jnp.zeros_like(target)
        targets.append(target)
    for node in range(nodes):
        ancestor = col * nodes + node
        for distance in range(1, height + 1):
            place = place_of(height, distance)
            level = height - distance
            ancestor = parents[level, ancestor]
            slot = lax.rem(ancestor, nodes)
            where = partner_of(lax.div(ancestor, nodes), col, col_count)
            term = product(blocks[place, node], high, both)
            term = pltpu.roll(term, lax.rem(slot - node + nodes, nodes) * own, 1)
            keep = jnp.where(pattern[place, node] != 0, slot, -1)
            targets[level][where] += jnp.where(lane == keep, term, 0.0)
    for step in range(col_count):
        sends[step][...] = urgent[step]


def forward_step(height, pieces, parents, pattern, inverse, blocks, pending, sizes):
    nodes, part, own, row_count, col_count = sizes
    lanes = nodes * own
    rows = row_count * part
    smem = pl.BlockSpec(memory_space=pltpu.SMEM)
    vmem = pl.BlockSpec(memory_space=pltpu.VMEM)
    piece = jax.ShapeDtypeStruct((part, lanes), F32)
    stack = jax.ShapeDtypeStruct((col_count, part, lanes), F32)
    out_shape = [jax.ShapeDtypeStruct((rows, lanes), F32)]
    if height:
        out_shape += [piece] * col_count + [stack] * (height - 1)
    results = pl.pallas_call(
        functools.partial(forward_kernel, height, sizes),
        out_shape=out_shape,
        grid=(1,),
        in_specs=[vmem] * row_count
        + [smem, smem, pl.BlockSpec((1,) + inverse.shape[1:], lambda i: (height, 0, 0, 0)), vmem]
        + [vmem] * len(pending),
        out_specs=[vmem] * len(out_shape),
        scratch_shapes=[
            pltpu.VMEM((rows, lanes), F32),
            pltpu.VMEM((col_count, part, lanes), F32),
        ],
        compiler_params=pltpu.CompilerParams(vmem_limit_bytes=24 * 2**20),
        name="forward_level",
    )(*pieces, parents, pattern, inverse, blocks, *pending)
    solved = results[0]
    if height == 0:
        return solved, (), ()
    return solved, results[1 : 1 + col_count], results[1 + col_count :]


def solve_nodes(pieces, inverse):
    full_rows = lax.all_gather(pieces, "row", axis=1, tiled=True)
    return jnp.einsum("jvw,jwk->jvk", inverse, full_rows, precision=lax.Precision.HIGHEST)


def body(
    right_side,
    layer_sums,
    lower_blocks,
    upper_blocks,
    lower_inverse,
    upper_diagonal_inverses,
    pattern,
    parents,
):
    per_column = right_side.shape[1]
    part_rows = lower_blocks.shape[2]
    node_count = parents.shape[1]
    gz_count = lax.axis_size("gz")
    row_count = lax.axis_size("row")
    col_count = lax.axis_size("col")
    own_columns = COLUMNS // gz_count
    lanes = per_column * own_columns
    sizes = (per_column, part_rows, own_columns, row_count, col_count)
    grid_column = lax.axis_index("col")
    gz = lax.axis_index("gz")
    present = pattern.astype(F32)
    node_range = jnp.arange(node_count, dtype=jnp.int32)

    def columns_of(values, which):
        values = lax.dynamic_slice_in_dim(
            values.reshape(4, per_column, part_rows, COLUMNS), which * own_columns, own_columns, 3
        )
        return values.transpose(0, 2, 1, 3).reshape(4, part_rows, lanes)

    own_part = columns_of(right_side, gz) - columns_of(layer_sums[0], gz)
    away = [
        -columns_of(layer_sums[0], partner_of(gz, step, gz_count)) for step in range(1, gz_count)
    ]
    initial = [None] * 4
    count = gz_count * row_count

    def direct(value, gz_step, row_step):
        pairs = []
        for i in range(count):
            g, r = divmod(i, row_count)
            g, r = partner_of(g, gz_step, gz_count), partner_of(r, row_step, row_count)
            pairs.append((i, g * row_count + r))
        return lax.ppermute(value, ("gz", "row"), pairs)

    pieces = []
    for row_step in range(row_count):
        piece = own_part[3] if row_step == 0 else direct(own_part[3], 0, row_step)
        for gz_step in range(1, gz_count):
            piece = piece + direct(away[gz_step - 1][3], gz_step, row_step)
        pieces.append(piece)
    rest = own_part[:3]
    for gz_step in range(1, gz_count):
        rest = rest + exchange(away[gz_step - 1][:3], "gz", gz_step)

    forward = [None] * 4
    pending = ()
    for height in (3, 2, 1, 0):
        if height < 3:
            mine = rest[height] - sends[0]
            for step in range(1, col_count):
                mine = mine - exchange(sends[step], "col", step)
            pieces = [mine] + [exchange(mine, "row", step) for step in range(1, row_count)]
        forward[height], sends, pending = forward_step(
            height, pieces, parents, pattern, lower_inverse, lower_blocks, pending, sizes
        )
    forward = [
        value.reshape(WIDTH, per_column, own_columns).transpose(1, 0, 2) for value in forward
    ]

    picker_masks = {}
    for height in range(1, 4):
        current = lax.dynamic_slice_in_dim(
            parents[height - 1], grid_column * per_column, per_column, 0
        )
        for distance in range(1, height + 1):
            if distance > 1:
                lookup = parents[height - distance]
                current = jnp.sum(
                    jnp.where(current[:, None] == node_range[None, :], lookup[None, :], 0), axis=1
                )
            picker_masks[height, distance] = (current[:, None] == node_range[None, :]).astype(F32)
    backward = [None] * 4
    whole_levels = [None] * 3
    row_start = lax.axis_index("row") * part_rows
    for height in range(4):
        if height == 0:
            solved = jnp.einsum(
                "jvw,jwk->jvk",
                upper_diagonal_inverses[0],
                forward[0],
                precision=lax.Precision.HIGHEST,
            )
        else:
            remaining_right = lax.dynamic_slice_in_dim(forward[height], row_start, part_rows, 1)
            for distance in range(1, height + 1):
                block_place = place_of(height, distance)
                chosen = jnp.einsum(
                    "ja,awk->jwk",
                    picker_masks[height, distance],
                    whole_levels[height - distance],
                    precision=lax.Precision.HIGHEST,
                )
                update = jnp.einsum(
                    "jvw,jwk->jvk",
                    upper_blocks[block_place],
                    chosen,
                    precision=lax.Precision.HIGHEST,
                )
                remaining_right = remaining_right - update * present[block_place][:, None, None]
            solved = solve_nodes(remaining_right, upper_diagonal_inverses[height])
        backward[height] = solved
        if height < 3:
            whole_levels[height] = lax.all_gather(solved, "col", axis=0, tiled=True)
    forward_all = jnp.stack(forward)
    backward_sweep_levels = jnp.stack(backward)
    forward_all, backward_sweep_levels = (
        lax.all_gather(forward_all, "gz", axis=3, tiled=True),
        lax.all_gather(backward_sweep_levels, "gz", axis=3, tiled=True),
    )
    return (
        forward_all.reshape(4, per_column, WIDTH * COLUMNS),
        backward_sweep_levels.reshape(4, per_column, WIDTH * COLUMNS),
    )


def solution(mesh):
    in_specs = (
        P(None, "col", "row"),
        P("gz", None, "col", "row"),
        P(None, "col", "row", None),
        P(None, "col", "row", None),
        P(None, "col", None, None),
        P(None, "col", None, None),
        P(None, "col"),
        P(),
    )
    out_specs = (P(None, "col", None), P(None, "col", None))
    return jax.shard_map(body, mesh=mesh, in_specs=in_specs, out_specs=out_specs, check_vma=False)
```

time: 305 us -> 201 us (0.66)
  waiting for transfers between devices: 113 us -> 38.1 us
  blocking collectives: 125 us -> 73.4 us
  starting transfers between devices: 0.25 us -> 32.7 us
  matrix products: 29 us -> 15.1 us
  Pallas kernels: 0 us -> 5.61 us
    unnamed x9 -> x2, waiting for transfers between devices: 89.7 us -> 0.03 us
    all_gather x8 -> x3, blocking collectives: 80.2 us -> 28.9 us  [solve_nodes(): full_rows = lax.all_gather(pieces, 'row', axis=1, tiled=True)]
    ppermute x0 -> x26, starting transfers between devices: none -> 32.6 us  [the longest x19 24 us: exchange(): lax.ppermute(value, axis, [(i, partner_of(i, step, count)) for i in range...]
    ppermute x0 -> x26, waiting for transfers between devices: none -> 23.2 us  [the longest x19 20.3 us: exchange(): lax.ppermute(value, axis, [(i, partner_of(i, step, count)) for i in range...]
    reduce_scatter x1 -> x0, waiting for transfers between devices: 19.2 us -> none  [body(): lax.psum_scatter(jnp.stack(summand_terms, 1), 'col', scatter_dimension=0,...]
    dot_general x8 -> x3, matrix products: 18.7 us -> 6.98 us  [solve_nodes(): jnp.einsum('jvw,jwk->jvk', inverse, full_rows, precision=lax.Precision.HI...]
    all_gather x1, waiting for transfers between devices: 0.02 us -> 8.69 us  [body(): lax.all_gather(forward_all, 'gz', axis=3, tiled=True)]
    pallas_call x0 -> x4, Pallas kernels: none -> 5.61 us  [forward_step(): pl.pallas_call(functools.partial(forward_kernel, height, sizes), out_shap...]
  transfers between devices with their start and end apart: 6 -> 28, of which waited for: 5 -> 20; matrix products, arithmetic and copies ran while one was open for 3% -> 3% of each run, Pallas kernels for 0% -> 1%
where the time goes in v1:
time: 201 us
  blocking collectives  73.4 us (37%)
  waiting for transfers between devices  38.1 us (19%)
  starting transfers between devices  32.7 us (16%)
  local copies, waits for them, and re-layouts  19.1 us (10%)
  matrix products  15.1 us (8%)
  between operations  14.5 us (7%)
  Pallas kernels  5.61 us (3%)
  other arithmetic  2.21 us (1%)
    all_gather x3, blocking collectives, body(): whole_levels[height] = lax.all_gather(solved, 'col', axis=0, tiled=True)  44.5 us
    all_gather x3, blocking collectives, solve_nodes(): full_rows = lax.all_gather(pieces, 'row', axis=1, tiled=True)  28.9 us
    ppermute x19, starting transfers between devices, exchange(): lax.ppermute(value, axis, [(i, partner_of(i, step, count)) for i in range...  24 us
    ppermute x19, waiting for transfers between devices, exchange(): lax.ppermute(value, axis, [(i, partner_of(i, step, count)) for i in range...  20.3 us
    all_gather x1, waiting for transfers between devices, body(): lax.all_gather(forward_all, 'gz', axis=3, tiled=True)  8.69 us
    ppermute x7, starting transfers between devices, direct(): return lax.ppermute(value, ('gz', 'row'), pairs)  8.58 us
    unnamed x18, local copies, waits for them, and re-layouts  7.23 us
    dot_general x3, matrix products, solve_nodes(): jnp.einsum('jvw,jwk->jvk', inverse, full_rows, precision=lax.Precision.HI...  6.98 us
  transfers between devices with their start and end apart: 28, of which 20 were waited for; matrix products, arithmetic and copies ran while one was open for 3% of the time, Pallas kernels for 1%

profile of v1, /device:TPU:0, one launch (start us, length us, event | category | flops | bytes accessed | tf_op | source)
XLA Modules:
  0.0 200.6 jit_solution(2261804304182008719)
XLA Ops:
  10.5 3.4 %collective-permute-start.7 = (f32[64,128]{1,0:T(8,128)S(1)}, f32[64,128]{1,0:T(8,128)S(1)}, u32[]{:S(2)}, u32[]{:S(2)}) collective-permute-start(f32[64,128]{1,0:T(8,128)S(1)} %copy.53), channel_id=1, source_target_pairs={{0,28},{4,24},{8,20},{12,16},{16,12},{20,8},{24,4},{28,0},{1,29},{... | collective-permute-start | bytes 98312 | tf_op jit(solution)/shard_map/ppermute | solution.py:177
  15.3 3.0 %collective-permute-start.6 = (f32[64,128]{1,0:T(8,128)S(1)}, f32[64,128]{1,0:T(8,128)S(1)}, u32[]{:S(2)}, u32[]{:S(2)}) collective-permute-start(f32[64,128]{1,0:T(8,128)S(1)} %copy.54), channel_id=1, source_target_pairs={{0,12},{4,8},{8,4},{12,0},{16,28},{20,24},{24,20},{28,16},{1,13},{... | collective-permute-start | bytes 98312 | tf_op jit(solution)/shard_map/ppermute | solution.py:177
  22.8 2.2 %copy-done = f32[4,4,256,256]{3,2,1,0:T(8,128)S(1)} copy-done((f32[4,4,256,256]{3,2,1,0:T(8,128)S(1)}, f32[4,4,256,256]{3,2,1,0:T(8,128)}, u32[]{:S(2)}) %copy-start) | copy-done | bytes 4194328
  28.3 2.6 %collective-permute-start.9 = (f32[64,128]{1,0:T(8,128)S(1)}, f32[64,128]{1,0:T(8,128)S(1)}, u32[]{:S(2)}, u32[]{:S(2)}) collective-permute-start(f32[64,128]{1,0:T(8,128)S(1)} %get-tuple-element.22), channel_id=1, source_target_pairs={{0,2},{1,3},{2,0},{3,1},{4,6},{5,7},{6,4},{7,5},{8,10},{9,11},{10,... | collective-permute-start | bytes 98312 | tf_op jit(solution)/shard_map/ppermute | solution.py:27
  31.3 2.4 %collective-permute-done.9 = f32[64,128]{1,0:T(8,128)S(1)} collective-permute-done((f32[64,128]{1,0:T(8,128)S(1)}, f32[64,128]{1,0:T(8,128)S(1)}, u32[]{:S(2)}, u32[]{:S(2)}) %collective-permute-start.9) | collective-permute-done | bytes 32800 | tf_op jit(solution)/shard_map/ppermute | solution.py:27
  33.7 2.9 %collective-permute-done.10 = f32[64,128]{1,0:T(8,128)S(1)} collective-permute-done((f32[64,128]{1,0:T(8,128)S(1)}, f32[64,128]{1,0:T(8,128)S(1)}, u32[]{:S(2)}, u32[]{:S(2)}) %collective-permute-start.10) | collective-permute-done | bytes 32800 | tf_op jit(solution)/shard_map/ppermute | solution.py:27
  42.9 2.2 %copy-done.1 = f32[4,4,256,256]{3,2,1,0:T(8,128)S(1)} copy-done((f32[4,4,256,256]{3,2,1,0:T(8,128)S(1)}, f32[4,4,256,256]{3,2,1,0:T(8,128)}, u32[]{:S(2)}) %copy-start.1) | copy-done | bytes 4194328
  47.5 3.5 %collective-permute-start.16 = (f32[64,128]{1,0:T(8,128)S(1)}, f32[64,128]{1,0:T(8,128)S(1)}, u32[]{:S(2)}, u32[]{:S(2)}) collective-permute-start(f32[64,128]{1,0:T(8,128)S(1)} %get-tuple-element.29), channel_id=1, source_target_pairs={{0,3},{1,2},{2,1},{3,0},{4,7},{5,6},{6,5},{7,4},{8,11},{9,10},{10,... | collective-permute-start | bytes 98312 | tf_op jit(solution)/shard_map/ppermute | solution.py:27
  53.3 2.2 %collective-permute-start.19 = (f32[64,128]{1,0:T(8,128)S(1)}, f32[64,128]{1,0:T(8,128)S(1)}, u32[]{:S(2)}, u32[]{:S(2)}) collective-permute-start(f32[64,128]{1,0:T(8,128)S(1)} %fusion.63.refs_0_), channel_id=1, source_target_pairs={{0,12},{4,8},{8,4},{12,0},{1,13},{5,9},{9,5},{13,1},{2,14},{6,10},... | collective-permute-start | bytes 98312 | tf_op jit(solution)/shard_map/ppermute | solution.py:27
  61.6 3.8 %collective-permute-start.21 = (f32[64,128]{1,0:T(8,128)S(1)}, f32[64,128]{1,0:T(8,128)S(1)}, u32[]{:S(2)}, u32[]{:S(2)}) collective-permute-start(f32[64,128]{1,0:T(8,128)S(1)} %get-tuple-element.33), channel_id=1, source_target_pairs={{0,2},{1,3},{2,0},{3,1},{4,6},{5,7},{6,4},{7,5},{8,10},{9,11},{10,... | collective-permute-start | bytes 98312 | tf_op jit(solution)/shard_map/ppermute | solution.py:27
  67.3 3.8 %collective-permute-done.22 = f32[64,128]{1,0:T(8,128)S(1)} collective-permute-done((f32[64,128]{1,0:T(8,128)S(1)}, f32[64,128]{1,0:T(8,128)S(1)}, u32[]{:S(2)}, u32[]{:S(2)}) %collective-permute-start.22) | collective-permute-done | bytes 32800 | tf_op jit(solution)/shard_map/ppermute | solution.py:27
  77.4 2.2 %copy-done.2 = f32[4,4,256,256]{3,2,1,0:T(8,128)S(1)} copy-done((f32[4,4,256,256]{3,2,1,0:T(8,128)S(1)}, f32[4,4,256,256]{3,2,1,0:T(8,128)}, u32[]{:S(2)}) %copy-start.2) | copy-done | bytes 4194328
  80.8 2.4 %fusion.17 = f32[4,32,256]{2,1,0:T(8,128)S(1)} fusion(f32[4,256,32]{1,2,0:T(8,128)S(1)} %bitcast.166, f32[4,4,256,256]{3,2,1,0:T(8,128)} %param.13), kind=kOutput, calls=%fused_computation.24 | convolution fusion | flops 100663296 | bytes 1310720 | tf_op jit(solution)/shard_map/jvw,jwk->jvk/dot_general | solution.py:221
  83.2 14.8 %all_gather.25 = f32[16,256,32]{1,2,0:T(8,128)S(1)} all-gather(f32[4,256,32]{1,2,0:T(8,128)S(1)} %bitcast.164), channel_id=1, replica_groups=mesh['gz'=2,'row'=4,'col'=4] {'col'}, dimensions={0}, use_global_device_ids=true | all-gather | bytes 655360 | tf_op jit(solution)/shard_map/all_gather | solution.py:247
  99.0 9.8 %all_gather.26 = f32[4,256,32]{2,0,1:T(4,128)S(1)} all-gather(f32[4,64,32]{2,0,1:T(4,128)S(1)} %copy.72), channel_id=1, replica_groups=mesh['gz'=2,'row'=4,'col'=4] {'row'}, dimensions={1}, use_global_device_ids=true | all-gather | bytes 163840 | tf_op jit(solution)/shard_map/all_gather | solution.py:130
  108.8 2.3 %fusion.15 = f32[4,32,256]{2,1,0:T(8,128)S(1)} fusion(f32[4,4,256,256]{3,2,1,0:T(8,128)} %param.13, f32[4,256,32]{2,0,1:T(4,128)S(1)} %all_gather.26), kind=kOutput, calls=%fused_computation.22 | convolution fusion | flops 100663296 | bytes 1310720 | tf_op jit(solution)/shard_map/jvw,jwk->jvk/dot_general | solution.py:131
  111.1 15.0 %all_gather.27 = f32[16,256,32]{1,2,0:T(8,128)S(1)} all-gather(f32[4,256,32]{1,2,0:T(8,128)S(1)} %bitcast.168), channel_id=1, replica_groups=mesh['gz'=2,'row'=4,'col'=4] {'col'}, dimensions={0}, use_global_device_ids=true | all-gather | bytes 655360 | tf_op jit(solution)/shard_map/all_gather | solution.py:247
  129.4 10.6 %all_gather.28 = f32[4,256,32]{2,0,1:T(4,128)S(1)} all-gather(f32[4,64,32]{2,0,1:T(4,128)S(1)} %copy.78), channel_id=1, replica_groups=mesh['gz'=2,'row'=4,'col'=4] {'row'}, dimensions={1}, use_global_device_ids=true | all-gather | bytes 163840 | tf_op jit(solution)/shard_map/all_gather | solution.py:130
  139.9 2.3 %fusion.13 = f32[4,32,256]{2,1,0:T(8,128)S(1)} fusion(f32[4,4,256,256]{3,2,1,0:T(8,128)} %param.13, f32[4,256,32]{2,0,1:T(4,128)S(1)} %all_gather.28), kind=kOutput, calls=%fused_computation.20 | convolution fusion | flops 100663296 | bytes 1310720 | tf_op jit(solution)/shard_map/jvw,jwk->jvk/dot_general | solution.py:131
  142.3 14.8 %all_gather.29 = f32[16,256,32]{1,2,0:T(8,128)S(1)} all-gather(f32[4,256,32]{1,2,0:T(8,128)S(1)} %bitcast.170), channel_id=1, replica_groups=mesh['gz'=2,'row'=4,'col'=4] {'col'}, dimensions={0}, use_global_device_ids=true | all-gather | bytes 655360 | tf_op jit(solution)/shard_map/all_gather | solution.py:247
  158.8 8.5 %all_gather.30 = f32[4,256,32]{2,0,1:T(4,128)S(1)} all-gather(f32[4,64,32]{2,0,1:T(4,128)S(1)} %copy.86), channel_id=1, replica_groups=mesh['gz'=2,'row'=4,'col'=4] {'row'}, dimensions={1}, use_global_device_ids=true | all-gather | bytes 163840 | tf_op jit(solution)/shard_map/all_gather | solution.py:130
  167.4 2.3 %convolution_bitcast_fusion = f32[1,4,256,32]{2,3,1,0:T(8,128)S(1)} fusion(f32[4,4,256,256]{3,2,1,0:T(8,128)} %param.13, f32[4,256,32]{2,0,1:T(4,128)S(1)} %all_gather.30), kind=kOutput, calls=%fused_computation | convolution fusion | flops 100663296 | bytes 1310720 | tf_op jit(solution)/shard_map/jvw,jwk->jvk/dot_general | solution.py:131
  171.5 6.2 %all-gather.5.cloned.1.call-done = f32[4,4,256,64]{2,3,1,0:T(8,128)} async-done(((f32[4,4,256,32]{2,3,1,0:T(8,128)}), f32[4,4,256,64]{2,3,1,0:T(8,128)}) %all-gather.5.cloned.1.call-update) | async-done | bytes 1048592 | tf_op jit(solution)/shard_map/all_gather | solution.py:252
  181.4 8.7 %all-gather.3.cloned.1.call-done = f32[4,4,256,64]{2,3,1,0:T(8,128)} async-done(((f32[4,4,256,32]{2,3,1,0:T(8,128)}), f32[4,4,256,64]{2,3,1,0:T(8,128)}) %all-gather.3.cloned.1.call-update) | async-done | bytes 1048592 | tf_op jit(solution)/shard_map/all_gather | solution.py:251
  (120 shorter events, 54.3 us)
Async XLA Ops:
  7.2 170.6 %all-gather.5.cloned.1.call-start = ((), (), s32[]{:S(2)}) async-start(), calls=%async_computation.1 | async-start | bytes 1572864 | tf_op jit(solution)/shard_map/all_gather | solution.py:252
  10.5 7.9 %collective-permute-start.7 = (f32[64,128]{1,0:T(8,128)S(1)}, f32[64,128]{1,0:T(8,128)S(1)}, u32[]{:S(2)}, u32[]{:S(2)}) collective-permute-start(f32[64,128]{1,0:T(8,128)S(1)} %copy.53), channel_id=1, source_target_pairs={{0,28},{4,24},{8,20},{12,16},{16,12},{20,8},{24,4},{28,0},{1,29},{... | collective-permute-start | bytes 98312 | tf_op jit(solution)/shard_map/ppermute | solution.py:177
  13.9 6.4 %collective-permute-start.5 = (f32[64,128]{1,0:T(8,128)S(1)}, f32[64,128]{1,0:T(8,128)S(1)}, u32[]{:S(2)}, u32[]{:S(2)}) collective-permute-start(f32[64,128]{1,0:T(8,128)S(1)} %copy.53), channel_id=1, source_target_pairs={{0,24},{4,28},{8,16},{12,20},{16,8},{20,12},{24,0},{28,4},{1,25},{... | collective-permute-start | bytes 98312 | tf_op jit(solution)/shard_map/ppermute | solution.py:177
  14.7 7.6 %collective-permute-start.3 = (f32[64,128]{1,0:T(8,128)S(1)}, f32[64,128]{1,0:T(8,128)S(1)}, u32[]{:S(2)}, u32[]{:S(2)}) collective-permute-start(f32[64,128]{1,0:T(8,128)S(1)} %copy.53), channel_id=1, source_target_pairs={{0,20},{4,16},{8,28},{12,24},{16,4},{20,0},{24,12},{28,8},{1,21},{... | collective-permute-start | bytes 98312 | tf_op jit(solution)/shard_map/ppermute | solution.py:177
  14.8 4.0 %collective-permute-start.1 = (f32[64,128]{1,0:T(8,128)S(1)}, f32[64,128]{1,0:T(8,128)S(1)}, u32[]{:S(2)}, u32[]{:S(2)}) collective-permute-start(f32[64,128]{1,0:T(8,128)S(1)} %copy.53), channel_id=1, source_target_pairs={{0,16},{4,20},{8,24},{12,28},{16,0},{20,4},{24,8},{28,12},{1,17},{... | collective-permute-start | bytes 98312 | tf_op jit(solution)/shard_map/ppermute | solution.py:177
  15.3 4.9 %collective-permute-start.6 = (f32[64,128]{1,0:T(8,128)S(1)}, f32[64,128]{1,0:T(8,128)S(1)}, u32[]{:S(2)}, u32[]{:S(2)}) collective-permute-start(f32[64,128]{1,0:T(8,128)S(1)} %copy.54), channel_id=1, source_target_pairs={{0,12},{4,8},{8,4},{12,0},{16,28},{20,24},{24,20},{28,16},{1,13},{... | collective-permute-start | bytes 98312 | tf_op jit(solution)/shard_map/ppermute | solution.py:177
  18.4 3.9 %collective-permute-start.4 = (f32[64,128]{1,0:T(8,128)S(1)}, f32[64,128]{1,0:T(8,128)S(1)}, u32[]{:S(2)}, u32[]{:S(2)}) collective-permute-start(f32[64,128]{1,0:T(8,128)S(1)} %copy.54), channel_id=1, source_target_pairs={{0,8},{4,12},{8,0},{12,4},{16,24},{20,28},{24,16},{28,20},{1,9},{5... | collective-permute-start | bytes 98312 | tf_op jit(solution)/shard_map/ppermute | solution.py:177
  18.9 3.9 %collective-permute-start.2 = (f32[64,128]{1,0:T(8,128)S(1)}, f32[64,128]{1,0:T(8,128)S(1)}, u32[]{:S(2)}, u32[]{:S(2)}) collective-permute-start(f32[64,128]{1,0:T(8,128)S(1)} %copy.54), channel_id=1, source_target_pairs={{0,4},{4,0},{8,12},{12,8},{16,20},{20,16},{24,28},{28,24},{1,5},{5... | collective-permute-start | bytes 98312 | tf_op jit(solution)/shard_map/ppermute | solution.py:177
  20.2 11.0 %collective-permute-start = (f32[3,64,128]{2,1,0:T(8,128)S(1)}, f32[3,64,128]{2,1,0:T(8,128)S(1)}, u32[]{:S(2)}, u32[]{:S(2)}) collective-permute-start(f32[3,64,128]{2,1,0:T(8,128)S(1)} %copy.51), channel_id=1, source_target_pairs={{0,16},{16,0},{1,17},{17,1},{2,18},{18,2},{3,19},{19,3},{4,20},{20... | collective-permute-start | bytes 294920 | tf_op jit(solution)/shard_map/ppermute | solution.py:27
  26.6 4.7 %collective-permute-start.8 = (f32[64,128]{1,0:T(8,128)S(1)}, f32[64,128]{1,0:T(8,128)S(1)}, u32[]{:S(2)}, u32[]{:S(2)}) collective-permute-start(f32[64,128]{1,0:T(8,128)S(1)} %get-tuple-element.21), channel_id=1, source_target_pairs={{0,1},{1,0},{2,3},{3,2},{4,5},{5,4},{6,7},{7,6},{8,9},{9,8},{10,11... | collective-permute-start | bytes 98312 | tf_op jit(solution)/shard_map/ppermute | solution.py:27
  28.3 5.4 %collective-permute-start.9 = (f32[64,128]{1,0:T(8,128)S(1)}, f32[64,128]{1,0:T(8,128)S(1)}, u32[]{:S(2)}, u32[]{:S(2)}) collective-permute-start(f32[64,128]{1,0:T(8,128)S(1)} %get-tuple-element.22), channel_id=1, source_target_pairs={{0,2},{1,3},{2,0},{3,1},{4,6},{5,7},{6,4},{7,5},{8,10},{9,11},{10,... | collective-permute-start | bytes 98312 | tf_op jit(solution)/shard_map/ppermute | solution.py:27
  30.8 5.7 %collective-permute-start.10 = (f32[64,128]{1,0:T(8,128)S(1)}, f32[64,128]{1,0:T(8,128)S(1)}, u32[]{:S(2)}, u32[]{:S(2)}) collective-permute-start(f32[64,128]{1,0:T(8,128)S(1)} %get-tuple-element.23), channel_id=1, source_target_pairs={{0,3},{1,2},{2,1},{3,0},{4,7},{5,6},{6,5},{7,4},{8,11},{9,10},{10,... | collective-permute-start | bytes 98312 | tf_op jit(solution)/shard_map/ppermute | solution.py:27
  36.6 4.9 %collective-permute-start.13 = (f32[64,128]{1,0:T(8,128)S(1)}, f32[64,128]{1,0:T(8,128)S(1)}, u32[]{:S(2)}, u32[]{:S(2)}) collective-permute-start(f32[64,128]{1,0:T(8,128)S(1)} %fusion.59.refs_0_), channel_id=1, source_target_pairs={{0,12},{4,8},{8,4},{12,0},{1,13},{5,9},{9,5},{13,1},{2,14},{6,10},... | collective-permute-start | bytes 98312 | tf_op jit(solution)/shard_map/ppermute | solution.py:27
  38.1 3.9 %collective-permute-start.12 = (f32[64,128]{1,0:T(8,128)S(1)}, f32[64,128]{1,0:T(8,128)S(1)}, u32[]{:S(2)}, u32[]{:S(2)}) collective-permute-start(f32[64,128]{1,0:T(8,128)S(1)} %fusion.59.refs_0_), channel_id=1, source_target_pairs={{0,8},{4,12},{8,0},{12,4},{1,9},{5,13},{9,1},{13,5},{2,10},{6,14},... | collective-permute-start | bytes 98312 | tf_op jit(solution)/shard_map/ppermute | solution.py:27
  38.9 3.9 %collective-permute-start.11 = (f32[64,128]{1,0:T(8,128)S(1)}, f32[64,128]{1,0:T(8,128)S(1)}, u32[]{:S(2)}, u32[]{:S(2)}) collective-permute-start(f32[64,128]{1,0:T(8,128)S(1)} %fusion.59.refs_0_), channel_id=1, source_target_pairs={{0,4},{4,0},{8,12},{12,8},{1,5},{5,1},{9,13},{13,9},{2,6},{6,2},{1... | collective-permute-start | bytes 98312 | tf_op jit(solution)/shard_map/ppermute | solution.py:27
  46.6 4.5 %collective-permute-start.14 = (f32[64,128]{1,0:T(8,128)S(1)}, f32[64,128]{1,0:T(8,128)S(1)}, u32[]{:S(2)}, u32[]{:S(2)}) collective-permute-start(f32[64,128]{1,0:T(8,128)S(1)} %get-tuple-element.27), channel_id=1, source_target_pairs={{0,1},{1,0},{2,3},{3,2},{4,5},{5,4},{6,7},{7,6},{8,9},{9,8},{10,11... | collective-permute-start | bytes 98312 | tf_op jit(solution)/shard_map/ppermute | solution.py:27
  46.6 4.9 %collective-permute-start.15 = (f32[64,128]{1,0:T(8,128)S(1)}, f32[64,128]{1,0:T(8,128)S(1)}, u32[]{:S(2)}, u32[]{:S(2)}) collective-permute-start(f32[64,128]{1,0:T(8,128)S(1)} %get-tuple-element.28), channel_id=1, source_target_pairs={{0,2},{1,3},{2,0},{3,1},{4,6},{5,7},{6,4},{7,5},{8,10},{9,11},{10,... | collective-permute-start | bytes 98312 | tf_op jit(solution)/shard_map/ppermute | solution.py:27
  47.5 5.7 %collective-permute-start.16 = (f32[64,128]{1,0:T(8,128)S(1)}, f32[64,128]{1,0:T(8,128)S(1)}, u32[]{:S(2)}, u32[]{:S(2)}) collective-permute-start(f32[64,128]{1,0:T(8,128)S(1)} %get-tuple-element.29), channel_id=1, source_target_pairs={{0,3},{1,2},{2,1},{3,0},{4,7},{5,6},{6,5},{7,4},{8,11},{9,10},{10,... | collective-permute-start | bytes 98312 | tf_op jit(solution)/shard_map/ppermute | solution.py:27
  53.3 4.9 %collective-permute-start.19 = (f32[64,128]{1,0:T(8,128)S(1)}, f32[64,128]{1,0:T(8,128)S(1)}, u32[]{:S(2)}, u32[]{:S(2)}) collective-permute-start(f32[64,128]{1,0:T(8,128)S(1)} %fusion.63.refs_0_), channel_id=1, source_target_pairs={{0,12},{4,8},{8,4},{12,0},{1,13},{5,9},{9,5},{13,1},{2,14},{6,10},... | collective-permute-start | bytes 98312 | tf_op jit(solution)/shard_map/ppermute | solution.py:27
  61.3 4.7 %collective-permute-start.20 = (f32[64,128]{1,0:T(8,128)S(1)}, f32[64,128]{1,0:T(8,128)S(1)}, u32[]{:S(2)}, u32[]{:S(2)}) collective-permute-start(f32[64,128]{1,0:T(8,128)S(1)} %get-tuple-element.32), channel_id=1, source_target_pairs={{0,1},{1,0},{2,3},{3,2},{4,5},{5,4},{6,7},{7,6},{8,9},{9,8},{10,11... | collective-permute-start | bytes 98312 | tf_op jit(solution)/shard_map/ppermute | solution.py:27
  61.6 5.7 %collective-permute-start.21 = (f32[64,128]{1,0:T(8,128)S(1)}, f32[64,128]{1,0:T(8,128)S(1)}, u32[]{:S(2)}, u32[]{:S(2)}) collective-permute-start(f32[64,128]{1,0:T(8,128)S(1)} %get-tuple-element.33), channel_id=1, source_target_pairs={{0,2},{1,3},{2,0},{3,1},{4,6},{5,7},{6,4},{7,5},{8,10},{9,11},{10,... | collective-permute-start | bytes 98312 | tf_op jit(solution)/shard_map/ppermute | solution.py:27
  65.4 5.7 %collective-permute-start.22 = (f32[64,128]{1,0:T(8,128)S(1)}, f32[64,128]{1,0:T(8,128)S(1)}, u32[]{:S(2)}, u32[]{:S(2)}) collective-permute-start(f32[64,128]{1,0:T(8,128)S(1)} %get-tuple-element.34), channel_id=1, source_target_pairs={{0,3},{1,2},{2,1},{3,0},{4,7},{5,6},{6,5},{7,4},{8,11},{9,10},{10,... | collective-permute-start | bytes 98312 | tf_op jit(solution)/shard_map/ppermute | solution.py:27
  71.1 4.9 %collective-permute-start.25 = (f32[64,128]{1,0:T(8,128)S(1)}, f32[64,128]{1,0:T(8,128)S(1)}, u32[]{:S(2)}, u32[]{:S(2)}) collective-permute-start(f32[64,128]{1,0:T(8,128)S(1)} %fusion.67.refs_0_), channel_id=1, source_target_pairs={{0,12},{4,8},{8,4},{12,0},{1,13},{5,9},{9,5},{13,1},{2,14},{6,10},... | collective-permute-start | bytes 98312 | tf_op jit(solution)/shard_map/ppermute | solution.py:27
  170.6 19.5 %all-gather.3.cloned.1.call-start = ((), (), s32[]{:S(2)}) async-start(), calls=%async_computation | async-start | bytes 1572864 | tf_op jit(solution)/shard_map/all_gather | solution.py:251
  (11 other events, 66.3 us)
Sparse Core Ops, SparseCore 0:
  170.7 6.9 all-gather.4
  179.8 10.1 all-gather.2

commit v2 on v0

v2 whole, which is shorter than its diff:
```python
import functools

import jax
import jax.numpy as jnp
from jax import lax
from jax.experimental import pallas as pl
from jax.experimental.pallas import tpu as pltpu
from jax.sharding import PartitionSpec as P

WIDTH = 256
COLUMNS = 64
LANES = 128
F32 = jnp.float32
BF16 = jnp.bfloat16
SMEM = pl.BlockSpec(memory_space=pltpu.SMEM)
VMEM = pl.BlockSpec(memory_space=pltpu.VMEM)
HBM = pl.BlockSpec(memory_space=pltpu.HBM)
PARAMS = pltpu.CompilerParams(vmem_limit_bytes=24 * 2**20)


def place_of(height, distance):
    return height * (height - 1) // 2 + distance - 1


def shape_of(*dims, dtype=F32):
    return jax.ShapeDtypeStruct(dims, dtype)


def split(value):
    high = value.astype(BF16)
    return high, (value - high.astype(F32)).astype(BF16)


def dot(left, right):
    return jnp.dot(left, right, preferred_element_type=F32)


def dot_t(left, right):
    return lax.dot_general(left, right, (((1,), (1,)), ((), ())), preferred_element_type=F32)


def product(left, right_high, right_both):
    high, low = split(left)
    lanes = right_high.shape[1]
    both = dot(high, right_both)
    return both[:, :lanes] + both[:, lanes:] + dot(low, right_high)


def product_t(left, right_high, right_low):
    high, low = split(left)
    rows = left.shape[0]
    both = dot_t(jnp.concatenate([high, low], axis=0), right_high)
    return both[:rows] + both[rows:] + dot_t(high, right_low)


def gather_all(value, axes, count):
    return lax.all_to_all(jnp.broadcast_to(value[None], (count,) + value.shape), axes, 0, 0)


def input_kernel(gz_count, nodes, own, right, layer, out):
    gz = lax.axis_index("gz")
    tiles = right.shape[1]
    per_tile = LANES // COLUMNS
    block = lax.broadcasted_iota(jnp.int32, (1, LANES), 1) // own
    for level in range(right.shape[0]):
        for which in range(gz_count):
            mine = jnp.where(gz == which, 1.0, 0.0)
            for row in range(per_tile):
                total = jnp.zeros((tiles, LANES), F32)
                for node in range(nodes):
                    value = right[level, :, node, :] * mine - layer[level, :, node, :]
                    shift = (node * own - row * COLUMNS - which * own) % LANES
                    value = pltpu.roll(value, shift, 1) if shift else value
                    total = jnp.where(block == node, value, total)
                out[which, level, pl.ds(row, tiles, stride=per_tile), :] = total


def forward_kernel(height, sizes, *refs):
    nodes, part, own, row_count, col_count = sizes
    lanes = nodes * own
    full, parents, pattern, inverse_hbm = refs[:4]
    if height:
        blocks = refs[4]
        pending_in = refs[5 : 5 + height] if height < 3 else ()
        refs = refs[5 + len(pending_in) :]
        solved_ref, urgent = refs[:2]
        pending_out = refs[2 : 1 + height]
        inverse, sem = refs[1 + height :]
    else:
        other_hbm, solved_ref, next_ref, inverse, other, turned, sem = refs[4:]
        other_copy = pltpu.make_async_copy(other_hbm.at[0], other, sem.at[1])
        other_copy.start()
    copy = pltpu.make_async_copy(inverse_hbm.at[height], inverse, sem.at[0])
    copy.start()
    lane = lax.broadcasted_iota(jnp.int32, (1, lanes), 1) // own
    high, low = split(full[...])
    both = jnp.concatenate([high, low], axis=1)
    solved = jnp.zeros(full.shape, F32)
    copy.wait()
    for node in range(nodes):
        solved = jnp.where(lane == node, product(inverse[node], high, both), solved)
    solved_ref[...] = solved
    if height == 0:
        other_copy.wait()
        turn(solved, turned, other, next_ref, nodes, own, row_count)
        return
    col = lax.axis_index("col")
    high, low = split(solved)
    both = jnp.concatenate([high, low], axis=1)
    targets = []
    for level in range(height):
        target = urgent if level == height - 1 else pending_out[level]
        target[...] = pending_in[level][...] if pending_in else jnp.zeros(target.shape, F32)
        targets.append(target)
    for node in range(nodes):
        ancestor = col * nodes + node
        for distance in range(1, height + 1):
            place = place_of(height, distance)
            level = height - distance
            ancestor = parents[level, ancestor]
            slot = lax.rem(ancestor, nodes)
            term = product(blocks[place, node], high, both)
            term = pltpu.roll(term, lax.rem(slot - node + nodes, nodes) * own, 1)
            keep = jnp.where(pattern[place, node] != 0, slot, -1)
            targets[level][lax.div(ancestor, nodes)] += jnp.where(lane == keep, term, 0.0)


def forward_step(height, full, parents, pattern, inverse, blocks, pending, upper, sizes):
    nodes, part, own, row_count, col_count = sizes
    lanes = nodes * own
    rows = row_count * part
    stack = shape_of(col_count, part, lanes)
    kernel = functools.partial(forward_kernel, height, sizes)
    level_inverse = pltpu.VMEM((nodes, rows, rows), F32)
    if height == 0:
        return pl.pallas_call(
            kernel,
            out_shape=[shape_of(rows, lanes), shape_of(nodes, own // row_count, rows)],
            in_specs=[VMEM, SMEM, SMEM, HBM, HBM],
            out_specs=[VMEM] * 2,
            scratch_shapes=[
                level_inverse,
                level_inverse,
                pltpu.VMEM((lanes, rows), F32),
                pltpu.SemaphoreType.DMA((2,)),
            ],
            compiler_params=PARAMS,
            name="forward_last",
        )(full, parents, pattern, inverse, upper)
    out_shape = [shape_of(rows, lanes), stack] + [stack] * (height - 1)
    return pl.pallas_call(
        kernel,
        out_shape=out_shape,
        in_specs=[VMEM, SMEM, SMEM, HBM, VMEM] + [VMEM] * len(pending),
        out_specs=[VMEM] * len(out_shape),
        scratch_shapes=[level_inverse, pltpu.SemaphoreType.DMA((1,))],
        compiler_params=PARAMS,
        name="forward_level",
    )(full, parents, pattern, inverse, blocks, *pending)


def turn(solved, turned, inverse, out, nodes, own, row_count):
    turned[...] = solved.T
    few = own // row_count
    row = lax.axis_index("row")
    for node in range(nodes):
        start = pl.multiple_of(node * own + row * few, few)
        high, low = split(inverse[node])
        out[node] = product_t(turned[pl.ds(start, few), :], high, low)


def turn_kernel(height, sizes, solved, inverse_hbm, out, inverse, turned, sem):
    nodes, part, own, row_count, col_count = sizes
    copy = pltpu.make_async_copy(inverse_hbm.at[height], inverse, sem)
    copy.start()
    copy.wait()
    turn(solved[...], turned, inverse, out, nodes, own, row_count)


def turn_step(height, solved, inverse, sizes):
    nodes, part, own, row_count, col_count = sizes
    rows = row_count * part
    return pl.pallas_call(
        functools.partial(turn_kernel, height, sizes),
        out_shape=shape_of(nodes, own // row_count, rows),
        in_specs=[VMEM, HBM],
        out_specs=VMEM,
        scratch_shapes=[
            pltpu.VMEM((nodes, rows, rows), F32),
            pltpu.VMEM((nodes * own, rows), F32),
            pltpu.SemaphoreType.DMA,
        ],
        compiler_params=PARAMS,
        name="turn_level",
    )(solved, inverse)


def compose_kernel(nodes, gathered, inverse, high_out, low_out):
    for node in range(nodes):
        block = gathered[:, 0, node].reshape(WIDTH, WIDTH)
        right_high, right_low = split(block)
        high, low = split(inverse[0, node])
        whole = dot(high, right_high) + dot(low, right_high) + dot(high, right_low)
        high, low = split(whole)
        high_out[0, node] = high
        low_out[0, node] = low


def compose_step(height, gathered, inverse, row_count):
    per, nodes = gathered.shape[1:3]
    part = gathered.shape[3]
    first = place_of(height, 1)
    out = shape_of(height, nodes, WIDTH, WIDTH, dtype=BF16)
    out_spec = pl.BlockSpec((1, nodes, WIDTH, WIDTH), lambda i: (i, 0, 0, 0))
    return pl.pallas_call(
        functools.partial(compose_kernel, nodes),
        grid=(height,),
        out_shape=[out, out],
        in_specs=[
            pl.BlockSpec(
                (row_count, 1, nodes, part, WIDTH),
                lambda i: ((first + i) // per, (first + i) % per, 0, 0, 0),
            ),
            pl.BlockSpec((1, nodes, WIDTH, WIDTH), lambda i: (height, 0, 0, 0)),
        ],
        out_specs=[out_spec] * 2,
        compiler_params=PARAMS,
        cost_estimate=pl.CostEstimate(
            flops=6 * height * nodes * WIDTH**3,
            bytes_accessed=12 * height * nodes * WIDTH**2,
            transcendentals=0,
        ),
        name="compose_level",
    )(gathered, inverse)


def backward_kernel(height, nodes, parents, pattern, start, high, low, *refs):
    solved, out = refs[:height], refs[height]
    col = lax.axis_index("col")
    for node in range(nodes):
        total = start[node]
        ancestor = col * nodes + node
        for distance in range(1, height + 1):
            level = height - distance
            ancestor = parents[level, ancestor]
            value = solved[level][lax.div(ancestor, nodes), lax.rem(ancestor, nodes)]
            term = product_t(value, high[distance - 1, node], low[distance - 1, node])
            stored = pattern[place_of(height, distance), node] != 0
            total = total - jnp.where(stored, term, 0.0)
        out[node] = total


def backward_step(height, parents, pattern, start, composed, solved):
    return pl.pallas_call(
        functools.partial(backward_kernel, height, start.shape[0]),
        out_shape=shape_of(*start.shape),
        in_specs=[SMEM, SMEM] + [VMEM] * (3 + height),
        out_specs=VMEM,
        compiler_params=PARAMS,
        name="backward_level",
    )(parents, pattern, start, *composed, *solved)


def forward_out_kernel(gz_count, nodes, own, gathered, out):
    per_tile = LANES // COLUMNS
    tiles = out.shape[1]
    block = lax.broadcasted_iota(jnp.int32, (1, LANES), 1) // own
    for node in range(nodes):
        total = jnp.zeros((tiles, LANES), F32)
        for row in range(per_tile):
            for which in range(gz_count):
                value = gathered[which, 0, pl.ds(row, tiles, stride=per_tile), :]
                place = row * gz_count + which
                shift = ((place - node) * own) % LANES
                value = pltpu.roll(value, shift, 1) if shift else value
                total = jnp.where(block == place, value, total)
        out[0, :, node, :] = total


def backward_out_kernel(nodes, gathered, *refs):
    out, turned = refs[-2:]
    per_tile = LANES // COLUMNS
    tiles = out.shape[1]
    for node in range(nodes):
        turned[...] = gathered[:, 0, node].reshape(COLUMNS, WIDTH).T
        rows = [turned[pl.ds(row, tiles, stride=per_tile), :] for row in range(per_tile)]
        out[0, :, node, :] = jnp.concatenate(rows, axis=1)


def backward_out(gathered, before, first, nodes):
    count, levels, nodes, few, rows = gathered.shape
    tiles = rows * COLUMNS // LANES
    ready = [before] if before is not None else []
    return pl.pallas_call(
        functools.partial(backward_out_kernel, nodes),
        grid=(levels,),
        out_shape=shape_of(4, tiles, nodes, LANES),
        in_specs=[pl.BlockSpec((count, 1, nodes, few, rows), lambda i: (0, i, 0, 0, 0))]
        + [HBM] * len(ready),
        out_specs=pl.BlockSpec((1, tiles, nodes, LANES), lambda i: (first + i, 0, 0, 0)),
        scratch_shapes=[pltpu.VMEM((rows, COLUMNS), F32)],
        input_output_aliases={1: 0} if ready else {},
        compiler_params=PARAMS,
        name="backward_out",
    )(gathered, *ready)


def body(
    right_side,
    layer_sums,
    lower_blocks,
    upper_blocks,
    lower_inverse,
    upper_diagonal_inverses,
    pattern,
    parents,
):
    nodes = right_side.shape[1]
    part = lower_blocks.shape[2]
    gz_count = lax.axis_size("gz")
    row_count = lax.axis_size("row")
    col_count = lax.axis_size("col")
    own = COLUMNS // gz_count
    lanes = nodes * own
    layer_count = gz_count * row_count
    sizes = (nodes, part, own, row_count, col_count)
    gz = lax.axis_index("gz")

    per = upper_blocks.shape[0] // gz_count
    upper_rows = lax.all_gather(
        lax.dynamic_slice_in_dim(upper_blocks, gz * per, per, 0), ("gz", "row")
    )

    def tiled(value):
        return value.reshape(4, nodes, part * COLUMNS // LANES, LANES).transpose(0, 2, 1, 3)

    parts = pl.pallas_call(
        functools.partial(input_kernel, gz_count, nodes, own),
        out_shape=shape_of(gz_count, 4, part, lanes),
        in_specs=[VMEM, VMEM],
        out_specs=VMEM,
        compiler_params=PARAMS,
        name="input_parts",
    )(tiled(right_side), tiled(layer_sums[0]))

    top = jnp.broadcast_to(parts[:, None, 3], (gz_count, row_count, part, lanes))
    top = lax.all_to_all(top.reshape(layer_count, part, lanes), ("gz", "row"), 0, 0)
    full = top.reshape(gz_count, row_count * part, lanes).sum(0)
    rest = lax.all_to_all(parts[:, :3], "gz", 0, 0).sum(0)

    forward = [None] * 4
    pending = []
    for height in (3, 2, 1, 0):
        if height < 3:
            mine = rest[height] - lax.all_to_all(urgent, "col", 0, 0).sum(0)
            full = gather_all(mine, "row", row_count).reshape(row_count * part, lanes)
        results = forward_step(
            height,
            full,
            parents,
            pattern,
            lower_inverse,
            lower_blocks,
            pending,
            upper_diagonal_inverses,
            sizes,
        )
        forward[height], urgent, pending = results[0], results[1], results[2:]

    backward = [urgent, None, None, None]
    whole = []
    for height in (1, 2, 3):
        composed = compose_step(height, upper_rows, upper_diagonal_inverses, row_count)
        start = turn_step(height, forward[height], upper_diagonal_inverses, sizes)
        whole.append(gather_all(backward[height - 1], "col", col_count))
        backward[height] = backward_step(height, parents, pattern, start, composed, whole)

    tiles = WIDTH * COLUMNS // LANES
    forward_all = lax.all_gather(jnp.stack(forward), "gz")
    forward_all = pl.pallas_call(
        functools.partial(forward_out_kernel, gz_count, nodes, own),
        grid=(4,),
        out_shape=shape_of(4, tiles, nodes, LANES),
        in_specs=[pl.BlockSpec((gz_count, 1, WIDTH, lanes), lambda i: (0, i, 0, 0))],
        out_specs=pl.BlockSpec((1, tiles, nodes, LANES), lambda i: (i, 0, 0, 0)),
        compiler_params=PARAMS,
        name="forward_out",
    )(forward_all)
    early = lax.all_gather(jnp.stack(backward[:3]), ("gz", "row"))
    backward_all = backward_out(early, None, 0, nodes)
    late = gather_all(backward[3][None], ("gz", "row"), layer_count)
    backward_all = backward_out(late, backward_all, 3, nodes)
    return tuple(
        value.transpose(0, 2, 1, 3).reshape(4, nodes, WIDTH * COLUMNS)
        for value in (forward_all, backward_all)
    )


def solution(mesh):
    in_specs = (
        P(None, "col", "row"),
        P("gz", None, "col", "row"),
        P(None, "col", "row", None),
        P(None, "col", "row", None),
        P(None, "col", None, None),
        P(None, "col", None, None),
        P(None, "col"),
        P(),
    )
    out_specs = (P(None, "col", None), P(None, "col", None))
    return jax.shard_map(body, mesh=mesh, in_specs=in_specs, out_specs=out_specs, check_vma=False)
```

time: 305 us -> 211 us (0.69)
  waiting for transfers between devices: 113 us -> 11.8 us
  blocking collectives: 125 us -> 69.4 us
  starting transfers between devices: 0.25 us -> 31.9 us
  local copies, waits for them, and re-layouts: 19.8 us -> 50.3 us
  matrix products: 29 us -> 0 us
  Pallas kernels: 0 us -> 22.6 us
  other arithmetic: 2.47 us -> 8.5 us
    all_gather x11 -> x1, blocking collectives: 125 us -> 28.5 us  [body(): early = lax.all_gather(jnp.stack(backward[:3]), ('gz', 'row'))]
    unnamed x9 -> x2, waiting for transfers between devices: 89.7 us -> 0.03 us
    unnamed x21 -> x75, local copies, waits for them, and re-layouts: 3.64 us -> 45.2 us
    all_to_all x0 -> x5, blocking collectives: none -> 40.9 us  [the longest x3 23.6 us: gather_all(): lax.all_to_all(jnp.broadcast_to(value[None], (count,) + value.shape), axe...]
    all_to_all x0 -> x7, starting transfers between devices: none -> 31.8 us  [the longest x4 16.9 us: gather_all(): lax.all_to_all(jnp.broadcast_to(value[None], (count,) + value.shape), axe...]
    dot_general x32 -> x0, matrix products: 29 us -> none  [the longest x8 18.7 us: solve_nodes(): jnp.einsum('jvw,jwk->jvk', inverse, full_rows, precision=lax.Precision.HI...]
    pallas_call x0 -> x17, Pallas kernels: none -> 22.6 us  [the longest x3 4.75 us: forward_step(): pl.pallas_call(kernel, out_shape=out_shape, in_specs=[VMEM, SMEM, SMEM, H...]
    reduce_scatter x1 -> x0, waiting for transfers between devices: 19.2 us -> none  [body(): lax.psum_scatter(jnp.stack(summand_terms, 1), 'col', scatter_dimension=0,...]
  transfers between devices with their start and end apart: 6 -> 9, of which waited for: 5 -> 2; matrix products, arithmetic and copies ran while one was open for 3% -> 5% of each run, Pallas kernels for 0% -> 9%
where the time goes in v2:
time: 211 us; the launch traced here: 209 us
  blocking collectives  69.4 us (33%)
  local copies, waits for them, and re-layouts  50.3 us (24%)
  starting transfers between devices  31.9 us (15%)
  Pallas kernels  22.6 us (11%)
  between operations  14.4 us (7%)
  waiting for transfers between devices  11.8 us (6%)
  other arithmetic  8.5 us (4%)
    unnamed x75, local copies, waits for them, and re-layouts  45.2 us
    all_gather x1, blocking collectives, body(): early = lax.all_gather(jnp.stack(backward[:3]), ('gz', 'row'))  28.5 us
    all_to_all x3, blocking collectives, gather_all(): lax.all_to_all(jnp.broadcast_to(value[None], (count,) + value.shape), axe...  23.6 us
    all_to_all x2, blocking collectives, body(): mine = rest[height] - lax.all_to_all(urgent, 'col', 0, 0).sum(0)  17.3 us
    all_to_all x4, starting transfers between devices, gather_all(): lax.all_to_all(jnp.broadcast_to(value[None], (count,) + value.shape), axe...  16.9 us
    all_to_all x1, waiting for transfers between devices, body(): lax.all_to_all(top.reshape(layer_count, part, lanes), ('gz', 'row'), 0, 0)  6.71 us
    all_to_all x1, starting transfers between devices, body(): mine = rest[height] - lax.all_to_all(urgent, 'col', 0, 0).sum(0)  5.72 us
    all_to_all x1, starting transfers between devices, body(): lax.all_to_all(top.reshape(layer_count, part, lanes), ('gz', 'row'), 0, 0)  5.17 us
  transfers between devices with their start and end apart: 9, of which 2 were waited for; matrix products, arithmetic and copies ran while one was open for 5% of the time, Pallas kernels for 9%

profile of v2, /device:TPU:0, one launch (start us, length us, event | category | flops | bytes accessed | tf_op | source)
XLA Modules:
  0.0 208.9 jit_solution(3958274050329974232)
XLA Ops:
  13.4 5.2 %all-to-all-start.1 = ((f32[8,64,128]{2,1,0:T(8,128)}), f32[8,64,128]{2,1,0:T(8,128)}, u32[]{:S(2)}, u32[]{:S(2)}) async-start(f32[8,64,128]{2,1,0:T(8,128)} %bitcast.61), calls=%async_computation.1 | async-start | bytes 524288 | tf_op jit(solution)/shard_map/all_to_all | solution.py:347
  19.3 6.7 %all-to-all-done.1 = f32[8,64,128]{2,1,0:T(8,128)} async-done(((f32[8,64,128]{2,1,0:T(8,128)}), f32[8,64,128]{2,1,0:T(8,128)}, u32[]{:S(2)}, u32[]{:S(2)}) %all-to-all-start.1) | async-done | bytes 262176 | tf_op jit(solution)/shard_map/all_to_all | solution.py:347
  26.0 4.1 %all-to-all-start = ((f32[2,3,64,128]{3,2,1,0:T(8,128)}), f32[2,3,64,128]{3,2,1,0:T(8,128)}, u32[]{:S(2)}, u32[]{:S(2)}) async-start(f32[2,3,64,128]{3,2,1,0:T(8,128)} %slice.20), calls=%async_computation | async-start | bytes 393216 | tf_op jit(solution)/shard_map/all_to_all | solution.py:349
  35.7 5.7 %all-to-all-start.2 = ((f32[4,64,128]{2,1,0:T(8,128)}), f32[4,64,128]{2,1,0:T(8,128)}, u32[]{:S(2)}, u32[]{:S(2)}) async-start(f32[4,64,128]{2,1,0:T(8,128)} %copy-done.32), calls=%async_computation.2 | async-start | bytes 262144 | tf_op jit(solution)/shard_map/all_to_all | solution.py:355
  43.0 5.0 %all-to-all-done.2 = f32[4,64,128]{2,1,0:T(8,128)} async-done(((f32[4,64,128]{2,1,0:T(8,128)}), f32[4,64,128]{2,1,0:T(8,128)}, u32[]{:S(2)}, u32[]{:S(2)}) %all-to-all-start.2) | async-done | bytes 131104 | tf_op jit(solution)/shard_map/all_to_all | solution.py:355
  50.3 8.6 %all_to_all.60 = f32[4,64,128]{2,1,0:T(8,128)S(1)} all-to-all(f32[4,64,128]{2,1,0:T(8,128)S(1)} %broadcast_in_dim.63), channel_id=1, replica_groups=mesh['gz'=2,'row'=4,'col'=4] {'row'}, dimensions={0} | all-to-all | bytes 262144 | tf_op jit(solution)/shard_map/all_to_all | solution.py:57
  59.0 2.3 %copy-done.8 = f32[4,4,256,256]{3,2,1,0:T(8,128)S(1)} copy-done((f32[4,4,256,256]{3,2,1,0:T(8,128)S(1)}, f32[4,4,256,256]{3,2,1,0:T(8,128)}, u32[]{:S(2)}) %copy-start.8) | copy-done | bytes 4194328
  64.4 8.9 %all_to_all.61 = f32[4,64,128]{2,1,0:T(8,128)S(1)} all-to-all(f32[4,64,128]{2,1,0:T(8,128)S(1)} %get-tuple-element.22), channel_id=1, replica_groups=mesh['gz'=2,'row'=4,'col'=4] {'col'}, dimensions={0} | all-to-all | bytes 262144 | tf_op jit(solution)/shard_map/all_to_all | solution.py:355
  74.8 7.6 %all_to_all.62 = f32[4,64,128]{2,1,0:T(8,128)S(1)} all-to-all(f32[4,64,128]{2,1,0:T(8,128)S(1)} %broadcast_in_dim.65), channel_id=1, replica_groups=mesh['gz'=2,'row'=4,'col'=4] {'row'}, dimensions={0} | all-to-all | bytes 262144 | tf_op jit(solution)/shard_map/all_to_all | solution.py:57
  82.3 2.2 %copy-done.9 = f32[4,4,256,256]{3,2,1,0:T(8,128)S(1)} copy-done((f32[4,4,256,256]{3,2,1,0:T(8,128)S(1)}, f32[4,4,256,256]{3,2,1,0:T(8,128)}, u32[]{:S(2)}) %copy-start.9) | copy-done | bytes 4194328
  86.9 8.4 %all_to_all.63 = f32[4,64,128]{2,1,0:T(8,128)S(1)} all-to-all(f32[4,64,128]{2,1,0:T(8,128)S(1)} %get-tuple-element.24), channel_id=1, replica_groups=mesh['gz'=2,'row'=4,'col'=4] {'col'}, dimensions={0} | all-to-all | bytes 262144 | tf_op jit(solution)/shard_map/all_to_all | solution.py:355
  96.1 7.4 %all_to_all.64 = f32[4,64,128]{2,1,0:T(8,128)S(1)} all-to-all(f32[4,64,128]{2,1,0:T(8,128)S(1)} %broadcast_in_dim.67), channel_id=1, replica_groups=mesh['gz'=2,'row'=4,'col'=4] {'row'}, dimensions={0} | all-to-all | bytes 262144 | tf_op jit(solution)/shard_map/all_to_all | solution.py:57
  103.5 2.2 %copy-done.1 = f32[4,4,256,256]{3,2,1,0:T(8,128)S(1)} copy-done((f32[4,4,256,256]{3,2,1,0:T(8,128)S(1)}, f32[4,4,256,256]{3,2,1,0:T(8,128)}, u32[]{:S(2)}) %copy-start.1) | copy-done | bytes 4194328
  111.0 3.3 %all-to-all-start.8 = ((f32[4,4,8,256]{3,2,1,0:T(8,128)}), f32[4,4,8,256]{3,2,1,0:T(8,128)S(1)}, u32[]{:S(2)}, u32[]{:S(2)}) async-start(f32[4,4,8,256]{3,2,1,0:T(8,128)} %broadcast_in_dim.68), calls=%async_computation.8 | async-start | bytes 262144 | tf_op jit(solution)/shard_map/all_to_all | solution.py:57
  114.4 2.5 %copy-done.2 = f32[4,4,256,256]{3,2,1,0:T(8,128)S(1)} copy-done((f32[4,4,256,256]{3,2,1,0:T(8,128)S(1)}, f32[4,4,256,256]{3,2,1,0:T(8,128)}, u32[]{:S(2)}) %copy-start.2) | copy-done | bytes 4194328
  119.6 2.8 %copy-done.11 = f32[24,4,64,256]{3,2,1,0:T(8,128)S(1)} copy-done((f32[24,4,64,256]{3,2,1,0:T(8,128)S(1)}, f32[24,4,64,256]{3,2,1,0:T(8,128)}, u32[]{:S(2)}) %copy-start.11) | copy-done | bytes 6291480
  124.7 5.0 %all-to-all-start.9 = ((f32[4,4,8,256]{3,2,1,0:T(8,128)}), f32[4,4,8,256]{3,2,1,0:T(8,128)S(1)}, u32[]{:S(2)}, u32[]{:S(2)}) async-start(f32[4,4,8,256]{3,2,1,0:T(8,128)} %broadcast_in_dim.69), calls=%async_computation.9 | async-start | bytes 262144 | tf_op jit(solution)/shard_map/all_to_all | solution.py:57
  134.7 2.4 %forward_out.1 = f32[4,128,4,128]{3,2,1,0:T(4,128)} custom-call(f32[2,4,256,128]{3,2,1,0:T(8,128)S(1)} %bitcast.47), custom_call_target="tpu_custom_call" | custom-call | tf_op jit(solution)/shard_map/forward_out/pallas_call | solution.py:380
  139.3 2.8 %copy-done.12 = f32[24,4,64,256]{3,2,1,0:T(8,128)S(1)} copy-done((f32[24,4,64,256]{3,2,1,0:T(8,128)S(1)}, f32[24,4,64,256]{3,2,1,0:T(8,128)}, u32[]{:S(2)}) %copy-start.12) | copy-done | bytes 6291480
  148.3 5.1 %all-to-all-start.10 = ((f32[4,4,8,256]{3,2,1,0:T(8,128)}), f32[4,4,8,256]{3,2,1,0:T(8,128)S(1)}, u32[]{:S(2)}, u32[]{:S(2)}) async-start(f32[4,4,8,256]{3,2,1,0:T(8,128)} %broadcast_in_dim.70), calls=%async_computation.10 | async-start | bytes 262144 | tf_op jit(solution)/shard_map/all_to_all | solution.py:57
  155.6 2.8 %copy-done.13 = f32[24,4,64,256]{3,2,1,0:T(8,128)S(1)} copy-done((f32[24,4,64,256]{3,2,1,0:T(8,128)S(1)}, f32[24,4,64,256]{3,2,1,0:T(8,128)}, u32[]{:S(2)}) %copy-start.13) | copy-done | bytes 6291480
  166.8 3.4 %all-to-all-start.11 = ((f32[8,1,4,8,256]{4,3,2,1,0:T(8,128)}), f32[8,1,4,8,256]{4,3,2,1,0:T(8,128)S(1)}, u32[]{:S(2)}, u32[]{:S(2)}) async-start(f32[8,1,4,8,256]{4,3,2,1,0:T(8,128)} %broadcast_in_dim.71), calls=%async_computation.11 | async-start | bytes 524288 | tf_op jit(solution)/shard_map/all_to_all | solution.py:57
  170.2 28.5 %all-gather.2 = f32[24,4,8,256]{3,2,1,0:T(8,128)S(1)} all-gather(f32[3,4,8,256]{3,2,1,0:T(8,128)} %pad_maximum_fusion.1), channel_id=4, replica_groups=mesh['gz'=2,'row'=4,'col'=4] {'gz','row'}, dimensions={0}, use_global_device_ids=true | all-gather | bytes 884736 | tf_op jit(solution)/shard_map/all_gather | solution.py:389
  198.7 2.2 %backward_out.2.refs_0_ = f32[4,128,4,128]{3,2,1,0:T(4,128)} custom-call(f32[8,3,4,8,256]{4,3,2,1,0:T(8,128)S(1)} %bitcast.46), custom_call_target="tpu_custom_call" | custom-call | tf_op jit(solution)/shard_map/backward_out/pallas_call | solution.py:294
  (115 shorter events, 59.4 us)
Async XLA Ops:
  7.2 110.2 %all-gather.8.cloned.1.call-start = ((), (), s32[]{:S(2)}) async-start(), calls=%async_computation.13 | async-start | bytes 7077888 | tf_op jit(solution)/shard_map/all_gather | solution.py:330
  9.5 9.7 %copy-start.36 = (s32[6,4]{0,1:T(4,128)S(1)}, s32[6,4]{0,1:T(4,128)}, u32[]{:S(2)}) copy-start(s32[6,4]{0,1:T(4,128)} %param.14) | copy-start | bytes 292
  9.5 21.6 %copy-start.35 = (s32[3,16]{1,0:T(4,128)S(1)}, s32[3,16]{1,0:T(4,128)}, u32[]{:S(2)}) copy-start(s32[3,16]{1,0:T(4,128)} %parents.5) | copy-start | bytes 580
  9.6 21.6 %copy-start.14 = (f32[6,4,64,256]{3,2,1,0:T(8,128)S(1)}, f32[6,4,64,256]{3,2,1,0:T(8,128)}, u32[]{:S(2)}) copy-start(f32[6,4,64,256]{3,2,1,0:T(8,128)} %refs_4_.6) | copy-start | bytes 4718596
  13.4 12.7 %all-to-all-start.1 = ((f32[8,64,128]{2,1,0:T(8,128)}), f32[8,64,128]{2,1,0:T(8,128)}, u32[]{:S(2)}, u32[]{:S(2)}) async-start(f32[8,64,128]{2,1,0:T(8,128)} %bitcast.61), calls=%async_computation.1 | async-start | bytes 524288 | tf_op jit(solution)/shard_map/all_to_all | solution.py:347
  26.0 9.7 %all-to-all-start = ((f32[2,3,64,128]{3,2,1,0:T(8,128)}), f32[2,3,64,128]{3,2,1,0:T(8,128)}, u32[]{:S(2)}, u32[]{:S(2)}) async-start(f32[2,3,64,128]{3,2,1,0:T(8,128)} %slice.20), calls=%async_computation | async-start | bytes 393216 | tf_op jit(solution)/shard_map/all_to_all | solution.py:349
  31.1 2.2 %copy-start.7 = (f32[4,4,256,256]{3,2,1,0:T(8,128)S(1)}, f32[4,4,256,256]{3,2,1,0:T(8,128)}, u32[]{:S(2)}) copy-start(f32[4,4,256,256]{3,2,1,0:T(8,128)} %refs_3_.7) | copy-start | bytes 12582916
  35.7 23.3 %copy-start.28 = (f32[4,64,128]{2,1,0:T(8,128)}, f32[4,64,128]{2,1,0:T(8,128)S(1)}, u32[]{:S(2)}) copy-start(f32[4,64,128]{2,1,0:T(8,128)S(1)} %get-tuple-element.21.refs_6_) | copy-start | bytes 393220
  35.7 12.3 %all-to-all-start.2 = ((f32[4,64,128]{2,1,0:T(8,128)}), f32[4,64,128]{2,1,0:T(8,128)}, u32[]{:S(2)}, u32[]{:S(2)}) async-start(f32[4,64,128]{2,1,0:T(8,128)} %copy-done.32), calls=%async_computation.2 | async-start | bytes 262144 | tf_op jit(solution)/shard_map/all_to_all | solution.py:355
  41.4 92.1 %all-gather.6.cloned.1.call-start = ((), (), s32[]{:S(2)}) async-start(), calls=%async_computation.12 | async-start | bytes 1572864 | tf_op jit(solution)/shard_map/all_gather | solution.py:379
  59.0 2.3 %copy-start.8 = (f32[4,4,256,256]{3,2,1,0:T(8,128)S(1)}, f32[4,4,256,256]{3,2,1,0:T(8,128)}, u32[]{:S(2)}) copy-start(f32[4,4,256,256]{3,2,1,0:T(8,128)} %refs_3_.7) | copy-start | bytes 12582916
  82.3 2.2 %copy-start.9 = (f32[4,4,256,256]{3,2,1,0:T(8,128)S(1)}, f32[4,4,256,256]{3,2,1,0:T(8,128)}, u32[]{:S(2)}) copy-start(f32[4,4,256,256]{3,2,1,0:T(8,128)} %refs_3_.7) | copy-start | bytes 12582916
  111.0 11.9 %all-to-all-start.8 = ((f32[4,4,8,256]{3,2,1,0:T(8,128)}), f32[4,4,8,256]{3,2,1,0:T(8,128)S(1)}, u32[]{:S(2)}, u32[]{:S(2)}) async-start(f32[4,4,8,256]{3,2,1,0:T(8,128)} %broadcast_in_dim.68), calls=%async_computation.8 | async-start | bytes 262144 | tf_op jit(solution)/shard_map/all_to_all | solution.py:57
  114.4 2.5 %copy-start.2 = (f32[4,4,256,256]{3,2,1,0:T(8,128)S(1)}, f32[4,4,256,256]{3,2,1,0:T(8,128)}, u32[]{:S(2)}) copy-start(f32[4,4,256,256]{3,2,1,0:T(8,128)} %inverse.5) | copy-start | bytes 12582916
  117.4 2.2 %copy-start.3 = (f32[4,4,256,256]{3,2,1,0:T(8,128)S(1)}, f32[4,4,256,256]{3,2,1,0:T(8,128)}, u32[]{:S(2)}) copy-start(f32[4,4,256,256]{3,2,1,0:T(8,128)} %inverse.5) | copy-start | bytes 12582916
  119.6 2.8 %copy-start.11 = (f32[24,4,64,256]{3,2,1,0:T(8,128)S(1)}, f32[24,4,64,256]{3,2,1,0:T(8,128)}, u32[]{:S(2)}) copy-start(f32[24,4,64,256]{3,2,1,0:T(8,128)} %all-gather.8.cloned.1.call-done) | copy-start | bytes 18874372
  124.7 19.9 %all-to-all-start.9 = ((f32[4,4,8,256]{3,2,1,0:T(8,128)}), f32[4,4,8,256]{3,2,1,0:T(8,128)S(1)}, u32[]{:S(2)}, u32[]{:S(2)}) async-start(f32[4,4,8,256]{3,2,1,0:T(8,128)} %broadcast_in_dim.69), calls=%async_computation.9 | async-start | bytes 262144 | tf_op jit(solution)/shard_map/all_to_all | solution.py:57
  139.3 2.8 %copy-start.12 = (f32[24,4,64,256]{3,2,1,0:T(8,128)S(1)}, f32[24,4,64,256]{3,2,1,0:T(8,128)}, u32[]{:S(2)}) copy-start(f32[24,4,64,256]{3,2,1,0:T(8,128)} %all-gather.8.cloned.1.call-done) | copy-start | bytes 18874372
  148.3 14.0 %all-to-all-start.10 = ((f32[4,4,8,256]{3,2,1,0:T(8,128)}), f32[4,4,8,256]{3,2,1,0:T(8,128)S(1)}, u32[]{:S(2)}, u32[]{:S(2)}) async-start(f32[4,4,8,256]{3,2,1,0:T(8,128)} %broadcast_in_dim.70), calls=%async_computation.10 | async-start | bytes 262144 | tf_op jit(solution)/shard_map/all_to_all | solution.py:57
  155.6 2.8 %copy-start.13 = (f32[24,4,64,256]{3,2,1,0:T(8,128)S(1)}, f32[24,4,64,256]{3,2,1,0:T(8,128)}, u32[]{:S(2)}) copy-start(f32[24,4,64,256]{3,2,1,0:T(8,128)} %all-gather.8.cloned.1.call-done) | copy-start | bytes 18874372
  158.4 3.3 %copy-start.21 = (f32[4,8,256]{2,1,0:T(8,128)S(1)}, f32[4,8,256]{2,1,0:T(8,128)}, u32[]{:S(2)}) copy-start(f32[4,8,256]{2,1,0:T(8,128)} %copy-done.20) | copy-start | bytes 98308
  158.4 3.3 %copy-start.23 = (f32[4,8,256]{2,1,0:T(8,128)S(1)}, f32[4,8,256]{2,1,0:T(8,128)}, u32[]{:S(2)}) copy-start(f32[4,8,256]{2,1,0:T(8,128)} %copy-done.22) | copy-start | bytes 98308
  158.4 3.3 %copy-start.34 = (f32[4,8,256]{2,1,0:T(8,128)S(1)}, f32[4,8,256]{2,1,0:T(8,128)}, u32[]{:S(2)}) copy-start(f32[4,8,256]{2,1,0:T(8,128)} %copy-done.33) | copy-start | bytes 98308
  166.8 34.2 %all-to-all-start.11 = ((f32[8,1,4,8,256]{4,3,2,1,0:T(8,128)}), f32[8,1,4,8,256]{4,3,2,1,0:T(8,128)S(1)}, u32[]{:S(2)}, u32[]{:S(2)}) async-start(f32[8,1,4,8,256]{4,3,2,1,0:T(8,128)} %broadcast_in_dim.71), calls=%async_computation.11 | async-start | bytes 524288 | tf_op jit(solution)/shard_map/all_to_all | solution.py:57
  (22 other events, 27.7 us)
Sparse Core Ops, SparseCore 0:
  10.5 50.8 all-gather.7
  110.5 6.5 all-gather.5

commit v3 on v2

v3 whole, which is shorter than its diff:
```python
import functools

import jax
import jax.numpy as jnp
from jax import lax
from jax.experimental import pallas as pl
from jax.experimental.pallas import tpu as pltpu
from jax.sharding import PartitionSpec as P

WIDTH = 256
COLUMNS = 64
LANES = 128
F32 = jnp.float32
BF16 = jnp.bfloat16
SMEM = pl.BlockSpec(memory_space=pltpu.SMEM)
VMEM = pl.BlockSpec(memory_space=pltpu.VMEM)
HBM = pl.BlockSpec(memory_space=pltpu.HBM)
PARAMS = pltpu.CompilerParams(vmem_limit_bytes=16 * 2**20)
STREAM_PARAMS = pltpu.CompilerParams(vmem_limit_bytes=44 * 2**20)


def place_of(height, distance):
    return height * (height - 1) // 2 + distance - 1


def shape_of(*dims, dtype=F32):
    return jax.ShapeDtypeStruct(dims, dtype)


def split(value):
    high = value.astype(BF16)
    return high, (value - high.astype(F32)).astype(BF16)


def dot(left, right):
    return jnp.dot(left, right, preferred_element_type=F32)


def dot_t(left, right):
    return lax.dot_general(left, right, (((1,), (1,)), ((), ())), preferred_element_type=F32)


def product(left, right):
    lanes = right[0].shape[1]
    both = dot(left[0], jnp.concatenate(right, axis=1))
    return both[:, :lanes] + both[:, lanes:] + dot(left[1], right[0])


def product_t(left, right):
    rows = left[0].shape[0]
    both = dot_t(jnp.concatenate(left, axis=0), right[0])
    return both[:rows] + both[rows:] + dot_t(left[0], right[1])


def bits_of(count):
    assert count & (count - 1) == 0
    return count.bit_length() - 1


def swap(value, axis, bit):
    return lax.ppermute(value, axis, [(i, i ^ 1 << bit) for i in range(lax.axis_size(axis))])


def reversed_bits(index, bits):
    total = index & 0
    for bit in range(bits):
        total = total | ((index >> bit) & 1) << (bits - 1 - bit)
    return total


def gather(value, steps):
    pieces = [value[None]]
    for axis, bit in steps:
        whole = jnp.concatenate(pieces, 0) if len(pieces) > 1 else pieces[0]
        pieces.append(swap(whole, axis, bit))
    return pieces


def col_steps(count):
    return [("col", bit) for bit in reversed(range(bits_of(count)))]


def row_steps(count):
    return [("row", bit) for bit in range(bits_of(count))]


def input_kernel(gz_count, nodes, own, right, layer, keep, *away):
    gz = lax.axis_index("gz")
    tiles = right.shape[1]
    per_tile = LANES // COLUMNS
    block = lax.broadcasted_iota(jnp.int32, (1, LANES), 1) // own
    for level in range(right.shape[0]):
        for row in range(per_tile):
            totals = []
            for which in range(gz_count):
                mine = jnp.where(gz == which, 1.0, 0.0)
                total = jnp.zeros((tiles, LANES), F32)
                for node in range(nodes):
                    value = right[level, :, node, :] * mine - layer[level, :, node, :]
                    shift = (node * own - row * COLUMNS - which * own) % LANES
                    value = pltpu.roll(value, shift, 1) if shift else value
                    total = jnp.where(block == node, value, total)
                totals.append(total)
            for step in range(gz_count):
                chosen = totals[0]
                for which in range(1, gz_count):
                    chosen = jnp.where((gz ^ step) == which, totals[which], chosen)
                target = keep if step == 0 else away[step - 1]
                target[level, pl.ds(row, tiles, stride=per_tile), :] = chosen


def prepare_kernel(nodes, blocks, lower, upper, m_high, m_low, z_high, z_low):
    step = pl.program_id(0)
    for node in range(nodes):
        right = split(lower[0, node])
        left = split(upper[0, node])
        z_high[0, node], z_low[0, node] = split(product(left, right))
    for height in range(1, 4):

        @pl.when(step == height)
        def _():
            for node in range(nodes):
                right = split(lower[0, node])
                for distance in range(1, height + 1):
                    place = place_of(height, distance)
                    m_high[place, node], m_low[place, node] = split(
                        product(split(blocks[place, node]), right)
                    )


def prepare_step(blocks, lower, upper):
    nodes = lower.shape[1]
    level = pl.BlockSpec((1, nodes, WIDTH, WIDTH), lambda i: (i, 0, 0, 0))
    whole = pl.BlockSpec(blocks.shape, lambda i: (0, 0, 0, 0))
    m_shape = shape_of(*blocks.shape, dtype=BF16)
    z_shape = shape_of(*lower.shape, dtype=BF16)
    m_high, m_low, z_high, z_low = pl.pallas_call(
        functools.partial(prepare_kernel, nodes),
        grid=(4,),
        out_shape=[m_shape, m_shape, z_shape, z_shape],
        in_specs=[whole, level, level],
        out_specs=[whole, whole, level, level],
        compiler_params=STREAM_PARAMS,
        cost_estimate=pl.CostEstimate(
            flops=6 * 5 * nodes * WIDTH**3, bytes_accessed=20 * 2**20, transcendentals=0
        ),
        name="prepare",
    )(blocks, lower, upper)
    return (m_high, m_low), (z_high, z_low)


def assemble(pieces, full, part):
    row = lax.axis_index("row")
    place = 0
    for piece in pieces:
        for i in range(piece.shape[0]):
            start = pl.multiple_of((row ^ place) * part, part)
            full[pl.ds(start, part), :] = piece[i]
            place += 1


def forward_kernel(height, sizes, *refs):
    nodes, part, own, row_count, col_count = sizes
    lanes = nodes * own
    pieces, refs = refs[: 1 + bits_of(row_count)], refs[1 + bits_of(row_count) :]
    parents, pattern, m_high, m_low = refs[:4]
    pending_in = refs[4 : 4 + height] if height < 3 else ()
    full, keep, send = refs[4 + len(pending_in) :][:3]
    pending_out = refs[7 + len(pending_in) :][: height - 1]
    urgent = refs[-1]
    assemble(pieces, full, part)
    lane = lax.broadcasted_iota(jnp.int32, (1, lanes), 1) // own
    col = lax.axis_index("col")
    right = split(full[...])
    targets = []
    for level in range(height):
        target = urgent if level == height - 1 else pending_out[level]
        target[...] = pending_in[level][...] if pending_in else jnp.zeros(target.shape, F32)
        targets.append(target)
    for node in range(nodes):
        ancestor = col * nodes + node
        for distance in range(1, height + 1):
            place = place_of(height, distance)
            level = height - distance
            ancestor = parents[level, ancestor]
            slot = lax.rem(ancestor, nodes)
            where = reversed_bits(lax.div(ancestor, nodes) ^ col, bits_of(col_count))
            term = product((m_high[place, node], m_low[place, node]), right)
            term = pltpu.roll(term, lax.rem(slot - node + nodes, nodes) * own, 1)
            stored = jnp.where(pattern[place, node] != 0, slot, -1)
            targets[level][where] += jnp.where(lane == stored, term, 0.0)
    keep[...] = urgent[: col_count // 2]
    send[...] = urgent[col_count // 2 :]


def forward_step(height, pieces, parents, pattern, m, pending, sizes):
    nodes, part, own, row_count, col_count = sizes
    lanes = nodes * own
    half = shape_of(col_count // 2, part, lanes)
    stack = shape_of(col_count, part, lanes)
    out_shape = [shape_of(row_count * part, lanes), half, half] + [stack] * (height - 1)
    results = pl.pallas_call(
        functools.partial(forward_kernel, height, sizes),
        out_shape=out_shape,
        in_specs=[VMEM] * len(pieces) + [SMEM, SMEM] + [VMEM] * (2 + len(pending)),
        out_specs=[VMEM] * len(out_shape),
        scratch_shapes=[pltpu.VMEM(stack.shape, F32)],
        compiler_params=PARAMS,
        name="forward_level",
    )(*pieces, parents, pattern, *m, *pending)
    return results[0], results[1], results[2], results[3:]


def turn(full, turned, z_high, z_low, out, own, row_count):
    turned[...] = full.T
    few = own // row_count
    row = lax.axis_index("row")
    for node in range(out.shape[0]):
        start = pl.multiple_of(node * own + row * few, few)
        left = split(turned[pl.ds(start, few), :])
        out[node] = product_t(left, (z_high[0, node], z_low[0, node]))


def last_kernel(sizes, *refs):
    nodes, part, own, row_count, col_count = sizes
    pieces = refs[: 1 + bits_of(row_count)]
    z_high, z_low, full, out, turned = refs[len(pieces) :]
    assemble(pieces, full, part)
    turn(full[...], turned, z_high, z_low, out, own, row_count)


def last_step(pieces, z, sizes):
    nodes, part, own, row_count, col_count = sizes
    lanes, rows = nodes * own, row_count * part

    def whole(value):
        return pl.BlockSpec(value.shape, lambda i: (0,) * value.ndim)

    level = pl.BlockSpec((1, nodes, rows, rows), lambda i: (0, 0, 0, 0))
    outs = [shape_of(rows, lanes), shape_of(nodes, own // row_count, rows)]
    return pl.pallas_call(
        functools.partial(last_kernel, sizes),
        grid=(1,),
        out_shape=outs,
        in_specs=[whole(piece) for piece in pieces] + [level] * 2,
        out_specs=[whole(out) for out in outs],
        scratch_shapes=[pltpu.VMEM((lanes, rows), F32)],
        compiler_params=PARAMS,
        name="forward_last",
    )(*pieces, *z)


def turn_kernel(sizes, full, z_high, z_low, out, turned):
    nodes, part, own, row_count, col_count = sizes
    turn(full[...], turned, z_high, z_low, out, own, row_count)


def turn_step(height, full, z, sizes):
    nodes, part, own, row_count, col_count = sizes
    rows, lanes = full.shape
    out = shape_of(nodes, own // row_count, rows)
    level = pl.BlockSpec((1, nodes, rows, rows), lambda i: (height, 0, 0, 0))
    return pl.pallas_call(
        functools.partial(turn_kernel, sizes),
        grid=(1,),
        out_shape=out,
        in_specs=[pl.BlockSpec(full.shape, lambda i: (0, 0)), level, level],
        out_specs=pl.BlockSpec(out.shape, lambda i: (0, 0, 0)),
        scratch_shapes=[pltpu.VMEM((lanes, rows), F32)],
        compiler_params=PARAMS,
        name="turn_level",
    )(full, *z)


def solve_kernel(nodes, own, first, second, third, fourth, lower, out):
    step = pl.program_id(0)
    lane = lax.broadcasted_iota(jnp.int32, (1, nodes * own), 1) // own
    for height, full in enumerate((first, second, third, fourth)):

        @pl.when(step == height)
        def _():
            right = split(full[...])
            solved = jnp.zeros(full.shape, F32)
            for node in range(nodes):
                solved = jnp.where(lane == node, product(split(lower[0, node]), right), solved)
            out[0] = solved


def solve_step(fulls, lower, own):
    nodes = lower.shape[1]
    rows, lanes = fulls[0].shape
    whole = pl.BlockSpec((rows, lanes), lambda i: (0, 0))
    return pl.pallas_call(
        functools.partial(solve_kernel, nodes, own),
        grid=(4,),
        out_shape=shape_of(4, rows, lanes),
        in_specs=[whole] * 4 + [pl.BlockSpec((1, nodes, rows, rows), lambda i: (i, 0, 0, 0))],
        out_specs=pl.BlockSpec((1, rows, lanes), lambda i: (i, 0, 0)),
        compiler_params=STREAM_PARAMS,
        name="solve_levels",
    )(*fulls, lower)


def compose_kernel(nodes, gathered, inverse, high_out, low_out):
    for node in range(nodes):
        block = gathered[:, 0, node].reshape(WIDTH, WIDTH)
        whole = product(split(inverse[0, node]), split(block))
        high_out[0, node], low_out[0, node] = split(whole)


def compose_step(gathered, inverse, row_count):
    per, nodes, part = gathered.shape[1:4]
    pairs = place_of(4, 1)
    out = shape_of(pairs, nodes, WIDTH, WIDTH, dtype=BF16)
    out_spec = pl.BlockSpec((1, nodes, WIDTH, WIDTH), lambda i: (i, 0, 0, 0))

    def height_of(i):
        return 1 + sum((i >= place_of(height, 1)).astype(jnp.int32) for height in (2, 3))

    return pl.pallas_call(
        functools.partial(compose_kernel, nodes),
        grid=(pairs,),
        out_shape=[out, out],
        in_specs=[
            pl.BlockSpec((row_count, 1, nodes, part, WIDTH), lambda i: (i // per, i % per, 0, 0, 0)),
            pl.BlockSpec((1, nodes, WIDTH, WIDTH), lambda i: (height_of(i), 0, 0, 0)),
        ],
        out_specs=[out_spec] * 2,
        compiler_params=STREAM_PARAMS,
        cost_estimate=pl.CostEstimate(
            flops=6 * pairs * nodes * WIDTH**3,
            bytes_accessed=12 * pairs * nodes * WIDTH**2,
            transcendentals=0,
        ),
        name="compose",
    )(gathered, inverse)


def backward_kernel(height, nodes, col_count, parents, pattern, start, high, low, *refs):
    pieces_each = 1 + bits_of(col_count)
    out = refs[height * pieces_each]
    early = refs[height * pieces_each + 1] if height == 2 else None
    solved = refs[-1]
    for level in range(height):
        place = 0
        for piece in refs[level * pieces_each : (level + 1) * pieces_each]:
            solved[level, place : place + piece.shape[0]] = piece[...]
            place += piece.shape[0]
    col = lax.axis_index("col")
    for node in range(nodes):
        total = start[node]
        ancestor = col * nodes + node
        for distance in range(1, height + 1):
            level = height - distance
            place = place_of(height, distance)
            ancestor = parents[level, ancestor]
            where = reversed_bits(lax.div(ancestor, nodes) ^ col, bits_of(col_count))
            left = split(solved[level, where, lax.rem(ancestor, nodes)])
            term = product_t(left, (high[place, node], low[place, node]))
            total = total - jnp.where(pattern[place, node] != 0, term, 0.0)
        out[node] = total
        if early is not None:
            early[height, node] = total
    if early is not None:
        for level in range(height):
            early[level] = solved[level, 0]


def backward_step(height, parents, pattern, start, composed, solved):
    nodes = start.shape[0]
    col_count = lax.axis_size("col")
    pieces = [piece for level in solved for piece in level]
    outs = [start.shape] + ([(height + 1,) + start.shape] if height == 2 else [])
    return pl.pallas_call(
        functools.partial(backward_kernel, height, nodes, col_count),
        out_shape=[shape_of(*out) for out in outs],
        in_specs=[SMEM, SMEM] + [VMEM] * (3 + len(pieces)),
        out_specs=[VMEM] * len(outs),
        scratch_shapes=[pltpu.VMEM((height, col_count) + start.shape, F32)],
        compiler_params=PARAMS,
        name="backward_level",
    )(parents, pattern, start, *composed, *pieces)


def forward_out_kernel(gz_count, nodes, own, *refs):
    parts, out = refs[:gz_count], refs[gz_count]
    gz = lax.axis_index("gz")
    per_tile = LANES // COLUMNS
    tiles = out.shape[1]
    block = lax.broadcasted_iota(jnp.int32, (1, LANES), 1) // own
    values = []
    for row in range(per_tile):
        found = [part[0, pl.ds(row, tiles, stride=per_tile), :] for part in parts]
        for which in range(gz_count):
            value = found[0]
            for step in range(1, gz_count):
                value = jnp.where((gz ^ step) == which, found[step], value)
            values.append(value)
    for node in range(nodes):
        total = jnp.zeros((tiles, LANES), F32)
        for place, value in enumerate(values):
            shift = ((place - node) * own) % LANES
            value = pltpu.roll(value, shift, 1) if shift else value
            total = jnp.where(block == place, value, total)
        out[0, :, node, :] = total


def forward_out(parts, nodes, own):
    rows, lanes = parts[0].shape[1:]
    tiles = rows * COLUMNS // LANES
    part_spec = pl.BlockSpec((1, rows, lanes), lambda i: (i, 0, 0))
    return pl.pallas_call(
        functools.partial(forward_out_kernel, len(parts), nodes, own),
        grid=(4,),
        out_shape=shape_of(4, tiles, nodes, LANES),
        in_specs=[part_spec] * len(parts),
        out_specs=pl.BlockSpec((1, tiles, nodes, LANES), lambda i: (i, 0, 0, 0)),
        compiler_params=PARAMS,
        name="forward_out",
    )(*parts)


def backward_out_kernel(nodes, row_count, piece_count, *refs):
    pieces, (out, columns, turned) = refs[:piece_count], refs[-3:]
    per_tile = LANES // COLUMNS
    tiles = out.shape[1]
    few = pieces[0].shape[3]
    row = lax.axis_index("row")
    gz = lax.axis_index("gz")
    for node in range(nodes):
        place = 0
        for piece in pieces:
            for i in range(piece.shape[0]):
                index = (gz ^ (place // row_count)) * row_count + (row ^ (place % row_count))
                columns[pl.ds(pl.multiple_of(index * few, few), few), :] = piece[i, 0, node]
                place += 1
        turned[...] = columns[...].T
        rows = [turned[pl.ds(step, tiles, stride=per_tile), :] for step in range(per_tile)]
        out[0, :, node, :] = jnp.concatenate(rows, axis=1)


def backward_out(pieces, before, first, nodes, row_count):
    levels, nodes, few, rows = pieces[0].shape[1:]
    tiles = rows * COLUMNS // LANES
    ready = [before] if before is not None else []
    return pl.pallas_call(
        functools.partial(backward_out_kernel, nodes, row_count, len(pieces)),
        grid=(levels,),
        out_shape=shape_of(4, tiles, nodes, LANES),
        in_specs=[
            pl.BlockSpec((piece.shape[0], 1, nodes, few, rows), lambda i: (0, i, 0, 0, 0))
            for piece in pieces
        ]
        + [HBM] * len(ready),
        out_specs=pl.BlockSpec((1, tiles, nodes, LANES), lambda i: (first + i, 0, 0, 0)),
        scratch_shapes=[pltpu.VMEM((COLUMNS, rows), F32), pltpu.VMEM((rows, COLUMNS), F32)],
        input_output_aliases={len(pieces): 0} if ready else {},
        compiler_params=PARAMS,
        name="backward_out",
    )(*pieces, *ready)


def body(
    right_side,
    layer_sums,
    lower_blocks,
    upper_blocks,
    lower_inverse,
    upper_diagonal_inverses,
    pattern,
    parents,
):
    nodes = right_side.shape[1]
    part = lower_blocks.shape[2]
    gz_count = lax.axis_size("gz")
    row_count = lax.axis_size("row")
    col_count = lax.axis_size("col")
    own = COLUMNS // gz_count
    lanes = nodes * own
    sizes = (nodes, part, own, row_count, col_count)
    gz = lax.axis_index("gz")

    def tiled(value):
        return value.reshape(4, nodes, part * COLUMNS // LANES, LANES).transpose(0, 2, 1, 3)

    parts = pl.pallas_call(
        functools.partial(input_kernel, gz_count, nodes, own),
        out_shape=[shape_of(4, part, lanes)] * gz_count,
        in_specs=[VMEM, VMEM],
        out_specs=[VMEM] * gz_count,
        compiler_params=STREAM_PARAMS,
        name="input_parts",
    )(tiled(right_side), tiled(layer_sums[0]))

    per = upper_blocks.shape[0] // gz_count
    upper_rows = lax.all_gather(
        lax.dynamic_slice_in_dim(upper_blocks, gz * per, per, 0), ("gz", "row")
    )
    m, z = prepare_step(lower_blocks, lower_inverse, upper_diagonal_inverses)

    initial = parts[0]
    for step in range(1, gz_count):
        pairs = [(i, i ^ step) for i in range(gz_count)]
        initial = initial + lax.ppermute(parts[step], "gz", pairs)

    fulls = [None] * 4
    pending = []
    mine = initial[3]
    for height in (3, 2, 1):
        pieces = gather(mine, row_steps(row_count))
        fulls[height], keep, send, pending = forward_step(
            height, pieces, parents, pattern, m, pending, sizes
        )
        for bit in range(bits_of(col_count)):
            taken = swap(send, "col", bit)
            half = keep.shape[0] // 2
            keep, send = keep[:half] + taken[:half] if half else keep + taken, (
                keep[half:] + taken[half:] if half else None
            )
        mine = initial[height - 1] - keep[0]
    fulls[0], solved = last_step(gather(mine, row_steps(row_count)), z, sizes)

    composed = compose_step(upper_rows, upper_diagonal_inverses, row_count)
    starts = [None] + [turn_step(height, fulls[height], z, sizes) for height in (1, 2, 3)]
    forward = solve_step(fulls, lower_inverse, own)
    forward_parts = [forward] + [
        lax.ppermute(forward, "gz", [(i, i ^ step) for i in range(gz_count)])
        for step in range(1, gz_count)
    ]
    whole = []
    for height in (1, 2, 3):
        whole.append(gather(solved, col_steps(col_count)))
        results = backward_step(height, parents, pattern, starts[height], composed, whole)
        solved = results[0]
        if height == 2:
            early = results[1]

    forward_all = forward_out(forward_parts, nodes, own)
    layer_steps = row_steps(row_count) + [("gz", bit) for bit in range(bits_of(gz_count))]
    backward_all = backward_out(gather(early, layer_steps), None, 0, nodes, row_count)
    late = gather(solved[None], layer_steps)
    backward_all = backward_out(late, backward_all, 3, nodes, row_count)
    return tuple(
        value.transpose(0, 2, 1, 3).reshape(4, nodes, WIDTH * COLUMNS)
        for value in (forward_all, backward_all)
    )


def solution(mesh):
    in_specs = (
        P(None, "col", "row"),
        P("gz", None, "col", "row"),
        P(None, "col", "row", None),
        P(None, "col", "row", None),
        P(None, "col", None, None),
        P(None, "col", None, None),
        P(None, "col"),
        P(),
    )
    out_specs = (P(None, "col", None), P(None, "col", None))
    return jax.shard_map(body, mesh=mesh, in_specs=in_specs, out_specs=out_specs, check_vma=False)
```

time: 211 us -> 153 us (0.73)
  blocking collectives: 69.4 us -> 0 us
  waiting for transfers between devices: 11.8 us -> 55.5 us
  local copies, waits for them, and re-layouts: 50.3 us -> 9.99 us
  Pallas kernels: 22.6 us -> 30.9 us
  starting transfers between devices: 31.9 us -> 39.2 us
  other arithmetic: 8.5 us -> 2.44 us
    ppermute x0 -> x28, waiting for transfers between devices: none -> 55.5 us  [the longest x26 54.5 us: swap(): lax.ppermute(value, axis, [(i, i ^ 1 << bit) for i in range(lax.axis_size...]
    all_to_all x5 -> x0, blocking collectives: 40.9 us -> none  [the longest x3 23.6 us: gather_all(): lax.all_to_all(jnp.broadcast_to(value[None], (count,) + value.shape), axe...]
    ppermute x0 -> x28, starting transfers between devices: none -> 39.2 us  [the longest x26 38.6 us: swap(): lax.ppermute(value, axis, [(i, i ^ 1 << bit) for i in range(lax.axis_size...]
    unnamed x75 -> x33, local copies, waits for them, and re-layouts: 45.2 us -> 9.06 us
    all_to_all x7 -> x0, starting transfers between devices: 31.8 us -> none  [the longest x4 16.9 us: gather_all(): lax.all_to_all(jnp.broadcast_to(value[None], (count,) + value.shape), axe...]
    all_gather x1 -> x0, blocking collectives: 28.5 us -> none  [body(): early = lax.all_gather(jnp.stack(backward[:3]), ('gz', 'row'))]
    all_to_all x7 -> x0, waiting for transfers between devices: 11.7 us -> none  [the longest x1 6.71 us: body(): lax.all_to_all(top.reshape(layer_count, part, lanes), ('gz', 'row'), 0, 0)]
    pallas_call x16, Pallas kernels: 21.6 us -> 29.9 us  [the longest x1 7.03 us: compose_step(): pl.pallas_call(functools.partial(compose_kernel, nodes), grid=(pairs,), o...]
  transfers between devices with their start and end apart: 9 -> 29, of which waited for: 2 -> 22; matrix products, arithmetic and copies ran while one was open for 5% -> 2% of each run, Pallas kernels for 9% -> 18%
where the time goes in v3:
time: 153 us; the launch traced here: 152 us
  waiting for transfers between devices  55.5 us (36%)
  starting transfers between devices  39.2 us (26%)
  Pallas kernels  30.9 us (20%)
  between operations  14.3 us (9%)
  local copies, waits for them, and re-layouts  9.99 us (7%)
  other arithmetic  2.44 us (2%)
    ppermute x26, waiting for transfers between devices, swap(): lax.ppermute(value, axis, [(i, i ^ 1 << bit) for i in range(lax.axis_size...  54.5 us
    ppermute x26, starting transfers between devices, swap(): lax.ppermute(value, axis, [(i, i ^ 1 << bit) for i in range(lax.axis_size...  38.6 us
    unnamed x33, local copies, waits for them, and re-layouts  9.06 us
    pallas_call x1, Pallas kernels, compose_step(): pl.pallas_call(functools.partial(compose_kernel, nodes), grid=(pairs,), o...  7.03 us
    pallas_call x1, Pallas kernels, prepare_step(): pl.pallas_call(functools.partial(prepare_kernel, nodes), grid=(4,), out_s...  6.59 us
    pallas_call x3, Pallas kernels, backward_step(): pl.pallas_call(functools.partial(backward_kernel, height, nodes, col_coun...  3.82 us
    pallas_call x2, Pallas kernels, backward_out(): pl.pallas_call(functools.partial(backward_out_kernel, nodes, row_count, l...  3.39 us
    pallas_call x3, Pallas kernels, forward_step(): pl.pallas_call(functools.partial(forward_kernel, height, sizes), out_shap...  3.24 us
  transfers between devices with their start and end apart: 29, of which 22 were waited for; matrix products, arithmetic and copies ran while one was open for 2% of the time, Pallas kernels for 18%

profile of v3, /device:TPU:0, one launch (start us, length us, event | category | flops | bytes accessed | tf_op | source)
XLA Modules:
  0.0 152.4 jit_solution(6673843145927409181)
XLA Ops:
  14.1 2.9 %collective-permute-start.1 = (f32[1,64,128]{2,1,0:T(8,128)S(1)}, f32[1,64,128]{2,1,0:T(8,128)S(1)}, u32[]{:S(2)}, u32[]{:S(2)}) collective-permute-start(f32[1,64,128]{2,1,0:T(8,128)S(1)} %slice.67.refs_0_), channel_id=1, source_target_pairs={{0,4},{4,0},{8,12},{12,8},{1,5},{5,1},{9,13},{13,9},{2,6},{6,2},{1... | collective-permute-start | bytes 98312 | tf_op jit(solution)/shard_map/ppermute | solution.py:61
  22.5 6.6 %prepare.1 = (bf16[6,4,64,256]{3,2,1,0:T(8,128)(2,1)S(1)}, bf16[6,4,64,256]{3,2,1,0:T(8,128)(2,1)S(1)}, bf16[4,4,256,256]{3,2,1,0:T(8,128)(2,1)S(1)}, bf16[4,4,256,256]{3,2,1,0:T(8,128)(2,1)S(1)}) custom-call(f32[6,4,64,256]{3,2,1,0:T(8,128)S(1)} %copy-done.8, f32[4,4,256,256]{3,2,1,0:T(8,128)} %lower.3, f32[4,4,256,256]{3,2,1,0:T(8,128)} %inverse.1), custom_call_target="tpu_custom_call" | custom-call | flops 2013265920 | bytes 20971520 | tf_op jit(solution)/shard_map/prepare/pallas_call | solution.py:137
  36.2 2.7 %collective-permute-done.3 = f32[2,64,128]{2,1,0:T(8,128)S(1)} collective-permute-done((f32[2,64,128]{2,1,0:T(8,128)S(1)}, f32[2,64,128]{2,1,0:T(8,128)S(1)}, u32[]{:S(2)}, u32[]{:S(2)}) %collective-permute-start.3) | collective-permute-done | bytes 65568 | tf_op jit(solution)/shard_map/ppermute | solution.py:61
  38.9 2.5 %collective-permute-start.4 = (f32[1,64,128]{2,1,0:T(8,128)S(1)}, f32[1,64,128]{2,1,0:T(8,128)S(1)}, u32[]{:S(2)}, u32[]{:S(2)}) collective-permute-start(f32[1,64,128]{2,1,0:T(8,128)S(1)} %slice_add_fusion.4), channel_id=1, source_target_pairs={{0,2},{1,3},{2,0},{3,1},{4,6},{5,7},{6,4},{7,5},{8,10},{9,11},{10,... | collective-permute-start | bytes 98312 | tf_op jit(solution)/shard_map/ppermute | solution.py:61
  46.0 3.1 %collective-permute-done.5.refs_1_ = f32[1,64,128]{2,1,0:T(8,128)S(1)} collective-permute-done((f32[1,64,128]{2,1,0:T(8,128)S(1)}, f32[1,64,128]{2,1,0:T(8,128)S(1)}, u32[]{:S(2)}, u32[]{:S(2)}) %collective-permute-start.5) | collective-permute-done | bytes 32800 | tf_op jit(solution)/shard_map/ppermute | solution.py:61
  49.7 5.1 %collective-permute-done.6.refs_2_ = f32[2,64,128]{2,1,0:T(8,128)S(1)} collective-permute-done((f32[2,64,128]{2,1,0:T(8,128)S(1)}, f32[2,64,128]{2,1,0:T(8,128)S(1)}, u32[]{:S(2)}, u32[]{:S(2)}) %collective-permute-start.6) | collective-permute-done | bytes 65568 | tf_op jit(solution)/shard_map/ppermute | solution.py:61
  57.5 2.7 %collective-permute-done.7 = f32[2,64,128]{2,1,0:T(8,128)S(1)} collective-permute-done((f32[2,64,128]{2,1,0:T(8,128)S(1)}, f32[2,64,128]{2,1,0:T(8,128)S(1)}, u32[]{:S(2)}, u32[]{:S(2)}) %collective-permute-start.7) | collective-permute-done | bytes 65568 | tf_op jit(solution)/shard_map/ppermute | solution.py:61
  60.2 2.6 %collective-permute-start.8 = (f32[1,64,128]{2,1,0:T(8,128)S(1)}, f32[1,64,128]{2,1,0:T(8,128)S(1)}, u32[]{:S(2)}, u32[]{:S(2)}) collective-permute-start(f32[1,64,128]{2,1,0:T(8,128)S(1)} %slice_add_fusion.2), channel_id=1, source_target_pairs={{0,2},{1,3},{2,0},{3,1},{4,6},{5,7},{6,4},{7,5},{8,10},{9,11},{10,... | collective-permute-start | bytes 98312 | tf_op jit(solution)/shard_map/ppermute | solution.py:61
  67.3 2.5 %collective-permute-done.9.refs_1_ = f32[1,64,128]{2,1,0:T(8,128)S(1)} collective-permute-done((f32[1,64,128]{2,1,0:T(8,128)S(1)}, f32[1,64,128]{2,1,0:T(8,128)S(1)}, u32[]{:S(2)}, u32[]{:S(2)}) %collective-permute-start.9) | collective-permute-done | bytes 32800 | tf_op jit(solution)/shard_map/ppermute | solution.py:61
  70.3 3.7 %collective-permute-done.10.refs_2_ = f32[2,64,128]{2,1,0:T(8,128)S(1)} collective-permute-done((f32[2,64,128]{2,1,0:T(8,128)S(1)}, f32[2,64,128]{2,1,0:T(8,128)S(1)}, u32[]{:S(2)}, u32[]{:S(2)}) %collective-permute-start.10) | collective-permute-done | bytes 65568 | tf_op jit(solution)/shard_map/ppermute | solution.py:61
  76.7 2.7 %collective-permute-done.11 = f32[2,64,128]{2,1,0:T(8,128)S(1)} collective-permute-done((f32[2,64,128]{2,1,0:T(8,128)S(1)}, f32[2,64,128]{2,1,0:T(8,128)S(1)}, u32[]{:S(2)}, u32[]{:S(2)}) %collective-permute-start.11) | collective-permute-done | bytes 65568 | tf_op jit(solution)/shard_map/ppermute | solution.py:61
  79.4 2.6 %collective-permute-start.12 = (f32[1,64,128]{2,1,0:T(8,128)S(1)}, f32[1,64,128]{2,1,0:T(8,128)S(1)}, u32[]{:S(2)}, u32[]{:S(2)}) collective-permute-start(f32[1,64,128]{2,1,0:T(8,128)S(1)} %slice_add_fusion), channel_id=1, source_target_pairs={{0,2},{1,3},{2,0},{3,1},{4,6},{5,7},{6,4},{7,5},{8,10},{9,11},{10,... | collective-permute-start | bytes 98312 | tf_op jit(solution)/shard_map/ppermute | solution.py:61
  82.0 2.5 %collective-permute-done.12 = f32[1,64,128]{2,1,0:T(8,128)S(1)} collective-permute-done((f32[1,64,128]{2,1,0:T(8,128)S(1)}, f32[1,64,128]{2,1,0:T(8,128)S(1)}, u32[]{:S(2)}, u32[]{:S(2)}) %collective-permute-start.12) | collective-permute-done | bytes 32800 | tf_op jit(solution)/shard_map/ppermute | solution.py:61
  86.6 2.6 %collective-permute-done.13.refs_1_ = f32[1,64,128]{2,1,0:T(8,128)S(1)} collective-permute-done((f32[1,64,128]{2,1,0:T(8,128)S(1)}, f32[1,64,128]{2,1,0:T(8,128)S(1)}, u32[]{:S(2)}, u32[]{:S(2)}) %collective-permute-start.13) | collective-permute-done | bytes 32800 | tf_op jit(solution)/shard_map/ppermute | solution.py:61
  89.5 4.0 %collective-permute-done.14.refs_2_ = f32[2,64,128]{2,1,0:T(8,128)S(1)} collective-permute-done((f32[2,64,128]{2,1,0:T(8,128)S(1)}, f32[2,64,128]{2,1,0:T(8,128)S(1)}, u32[]{:S(2)}, u32[]{:S(2)}) %collective-permute-start.14) | collective-permute-done | bytes 65568 | tf_op jit(solution)/shard_map/ppermute | solution.py:61
  93.9 2.5 %collective-permute-start.16 = (f32[1,4,8,256]{3,2,1,0:T(8,128)S(1)}, f32[1,4,8,256]{3,2,1,0:T(8,128)S(1)}, u32[]{:S(2)}, u32[]{:S(2)}) collective-permute-start(f32[1,4,8,256]{3,2,1,0:T(8,128)S(1)} %bitcast.22), channel_id=1, source_target_pairs={{0,2},{1,3},{2,0},{3,1},{4,6},{5,7},{6,4},{7,5},{8,10},{9,11},{10,... | collective-permute-start | bytes 98312 | tf_op jit(solution)/shard_map/ppermute | solution.py:61
  100.6 7.0 %compose.1 = (bf16[6,4,256,256]{3,2,1,0:T(8,128)(2,1)S(1)}, bf16[6,4,256,256]{3,2,1,0:T(8,128)(2,1)S(1)}) custom-call(f32[8,3,4,64,256]{4,3,2,1,0:T(8,128)} %bitcast.40, f32[4,4,256,256]{3,2,1,0:T(8,128)} %inverse.1), custom_call_target="tpu_custom_call" | custom-call | flops 2415919104 | bytes 18874368 | tf_op jit(solution)/shard_map/compose/pallas_call | solution.py:320
  108.7 2.9 %collective-permute-start.18 = (f32[1,4,8,256]{3,2,1,0:T(8,128)S(1)}, f32[1,4,8,256]{3,2,1,0:T(8,128)S(1)}, u32[]{:S(2)}, u32[]{:S(2)}) collective-permute-start(f32[1,4,8,256]{3,2,1,0:T(8,128)S(1)} %bitcast.27), channel_id=1, source_target_pairs={{0,2},{1,3},{2,0},{3,1},{4,6},{5,7},{6,4},{7,5},{8,10},{9,11},{10,... | collective-permute-start | bytes 98312 | tf_op jit(solution)/shard_map/ppermute | solution.py:61
  114.6 3.5 %collective-permute-done.19.refs_5_ = f32[2,4,8,256]{3,2,1,0:T(8,128)S(1)} collective-permute-done((f32[2,4,8,256]{3,2,1,0:T(8,128)S(1)}, f32[2,4,8,256]{3,2,1,0:T(8,128)S(1)}, u32[]{:S(2)}, u32[]{:S(2)}) %collective-permute-start.19) | collective-permute-done | bytes 65568 | tf_op jit(solution)/shard_map/ppermute | solution.py:61
  120.8 2.8 %collective-permute-start.20 = (f32[1,4,8,256]{3,2,1,0:T(8,128)S(1)}, f32[1,4,8,256]{3,2,1,0:T(8,128)S(1)}, u32[]{:S(2)}, u32[]{:S(2)}) collective-permute-start(f32[1,4,8,256]{3,2,1,0:T(8,128)S(1)} %bitcast.37), channel_id=1, source_target_pairs={{0,2},{1,3},{2,0},{3,1},{4,6},{5,7},{6,4},{7,5},{8,10},{9,11},{10,... | collective-permute-start | bytes 98312 | tf_op jit(solution)/shard_map/ppermute | solution.py:61
  132.4 2.9 %collective-permute-done.22.refs_1_ = f32[1,1,4,8,256]{4,3,2,1,0:T(8,128)S(1)} collective-permute-done((f32[1,1,4,8,256]{4,3,2,1,0:T(8,128)S(1)}, f32[1,1,4,8,256]{4,3,2,1,0:T(8,128)S(1)}, u32[]{:S(2)}, u32[]{:S(2)}) %collective-permute-start.22) | collective-permute-done | bytes 32800 | tf_op jit(solution)/shard_map/ppermute | solution.py:61
  136.5 3.1 %collective-permute-done.23.refs_2_ = f32[2,1,4,8,256]{4,3,2,1,0:T(8,128)S(1)} collective-permute-done((f32[2,1,4,8,256]{4,3,2,1,0:T(8,128)S(1)}, f32[2,1,4,8,256]{4,3,2,1,0:T(8,128)S(1)}, u32[]{:S(2)}, u32[]{:S(2)}) %collective-permute-start.23) | collective-permute-done | bytes 65568 | tf_op jit(solution)/shard_map/ppermute | solution.py:61
  139.7 2.4 %forward_out.1 = f32[4,128,4,128]{3,2,1,0:T(4,128)} custom-call(f32[4,256,128]{2,1,0:T(8,128)S(1)} %solve_levels.1.refs_0_, f32[4,256,128]{2,1,0:T(8,128)S(1)} %collective-permute-done.15.refs_1_), custom_call_target="tpu_custom_call" | custom-call | tf_op jit(solution)/shard_map/forward_out/pallas_call | solution.py:412
  142.1 2.3 %backward_out.2.refs_4_ = f32[4,128,4,128]{3,2,1,0:T(4,128)} custom-call(f32[1,3,4,8,256]{4,3,2,1,0:T(8,128)S(1)} %bitcast.21, f32[1,3,4,8,256]{4,3,2,1,0:T(8,128)S(1)} %collective-permute-done.25.refs_1_, f32[2,3,4,8,256]{4,3,2,1,0:T(8,128)S(1)} %collective-permute-done.26.refs_2_, f32[4,3,4,8,256]{4,3,2,1,0:T(8,128)S(1)} %collective-permute-done.27.refs_3_), custom_call_target="tpu_custom_call" | custom-call | tf_op jit(solution)/shard_map/backward_out/pallas_call | solution.py:446
  (105 shorter events, 59.7 us)
Async XLA Ops:
  7.2 93.5 %all-gather.3.cloned.1.call-start = ((), (), s32[]{:S(2)}) async-start(), calls=%async_computation | async-start | bytes 7077888 | tf_op jit(solution)/shard_map/all_gather | solution.py:496
  14.1 4.8 %collective-permute-start.1 = (f32[1,64,128]{2,1,0:T(8,128)S(1)}, f32[1,64,128]{2,1,0:T(8,128)S(1)}, u32[]{:S(2)}, u32[]{:S(2)}) collective-permute-start(f32[1,64,128]{2,1,0:T(8,128)S(1)} %slice.67.refs_0_), channel_id=1, source_target_pairs={{0,4},{4,0},{8,12},{12,8},{1,5},{5,1},{9,13},{13,9},{2,6},{6,2},{1... | collective-permute-start | bytes 98312 | tf_op jit(solution)/shard_map/ppermute | solution.py:61
  18.9 13.0 %collective-permute-start.2 = (f32[2,64,128]{2,1,0:T(8,128)S(1)}, f32[2,64,128]{2,1,0:T(8,128)S(1)}, u32[]{:S(2)}, u32[]{:S(2)}) collective-permute-start(f32[2,64,128]{2,1,0:T(8,128)S(1)} %pad_maximum_fusion.3), channel_id=1, source_target_pairs={{0,8},{4,12},{8,0},{12,4},{1,9},{5,13},{9,1},{13,5},{2,10},{6,14},... | collective-permute-start | bytes 196616 | tf_op jit(solution)/shard_map/ppermute | solution.py:61
  34.6 4.3 %collective-permute-start.3 = (f32[2,64,128]{2,1,0:T(8,128)S(1)}, f32[2,64,128]{2,1,0:T(8,128)S(1)}, u32[]{:S(2)}, u32[]{:S(2)}) collective-permute-start(f32[2,64,128]{2,1,0:T(8,128)S(1)} %get-tuple-element.31), channel_id=1, source_target_pairs={{0,1},{1,0},{2,3},{3,2},{4,5},{5,4},{6,7},{7,6},{8,9},{9,8},{10,11... | collective-permute-start | bytes 196616 | tf_op jit(solution)/shard_map/ppermute | solution.py:61
  38.9 4.8 %collective-permute-start.4 = (f32[1,64,128]{2,1,0:T(8,128)S(1)}, f32[1,64,128]{2,1,0:T(8,128)S(1)}, u32[]{:S(2)}, u32[]{:S(2)}) collective-permute-start(f32[1,64,128]{2,1,0:T(8,128)S(1)} %slice_add_fusion.4), channel_id=1, source_target_pairs={{0,2},{1,3},{2,0},{3,1},{4,6},{5,7},{6,4},{7,5},{8,10},{9,11},{10,... | collective-permute-start | bytes 98312 | tf_op jit(solution)/shard_map/ppermute | solution.py:61
  44.5 4.7 %collective-permute-start.5 = (f32[1,64,128]{2,1,0:T(8,128)S(1)}, f32[1,64,128]{2,1,0:T(8,128)S(1)}, u32[]{:S(2)}, u32[]{:S(2)}) collective-permute-start(f32[1,64,128]{2,1,0:T(8,128)S(1)} %fusion.5.refs_0_), channel_id=1, source_target_pairs={{0,4},{4,0},{8,12},{12,8},{1,5},{5,1},{9,13},{13,9},{2,6},{6,2},{1... | collective-permute-start | bytes 98312 | tf_op jit(solution)/shard_map/ppermute | solution.py:61
  49.2 5.6 %collective-permute-start.6 = (f32[2,64,128]{2,1,0:T(8,128)S(1)}, f32[2,64,128]{2,1,0:T(8,128)S(1)}, u32[]{:S(2)}, u32[]{:S(2)}) collective-permute-start(f32[2,64,128]{2,1,0:T(8,128)S(1)} %pad_maximum_fusion.4), channel_id=1, source_target_pairs={{0,8},{4,12},{8,0},{12,4},{1,9},{5,13},{9,1},{13,5},{2,10},{6,14},... | collective-permute-start | bytes 196616 | tf_op jit(solution)/shard_map/ppermute | solution.py:61
  55.9 4.3 %collective-permute-start.7 = (f32[2,64,128]{2,1,0:T(8,128)S(1)}, f32[2,64,128]{2,1,0:T(8,128)S(1)}, u32[]{:S(2)}, u32[]{:S(2)}) collective-permute-start(f32[2,64,128]{2,1,0:T(8,128)S(1)} %get-tuple-element.35), channel_id=1, source_target_pairs={{0,1},{1,0},{2,3},{3,2},{4,5},{5,4},{6,7},{7,6},{8,9},{9,8},{10,11... | collective-permute-start | bytes 196616 | tf_op jit(solution)/shard_map/ppermute | solution.py:61
  60.2 4.8 %collective-permute-start.8 = (f32[1,64,128]{2,1,0:T(8,128)S(1)}, f32[1,64,128]{2,1,0:T(8,128)S(1)}, u32[]{:S(2)}, u32[]{:S(2)}) collective-permute-start(f32[1,64,128]{2,1,0:T(8,128)S(1)} %slice_add_fusion.2), channel_id=1, source_target_pairs={{0,2},{1,3},{2,0},{3,1},{4,6},{5,7},{6,4},{7,5},{8,10},{9,11},{10,... | collective-permute-start | bytes 98312 | tf_op jit(solution)/shard_map/ppermute | solution.py:61
  69.8 4.3 %collective-permute-start.10 = (f32[2,64,128]{2,1,0:T(8,128)S(1)}, f32[2,64,128]{2,1,0:T(8,128)S(1)}, u32[]{:S(2)}, u32[]{:S(2)}) collective-permute-start(f32[2,64,128]{2,1,0:T(8,128)S(1)} %pad_maximum_fusion.5), channel_id=1, source_target_pairs={{0,8},{4,12},{8,0},{12,4},{1,9},{5,13},{9,1},{13,5},{2,10},{6,14},... | collective-permute-start | bytes 196616 | tf_op jit(solution)/shard_map/ppermute | solution.py:61
  75.1 4.3 %collective-permute-start.11 = (f32[2,64,128]{2,1,0:T(8,128)S(1)}, f32[2,64,128]{2,1,0:T(8,128)S(1)}, u32[]{:S(2)}, u32[]{:S(2)}) collective-permute-start(f32[2,64,128]{2,1,0:T(8,128)S(1)} %get-tuple-element.38), channel_id=1, source_target_pairs={{0,1},{1,0},{2,3},{3,2},{4,5},{5,4},{6,7},{7,6},{8,9},{9,8},{10,11... | collective-permute-start | bytes 196616 | tf_op jit(solution)/shard_map/ppermute | solution.py:61
  79.4 5.0 %collective-permute-start.12 = (f32[1,64,128]{2,1,0:T(8,128)S(1)}, f32[1,64,128]{2,1,0:T(8,128)S(1)}, u32[]{:S(2)}, u32[]{:S(2)}) collective-permute-start(f32[1,64,128]{2,1,0:T(8,128)S(1)} %slice_add_fusion), channel_id=1, source_target_pairs={{0,2},{1,3},{2,0},{3,1},{4,6},{5,7},{6,4},{7,5},{8,10},{9,11},{10,... | collective-permute-start | bytes 98312 | tf_op jit(solution)/shard_map/ppermute | solution.py:61
  89.2 4.3 %collective-permute-start.14 = (f32[2,64,128]{2,1,0:T(8,128)S(1)}, f32[2,64,128]{2,1,0:T(8,128)S(1)}, u32[]{:S(2)}, u32[]{:S(2)}) collective-permute-start(f32[2,64,128]{2,1,0:T(8,128)S(1)} %pad_maximum_fusion.6), channel_id=1, source_target_pairs={{0,8},{4,12},{8,0},{12,4},{1,9},{5,13},{9,1},{13,5},{2,10},{6,14},... | collective-permute-start | bytes 196616 | tf_op jit(solution)/shard_map/ppermute | solution.py:61
  93.9 5.0 %collective-permute-start.16 = (f32[1,4,8,256]{3,2,1,0:T(8,128)S(1)}, f32[1,4,8,256]{3,2,1,0:T(8,128)S(1)}, u32[]{:S(2)}, u32[]{:S(2)}) collective-permute-start(f32[1,4,8,256]{3,2,1,0:T(8,128)S(1)} %bitcast.22), channel_id=1, source_target_pairs={{0,2},{1,3},{2,0},{3,1},{4,6},{5,7},{6,4},{7,5},{8,10},{9,11},{10,... | collective-permute-start | bytes 98312 | tf_op jit(solution)/shard_map/ppermute | solution.py:61
  98.9 8.8 %collective-permute-start.17 = (f32[2,4,8,256]{3,2,1,0:T(8,128)S(1)}, f32[2,4,8,256]{3,2,1,0:T(8,128)S(1)}, u32[]{:S(2)}, u32[]{:S(2)}) collective-permute-start(f32[2,4,8,256]{3,2,1,0:T(8,128)S(1)} %pad_maximum_fusion.7), channel_id=1, source_target_pairs={{0,1},{1,0},{2,3},{3,2},{4,5},{5,4},{6,7},{7,6},{8,9},{9,8},{10,11... | collective-permute-start | bytes 196616 | tf_op jit(solution)/shard_map/ppermute | solution.py:61
  108.7 5.1 %collective-permute-start.18 = (f32[1,4,8,256]{3,2,1,0:T(8,128)S(1)}, f32[1,4,8,256]{3,2,1,0:T(8,128)S(1)}, u32[]{:S(2)}, u32[]{:S(2)}) collective-permute-start(f32[1,4,8,256]{3,2,1,0:T(8,128)S(1)} %bitcast.27), channel_id=1, source_target_pairs={{0,2},{1,3},{2,0},{3,1},{4,6},{5,7},{6,4},{7,5},{8,10},{9,11},{10,... | collective-permute-start | bytes 98312 | tf_op jit(solution)/shard_map/ppermute | solution.py:61
  113.8 4.3 %collective-permute-start.19 = (f32[2,4,8,256]{3,2,1,0:T(8,128)S(1)}, f32[2,4,8,256]{3,2,1,0:T(8,128)S(1)}, u32[]{:S(2)}, u32[]{:S(2)}) collective-permute-start(f32[2,4,8,256]{3,2,1,0:T(8,128)S(1)} %pad_maximum_fusion.8), channel_id=1, source_target_pairs={{0,1},{1,0},{2,3},{3,2},{4,5},{5,4},{6,7},{7,6},{8,9},{9,8},{10,11... | collective-permute-start | bytes 196616 | tf_op jit(solution)/shard_map/ppermute | solution.py:61
  119.3 4.7 %collective-permute-start.25 = (f32[1,3,4,8,256]{4,3,2,1,0:T(8,128)S(1)}, f32[1,3,4,8,256]{4,3,2,1,0:T(8,128)S(1)}, u32[]{:S(2)}, u32[]{:S(2)}) collective-permute-start(f32[1,3,4,8,256]{4,3,2,1,0:T(8,128)S(1)} %bitcast.18), channel_id=1, source_target_pairs={{0,4},{4,0},{8,12},{12,8},{1,5},{5,1},{9,13},{13,9},{2,6},{6,2},{1... | collective-permute-start | bytes 294920 | tf_op jit(solution)/shard_map/ppermute | solution.py:61
  120.8 4.8 %collective-permute-start.20 = (f32[1,4,8,256]{3,2,1,0:T(8,128)S(1)}, f32[1,4,8,256]{3,2,1,0:T(8,128)S(1)}, u32[]{:S(2)}, u32[]{:S(2)}) collective-permute-start(f32[1,4,8,256]{3,2,1,0:T(8,128)S(1)} %bitcast.37), channel_id=1, source_target_pairs={{0,2},{1,3},{2,0},{3,1},{4,6},{5,7},{6,4},{7,5},{8,10},{9,11},{10,... | collective-permute-start | bytes 98312 | tf_op jit(solution)/shard_map/ppermute | solution.py:61
  124.0 8.3 %collective-permute-start.26 = (f32[2,3,4,8,256]{4,3,2,1,0:T(8,128)S(1)}, f32[2,3,4,8,256]{4,3,2,1,0:T(8,128)S(1)}, u32[]{:S(2)}, u32[]{:S(2)}) collective-permute-start(f32[2,3,4,8,256]{4,3,2,1,0:T(8,128)S(1)} %pad_maximum_fusion.1), channel_id=1, source_target_pairs={{0,8},{4,12},{8,0},{12,4},{1,9},{5,13},{9,1},{13,5},{2,10},{6,14},... | collective-permute-start | bytes 589832 | tf_op jit(solution)/shard_map/ppermute | solution.py:61
  125.6 4.3 %collective-permute-start.21 = (f32[2,4,8,256]{3,2,1,0:T(8,128)S(1)}, f32[2,4,8,256]{3,2,1,0:T(8,128)S(1)}, u32[]{:S(2)}, u32[]{:S(2)}) collective-permute-start(f32[2,4,8,256]{3,2,1,0:T(8,128)S(1)} %pad_maximum_fusion.9), channel_id=1, source_target_pairs={{0,1},{1,0},{2,3},{3,2},{4,5},{5,4},{6,7},{7,6},{8,9},{9,8},{10,11... | collective-permute-start | bytes 196616 | tf_op jit(solution)/shard_map/ppermute | solution.py:61
  128.0 11.7 %collective-permute-start.15 = (f32[4,256,128]{2,1,0:T(8,128)S(1)}, f32[4,256,128]{2,1,0:T(8,128)S(1)}, u32[]{:S(2)}, u32[]{:S(2)}) collective-permute-start(f32[4,256,128]{2,1,0:T(8,128)S(1)} %solve_levels.1.refs_0_), channel_id=1, source_target_pairs={{0,16},{16,0},{1,17},{17,1},{2,18},{18,2},{3,19},{19,3},{4,20},{20... | collective-permute-start | bytes 1572872 | tf_op jit(solution)/shard_map/ppermute | solution.py:527
  132.4 9.8 %collective-permute-start.27 = (f32[4,3,4,8,256]{4,3,2,1,0:T(8,128)S(1)}, f32[4,3,4,8,256]{4,3,2,1,0:T(8,128)S(1)}, u32[]{:S(2)}, u32[]{:S(2)}) collective-permute-start(f32[4,3,4,8,256]{4,3,2,1,0:T(8,128)S(1)} %pad_maximum_fusion), channel_id=1, source_target_pairs={{0,16},{16,0},{1,17},{17,1},{2,18},{18,2},{3,19},{19,3},{4,20},{20... | collective-permute-start | bytes 1179656 | tf_op jit(solution)/shard_map/ppermute | solution.py:61
  139.6 4.8 %collective-permute-start.24 = (f32[4,1,4,8,256]{4,3,2,1,0:T(8,128)S(1)}, f32[4,1,4,8,256]{4,3,2,1,0:T(8,128)S(1)}, u32[]{:S(2)}, u32[]{:S(2)}) collective-permute-start(f32[4,1,4,8,256]{4,3,2,1,0:T(8,128)S(1)} %pad_maximum_fusion.2), channel_id=1, source_target_pairs={{0,16},{16,0},{1,17},{17,1},{2,18},{18,2},{3,19},{19,3},{4,20},{20... | collective-permute-start | bytes 393224 | tf_op jit(solution)/shard_map/ppermute | solution.py:61
  (21 other events, 190.9 us)
Sparse Core Ops, SparseCore 0:
  10.5 50.3 all-gather.2

commit v4 on v3

v4 whole, which is shorter than its diff:
```python
import functools

import jax
import jax.numpy as jnp
from jax import lax
from jax.experimental import pallas as pl
from jax.experimental.pallas import tpu as pltpu
from jax.sharding import PartitionSpec as P

WIDTH = 256
COLUMNS = 64
LANES = 128
F32 = jnp.float32
BF16 = jnp.bfloat16
SPLIT = False
SMEM = pl.BlockSpec(memory_space=pltpu.SMEM)
VMEM = pl.BlockSpec(memory_space=pltpu.VMEM)
HBM = pl.BlockSpec(memory_space=pltpu.HBM)
PARAMS = pltpu.CompilerParams(vmem_limit_bytes=16 * 2**20)
STREAM_PARAMS = pltpu.CompilerParams(vmem_limit_bytes=53 * 2**20)


def place_of(height, distance):
    return height * (height - 1) // 2 + distance - 1


def shape_of(*dims, dtype=F32):
    return jax.ShapeDtypeStruct(dims, dtype)


def split(value):
    high = value.astype(BF16)
    return high, (value - high.astype(F32)).astype(BF16)


def dot(left, right):
    return jnp.dot(left, right, preferred_element_type=F32)


def dot_t(left, right):
    return lax.dot_general(left, right, (((1,), (1,)), ((), ())), preferred_element_type=F32)


def product(left, right):
    lanes = right[0].shape[1]
    both = dot(left[0], jnp.concatenate(right, axis=1))
    return both[:, :lanes] + both[:, lanes:] + dot(left[1], right[0])


def product_t(left, right):
    rows = left[0].shape[0]
    both = dot_t(jnp.concatenate(left, axis=0), right[0])
    return both[:rows] + both[rows:] + dot_t(left[0], right[1])


def steps_of(count):
    assert count & (count - 1) == 0
    return range(1, count)


def swap(value, axis, step):
    count = lax.axis_size(axis)
    gz_count = lax.axis_size("gz")
    cores = range(gz_count) if SPLIT else [gz_count - 1]
    pairs = [(g * count + i, g * count + (i ^ step)) for g in cores for i in range(count)]
    return lax.ppermute(value, ("gz", axis), pairs)


def swap_layers(value, step):
    return lax.ppermute(value, "gz", [(i, i ^ step) for i in range(lax.axis_size("gz"))])


def share_layers(value):
    gz_count = lax.axis_size("gz")
    if SPLIT:
        return [swap_layers(value, step) for step in steps_of(gz_count)]
    chief = gz_count - 1
    return [lax.ppermute(value, "gz", [(chief, chief ^ step)]) for step in steps_of(gz_count)]


def gather(value, axis):
    return [value] + [swap(value, axis, step) for step in steps_of(lax.axis_size(axis))]


def input_kernel(gz_count, nodes, own, right, layer, *outs):
    groups = COLUMNS // own
    kept, away, stage = outs[:4], outs[4:-1], outs[-1]
    gz = lax.axis_index("gz")
    tiles = right.shape[1]
    per_tile = LANES // COLUMNS
    block = lax.broadcasted_iota(jnp.int32, (1, LANES), 1) // own
    for level in range(right.shape[0]):
        for chunk in range(nodes * own // LANES):
            start = chunk * LANES
            lanes = slice(start, start + LANES)
            for row in range(per_tile):
                for which in range(groups):
                    mine = jnp.where(gz == (which if groups > 1 else gz_count - 1), 1.0, 0.0)
                    total = jnp.zeros((tiles, LANES), F32)
                    for node in range(start // own, (start + LANES) // own):
                        value = right[level, :, node, :] * mine - layer[level, :, node, :]
                        target = node * own - start
                        shift = (target - row * COLUMNS - which * own) % LANES
                        value = pltpu.roll(value, shift, 1) if shift else value
                        total = jnp.where(block == target // own, value, total)
                    stage[level, chunk, which, pl.ds(row, tiles, stride=per_tile), :] = total
            found = [stage[level, chunk, which] for which in range(groups)]
            for step in range(groups):
                chosen = found[0]
                for which in range(1, groups):
                    chosen = jnp.where((gz ^ step) == which, found[which], chosen)
                if step == 0:
                    kept[level][:, lanes] = chosen
                if step or groups == 1:
                    away[max(step - 1, 0)][level, :, lanes] = chosen


def lower_kernel(nodes, blocks, inverse, high_out, low_out, high, low):
    @pl.when(pl.program_id(0) == 0)
    def _():
        for node in range(nodes):
            high[node], low[node] = split(inverse[0, node])

    for node in range(nodes):
        high_out[0, node], low_out[0, node] = split(
            product(split(blocks[0, node]), (high[node], low[node]))
        )


def lower_step(height, blocks, inverse):
    nodes, part = blocks.shape[1:3]
    first = place_of(height, 1)
    out = shape_of(height, nodes, part, WIDTH, dtype=BF16)
    return pl.pallas_call(
        functools.partial(lower_kernel, nodes),
        grid=(height,),
        out_shape=[out, out],
        in_specs=[
            pl.BlockSpec((1, nodes, part, WIDTH), lambda i: (first + i, 0, 0, 0)),
            pl.BlockSpec((1, nodes, WIDTH, WIDTH), lambda i: (height, 0, 0, 0)),
        ],
        out_specs=[pl.BlockSpec((1, nodes, part, WIDTH), lambda i: (i, 0, 0, 0))] * 2,
        scratch_shapes=[pltpu.VMEM((nodes, WIDTH, WIDTH), BF16)] * 2,
        compiler_params=STREAM_PARAMS,
        name="lower_products",
    )(blocks, inverse)


def middle_kernel(nodes, upper, lower, high_out, low_out):
    for node in range(nodes):
        high_out[node], low_out[node] = split(product(split(upper[0, node]), split(lower[0, node])))


def middle_step(upper, lower):
    nodes = lower.shape[1]
    out = shape_of(nodes, WIDTH, WIDTH, dtype=BF16)
    level = pl.BlockSpec((1, nodes, WIDTH, WIDTH), lambda i: (0, 0, 0, 0))
    return pl.pallas_call(
        functools.partial(middle_kernel, nodes),
        grid=(1,),
        out_shape=[out, out],
        in_specs=[level, level],
        out_specs=[pl.BlockSpec((nodes, WIDTH, WIDTH), lambda i: (0, 0, 0))] * 2,
        compiler_params=STREAM_PARAMS,
        name="middle_product",
    )(upper, lower)


def assemble(pieces, full, part):
    row = lax.axis_index("row")
    for step, piece in enumerate(pieces):
        full[pl.ds(pl.multiple_of((row ^ step) * part, part), part), :] = piece[...]


def forward_kernel(height, sizes, *refs):
    nodes, part, own, row_count, col_count = sizes
    lanes = nodes * own
    pieces, refs = refs[:row_count], refs[row_count:]
    parents, pattern, m_high, m_low = refs[:4]
    pending_in = refs[4 : 4 + height] if height < 3 else ()
    refs = refs[4 + len(pending_in) :]
    full, sends = refs[0], refs[1 : 1 + col_count]
    pending_out = refs[1 + col_count : col_count + height]
    urgent = refs[-1]
    assemble(pieces, full, part)
    lane = lax.broadcasted_iota(jnp.int32, (1, lanes), 1) // own
    col = lax.axis_index("col")
    right = split(full[...])
    targets = []
    for level in range(height):
        target = urgent if level == height - 1 else pending_out[level]
        target[...] = pending_in[level][...] if pending_in else jnp.zeros(target.shape, F32)
        targets.append(target)
    for node in range(nodes):
        ancestor = col * nodes + node
        for distance in range(1, height + 1):
            level = height - distance
            ancestor = parents[level, ancestor]
            slot = lax.rem(ancestor, nodes)
            where = lax.div(ancestor, nodes) ^ col
            term = product((m_high[distance - 1, node], m_low[distance - 1, node]), right)
            term = pltpu.roll(term, lax.rem(slot - node + nodes, nodes) * own, 1)
            stored = jnp.where(pattern[place_of(height, distance), node] != 0, slot, -1)
            targets[level][where] += jnp.where(lane == stored, term, 0.0)
    for step in range(col_count):
        sends[step][...] = urgent[step]


def forward_step(height, pieces, parents, pattern, m, pending, sizes):
    nodes, part, own, row_count, col_count = sizes
    lanes = nodes * own
    piece = shape_of(part, lanes)
    stack = shape_of(col_count, part, lanes)
    out_shape = [shape_of(row_count * part, lanes)] + [piece] * col_count + [stack] * (height - 1)
    results = pl.pallas_call(
        functools.partial(forward_kernel, height, sizes),
        out_shape=out_shape,
        in_specs=[VMEM] * len(pieces) + [SMEM, SMEM] + [VMEM] * (2 + len(pending)),
        out_specs=[VMEM] * len(out_shape),
        scratch_shapes=[pltpu.VMEM(stack.shape, F32)],
        compiler_params=PARAMS,
        name="forward_level",
    )(*pieces, parents, pattern, *m, *pending)
    return results[0], results[1 : 1 + col_count], results[1 + col_count :]


def turn(value, turned, pair_of, out, own, row_count):
    turned[...] = value.T
    few = own // row_count
    row = lax.axis_index("row")
    for node in range(out.shape[0]):
        start = pl.multiple_of(node * own + row * few, few)
        out[node] = product_t(split(turned[pl.ds(start, few), :]), pair_of(node))


def last_kernel(sizes, *refs):
    nodes, part, own, row_count, col_count = sizes
    pieces = refs[:row_count]
    z_high, z_low, full, out, turned = refs[row_count:]
    assemble(pieces, full, part)
    turn(full[...], turned, lambda node: (z_high[node], z_low[node]), out, own, row_count)


def last_step(pieces, z, sizes):
    nodes, part, own, row_count, col_count = sizes
    lanes, rows = nodes * own, row_count * part
    return pl.pallas_call(
        functools.partial(last_kernel, sizes),
        out_shape=[shape_of(rows, lanes), shape_of(nodes, own // row_count, rows)],
        in_specs=[VMEM] * (len(pieces) + 2),
        out_specs=[VMEM] * 2,
        scratch_shapes=[pltpu.VMEM((lanes, rows), F32)],
        compiler_params=PARAMS,
        name="forward_last",
    )(*pieces, *z)


def solve_kernel(sizes, full, lower, *refs):
    nodes, part, own, row_count, col_count = sizes
    lane = lax.broadcasted_iota(jnp.int32, (1, nodes * own), 1) // own
    right = split(full[...])
    solved = jnp.zeros(full.shape, F32)
    for node in range(nodes):
        solved = jnp.where(lane == node, product(split(lower[0, node]), right), solved)
    if len(refs) == 1:
        refs[0][...] = solved
        return
    upper, out, start, turned = refs
    out[...] = solved
    turn(solved, turned, lambda node: split(upper[0, node]), start, own, row_count)


def solve_step(height, full, lower, upper, sizes):
    nodes, part, own, row_count, col_count = sizes
    rows, lanes = full.shape
    level = pl.BlockSpec((1, nodes, rows, rows), lambda i: (height, 0, 0, 0))
    whole = pl.BlockSpec((rows, lanes), lambda i: (0, 0))
    few = own // row_count
    more = height > 0
    return pl.pallas_call(
        functools.partial(solve_kernel, sizes),
        grid=(1,),
        out_shape=[shape_of(rows, lanes)] + [shape_of(nodes, few, rows)] * more,
        in_specs=[whole, level] + [level] * more,
        out_specs=[whole] + [pl.BlockSpec((nodes, few, rows), lambda i: (0, 0, 0))] * more,
        scratch_shapes=[pltpu.VMEM((lanes, rows), F32)] * more,
        compiler_params=STREAM_PARAMS,
        name="solve_level",
    )(full, lower, *([upper] * more))


def compose_kernel(nodes, gathered, inverse, high_out, low_out):
    for node in range(nodes):
        block = gathered[:, 0, node].reshape(WIDTH, WIDTH)
        whole = product(split(inverse[0, node]), split(block))
        high_out[0, node], low_out[0, node] = split(whole)


def compose_step(height, gathered, inverse, row_count):
    per, nodes, part = gathered.shape[1:4]
    first = place_of(height, 1)
    out = shape_of(height, nodes, WIDTH, WIDTH, dtype=BF16)
    out_spec = pl.BlockSpec((1, nodes, WIDTH, WIDTH), lambda i: (i, 0, 0, 0))
    return pl.pallas_call(
        functools.partial(compose_kernel, nodes),
        grid=(height,),
        out_shape=[out, out],
        in_specs=[
            pl.BlockSpec(
                (row_count, 1, nodes, part, WIDTH),
                lambda i: ((first + i) // per, (first + i) % per, 0, 0, 0),
            ),
            pl.BlockSpec((1, nodes, WIDTH, WIDTH), lambda i: (height, 0, 0, 0)),
        ],
        out_specs=[out_spec] * 2,
        compiler_params=STREAM_PARAMS,
        name="compose_level",
    )(gathered, inverse)


def backward_kernel(height, nodes, col_count, parents, pattern, start, high, low, *refs):
    pieces, out = refs[: height * col_count], refs[height * col_count]
    early = refs[height * col_count + 1] if height == 2 else None
    solved = refs[-1]
    for level in range(height):
        for step in range(col_count):
            solved[level, step] = pieces[level * col_count + step][...]
    col = lax.axis_index("col")
    for node in range(nodes):
        total = start[node]
        ancestor = col * nodes + node
        for distance in range(1, height + 1):
            level = height - distance
            ancestor = parents[level, ancestor]
            where = lax.div(ancestor, nodes) ^ col
            left = split(solved[level, where, lax.rem(ancestor, nodes)])
            term = product_t(left, (high[distance - 1, node], low[distance - 1, node]))
            stored = pattern[place_of(height, distance), node] != 0
            total = total - jnp.where(stored, term, 0.0)
        out[node] = total
        if early is not None:
            early[height, node] = total
    if early is not None:
        for level in range(height):
            early[level] = solved[level, 0]


def backward_step(height, parents, pattern, start, composed, solved):
    nodes = start.shape[0]
    col_count = lax.axis_size("col")
    pieces = [piece for level in solved for piece in level]
    outs = [start.shape] + ([(height + 1,) + start.shape] if height == 2 else [])
    return pl.pallas_call(
        functools.partial(backward_kernel, height, nodes, col_count),
        out_shape=[shape_of(*out) for out in outs],
        in_specs=[SMEM, SMEM] + [VMEM] * (3 + len(pieces)),
        out_specs=[VMEM] * len(outs),
        scratch_shapes=[pltpu.VMEM((height, col_count) + start.shape, F32)],
        compiler_params=PARAMS,
        name="backward_level",
    )(parents, pattern, start, *composed, *pieces)


def groups_found(found, groups):
    gz = lax.axis_index("gz")
    if groups == 1:
        others = found[1]
        for value in found[2:]:
            others = others + value
        return [jnp.where(gz == len(found) - 1, found[0], others)]
    values = []
    for which in range(groups):
        value = found[0]
        for step in range(1, groups):
            value = jnp.where((gz ^ step) == which, found[step], value)
        values.append(value)
    return values


def forward_out_kernel(gz_count, nodes, own, *refs):
    parts, out, stage = refs[:-2], refs[-2], refs[-1]
    groups = COLUMNS // own
    per_tile = LANES // COLUMNS
    tiles = out.shape[1]
    block = lax.broadcasted_iota(jnp.int32, (1, LANES), 1) // own
    for level in range(out.shape[0]):
        for chunk in range(nodes * own // LANES):
            start = chunk * LANES
            lanes = slice(start, start + LANES)
            found = [part[:, lanes] for part in parts[level * gz_count : (level + 1) * gz_count]]
            for which, value in enumerate(groups_found(found, groups)):
                stage[chunk, which] = value
            values = [
                stage[chunk, which, pl.ds(row, tiles, stride=per_tile), :]
                for row in range(per_tile)
                for which in range(groups)
            ]
            for node in range(start // own, (start + LANES) // own):
                total = jnp.zeros((tiles, LANES), F32)
                for place, value in enumerate(values):
                    shift = (place * own - (node * own - start)) % LANES
                    value = pltpu.roll(value, shift, 1) if shift else value
                    total = jnp.where(block == place, value, total)
                out[level, :, node, :] = total


def forward_out(parts, nodes, own, gz_count):
    rows, lanes = parts[0].shape
    tiles = rows * COLUMNS // LANES
    return pl.pallas_call(
        functools.partial(forward_out_kernel, gz_count, nodes, own),
        out_shape=shape_of(len(parts) // gz_count, tiles, nodes, LANES),
        in_specs=[VMEM] * len(parts),
        out_specs=VMEM,
        scratch_shapes=[pltpu.VMEM((lanes // LANES, COLUMNS // own, rows, LANES), F32)],
        compiler_params=PARAMS,
        name="forward_out",
    )(*parts)


def backward_out_kernel(nodes, gz_count, own, *refs):
    parts, (out, columns, turned) = refs[:gz_count], refs[-3:]
    groups = COLUMNS // own
    per_tile = LANES // COLUMNS
    tiles = out.shape[1]
    row_count, _, _, few, _ = parts[0].shape
    row = lax.axis_index("row")
    for node in range(nodes):
        for step in range(row_count):
            values = groups_found([part[step, 0, node] for part in parts], groups)
            for which, value in enumerate(values):
                index = which * row_count + (row ^ step)
                columns[pl.ds(pl.multiple_of(index * few, few), few), :] = value
        turned[...] = columns[...].T
        rows = [turned[pl.ds(step, tiles, stride=per_tile), :] for step in range(per_tile)]
        out[0, :, node, :] = jnp.concatenate(rows, axis=1)


def backward_out(parts, before, first, own):
    row_count, levels, nodes, few, rows = parts[0].shape
    tiles = rows * COLUMNS // LANES
    ready = [before] if before is not None else []
    return pl.pallas_call(
        functools.partial(backward_out_kernel, nodes, len(parts), own),
        grid=(levels,),
        out_shape=shape_of(4, tiles, nodes, LANES),
        in_specs=[
            pl.BlockSpec((row_count, 1, nodes, few, rows), lambda i: (0, i, 0, 0, 0))
            for part in parts
        ]
        + [HBM] * len(ready),
        out_specs=pl.BlockSpec((1, tiles, nodes, LANES), lambda i: (first + i, 0, 0, 0)),
        scratch_shapes=[pltpu.VMEM((COLUMNS, rows), F32), pltpu.VMEM((rows, COLUMNS), F32)],
        input_output_aliases={len(parts): 0} if ready else {},
        compiler_params=PARAMS,
        name="backward_out",
    )(*parts, *ready)


def layers_of(value):
    whole = jnp.stack(gather(value, "row"))
    return [whole] + share_layers(whole)


def body(
    right_side,
    layer_sums,
    lower_blocks,
    upper_blocks,
    lower_inverse,
    upper_diagonal_inverses,
    pattern,
    parents,
):
    nodes = right_side.shape[1]
    part = lower_blocks.shape[2]
    gz_count = lax.axis_size("gz")
    row_count = lax.axis_size("row")
    col_count = lax.axis_size("col")
    own = COLUMNS // gz_count if SPLIT else COLUMNS
    lanes = nodes * own
    sizes = (nodes, part, own, row_count, col_count)
    gz = lax.axis_index("gz")

    def tiled(value):
        return value.reshape(4, nodes, part * COLUMNS // LANES, LANES).transpose(0, 2, 1, 3)

    aways = gz_count - 1 if SPLIT else 1
    parts = pl.pallas_call(
        functools.partial(input_kernel, gz_count, nodes, own),
        out_shape=[shape_of(part, lanes)] * 4 + [shape_of(4, part, lanes)] * aways,
        in_specs=[VMEM, VMEM],
        out_specs=[VMEM] * (4 + aways),
        scratch_shapes=[pltpu.VMEM((4, lanes // LANES, COLUMNS // own, part, LANES), F32)],
        compiler_params=STREAM_PARAMS,
        name="input_parts",
    )(tiled(right_side), tiled(layer_sums[0]))
    kept, away = parts[:4], list(parts[4:])

    per = upper_blocks.shape[0] // gz_count
    later, away[0] = lax.optimization_barrier((upper_blocks, away[0]))
    upper_rows = lax.all_gather(
        lax.dynamic_slice_in_dim(later, gz * per, per, 0), ("gz", "row")
    )
    others = [swap_layers(away[min(step, aways) - 1], step) for step in steps_of(gz_count)]
    initial = [kept[level] + sum(other[level] for other in others) for level in range(4)]

    fulls = [None] * 4
    forward = [None] * 4
    starts = [None] * 4
    pending = []
    mine = initial[3]
    for height in (3, 2, 1):
        m = lower_step(height, lower_blocks, lower_inverse)
        fulls[height], sends, pending = forward_step(
            height, gather(mine, "row"), parents, pattern, m, pending, sizes
        )
        mine = initial[height - 1] - sends[0]
        for step in steps_of(col_count):
            mine = mine - swap(sends[step], "col", step)
    z = middle_step(upper_diagonal_inverses, lower_inverse)
    fulls[0], solved = last_step(gather(mine, "row"), z, sizes)

    for height in range(4):
        results = solve_step(height, fulls[height], lower_inverse, upper_diagonal_inverses, sizes)
        forward[height], starts[height] = results[0], results[-1]
    whole = []
    for height in (1, 2, 3):
        composed = compose_step(height, upper_rows, upper_diagonal_inverses, row_count)
        whole.append(gather(solved, "col"))
        results = backward_step(height, parents, pattern, starts[height], composed, whole)
        solved = results[0]
        if height == 2:
            early = results[1]

    forward_parts = []
    for value in forward:
        forward_parts += [value] + share_layers(value)
    forward_all = forward_out(forward_parts, nodes, own, gz_count)
    backward_all = backward_out(layers_of(early), None, 0, own)
    backward_all = backward_out(layers_of(solved[None]), backward_all, 3, own)
    return tuple(
        value.transpose(0, 2, 1, 3).reshape(4, nodes, WIDTH * COLUMNS)
        for value in (forward_all, backward_all)
    )


def solution(mesh):
    in_specs = (
        P(None, "col", "row"),
        P("gz", None, "col", "row"),
        P(None, "col", "row", None),
        P(None, "col", "row", None),
        P(None, "col", None, None),
        P(None, "col", None, None),
        P(None, "col"),
        P(),
    )
    out_specs = (P(None, "col", None), P(None, "col", None))
    return jax.shard_map(body, mesh=mesh, in_specs=in_specs, out_specs=out_specs, check_vma=False)
```

time: 153 us -> 210 us (1.37)
  waiting for transfers between devices: 55.5 us -> 104 us
  Pallas kernels: 30.9 us -> 47.9 us
  starting transfers between devices: 39.2 us -> 32.5 us
  other arithmetic: 2.44 us -> 0.19 us
    ppermute x28 -> x43, waiting for transfers between devices: 55.5 us -> 90.7 us  [the longest x6 89.5 us: share_layers(): lax.ppermute(value, 'gz', [(chief, chief ^ step)])]
    pallas_call x10 -> x15, Pallas kernels: 22.8 us -> 38.1 us  [the longest x3 12.3 us: compose_step(): pl.pallas_call(functools.partial(compose_kernel, nodes), grid=(height,),...]
    all_gather x1, waiting for transfers between devices: 0.01 us -> 12.9 us  [body(): lax.all_gather(lax.dynamic_slice_in_dim(later, gz * per, per, 0), ('gz',...]
    ppermute x28 -> x43, starting transfers between devices: 39.2 us -> 32.4 us  [the longest x36 24.2 us: swap(): return lax.ppermute(value, ('gz', axis), pairs)]
    sub x3, other arithmetic: 2.31 us -> 0.09 us  [body(): mine = mine - swap(sends[step], 'col', step)]
    unnamed x33 -> x21, local copies, waits for them, and re-layouts: 9.06 us -> 8.49 us
  transfers between devices with their start and end apart: 29 -> 44, of which waited for: 22 -> 6; matrix products, arithmetic and copies ran while one was open for 2% -> 0% of each run, Pallas kernels for 18% -> 21%
where the time goes in v4:
time: 210 us; the launch traced here: 208 us
  waiting for transfers between devices  104 us (50%)
  Pallas kernels  47.9 us (23%)
  starting transfers between devices  32.5 us (15%)
  between operations  14.8 us (7%)
  local copies, waits for them, and re-layouts  9.46 us (5%)
    ppermute x6, waiting for transfers between devices, share_layers(): lax.ppermute(value, 'gz', [(chief, chief ^ step)])  89.5 us
    ppermute x36, starting transfers between devices, swap(): return lax.ppermute(value, ('gz', axis), pairs)  24.2 us
    all_gather x1, waiting for transfers between devices, body(): lax.all_gather(lax.dynamic_slice_in_dim(later, gz * per, per, 0), ('gz',...  12.9 us
    pallas_call x3, Pallas kernels, compose_step(): pl.pallas_call(functools.partial(compose_kernel, nodes), grid=(height,),...  12.3 us
    pallas_call x4, Pallas kernels, solve_step(): pl.pallas_call(functools.partial(solve_kernel, sizes), grid=(1,), out_sha...  9.4 us
    unnamed x21, local copies, waits for them, and re-layouts  8.49 us
    ppermute x6, starting transfers between devices, share_layers(): lax.ppermute(value, 'gz', [(chief, chief ^ step)])  7.75 us
    pallas_call x3, Pallas kernels, lower_step(): pl.pallas_call(functools.partial(lower_kernel, nodes), grid=(height,), ou...  7.31 us
  transfers between devices with their start and end apart: 44, of which 6 were waited for; matrix products, arithmetic and copies ran while one was open for 0% of the time, Pallas kernels for 21%

profile of v4, /device:TPU:0, one launch (start us, length us, event | category | flops | bytes accessed | tf_op | source)
XLA Modules:
  0.0 208.4 jit_solution(7724937243853962065)
XLA Ops:
  8.3 1.5 input_parts.1
  14.7 3.2 %lower_products.3 = (bf16[3,4,64,256]{3,2,1,0:T(8,128)(2,1)S(1)}, bf16[3,4,64,256]{3,2,1,0:T(8,128)(2,1)S(1)}) custom-call(f32[6,4,64,256]{3,2,1,0:T(8,128)} %blocks.5, f32[4,4,256,256]{3,2,1,0:T(8,128)} %lower.9), custom_call_target="tpu_custom_call" | custom-call | tf_op jit(solution)/shard_map/lower_products/pallas_call | solution.py:134
  18.0 1.7 forward_level.3
  23.8 2.3 %lower_products.4 = (bf16[2,4,64,256]{3,2,1,0:T(8,128)(2,1)S(1)}, bf16[2,4,64,256]{3,2,1,0:T(8,128)(2,1)S(1)}) custom-call(f32[6,4,64,256]{3,2,1,0:T(8,128)} %blocks.5, f32[4,4,256,256]{3,2,1,0:T(8,128)} %lower.9), custom_call_target="tpu_custom_call" | custom-call | tf_op jit(solution)/shard_map/lower_products/pallas_call | solution.py:134
  26.1 1.4 forward_level.4
  31.7 1.7 lower_products.5
  38.7 3.6 %middle_product.1 = (bf16[4,256,256]{2,1,0:T(8,128)(2,1)S(1)}, bf16[4,256,256]{2,1,0:T(8,128)(2,1)}) custom-call(f32[4,4,256,256]{3,2,1,0:T(8,128)} %inverse.11, f32[4,4,256,256]{3,2,1,0:T(8,128)} %lower.9), custom_call_target="tpu_custom_call" | custom-call | tf_op jit(solution)/shard_map/middle_product/pallas_call | solution.py:158
  45.8 2.6 %solve_level.5 = (f32[256,256]{1,0:T(8,128)S(1)}, f32[4,16,256]{2,1,0:T(8,128)S(1)}) custom-call(f32[256,256]{1,0:T(8,128)S(1)} %get-tuple-element.81.full, f32[4,4,256,256]{3,2,1,0:T(8,128)} %lower.9, f32[4,4,256,256]{3,2,1,0:T(8,128)} %inverse.11), custom_call_target="tpu_custom_call" | custom-call | tf_op jit(solution)/shard_map/solve_level/pallas_call | solution.py:280
  48.4 12.9 %all-gather.3.cloned.1.call-done = f32[24,4,64,256]{3,2,1,0:T(8,128)} async-done(((f32[3,4,64,256]{3,2,1,0:T(8,128)}), f32[24,4,64,256]{3,2,1,0:T(8,128)}) %all-gather.3.cloned.1.call-update) | async-done | bytes 6291472 | tf_op jit(solution)/shard_map/all_gather | solution.py:502
  61.3 2.9 %compose_level.4 = (bf16[1,4,256,256]{3,2,1,0:T(8,128)(2,1)S(1)}, bf16[1,4,256,256]{3,2,1,0:T(8,128)(2,1)}) custom-call(f32[8,3,4,64,256]{4,3,2,1,0:T(8,128)} %bitcast.68, f32[4,4,256,256]{3,2,1,0:T(8,128)} %inverse.11), custom_call_target="tpu_custom_call" | custom-call | tf_op jit(solution)/shard_map/compose_level/pallas_call | solution.py:304
  68.4 2.5 %solve_level.6 = (f32[256,256]{1,0:T(8,128)S(1)}, f32[4,16,256]{2,1,0:T(8,128)S(1)}) custom-call(f32[256,256]{1,0:T(8,128)S(1)} %get-tuple-element.83.full, f32[4,4,256,256]{3,2,1,0:T(8,128)} %lower.9, f32[4,4,256,256]{3,2,1,0:T(8,128)} %inverse.11), custom_call_target="tpu_custom_call" | custom-call | tf_op jit(solution)/shard_map/solve_level/pallas_call | solution.py:280
  70.9 3.8 %compose_level.5 = (bf16[2,4,256,256]{3,2,1,0:T(8,128)(2,1)}, bf16[2,4,256,256]{3,2,1,0:T(8,128)(2,1)}) custom-call(f32[8,3,4,64,256]{4,3,2,1,0:T(8,128)} %bitcast.69, f32[4,4,256,256]{3,2,1,0:T(8,128)} %inverse.11), custom_call_target="tpu_custom_call" | custom-call | tf_op jit(solution)/shard_map/compose_level/pallas_call | solution.py:304
  81.9 2.5 %solve_level.7 = (f32[256,256]{1,0:T(8,128)S(1)}, f32[4,16,256]{2,1,0:T(8,128)S(1)}) custom-call(f32[256,256]{1,0:T(8,128)S(1)} %get-tuple-element.85.full, f32[4,4,256,256]{3,2,1,0:T(8,128)} %lower.9, f32[4,4,256,256]{3,2,1,0:T(8,128)} %inverse.11), custom_call_target="tpu_custom_call" | custom-call | tf_op jit(solution)/shard_map/solve_level/pallas_call | solution.py:280
  87.9 5.5 %compose_level.3 = (bf16[3,4,256,256]{3,2,1,0:T(8,128)(2,1)}, bf16[3,4,256,256]{3,2,1,0:T(8,128)(2,1)}) custom-call(f32[8,3,4,64,256]{4,3,2,1,0:T(8,128)} %bitcast.70, f32[4,4,256,256]{3,2,1,0:T(8,128)} %inverse.11), custom_call_target="tpu_custom_call" | custom-call | tf_op jit(solution)/shard_map/compose_level/pallas_call | solution.py:304
  93.4 1.4 copy-done.1
  94.9 1.4 copy-done.2
  96.3 1.6 backward_level.5
  99.9 1.8 solve_level.4.refs_0_
  105.6 57.1 %collective-permute-done.25.refs_7_ = f32[256,256]{1,0:T(8,128)S(1)} collective-permute-done((f32[256,256]{1,0:T(8,128)S(1)}, f32[256,256]{1,0:T(8,128)S(1)}, u32[]{:S(2)}, u32[]{:S(2)}) %collective-permute-start.25) | collective-permute-done | bytes 262176 | tf_op jit(solution)/shard_map/ppermute | solution.py:78
  164.1 29.7 %collective-permute-done.24.refs_5_ = f32[256,256]{1,0:T(8,128)S(1)} collective-permute-done((f32[256,256]{1,0:T(8,128)S(1)}, f32[256,256]{1,0:T(8,128)S(1)}, u32[]{:S(2)}, u32[]{:S(2)}) %collective-permute-start.24) | collective-permute-done | bytes 262176 | tf_op jit(solution)/shard_map/ppermute | solution.py:78
  193.7 1.3 collective-permute-done.23.refs_3_
  195.1 1.3 collective-permute-done.22.refs_1_
  196.4 1.7 forward_out.1
  198.1 2.3 %backward_out.2.refs_2_ = f32[4,128,4,128]{3,2,1,0:T(4,128)} custom-call(f32[4,3,4,16,256]{4,3,2,1,0:T(8,128)S(1)} %pad_maximum_fusion.refs_0_, f32[4,3,4,16,256]{4,3,2,1,0:T(8,128)S(1)} %collective-permute-done.42.refs_1_), custom_call_target="tpu_custom_call" | custom-call | tf_op jit(solution)/shard_map/backward_out/pallas_call | solution.py:443
  (115 shorter events, 45.6 us)
Async XLA Ops:
  7.2 54.1 %all-gather.3.cloned.1.call-start = ((), (), s32[]{:S(2)}) async-start(), calls=%async_computation | async-start | bytes 7077888 | tf_op jit(solution)/shard_map/all_gather | solution.py:502
  12.5 5.4 %collective-permute-start.1 = (f32[64,256]{1,0:T(8,128)S(1)}, f32[64,256]{1,0:T(8,128)S(1)}, u32[]{:S(2)}, u32[]{:S(2)}) collective-permute-start(f32[64,256]{1,0:T(8,128)S(1)} %fusion.refs_0_), channel_id=1, source_target_pairs={{16,20},{20,16},{24,28},{28,24},{17,21},{21,17},{25,29},{29,25},{1... | collective-permute-start | bytes 196616 | tf_op jit(solution)/shard_map/ppermute | solution.py:66
  13.2 4.7 %collective-permute-start.2 = (f32[64,256]{1,0:T(8,128)S(1)}, f32[64,256]{1,0:T(8,128)S(1)}, u32[]{:S(2)}, u32[]{:S(2)}) collective-permute-start(f32[64,256]{1,0:T(8,128)S(1)} %fusion.refs_0_), channel_id=1, source_target_pairs={{16,24},{20,28},{24,16},{28,20},{17,25},{21,29},{25,17},{29,21},{1... | collective-permute-start | bytes 196616 | tf_op jit(solution)/shard_map/ppermute | solution.py:66
  21.8 4.3 %collective-permute-start.7 = (f32[64,256]{1,0:T(8,128)S(1)}, f32[64,256]{1,0:T(8,128)S(1)}, u32[]{:S(2)}, u32[]{:S(2)}) collective-permute-start(f32[64,256]{1,0:T(8,128)S(1)} %fusion.5.refs_0_), channel_id=1, source_target_pairs={{16,20},{20,16},{24,28},{28,24},{17,21},{21,17},{25,29},{29,25},{1... | collective-permute-start | bytes 196616 | tf_op jit(solution)/shard_map/ppermute | solution.py:66
  36.7 5.6 %collective-permute-start.19 = (f32[64,256]{1,0:T(8,128)S(1)}, f32[64,256]{1,0:T(8,128)S(1)}, u32[]{:S(2)}, u32[]{:S(2)}) collective-permute-start(f32[64,256]{1,0:T(8,128)S(1)} %fusion.15.refs_0_), channel_id=1, source_target_pairs={{16,20},{20,16},{24,28},{28,24},{17,21},{21,17},{25,29},{29,25},{1... | collective-permute-start | bytes 196616 | tf_op jit(solution)/shard_map/ppermute | solution.py:66
  37.4 4.9 %collective-permute-start.20 = (f32[64,256]{1,0:T(8,128)S(1)}, f32[64,256]{1,0:T(8,128)S(1)}, u32[]{:S(2)}, u32[]{:S(2)}) collective-permute-start(f32[64,256]{1,0:T(8,128)S(1)} %fusion.15.refs_0_), channel_id=1, source_target_pairs={{16,24},{20,28},{24,16},{28,20},{17,25},{21,29},{25,17},{29,21},{1... | collective-permute-start | bytes 196616 | tf_op jit(solution)/shard_map/ppermute | solution.py:66
  38.1 4.2 %collective-permute-start.21 = (f32[64,256]{1,0:T(8,128)S(1)}, f32[64,256]{1,0:T(8,128)S(1)}, u32[]{:S(2)}, u32[]{:S(2)}) collective-permute-start(f32[64,256]{1,0:T(8,128)S(1)} %fusion.15.refs_0_), channel_id=1, source_target_pairs={{16,28},{20,24},{24,20},{28,16},{17,29},{21,25},{25,21},{29,17},{1... | collective-permute-start | bytes 196616 | tf_op jit(solution)/shard_map/ppermute | solution.py:66
  43.8 20.5 %collective-permute-start.26 = (f32[4,16,256]{2,1,0:T(8,128)S(1)}, f32[4,16,256]{2,1,0:T(8,128)S(1)}, u32[]{:S(2)}, u32[]{:S(2)}) collective-permute-start(f32[4,16,256]{2,1,0:T(8,128)S(1)} %get-tuple-element.91.refs_0_), channel_id=1, source_target_pairs={{16,17},{17,16},{18,19},{19,18},{20,21},{21,20},{22,23},{23,22},{2... | collective-permute-start | bytes 196616 | tf_op jit(solution)/shard_map/ppermute | solution.py:66
  44.5 19.8 %collective-permute-start.27 = (f32[4,16,256]{2,1,0:T(8,128)S(1)}, f32[4,16,256]{2,1,0:T(8,128)S(1)}, u32[]{:S(2)}, u32[]{:S(2)}) collective-permute-start(f32[4,16,256]{2,1,0:T(8,128)S(1)} %get-tuple-element.91.refs_0_), channel_id=1, source_target_pairs={{16,18},{17,19},{18,16},{19,17},{20,22},{21,23},{22,20},{23,21},{2... | collective-permute-start | bytes 196616 | tf_op jit(solution)/shard_map/ppermute | solution.py:66
  45.1 19.1 %collective-permute-start.28 = (f32[4,16,256]{2,1,0:T(8,128)S(1)}, f32[4,16,256]{2,1,0:T(8,128)S(1)}, u32[]{:S(2)}, u32[]{:S(2)}) collective-permute-start(f32[4,16,256]{2,1,0:T(8,128)S(1)} %get-tuple-element.91.refs_0_), channel_id=1, source_target_pairs={{16,19},{17,18},{18,17},{19,16},{20,23},{21,22},{22,21},{23,20},{2... | collective-permute-start | bytes 196616 | tf_op jit(solution)/shard_map/ppermute | solution.py:66
  66.3 8.3 %collective-permute-start.29 = (f32[4,16,256]{2,1,0:T(8,128)S(1)}, f32[4,16,256]{2,1,0:T(8,128)S(1)}, u32[]{:S(2)}, u32[]{:S(2)}) collective-permute-start(f32[4,16,256]{2,1,0:T(8,128)S(1)} %backward_level.3.refs_4_), channel_id=1, source_target_pairs={{16,17},{17,16},{18,19},{19,18},{20,21},{21,20},{22,23},{23,22},{2... | collective-permute-start | bytes 196616 | tf_op jit(solution)/shard_map/ppermute | solution.py:66
  67.0 7.7 %collective-permute-start.30 = (f32[4,16,256]{2,1,0:T(8,128)S(1)}, f32[4,16,256]{2,1,0:T(8,128)S(1)}, u32[]{:S(2)}, u32[]{:S(2)}) collective-permute-start(f32[4,16,256]{2,1,0:T(8,128)S(1)} %backward_level.3.refs_4_), channel_id=1, source_target_pairs={{16,18},{17,19},{18,16},{19,17},{20,22},{21,23},{22,20},{23,21},{2... | collective-permute-start | bytes 196616 | tf_op jit(solution)/shard_map/ppermute | solution.py:66
  67.7 7.0 %collective-permute-start.31 = (f32[4,16,256]{2,1,0:T(8,128)S(1)}, f32[4,16,256]{2,1,0:T(8,128)S(1)}, u32[]{:S(2)}, u32[]{:S(2)}) collective-permute-start(f32[4,16,256]{2,1,0:T(8,128)S(1)} %backward_level.3.refs_4_), channel_id=1, source_target_pairs={{16,19},{17,18},{18,17},{19,16},{20,23},{21,22},{22,21},{23,20},{2... | collective-permute-start | bytes 196616 | tf_op jit(solution)/shard_map/ppermute | solution.py:66
  80.6 117.6 %collective-permute-start.42 = (f32[4,3,4,16,256]{4,3,2,1,0:T(8,128)S(1)}, f32[4,3,4,16,256]{4,3,2,1,0:T(8,128)S(1)}, u32[]{:S(2)}, u32[]{:S(2)}) collective-permute-start(f32[4,3,4,16,256]{4,3,2,1,0:T(8,128)S(1)} %pad_maximum_fusion.refs_0_), channel_id=1, source_target_pairs={{16,0},{17,1},{18,2},{19,3},{20,4},{21,5},{22,6},{23,7},{24,8},{25... | collective-permute-start | bytes 2359304 | tf_op jit(solution)/shard_map/ppermute | solution.py:78
  84.4 78.4 %collective-permute-start.25 = (f32[256,256]{1,0:T(8,128)S(1)}, f32[256,256]{1,0:T(8,128)S(1)}, u32[]{:S(2)}, u32[]{:S(2)}) collective-permute-start(f32[256,256]{1,0:T(8,128)S(1)} %get-tuple-element.86.refs_6_), channel_id=1, source_target_pairs={{16,0},{17,1},{18,2},{19,3},{20,4},{21,5},{22,6},{23,7},{24,8},{25... | collective-permute-start | bytes 786440 | tf_op jit(solution)/shard_map/ppermute | solution.py:78
  85.7 7.7 %collective-permute-start.32 = (f32[4,16,256]{2,1,0:T(8,128)S(1)}, f32[4,16,256]{2,1,0:T(8,128)S(1)}, u32[]{:S(2)}, u32[]{:S(2)}) collective-permute-start(f32[4,16,256]{2,1,0:T(8,128)S(1)} %get-tuple-element.98.refs_8_), channel_id=1, source_target_pairs={{16,17},{17,16},{18,19},{19,18},{20,21},{21,20},{22,23},{23,22},{2... | collective-permute-start | bytes 196616 | tf_op jit(solution)/shard_map/ppermute | solution.py:66
  86.4 7.1 %collective-permute-start.33 = (f32[4,16,256]{2,1,0:T(8,128)S(1)}, f32[4,16,256]{2,1,0:T(8,128)S(1)}, u32[]{:S(2)}, u32[]{:S(2)}) collective-permute-start(f32[4,16,256]{2,1,0:T(8,128)S(1)} %get-tuple-element.98.refs_8_), channel_id=1, source_target_pairs={{16,18},{17,19},{18,16},{19,17},{20,22},{21,23},{22,20},{23,21},{2... | collective-permute-start | bytes 196616 | tf_op jit(solution)/shard_map/ppermute | solution.py:66
  87.0 6.4 %collective-permute-start.34 = (f32[4,16,256]{2,1,0:T(8,128)S(1)}, f32[4,16,256]{2,1,0:T(8,128)S(1)}, u32[]{:S(2)}, u32[]{:S(2)}) collective-permute-start(f32[4,16,256]{2,1,0:T(8,128)S(1)} %get-tuple-element.98.refs_8_), channel_id=1, source_target_pairs={{16,19},{17,18},{18,17},{19,16},{20,23},{21,22},{22,21},{23,20},{2... | collective-permute-start | bytes 196616 | tf_op jit(solution)/shard_map/ppermute | solution.py:66
  98.5 4.5 %collective-permute-start.36 = (f32[1,4,16,256]{3,2,1,0:T(8,128)S(1)}, f32[1,4,16,256]{3,2,1,0:T(8,128)S(1)}, u32[]{:S(2)}, u32[]{:S(2)}) collective-permute-start(f32[1,4,16,256]{3,2,1,0:T(8,128)S(1)} %bitcast.63), channel_id=1, source_target_pairs={{16,24},{20,28},{24,16},{28,20},{17,25},{21,29},{25,17},{29,21},{1... | collective-permute-start | bytes 196616 | tf_op jit(solution)/shard_map/ppermute | solution.py:66
  99.2 5.1 %collective-permute-start.37 = (f32[1,4,16,256]{3,2,1,0:T(8,128)S(1)}, f32[1,4,16,256]{3,2,1,0:T(8,128)S(1)}, u32[]{:S(2)}, u32[]{:S(2)}) collective-permute-start(f32[1,4,16,256]{3,2,1,0:T(8,128)S(1)} %bitcast.64), channel_id=1, source_target_pairs={{16,28},{20,24},{24,20},{28,16},{17,29},{21,25},{25,21},{29,17},{1... | collective-permute-start | bytes 196616 | tf_op jit(solution)/shard_map/ppermute | solution.py:66
  101.7 92.1 %collective-permute-start.24 = (f32[256,256]{1,0:T(8,128)S(1)}, f32[256,256]{1,0:T(8,128)S(1)}, u32[]{:S(2)}, u32[]{:S(2)}) collective-permute-start(f32[256,256]{1,0:T(8,128)S(1)} %get-tuple-element.84.refs_4_), channel_id=1, source_target_pairs={{16,0},{17,1},{18,2},{19,3},{20,4},{21,5},{22,6},{23,7},{24,8},{25... | collective-permute-start | bytes 786440 | tf_op jit(solution)/shard_map/ppermute | solution.py:78
  103.0 92.1 %collective-permute-start.23 = (f32[256,256]{1,0:T(8,128)S(1)}, f32[256,256]{1,0:T(8,128)S(1)}, u32[]{:S(2)}, u32[]{:S(2)}) collective-permute-start(f32[256,256]{1,0:T(8,128)S(1)} %get-tuple-element.82.refs_2_), channel_id=1, source_target_pairs={{16,0},{17,1},{18,2},{19,3},{20,4},{21,5},{22,6},{23,7},{24,8},{25... | collective-permute-start | bytes 786440 | tf_op jit(solution)/shard_map/ppermute | solution.py:78
  104.3 92.1 %collective-permute-start.22 = (f32[256,256]{1,0:T(8,128)S(1)}, f32[256,256]{1,0:T(8,128)S(1)}, u32[]{:S(2)}, u32[]{:S(2)}) collective-permute-start(f32[256,256]{1,0:T(8,128)S(1)} %solve_level.4.refs_0_), channel_id=1, source_target_pairs={{16,0},{17,1},{18,2},{19,3},{20,4},{21,5},{22,6},{23,7},{24,8},{25... | collective-permute-start | bytes 786440 | tf_op jit(solution)/shard_map/ppermute | solution.py:78
  162.8 37.7 %collective-permute-start.38 = (f32[4,1,4,16,256]{4,3,2,1,0:T(8,128)S(1)}, f32[4,1,4,16,256]{4,3,2,1,0:T(8,128)S(1)}, u32[]{:S(2)}, u32[]{:S(2)}) collective-permute-start(f32[4,1,4,16,256]{4,3,2,1,0:T(8,128)S(1)} %pad_maximum_fusion.1.refs_0_), channel_id=1, source_target_pairs={{16,0},{17,1},{18,2},{19,3},{20,4},{21,5},{22,6},{23,7},{24,8},{25... | collective-permute-start | bytes 786440 | tf_op jit(solution)/shard_map/ppermute | solution.py:78
  (30 other events, 63.7 us)
Sparse Core Ops, SparseCore 0:
  11.0 50.3 all-gather.2

commit v5 on v4

--- a/solution.py
+++ b/solution.py
@@ -63,7 +63,8 @@
     gz_count = lax.axis_size("gz")
     cores = range(gz_count) if SPLIT else [gz_count - 1]
     pairs = [(g * count + i, g * count + (i ^ step)) for g in cores for i in range(count)]
-    return lax.ppermute(value, ("gz", axis), pairs)
+    idle = range(gz_count * count - len(pairs))
+    return lax.ppermute(value, ("gz", axis), pairs + [(i, i) for i in idle])
 
 
 def swap_layers(value, step):

time: 210 us -> 210 us (level)
  no operation moved by 1% of the time
where the time goes in v5:
time: 210 us; the launch traced here: 208 us
  waiting for transfers between devices  104 us (50%)
  Pallas kernels  47.9 us (23%)
  starting transfers between devices  32.5 us (15%)
  between operations  14.8 us (7%)
  local copies, waits for them, and re-layouts  9.46 us (5%)
    ppermute x6, waiting for transfers between devices, share_layers(): lax.ppermute(value, 'gz', [(chief, chief ^ step)])  89.4 us
    ppermute x36, starting transfers between devices, swap(): return lax.ppermute(value, ('gz', axis), pairs + [(i, i) for i in idle])  24.2 us
    all_gather x1, waiting for transfers between devices, body(): lax.all_gather(lax.dynamic_slice_in_dim(later, gz * per, per, 0), ('gz',...  12.9 us
    pallas_call x3, Pallas kernels, compose_step(): pl.pallas_call(functools.partial(compose_kernel, nodes), grid=(height,),...  12.3 us
    pallas_call x4, Pallas kernels, solve_step(): pl.pallas_call(functools.partial(solve_kernel, sizes), grid=(1,), out_sha...  9.4 us
    unnamed x21, local copies, waits for them, and re-layouts  8.49 us
    ppermute x6, starting transfers between devices, share_layers(): lax.ppermute(value, 'gz', [(chief, chief ^ step)])  7.75 us
    pallas_call x3, Pallas kernels, lower_step(): pl.pallas_call(functools.partial(lower_kernel, nodes), grid=(height,), ou...  7.31 us
  transfers between devices with their start and end apart: 44, of which 6 were waited for; matrix products, arithmetic and copies ran while one was open for 0% of the time, Pallas kernels for 21%

profile of v5, /device:TPU:0, one launch (start us, length us, event | category | flops | bytes accessed | tf_op | source)
XLA Modules:
  0.0 208.4 jit_solution(11425094624833645346)
XLA Ops:
  8.3 1.5 input_parts.1
  14.7 3.2 %lower_products.3 = (bf16[3,4,64,256]{3,2,1,0:T(8,128)(2,1)S(1)}, bf16[3,4,64,256]{3,2,1,0:T(8,128)(2,1)S(1)}) custom-call(f32[6,4,64,256]{3,2,1,0:T(8,128)} %blocks.5, f32[4,4,256,256]{3,2,1,0:T(8,128)} %lower.9), custom_call_target="tpu_custom_call" | custom-call | tf_op jit(solution)/shard_map/lower_products/pallas_call | solution.py:135
  18.0 1.7 forward_level.3
  23.8 2.3 %lower_products.4 = (bf16[2,4,64,256]{3,2,1,0:T(8,128)(2,1)S(1)}, bf16[2,4,64,256]{3,2,1,0:T(8,128)(2,1)S(1)}) custom-call(f32[6,4,64,256]{3,2,1,0:T(8,128)} %blocks.5, f32[4,4,256,256]{3,2,1,0:T(8,128)} %lower.9), custom_call_target="tpu_custom_call" | custom-call | tf_op jit(solution)/shard_map/lower_products/pallas_call | solution.py:135
  26.1 1.4 forward_level.4
  31.7 1.7 lower_products.5
  38.7 3.6 %middle_product.1 = (bf16[4,256,256]{2,1,0:T(8,128)(2,1)S(1)}, bf16[4,256,256]{2,1,0:T(8,128)(2,1)}) custom-call(f32[4,4,256,256]{3,2,1,0:T(8,128)} %inverse.11, f32[4,4,256,256]{3,2,1,0:T(8,128)} %lower.9), custom_call_target="tpu_custom_call" | custom-call | tf_op jit(solution)/shard_map/middle_product/pallas_call | solution.py:159
  45.8 2.6 %solve_level.5 = (f32[256,256]{1,0:T(8,128)S(1)}, f32[4,16,256]{2,1,0:T(8,128)S(1)}) custom-call(f32[256,256]{1,0:T(8,128)S(1)} %get-tuple-element.81.full, f32[4,4,256,256]{3,2,1,0:T(8,128)} %lower.9, f32[4,4,256,256]{3,2,1,0:T(8,128)} %inverse.11), custom_call_target="tpu_custom_call" | custom-call | tf_op jit(solution)/shard_map/solve_level/pallas_call | solution.py:281
  48.4 12.9 %all-gather.3.cloned.1.call-done = f32[24,4,64,256]{3,2,1,0:T(8,128)} async-done(((f32[3,4,64,256]{3,2,1,0:T(8,128)}), f32[24,4,64,256]{3,2,1,0:T(8,128)}) %all-gather.3.cloned.1.call-update) | async-done | bytes 6291472 | tf_op jit(solution)/shard_map/all_gather | solution.py:503
  61.3 2.9 %compose_level.4 = (bf16[1,4,256,256]{3,2,1,0:T(8,128)(2,1)S(1)}, bf16[1,4,256,256]{3,2,1,0:T(8,128)(2,1)}) custom-call(f32[8,3,4,64,256]{4,3,2,1,0:T(8,128)} %bitcast.68, f32[4,4,256,256]{3,2,1,0:T(8,128)} %inverse.11), custom_call_target="tpu_custom_call" | custom-call | tf_op jit(solution)/shard_map/compose_level/pallas_call | solution.py:305
  68.4 2.5 %solve_level.6 = (f32[256,256]{1,0:T(8,128)S(1)}, f32[4,16,256]{2,1,0:T(8,128)S(1)}) custom-call(f32[256,256]{1,0:T(8,128)S(1)} %get-tuple-element.83.full, f32[4,4,256,256]{3,2,1,0:T(8,128)} %lower.9, f32[4,4,256,256]{3,2,1,0:T(8,128)} %inverse.11), custom_call_target="tpu_custom_call" | custom-call | tf_op jit(solution)/shard_map/solve_level/pallas_call | solution.py:281
  70.9 3.8 %compose_level.5 = (bf16[2,4,256,256]{3,2,1,0:T(8,128)(2,1)}, bf16[2,4,256,256]{3,2,1,0:T(8,128)(2,1)}) custom-call(f32[8,3,4,64,256]{4,3,2,1,0:T(8,128)} %bitcast.69, f32[4,4,256,256]{3,2,1,0:T(8,128)} %inverse.11), custom_call_target="tpu_custom_call" | custom-call | tf_op jit(solution)/shard_map/compose_level/pallas_call | solution.py:305
  81.9 2.5 %solve_level.7 = (f32[256,256]{1,0:T(8,128)S(1)}, f32[4,16,256]{2,1,0:T(8,128)S(1)}) custom-call(f32[256,256]{1,0:T(8,128)S(1)} %get-tuple-element.85.full, f32[4,4,256,256]{3,2,1,0:T(8,128)} %lower.9, f32[4,4,256,256]{3,2,1,0:T(8,128)} %inverse.11), custom_call_target="tpu_custom_call" | custom-call | tf_op jit(solution)/shard_map/solve_level/pallas_call | solution.py:281
  87.9 5.5 %compose_level.3 = (bf16[3,4,256,256]{3,2,1,0:T(8,128)(2,1)}, bf16[3,4,256,256]{3,2,1,0:T(8,128)(2,1)}) custom-call(f32[8,3,4,64,256]{4,3,2,1,0:T(8,128)} %bitcast.70, f32[4,4,256,256]{3,2,1,0:T(8,128)} %inverse.11), custom_call_target="tpu_custom_call" | custom-call | tf_op jit(solution)/shard_map/compose_level/pallas_call | solution.py:305
  93.4 1.4 copy-done.1
  94.9 1.4 copy-done.2
  96.3 1.6 backward_level.5
  99.9 1.8 solve_level.4.refs_0_
  105.6 57.1 %collective-permute-done.25.refs_7_ = f32[256,256]{1,0:T(8,128)S(1)} collective-permute-done((f32[256,256]{1,0:T(8,128)S(1)}, f32[256,256]{1,0:T(8,128)S(1)}, u32[]{:S(2)}, u32[]{:S(2)}) %collective-permute-start.25) | collective-permute-done | bytes 262176 | tf_op jit(solution)/shard_map/ppermute | solution.py:79
  164.0 29.7 %collective-permute-done.24.refs_5_ = f32[256,256]{1,0:T(8,128)S(1)} collective-permute-done((f32[256,256]{1,0:T(8,128)S(1)}, f32[256,256]{1,0:T(8,128)S(1)}, u32[]{:S(2)}, u32[]{:S(2)}) %collective-permute-start.24) | collective-permute-done | bytes 262176 | tf_op jit(solution)/shard_map/ppermute | solution.py:79
  193.7 1.3 collective-permute-done.23.refs_3_
  195.0 1.3 collective-permute-done.22.refs_1_
  196.4 1.7 forward_out.1
  198.1 2.3 %backward_out.2.refs_2_ = f32[4,128,4,128]{3,2,1,0:T(4,128)} custom-call(f32[4,3,4,16,256]{4,3,2,1,0:T(8,128)S(1)} %pad_maximum_fusion.refs_0_, f32[4,3,4,16,256]{4,3,2,1,0:T(8,128)S(1)} %collective-permute-done.42.refs_1_), custom_call_target="tpu_custom_call" | custom-call | tf_op jit(solution)/shard_map/backward_out/pallas_call | solution.py:444
  (115 shorter events, 45.6 us)
Async XLA Ops:
  7.2 54.1 %all-gather.3.cloned.1.call-start = ((), (), s32[]{:S(2)}) async-start(), calls=%async_computation | async-start | bytes 7077888 | tf_op jit(solution)/shard_map/all_gather | solution.py:503
  12.5 5.4 %collective-permute-start.1 = (f32[64,256]{1,0:T(8,128)S(1)}, f32[64,256]{1,0:T(8,128)S(1)}, u32[]{:S(2)}, u32[]{:S(2)}) collective-permute-start(f32[64,256]{1,0:T(8,128)S(1)} %fusion.refs_0_), channel_id=1, source_target_pairs={{16,20},{20,16},{24,28},{28,24},{0,0},{4,4},{8,8},{12,12},{17,21},... | collective-permute-start | bytes 196616 | tf_op jit(solution)/shard_map/ppermute | solution.py:67
  13.2 4.7 %collective-permute-start.2 = (f32[64,256]{1,0:T(8,128)S(1)}, f32[64,256]{1,0:T(8,128)S(1)}, u32[]{:S(2)}, u32[]{:S(2)}) collective-permute-start(f32[64,256]{1,0:T(8,128)S(1)} %fusion.refs_0_), channel_id=1, source_target_pairs={{16,24},{20,28},{24,16},{28,20},{0,0},{4,4},{8,8},{12,12},{17,25},... | collective-permute-start | bytes 196616 | tf_op jit(solution)/shard_map/ppermute | solution.py:67
  21.8 4.3 %collective-permute-start.7 = (f32[64,256]{1,0:T(8,128)S(1)}, f32[64,256]{1,0:T(8,128)S(1)}, u32[]{:S(2)}, u32[]{:S(2)}) collective-permute-start(f32[64,256]{1,0:T(8,128)S(1)} %fusion.5.refs_0_), channel_id=1, source_target_pairs={{16,20},{20,16},{24,28},{28,24},{0,0},{4,4},{8,8},{12,12},{17,21},... | collective-permute-start | bytes 196616 | tf_op jit(solution)/shard_map/ppermute | solution.py:67
  36.7 5.6 %collective-permute-start.19 = (f32[64,256]{1,0:T(8,128)S(1)}, f32[64,256]{1,0:T(8,128)S(1)}, u32[]{:S(2)}, u32[]{:S(2)}) collective-permute-start(f32[64,256]{1,0:T(8,128)S(1)} %fusion.15.refs_0_), channel_id=1, source_target_pairs={{16,20},{20,16},{24,28},{28,24},{0,0},{4,4},{8,8},{12,12},{17,21},... | collective-permute-start | bytes 196616 | tf_op jit(solution)/shard_map/ppermute | solution.py:67
  37.4 4.9 %collective-permute-start.20 = (f32[64,256]{1,0:T(8,128)S(1)}, f32[64,256]{1,0:T(8,128)S(1)}, u32[]{:S(2)}, u32[]{:S(2)}) collective-permute-start(f32[64,256]{1,0:T(8,128)S(1)} %fusion.15.refs_0_), channel_id=1, source_target_pairs={{16,24},{20,28},{24,16},{28,20},{0,0},{4,4},{8,8},{12,12},{17,25},... | collective-permute-start | bytes 196616 | tf_op jit(solution)/shard_map/ppermute | solution.py:67
  38.1 4.2 %collective-permute-start.21 = (f32[64,256]{1,0:T(8,128)S(1)}, f32[64,256]{1,0:T(8,128)S(1)}, u32[]{:S(2)}, u32[]{:S(2)}) collective-permute-start(f32[64,256]{1,0:T(8,128)S(1)} %fusion.15.refs_0_), channel_id=1, source_target_pairs={{16,28},{20,24},{24,20},{28,16},{0,0},{4,4},{8,8},{12,12},{17,29},... | collective-permute-start | bytes 196616 | tf_op jit(solution)/shard_map/ppermute | solution.py:67
  43.8 20.5 %collective-permute-start.26 = (f32[4,16,256]{2,1,0:T(8,128)S(1)}, f32[4,16,256]{2,1,0:T(8,128)S(1)}, u32[]{:S(2)}, u32[]{:S(2)}) collective-permute-start(f32[4,16,256]{2,1,0:T(8,128)S(1)} %get-tuple-element.91.refs_0_), channel_id=1, source_target_pairs={{16,17},{17,16},{18,19},{19,18},{0,0},{1,1},{2,2},{3,3},{20,21},{2... | collective-permute-start | bytes 196616 | tf_op jit(solution)/shard_map/ppermute | solution.py:67
  44.5 19.8 %collective-permute-start.27 = (f32[4,16,256]{2,1,0:T(8,128)S(1)}, f32[4,16,256]{2,1,0:T(8,128)S(1)}, u32[]{:S(2)}, u32[]{:S(2)}) collective-permute-start(f32[4,16,256]{2,1,0:T(8,128)S(1)} %get-tuple-element.91.refs_0_), channel_id=1, source_target_pairs={{16,18},{17,19},{18,16},{19,17},{0,0},{1,1},{2,2},{3,3},{20,22},{2... | collective-permute-start | bytes 196616 | tf_op jit(solution)/shard_map/ppermute | solution.py:67
  45.1 19.1 %collective-permute-start.28 = (f32[4,16,256]{2,1,0:T(8,128)S(1)}, f32[4,16,256]{2,1,0:T(8,128)S(1)}, u32[]{:S(2)}, u32[]{:S(2)}) collective-permute-start(f32[4,16,256]{2,1,0:T(8,128)S(1)} %get-tuple-element.91.refs_0_), channel_id=1, source_target_pairs={{16,19},{17,18},{18,17},{19,16},{0,0},{1,1},{2,2},{3,3},{20,23},{2... | collective-permute-start | bytes 196616 | tf_op jit(solution)/shard_map/ppermute | solution.py:67
  66.3 8.3 %collective-permute-start.29 = (f32[4,16,256]{2,1,0:T(8,128)S(1)}, f32[4,16,256]{2,1,0:T(8,128)S(1)}, u32[]{:S(2)}, u32[]{:S(2)}) collective-permute-start(f32[4,16,256]{2,1,0:T(8,128)S(1)} %backward_level.3.refs_4_), channel_id=1, source_target_pairs={{16,17},{17,16},{18,19},{19,18},{0,0},{1,1},{2,2},{3,3},{20,21},{2... | collective-permute-start | bytes 196616 | tf_op jit(solution)/shard_map/ppermute | solution.py:67
  67.0 7.7 %collective-permute-start.30 = (f32[4,16,256]{2,1,0:T(8,128)S(1)}, f32[4,16,256]{2,1,0:T(8,128)S(1)}, u32[]{:S(2)}, u32[]{:S(2)}) collective-permute-start(f32[4,16,256]{2,1,0:T(8,128)S(1)} %backward_level.3.refs_4_), channel_id=1, source_target_pairs={{16,18},{17,19},{18,16},{19,17},{0,0},{1,1},{2,2},{3,3},{20,22},{2... | collective-permute-start | bytes 196616 | tf_op jit(solution)/shard_map/ppermute | solution.py:67
  67.7 7.0 %collective-permute-start.31 = (f32[4,16,256]{2,1,0:T(8,128)S(1)}, f32[4,16,256]{2,1,0:T(8,128)S(1)}, u32[]{:S(2)}, u32[]{:S(2)}) collective-permute-start(f32[4,16,256]{2,1,0:T(8,128)S(1)} %backward_level.3.refs_4_), channel_id=1, source_target_pairs={{16,19},{17,18},{18,17},{19,16},{0,0},{1,1},{2,2},{3,3},{20,23},{2... | collective-permute-start | bytes 196616 | tf_op jit(solution)/shard_map/ppermute | solution.py:67
  80.6 117.5 %collective-permute-start.42 = (f32[4,3,4,16,256]{4,3,2,1,0:T(8,128)S(1)}, f32[4,3,4,16,256]{4,3,2,1,0:T(8,128)S(1)}, u32[]{:S(2)}, u32[]{:S(2)}) collective-permute-start(f32[4,3,4,16,256]{4,3,2,1,0:T(8,128)S(1)} %pad_maximum_fusion.refs_0_), channel_id=1, source_target_pairs={{16,0},{17,1},{18,2},{19,3},{20,4},{21,5},{22,6},{23,7},{24,8},{25... | collective-permute-start | bytes 2359304 | tf_op jit(solution)/shard_map/ppermute | solution.py:79
  84.4 78.4 %collective-permute-start.25 = (f32[256,256]{1,0:T(8,128)S(1)}, f32[256,256]{1,0:T(8,128)S(1)}, u32[]{:S(2)}, u32[]{:S(2)}) collective-permute-start(f32[256,256]{1,0:T(8,128)S(1)} %get-tuple-element.86.refs_6_), channel_id=1, source_target_pairs={{16,0},{17,1},{18,2},{19,3},{20,4},{21,5},{22,6},{23,7},{24,8},{25... | collective-permute-start | bytes 786440 | tf_op jit(solution)/shard_map/ppermute | solution.py:79
  85.7 7.7 %collective-permute-start.32 = (f32[4,16,256]{2,1,0:T(8,128)S(1)}, f32[4,16,256]{2,1,0:T(8,128)S(1)}, u32[]{:S(2)}, u32[]{:S(2)}) collective-permute-start(f32[4,16,256]{2,1,0:T(8,128)S(1)} %get-tuple-element.98.refs_8_), channel_id=1, source_target_pairs={{16,17},{17,16},{18,19},{19,18},{0,0},{1,1},{2,2},{3,3},{20,21},{2... | collective-permute-start | bytes 196616 | tf_op jit(solution)/shard_map/ppermute | solution.py:67
  86.4 7.1 %collective-permute-start.33 = (f32[4,16,256]{2,1,0:T(8,128)S(1)}, f32[4,16,256]{2,1,0:T(8,128)S(1)}, u32[]{:S(2)}, u32[]{:S(2)}) collective-permute-start(f32[4,16,256]{2,1,0:T(8,128)S(1)} %get-tuple-element.98.refs_8_), channel_id=1, source_target_pairs={{16,18},{17,19},{18,16},{19,17},{0,0},{1,1},{2,2},{3,3},{20,22},{2... | collective-permute-start | bytes 196616 | tf_op jit(solution)/shard_map/ppermute | solution.py:67
  87.0 6.4 %collective-permute-start.34 = (f32[4,16,256]{2,1,0:T(8,128)S(1)}, f32[4,16,256]{2,1,0:T(8,128)S(1)}, u32[]{:S(2)}, u32[]{:S(2)}) collective-permute-start(f32[4,16,256]{2,1,0:T(8,128)S(1)} %get-tuple-element.98.refs_8_), channel_id=1, source_target_pairs={{16,19},{17,18},{18,17},{19,16},{0,0},{1,1},{2,2},{3,3},{20,23},{2... | collective-permute-start | bytes 196616 | tf_op jit(solution)/shard_map/ppermute | solution.py:67
  98.5 4.5 %collective-permute-start.36 = (f32[1,4,16,256]{3,2,1,0:T(8,128)S(1)}, f32[1,4,16,256]{3,2,1,0:T(8,128)S(1)}, u32[]{:S(2)}, u32[]{:S(2)}) collective-permute-start(f32[1,4,16,256]{3,2,1,0:T(8,128)S(1)} %bitcast.63), channel_id=1, source_target_pairs={{16,24},{20,28},{24,16},{28,20},{0,0},{4,4},{8,8},{12,12},{17,25},... | collective-permute-start | bytes 196616 | tf_op jit(solution)/shard_map/ppermute | solution.py:67
  99.2 5.1 %collective-permute-start.37 = (f32[1,4,16,256]{3,2,1,0:T(8,128)S(1)}, f32[1,4,16,256]{3,2,1,0:T(8,128)S(1)}, u32[]{:S(2)}, u32[]{:S(2)}) collective-permute-start(f32[1,4,16,256]{3,2,1,0:T(8,128)S(1)} %bitcast.64), channel_id=1, source_target_pairs={{16,28},{20,24},{24,20},{28,16},{0,0},{4,4},{8,8},{12,12},{17,29},... | collective-permute-start | bytes 196616 | tf_op jit(solution)/shard_map/ppermute | solution.py:67
  101.7 92.0 %collective-permute-start.24 = (f32[256,256]{1,0:T(8,128)S(1)}, f32[256,256]{1,0:T(8,128)S(1)}, u32[]{:S(2)}, u32[]{:S(2)}) collective-permute-start(f32[256,256]{1,0:T(8,128)S(1)} %get-tuple-element.84.refs_4_), channel_id=1, source_target_pairs={{16,0},{17,1},{18,2},{19,3},{20,4},{21,5},{22,6},{23,7},{24,8},{25... | collective-permute-start | bytes 786440 | tf_op jit(solution)/shard_map/ppermute | solution.py:79
  103.0 92.0 %collective-permute-start.23 = (f32[256,256]{1,0:T(8,128)S(1)}, f32[256,256]{1,0:T(8,128)S(1)}, u32[]{:S(2)}, u32[]{:S(2)}) collective-permute-start(f32[256,256]{1,0:T(8,128)S(1)} %get-tuple-element.82.refs_2_), channel_id=1, source_target_pairs={{16,0},{17,1},{18,2},{19,3},{20,4},{21,5},{22,6},{23,7},{24,8},{25... | collective-permute-start | bytes 786440 | tf_op jit(solution)/shard_map/ppermute | solution.py:79
  104.3 92.1 %collective-permute-start.22 = (f32[256,256]{1,0:T(8,128)S(1)}, f32[256,256]{1,0:T(8,128)S(1)}, u32[]{:S(2)}, u32[]{:S(2)}) collective-permute-start(f32[256,256]{1,0:T(8,128)S(1)} %solve_level.4.refs_0_), channel_id=1, source_target_pairs={{16,0},{17,1},{18,2},{19,3},{20,4},{21,5},{22,6},{23,7},{24,8},{25... | collective-permute-start | bytes 786440 | tf_op jit(solution)/shard_map/ppermute | solution.py:79
  162.8 37.7 %collective-permute-start.38 = (f32[4,1,4,16,256]{4,3,2,1,0:T(8,128)S(1)}, f32[4,1,4,16,256]{4,3,2,1,0:T(8,128)S(1)}, u32[]{:S(2)}, u32[]{:S(2)}) collective-permute-start(f32[4,1,4,16,256]{4,3,2,1,0:T(8,128)S(1)} %pad_maximum_fusion.1.refs_0_), channel_id=1, source_target_pairs={{16,0},{17,1},{18,2},{19,3},{20,4},{21,5},{22,6},{23,7},{24,8},{25... | collective-permute-start | bytes 786440 | tf_op jit(solution)/shard_map/ppermute | solution.py:79
  (30 other events, 63.7 us)
Sparse Core Ops, SparseCore 0:
  11.0 50.3 all-gather.2

commit v6 on v4

--- a/solution.py
+++ b/solution.py
@@ -12,12 +12,11 @@
 LANES = 128
 F32 = jnp.float32
 BF16 = jnp.bfloat16
-SPLIT = False
 SMEM = pl.BlockSpec(memory_space=pltpu.SMEM)
 VMEM = pl.BlockSpec(memory_space=pltpu.VMEM)
 HBM = pl.BlockSpec(memory_space=pltpu.HBM)
 PARAMS = pltpu.CompilerParams(vmem_limit_bytes=16 * 2**20)
-STREAM_PARAMS = pltpu.CompilerParams(vmem_limit_bytes=53 * 2**20)
+STREAM_PARAMS = pltpu.CompilerParams(vmem_limit_bytes=52 * 2**20)
 
 
 def place_of(height, distance):
@@ -59,23 +58,15 @@
 
 
 def swap(value, axis, step):
-    count = lax.axis_size(axis)
-    gz_count = lax.axis_size("gz")
-    cores = range(gz_count) if SPLIT else [gz_count - 1]
-    pairs = [(g * count + i, g * count + (i ^ step)) for g in cores for i in range(count)]
-    return lax.ppermute(value, ("gz", axis), pairs)
-
-
-def swap_layers(value, step):
-    return lax.ppermute(value, "gz", [(i, i ^ step) for i in range(lax.axis_size("gz"))])
-
-
-def share_layers(value):
-    gz_count = lax.axis_size("gz")
-    if SPLIT:
-        return [swap_layers(value, step) for step in steps_of(gz_count)]
-    chief = gz_count - 1
-    return [lax.ppermute(value, "gz", [(chief, chief ^ step)]) for step in steps_of(gz_count)]
+    return lax.ppermute(value, axis, [(i, i ^ step) for i in range(lax.axis_size(axis))])
+
+
+def with_layers(value):
+    return [value] + [swap(value, "gz", step) for step in steps_of(lax.axis_size("gz"))]
+
+
+def after(value, *others):
+    return lax.optimization_barrier((value, *others))[0]
 
 
 def gather(value, axis):
@@ -95,7 +86,7 @@
             lanes = slice(start, start + LANES)
             for row in range(per_tile):
                 for which in range(groups):
-                    mine = jnp.where(gz == (which if groups > 1 else gz_count - 1), 1.0, 0.0)
+                    mine = jnp.where(gz == which, 1.0, 0.0)
                     total = jnp.zeros((tiles, LANES), F32)
                     for node in range(start // own, (start + LANES) // own):
                         value = right[level, :, node, :] * mine - layer[level, :, node, :]
@@ -111,56 +102,48 @@
                     chosen = jnp.where((gz ^ step) == which, found[which], chosen)
                 if step == 0:
                     kept[level][:, lanes] = chosen
-                if step or groups == 1:
-                    away[max(step - 1, 0)][level, :, lanes] = chosen
-
-
-def lower_kernel(nodes, blocks, inverse, high_out, low_out, high, low):
-    @pl.when(pl.program_id(0) == 0)
-    def _():
-        for node in range(nodes):
-            high[node], low[node] = split(inverse[0, node])
-
-    for node in range(nodes):
-        high_out[0, node], low_out[0, node] = split(
-            product(split(blocks[0, node]), (high[node], low[node]))
-        )
+                else:
+                    away[step - 1][level, :, lanes] = chosen
+
+
+def lower_kernel(height, blocks, inverse, high_out, low_out):
+    first = place_of(height, 1)
+    part, width = blocks.shape[2:]
+    left = blocks[first : first + height, 0].reshape(height * part, width)
+    whole = product(split(left), split(inverse[0, 0])).reshape(height, part, width)
+    high_out[:, 0], low_out[:, 0] = split(whole)
 
 
 def lower_step(height, blocks, inverse):
-    nodes, part = blocks.shape[1:3]
-    first = place_of(height, 1)
+    pairs, nodes, part = blocks.shape[:3]
     out = shape_of(height, nodes, part, WIDTH, dtype=BF16)
     return pl.pallas_call(
-        functools.partial(lower_kernel, nodes),
-        grid=(height,),
+        functools.partial(lower_kernel, height),
+        grid=(nodes,),
         out_shape=[out, out],
         in_specs=[
-            pl.BlockSpec((1, nodes, part, WIDTH), lambda i: (first + i, 0, 0, 0)),
-            pl.BlockSpec((1, nodes, WIDTH, WIDTH), lambda i: (height, 0, 0, 0)),
+            pl.BlockSpec((pairs, 1, part, WIDTH), lambda i: (0, i, 0, 0)),
+            pl.BlockSpec((1, 1, WIDTH, WIDTH), lambda i: (height, i, 0, 0)),
         ],
-        out_specs=[pl.BlockSpec((1, nodes, part, WIDTH), lambda i: (i, 0, 0, 0))] * 2,
-        scratch_shapes=[pltpu.VMEM((nodes, WIDTH, WIDTH), BF16)] * 2,
+        out_specs=[pl.BlockSpec((height, 1, part, WIDTH), lambda i: (0, i, 0, 0))] * 2,
         compiler_params=STREAM_PARAMS,
         name="lower_products",
     )(blocks, inverse)
 
 
-def middle_kernel(nodes, upper, lower, high_out, low_out):
-    for node in range(nodes):
-        high_out[node], low_out[node] = split(product(split(upper[0, node]), split(lower[0, node])))
+def middle_kernel(upper, lower, high_out, low_out):
+    high_out[0], low_out[0] = split(product(split(upper[0, 0]), split(lower[0, 0])))
 
 
 def middle_step(upper, lower):
     nodes = lower.shape[1]
     out = shape_of(nodes, WIDTH, WIDTH, dtype=BF16)
-    level = pl.BlockSpec((1, nodes, WIDTH, WIDTH), lambda i: (0, 0, 0, 0))
-    return pl.pallas_call(
-        functools.partial(middle_kernel, nodes),
-        grid=(1,),
+    return pl.pallas_call(
+        middle_kernel,
+        grid=(nodes,),
         out_shape=[out, out],
-        in_specs=[level, level],
-        out_specs=[pl.BlockSpec((nodes, WIDTH, WIDTH), lambda i: (0, 0, 0))] * 2,
+        in_specs=[pl.BlockSpec((1, 1, WIDTH, WIDTH), lambda i: (0, i, 0, 0))] * 2,
+        out_specs=[pl.BlockSpec((1, WIDTH, WIDTH), lambda i: (i, 0, 0))] * 2,
         compiler_params=STREAM_PARAMS,
         name="middle_product",
     )(upper, lower)
@@ -224,13 +207,10 @@
     return results[0], results[1 : 1 + col_count], results[1 + col_count :]
 
 
-def turn(value, turned, pair_of, out, own, row_count):
-    turned[...] = value.T
+def own_rows(turned, node, own, row_count):
     few = own // row_count
-    row = lax.axis_index("row")
-    for node in range(out.shape[0]):
-        start = pl.multiple_of(node * own + row * few, few)
-        out[node] = product_t(split(turned[pl.ds(start, few), :]), pair_of(node))
+    start = node * own + lax.axis_index("row") * few
+    return turned[pl.ds(pl.multiple_of(start, few), few), :]
 
 
 def last_kernel(sizes, *refs):
@@ -238,7 +218,10 @@
     pieces = refs[:row_count]
     z_high, z_low, full, out, turned = refs[row_count:]
     assemble(pieces, full, part)
-    turn(full[...], turned, lambda node: (z_high[node], z_low[node]), out, own, row_count)
+    turned[...] = full[...].T
+    for node in range(nodes):
+        left = split(own_rows(turned, node, own, row_count))
+        out[node] = product_t(left, (z_high[node], z_low[node]))
 
 
 def last_step(pieces, z, sizes):
@@ -255,107 +238,134 @@
     )(*pieces, *z)
 
 
-def solve_kernel(sizes, full, lower, *refs):
+def solve_kernel(sizes, full, lower, out, own_out, turned):
     nodes, part, own, row_count, col_count = sizes
+    node = pl.program_id(0)
     lane = lax.broadcasted_iota(jnp.int32, (1, nodes * own), 1) // own
-    right = split(full[...])
-    solved = jnp.zeros(full.shape, F32)
-    for node in range(nodes):
-        solved = jnp.where(lane == node, product(split(lower[0, node]), right), solved)
-    if len(refs) == 1:
-        refs[0][...] = solved
-        return
-    upper, out, start, turned = refs
-    out[...] = solved
-    turn(solved, turned, lambda node: split(upper[0, node]), start, own, row_count)
-
-
-def solve_step(height, full, lower, upper, sizes):
+
+    @pl.when(node == 0)
+    def _():
+        turned[...] = full[...].T
+        out[...] = jnp.zeros(out.shape, F32)
+
+    inverse = split(lower[0, 0])
+    out[...] = jnp.where(lane == node, product(inverse, split(full[...])), out[...])
+    own_out[0] = product_t(split(own_rows(turned, node, own, row_count)), inverse)
+
+
+def solve_step(height, full, lower, sizes):
     nodes, part, own, row_count, col_count = sizes
     rows, lanes = full.shape
-    level = pl.BlockSpec((1, nodes, rows, rows), lambda i: (height, 0, 0, 0))
+    few = own // row_count
     whole = pl.BlockSpec((rows, lanes), lambda i: (0, 0))
-    few = own // row_count
-    more = height > 0
     return pl.pallas_call(
         functools.partial(solve_kernel, sizes),
-        grid=(1,),
-        out_shape=[shape_of(rows, lanes)] + [shape_of(nodes, few, rows)] * more,
-        in_specs=[whole, level] + [level] * more,
-        out_specs=[whole] + [pl.BlockSpec((nodes, few, rows), lambda i: (0, 0, 0))] * more,
-        scratch_shapes=[pltpu.VMEM((lanes, rows), F32)] * more,
+        grid=(nodes,),
+        out_shape=[shape_of(rows, lanes), shape_of(nodes, few, rows)],
+        in_specs=[whole, pl.BlockSpec((1, 1, rows, rows), lambda i: (height, i, 0, 0))],
+        out_specs=[whole, pl.BlockSpec((1, few, rows), lambda i: (i, 0, 0))],
+        scratch_shapes=[pltpu.VMEM((lanes, rows), F32)],
         compiler_params=STREAM_PARAMS,
         name="solve_level",
-    )(full, lower, *([upper] * more))
-
-
-def compose_kernel(nodes, gathered, inverse, high_out, low_out):
-    for node in range(nodes):
-        block = gathered[:, 0, node].reshape(WIDTH, WIDTH)
-        whole = product(split(inverse[0, node]), split(block))
-        high_out[0, node], low_out[0, node] = split(whole)
+    )(full, lower)
+
+
+def start_kernel(height, nodes, col_count, parents, pattern, value, inverse, *refs):
+    blocks, pieces, out = refs[: height - 1], refs[height - 1 : -1], refs[-1]
+    col = lax.axis_index("col")
+    node = pl.program_id(0)
+    rest = value[0]
+    ancestor = parents[height - 1, col * nodes + node]
+    for distance in range(2, height + 1):
+        level = height - distance
+        ancestor = parents[level, ancestor]
+        where = lax.div(ancestor, nodes) ^ col
+        slot = lax.rem(ancestor, nodes)
+        chosen = pieces[level * col_count][slot]
+        for step in range(1, col_count):
+            piece = pieces[level * col_count + step][slot]
+            chosen = jnp.where(where == step, piece, chosen)
+        block = blocks[distance - 2][:, 0, 0].reshape(WIDTH, WIDTH)
+        term = product_t(split(chosen), split(block))
+        stored = pattern[place_of(height, distance), node] != 0
+        rest = rest - jnp.where(stored, term, 0.0)
+    out[0] = product_t(split(rest), split(inverse[0, 0]))
+
+
+def start_step(height, parents, pattern, value, gathered, inverse, solved, row_count):
+    per, nodes, part = gathered.shape[1:4]
+    col_count = lax.axis_size("col")
+    few, rows = value.shape[1:]
+    pieces = [piece for level in solved for piece in level]
+
+    def block_spec(distance):
+        place = place_of(height, distance)
+        return pl.BlockSpec(
+            (row_count, 1, 1, part, WIDTH), lambda i: (place // per, place % per, i, 0, 0)
+        )
+
+    each = pl.BlockSpec((1, few, rows), lambda i: (i, 0, 0))
+    whole = pl.BlockSpec((nodes, few, rows), lambda i: (0, 0, 0))
+    return pl.pallas_call(
+        functools.partial(start_kernel, height, nodes, col_count),
+        grid=(nodes,),
+        out_shape=shape_of(nodes, few, rows),
+        in_specs=[SMEM, SMEM, each]
+        + [pl.BlockSpec((1, 1, WIDTH, WIDTH), lambda i: (height, i, 0, 0))]
+        + [block_spec(distance) for distance in range(2, height + 1)]
+        + [whole] * len(pieces),
+        out_specs=each,
+        compiler_params=STREAM_PARAMS,
+        name="start_level",
+    )(parents, pattern, value, inverse, *([gathered] * (height - 1)), *pieces)
+
+
+def compose_kernel(gathered, inverse, high_out, low_out):
+    block = gathered[:, 0, 0].reshape(WIDTH, WIDTH)
+    high_out[0], low_out[0] = split(product(split(inverse[0, 0]), split(block)))
 
 
 def compose_step(height, gathered, inverse, row_count):
     per, nodes, part = gathered.shape[1:4]
-    first = place_of(height, 1)
-    out = shape_of(height, nodes, WIDTH, WIDTH, dtype=BF16)
-    out_spec = pl.BlockSpec((1, nodes, WIDTH, WIDTH), lambda i: (i, 0, 0, 0))
-    return pl.pallas_call(
-        functools.partial(compose_kernel, nodes),
-        grid=(height,),
+    place = place_of(height, 1)
+    out = shape_of(nodes, WIDTH, WIDTH, dtype=BF16)
+    return pl.pallas_call(
+        compose_kernel,
+        grid=(nodes,),
         out_shape=[out, out],
         in_specs=[
             pl.BlockSpec(
-                (row_count, 1, nodes, part, WIDTH),
-                lambda i: ((first + i) // per, (first + i) % per, 0, 0, 0),
+                (row_count, 1, 1, part, WIDTH), lambda i: (place // per, place % per, i, 0, 0)
             ),
-            pl.BlockSpec((1, nodes, WIDTH, WIDTH), lambda i: (height, 0, 0, 0)),
+            pl.BlockSpec((1, 1, WIDTH, WIDTH), lambda i: (height, i, 0, 0)),
         ],
-        out_specs=[out_spec] * 2,
+        out_specs=[pl.BlockSpec((1, WIDTH, WIDTH), lambda i: (i, 0, 0))] * 2,
         compiler_params=STREAM_PARAMS,
         name="compose_level",
     )(gathered, inverse)
 
 
-def backward_kernel(height, nodes, col_count, parents, pattern, start, high, low, *refs):
-    pieces, out = refs[: height * col_count], refs[height * col_count]
-    early = refs[height * col_count + 1] if height == 2 else None
-    solved = refs[-1]
-    for level in range(height):
-        for step in range(col_count):
-            solved[level, step] = pieces[level * col_count + step][...]
+def backward_kernel(height, nodes, parents, pattern, start, high, low, *refs):
+    pieces, out, solved = refs[:-2], refs[-2], refs[-1]
+    for step, piece in enumerate(pieces):
+        solved[step] = piece[...]
     col = lax.axis_index("col")
     for node in range(nodes):
-        total = start[node]
-        ancestor = col * nodes + node
-        for distance in range(1, height + 1):
-            level = height - distance
-            ancestor = parents[level, ancestor]
-            where = lax.div(ancestor, nodes) ^ col
-            left = split(solved[level, where, lax.rem(ancestor, nodes)])
-            term = product_t(left, (high[distance - 1, node], low[distance - 1, node]))
-            stored = pattern[place_of(height, distance), node] != 0
-            total = total - jnp.where(stored, term, 0.0)
-        out[node] = total
-        if early is not None:
-            early[height, node] = total
-    if early is not None:
-        for level in range(height):
-            early[level] = solved[level, 0]
-
-
-def backward_step(height, parents, pattern, start, composed, solved):
-    nodes = start.shape[0]
-    col_count = lax.axis_size("col")
-    pieces = [piece for level in solved for piece in level]
-    outs = [start.shape] + ([(height + 1,) + start.shape] if height == 2 else [])
-    return pl.pallas_call(
-        functools.partial(backward_kernel, height, nodes, col_count),
-        out_shape=[shape_of(*out) for out in outs],
+        ancestor = parents[height - 1, col * nodes + node]
+        where = lax.div(ancestor, nodes) ^ col
+        left = split(solved[where, lax.rem(ancestor, nodes)])
+        term = product_t(left, (high[node], low[node]))
+        stored = pattern[place_of(height, 1), node] != 0
+        out[node] = start[node] - jnp.where(stored, term, 0.0)
+
+
+def backward_step(height, parents, pattern, start, composed, pieces):
+    return pl.pallas_call(
+        functools.partial(backward_kernel, height, start.shape[0]),
+        out_shape=shape_of(*start.shape),
         in_specs=[SMEM, SMEM] + [VMEM] * (3 + len(pieces)),
-        out_specs=[VMEM] * len(outs),
-        scratch_shapes=[pltpu.VMEM((height, col_count) + start.shape, F32)],
+        out_specs=VMEM,
+        scratch_shapes=[pltpu.VMEM((len(pieces),) + start.shape, F32)],
         compiler_params=PARAMS,
         name="backward_level",
     )(parents, pattern, start, *composed, *pieces)
@@ -363,11 +373,6 @@
 
 def groups_found(found, groups):
     gz = lax.axis_index("gz")
-    if groups == 1:
-        others = found[1]
-        for value in found[2:]:
-            others = others + value
-        return [jnp.where(gz == len(found) - 1, found[0], others)]
     values = []
     for which in range(groups):
         value = found[0]
@@ -458,8 +463,7 @@
 
 
 def layers_of(value):
-    whole = jnp.stack(gather(value, "row"))
-    return [whole] + share_layers(whole)
+    return with_layers(jnp.stack(gather(value, "row")))
 
 
 def body(
@@ -477,7 +481,7 @@
     gz_count = lax.axis_size("gz")
     row_count = lax.axis_size("row")
     col_count = lax.axis_size("col")
-    own = COLUMNS // gz_count if SPLIT else COLUMNS
+    own = COLUMNS // gz_count
     lanes = nodes * own
     sizes = (nodes, part, own, row_count, col_count)
     gz = lax.axis_index("gz")
@@ -485,60 +489,64 @@
     def tiled(value):
         return value.reshape(4, nodes, part * COLUMNS // LANES, LANES).transpose(0, 2, 1, 3)
 
-    aways = gz_count - 1 if SPLIT else 1
     parts = pl.pallas_call(
         functools.partial(input_kernel, gz_count, nodes, own),
-        out_shape=[shape_of(part, lanes)] * 4 + [shape_of(4, part, lanes)] * aways,
+        out_shape=[shape_of(part, lanes)] * 4 + [shape_of(4, part, lanes)] * (gz_count - 1),
         in_specs=[VMEM, VMEM],
-        out_specs=[VMEM] * (4 + aways),
+        out_specs=[VMEM] * (3 + gz_count),
         scratch_shapes=[pltpu.VMEM((4, lanes // LANES, COLUMNS // own, part, LANES), F32)],
         compiler_params=STREAM_PARAMS,
         name="input_parts",
     )(tiled(right_side), tiled(layer_sums[0]))
-    kept, away = parts[:4], list(parts[4:])
+    kept, away = parts[:4], parts[4:]
 
     per = upper_blocks.shape[0] // gz_count
-    later, away[0] = lax.optimization_barrier((upper_blocks, away[0]))
-    upper_rows = lax.all_gather(
-        lax.dynamic_slice_in_dim(later, gz * per, per, 0), ("gz", "row")
-    )
-    others = [swap_layers(away[min(step, aways) - 1], step) for step in steps_of(gz_count)]
+    half = lax.dynamic_slice_in_dim(after(upper_blocks, *away), gz * per, per, 0)
+    upper_rows = lax.all_gather(half, ("gz", "row"))
+    others = [swap(away[step - 1], "gz", step) for step in steps_of(gz_count)]
     initial = [kept[level] + sum(other[level] for other in others) for level in range(4)]
 
     fulls = [None] * 4
     forward = [None] * 4
-    starts = [None] * 4
     pending = []
     mine = initial[3]
+    m = lower_step(3, lower_blocks, lower_inverse)
     for height in (3, 2, 1):
-        m = lower_step(height, lower_blocks, lower_inverse)
+        pieces = gather(mine, "row")
+        if height < 3:
+            m = lower_step(height, lower_blocks, lower_inverse)
         fulls[height], sends, pending = forward_step(
-            height, gather(mine, "row"), parents, pattern, m, pending, sizes
+            height, pieces, parents, pattern, m, pending, sizes
         )
-        mine = initial[height - 1] - sends[0]
-        for step in steps_of(col_count):
-            mine = mine - swap(sends[step], "col", step)
+        forward[height] = solve_step(height, fulls[height], lower_inverse, sizes)
+        taken = [swap(sends[step], "col", step) for step in steps_of(col_count)]
+        taken[-1] = after(taken[-1], *forward[height])
+        mine = initial[height - 1] - sends[0] - sum(taken)
     z = middle_step(upper_diagonal_inverses, lower_inverse)
     fulls[0], solved = last_step(gather(mine, "row"), z, sizes)
-
-    for height in range(4):
-        results = solve_step(height, fulls[height], lower_inverse, upper_diagonal_inverses, sizes)
-        forward[height], starts[height] = results[0], results[-1]
+    forward[0] = solve_step(0, fulls[0], lower_inverse, sizes)
+
+    backward = [solved]
     whole = []
     for height in (1, 2, 3):
         composed = compose_step(height, upper_rows, upper_diagonal_inverses, row_count)
-        whole.append(gather(solved, "col"))
-        results = backward_step(height, parents, pattern, starts[height], composed, whole)
-        solved = results[0]
-        if height == 2:
-            early = results[1]
-
-    forward_parts = []
-    for value in forward:
-        forward_parts += [value] + share_layers(value)
+        start = start_step(
+            height,
+            parents,
+            pattern,
+            forward[height][1],
+            upper_rows,
+            upper_diagonal_inverses,
+            whole,
+            row_count,
+        )
+        whole = whole + [gather(backward[-1], "col")]
+        backward.append(backward_step(height, parents, pattern, start, composed, whole[-1]))
+
+    forward_parts = [piece for level in forward for piece in with_layers(level[0])]
     forward_all = forward_out(forward_parts, nodes, own, gz_count)
-    backward_all = backward_out(layers_of(early), None, 0, own)
-    backward_all = backward_out(layers_of(solved[None]), backward_all, 3, own)
+    backward_all = backward_out(layers_of(jnp.stack(backward[:3])), None, 0, own)
+    backward_all = backward_out(layers_of(backward[3][None]), backward_all, 3, own)
     return tuple(
         value.transpose(0, 2, 1, 3).reshape(4, nodes, WIDTH * COLUMNS)
         for value in (forward_all, backward_all)

time: 210 us -> 135 us (0.64)
  waiting for transfers between devices: 104 us -> 10.5 us
  starting transfers between devices: 32.5 us -> 50.6 us
  Pallas kernels: 47.9 us -> 55 us
  local copies, waits for them, and re-layouts: 9.46 us -> 3.76 us
    ppermute x43, waiting for transfers between devices: 90.7 us -> 10.5 us  [swap(): lax.ppermute(value, axis, [(i, i ^ step) for i in range(lax.axis_size(axi...]
    ppermute x43, starting transfers between devices: 32.4 us -> 50.6 us  [swap(): lax.ppermute(value, axis, [(i, i ^ step) for i in range(lax.axis_size(axi...]
    all_gather x1, waiting for transfers between devices: 12.9 us -> 0.01 us  [body(): upper_rows = lax.all_gather(half, ('gz', 'row'))]
    pallas_call x14 -> x17, Pallas kernels: 36.4 us -> 44.8 us  [the longest x4 12.1 us: solve_step(): pl.pallas_call(functools.partial(solve_kernel, sizes), grid=(nodes,), out...]
    unnamed x21 -> x11, local copies, waits for them, and re-layouts: 8.49 us -> 2.79 us
  transfers between devices with their start and end apart: 44 -> 44, of which waited for: 6 -> 14; matrix products, arithmetic and copies ran while one was open for 0% -> 1% of each run, Pallas kernels for 21% -> 38%
where the time goes in v6:
time: 135 us; the launch traced here: 134 us
  Pallas kernels  55 us (41%)
  starting transfers between devices  50.6 us (37%)
  between operations  14.5 us (11%)
  waiting for transfers between devices  10.5 us (8%)
  local copies, waits for them, and re-layouts  3.76 us (3%)
    ppermute x43, starting transfers between devices, swap(): lax.ppermute(value, axis, [(i, i ^ step) for i in range(lax.axis_size(axi...  50.6 us
    pallas_call x4, Pallas kernels, solve_step(): pl.pallas_call(functools.partial(solve_kernel, sizes), grid=(nodes,), out...  12.1 us
    ppermute x43, waiting for transfers between devices, swap(): lax.ppermute(value, axis, [(i, i ^ step) for i in range(lax.axis_size(axi...  10.5 us
    pallas_call x3, Pallas kernels, start_step(): pl.pallas_call(functools.partial(start_kernel, height, nodes, col_count),...  9.02 us
    pallas_call x3, Pallas kernels, compose_step(): pl.pallas_call(compose_kernel, grid=(nodes,), out_shape=[out, out], in_sp...  8.99 us
    pallas_call x3, Pallas kernels, lower_step(): pl.pallas_call(functools.partial(lower_kernel, height), grid=(nodes,), ou...  8.76 us
    pallas_call x2, Pallas kernels, backward_out(): pl.pallas_call(functools.partial(backward_out_kernel, nodes, len(parts),...  3.39 us
    pallas_call x3, Pallas kernels, forward_step(): pl.pallas_call(functools.partial(forward_kernel, height, sizes), out_shap...  3.23 us
  transfers between devices with their start and end apart: 44, of which 14 were waited for; matrix products, arithmetic and copies ran while one was open for 1% of the time, Pallas kernels for 38%

profile of v6, /device:TPU:0, one launch (start us, length us, event | category | flops | bytes accessed | tf_op | source)
XLA Modules:
  0.0 134.5 jit_solution(2051740352586706671)
XLA Ops:
  12.8 2.8 %collective-permute-start.1 = (f32[64,128]{1,0:T(8,128)S(1)}, f32[64,128]{1,0:T(8,128)S(1)}, u32[]{:S(2)}, u32[]{:S(2)}) collective-permute-start(f32[64,128]{1,0:T(8,128)S(1)} %fusion.refs_0_), channel_id=1, source_target_pairs={{0,4},{4,0},{8,12},{12,8},{1,5},{5,1},{9,13},{13,9},{2,6},{6,2},{1... | collective-permute-start | bytes 98312 | tf_op jit(solution)/shard_map/ppermute | solution.py:61
  18.0 3.1 %lower_products.3 = (bf16[3,4,64,256]{3,2,1,0:T(8,128)(2,1)S(1)}, bf16[3,4,64,256]{3,2,1,0:T(8,128)(2,1)S(1)}) custom-call(f32[6,4,64,256]{3,2,1,0:T(8,128)} %blocks.5, f32[4,4,256,256]{3,2,1,0:T(8,128)} %lower.9), custom_call_target="tpu_custom_call" | custom-call | tf_op jit(solution)/shard_map/lower_products/pallas_call | solution.py:120
  23.2 3.7 %collective-permute-start.6 = (f32[64,128]{1,0:T(8,128)S(1)}, f32[64,128]{1,0:T(8,128)S(1)}, u32[]{:S(2)}, u32[]{:S(2)}) collective-permute-start(f32[64,128]{1,0:T(8,128)S(1)} %get-tuple-element.62), channel_id=1, source_target_pairs={{0,3},{1,2},{2,1},{3,0},{4,7},{5,6},{6,5},{7,4},{8,11},{9,10},{10,... | collective-permute-start | bytes 98312 | tf_op jit(solution)/shard_map/ppermute | solution.py:61
  27.7 2.8 %solve_level.4 = (f32[256,128]{1,0:T(8,128)S(1)}, f32[4,8,256]{2,1,0:T(8,128)S(1)}) custom-call(f32[256,128]{1,0:T(8,128)S(1)} %get-tuple-element.63.full, f32[4,4,256,256]{3,2,1,0:T(8,128)} %lower.9), custom_call_target="tpu_custom_call" | custom-call | tf_op jit(solution)/shard_map/solve_level/pallas_call | solution.py:261
  35.3 2.9 %lower_products.4 = (bf16[2,4,64,256]{3,2,1,0:T(8,128)(2,1)S(1)}, bf16[2,4,64,256]{3,2,1,0:T(8,128)(2,1)S(1)}) custom-call(f32[6,4,64,256]{3,2,1,0:T(8,128)} %blocks.5, f32[4,4,256,256]{3,2,1,0:T(8,128)} %lower.9), custom_call_target="tpu_custom_call" | custom-call | tf_op jit(solution)/shard_map/lower_products/pallas_call | solution.py:120
  40.3 2.5 %collective-permute-start.12 = (f32[64,128]{1,0:T(8,128)S(1)}, f32[64,128]{1,0:T(8,128)S(1)}, u32[]{:S(2)}, u32[]{:S(2)}) collective-permute-start(f32[64,128]{1,0:T(8,128)S(1)} %get-tuple-element.74), channel_id=1, source_target_pairs={{0,3},{1,2},{2,1},{3,0},{4,7},{5,6},{6,5},{7,4},{8,11},{9,10},{10,... | collective-permute-start | bytes 98312 | tf_op jit(solution)/shard_map/ppermute | solution.py:61
  42.8 2.0 %collective-permute-start.11 = (f32[64,128]{1,0:T(8,128)S(1)}, f32[64,128]{1,0:T(8,128)S(1)}, u32[]{:S(2)}, u32[]{:S(2)}) collective-permute-start(f32[64,128]{1,0:T(8,128)S(1)} %get-tuple-element.73), channel_id=1, source_target_pairs={{0,2},{1,3},{2,0},{3,1},{4,6},{5,7},{6,4},{7,5},{8,10},{9,11},{10,... | collective-permute-start | bytes 98312 | tf_op jit(solution)/shard_map/ppermute | solution.py:61
  44.8 2.8 %solve_level.5 = (f32[256,128]{1,0:T(8,128)S(1)}, f32[4,8,256]{2,1,0:T(8,128)S(1)}) custom-call(f32[256,128]{1,0:T(8,128)S(1)} %get-tuple-element.75.full, f32[4,4,256,256]{3,2,1,0:T(8,128)} %lower.9), custom_call_target="tpu_custom_call" | custom-call | tf_op jit(solution)/shard_map/solve_level/pallas_call | solution.py:261
  51.2 2.7 %lower_products.5 = (bf16[1,4,64,256]{3,2,1,0:T(8,128)(2,1)S(1)}, bf16[1,4,64,256]{3,2,1,0:T(8,128)(2,1)S(1)}) custom-call(f32[6,4,64,256]{3,2,1,0:T(8,128)S(1)} %copy-done.1, f32[4,4,256,256]{3,2,1,0:T(8,128)} %lower.9), custom_call_target="tpu_custom_call" | custom-call | tf_op jit(solution)/shard_map/lower_products/pallas_call | solution.py:120
  55.8 2.6 %collective-permute-start.18 = (f32[64,128]{1,0:T(8,128)S(1)}, f32[64,128]{1,0:T(8,128)S(1)}, u32[]{:S(2)}, u32[]{:S(2)}) collective-permute-start(f32[64,128]{1,0:T(8,128)S(1)} %get-tuple-element.85), channel_id=1, source_target_pairs={{0,3},{1,2},{2,1},{3,0},{4,7},{5,6},{6,5},{7,4},{8,11},{9,10},{10,... | collective-permute-start | bytes 98312 | tf_op jit(solution)/shard_map/ppermute | solution.py:61
  60.3 2.8 %solve_level.6 = (f32[256,128]{1,0:T(8,128)S(1)}, f32[4,8,256]{2,1,0:T(8,128)S(1)}) custom-call(f32[256,128]{1,0:T(8,128)S(1)} %get-tuple-element.86.full, f32[4,4,256,256]{3,2,1,0:T(8,128)} %lower.9), custom_call_target="tpu_custom_call" | custom-call | tf_op jit(solution)/shard_map/solve_level/pallas_call | solution.py:261
  66.8 3.0 %middle_product.1 = (bf16[4,256,256]{2,1,0:T(8,128)(2,1)S(1)}, bf16[4,256,256]{2,1,0:T(8,128)(2,1)S(1)}) custom-call(f32[4,4,256,256]{3,2,1,0:T(8,128)} %inverse.17, f32[4,4,256,256]{3,2,1,0:T(8,128)} %lower.9), custom_call_target="tpu_custom_call" | custom-call | tf_op jit(solution)/shard_map/middle_product/pallas_call | solution.py:141
  70.9 2.1 %collective-permute-start.26 = (f32[4,8,256]{2,1,0:T(8,128)S(1)}, f32[4,8,256]{2,1,0:T(8,128)S(1)}, u32[]{:S(2)}, u32[]{:S(2)}) collective-permute-start(f32[4,8,256]{2,1,0:T(8,128)S(1)} %get-tuple-element.95.refs_0_.refs_2_.refs_1_), channel_id=1, source_target_pairs={{0,1},{1,0},{2,3},{3,2},{4,5},{5,4},{6,7},{7,6},{8,9},{9,8},{10,11... | collective-permute-start | bytes 98312 | tf_op jit(solution)/shard_map/ppermute | solution.py:61
  75.4 2.5 %start_level.3.start = f32[4,8,256]{2,1,0:T(8,128)S(1)} custom-call(s32[3,16]{1,0:T(4,128)S(1)} %copy-done.4, s32[6,4]{1,0:T(8,128)S(1)} %copy.20.refs_5_.pattern, f32[4,8,256]{2,1,0:T(8,128)S(1)} %get-tuple-element.88.value, f32[4,4,256,256]{3,2,1,0:T(8,128)} %inverse.17), custom_call_target="tpu_custom_call" | custom-call | tf_op jit(solution)/shard_map/start_level/pallas_call | solution.py:309
  77.9 3.0 %compose_level.3 = (bf16[4,256,256]{2,1,0:T(8,128)(2,1)S(1)}, bf16[4,256,256]{2,1,0:T(8,128)(2,1)S(1)}) custom-call(f32[8,3,4,64,256]{4,3,2,1,0:T(8,128)} %bitcast.63, f32[4,4,256,256]{3,2,1,0:T(8,128)} %inverse.17), custom_call_target="tpu_custom_call" | custom-call | tf_op jit(solution)/shard_map/compose_level/pallas_call | solution.py:332
  86.4 3.0 %compose_level.5 = (bf16[4,256,256]{2,1,0:T(8,128)(2,1)S(1)}, bf16[4,256,256]{2,1,0:T(8,128)(2,1)S(1)}) custom-call(f32[8,3,4,64,256]{4,3,2,1,0:T(8,128)} %bitcast.64, f32[4,4,256,256]{3,2,1,0:T(8,128)} %inverse.17), custom_call_target="tpu_custom_call" | custom-call | tf_op jit(solution)/shard_map/compose_level/pallas_call | solution.py:332
  89.4 3.1 %start_level.5.start = f32[4,8,256]{2,1,0:T(8,128)S(1)} custom-call(s32[3,16]{1,0:T(4,128)S(1)} %copy-done.4, s32[6,4]{1,0:T(8,128)S(1)} %copy.20.refs_5_.pattern, f32[4,8,256]{2,1,0:T(8,128)S(1)} %get-tuple-element.77.value, f32[4,4,256,256]{3,2,1,0:T(8,128)} %inverse.17, f32[8,3,4,64,256]{4,3,2,1,0:T(8,128)} %bitcast.65, ...), custom_call_target="tpu_custom_call" | custom-call | tf_op jit(solution)/shard_map/start_level/pallas_call | solution.py:309
  98.8 2.1 %collective-permute-done.41 = f32[3,4,8,256]{3,2,1,0:T(8,128)S(1)} collective-permute-done((f32[3,4,8,256]{3,2,1,0:T(8,128)S(1)}, f32[3,4,8,256]{3,2,1,0:T(8,128)S(1)}, u32[]{:S(2)}, u32[]{:S(2)}) %collective-permute-start.41) | collective-permute-done | bytes 98336 | tf_op jit(solution)/shard_map/ppermute | solution.py:61
  101.2 2.7 %collective-permute-start.33 = (f32[4,8,256]{2,1,0:T(8,128)S(1)}, f32[4,8,256]{2,1,0:T(8,128)S(1)}, u32[]{:S(2)}, u32[]{:S(2)}) collective-permute-start(f32[4,8,256]{2,1,0:T(8,128)S(1)} %backward_level.4.refs_0_), channel_id=1, source_target_pairs={{0,2},{1,3},{2,0},{3,1},{4,6},{5,7},{6,4},{7,5},{8,10},{9,11},{10,... | collective-permute-start | bytes 98312 | tf_op jit(solution)/shard_map/ppermute | solution.py:61
  105.4 3.0 %compose_level.4 = (bf16[4,256,256]{2,1,0:T(8,128)(2,1)S(1)}, bf16[4,256,256]{2,1,0:T(8,128)(2,1)S(1)}) custom-call(f32[8,3,4,64,256]{4,3,2,1,0:T(8,128)} %bitcast.66, f32[4,4,256,256]{3,2,1,0:T(8,128)} %inverse.17), custom_call_target="tpu_custom_call" | custom-call | tf_op jit(solution)/shard_map/compose_level/pallas_call | solution.py:332
  108.4 3.5 %start_level.4.start = f32[4,8,256]{2,1,0:T(8,128)S(1)} custom-call(s32[3,16]{1,0:T(4,128)S(1)} %copy-done.4, s32[6,4]{1,0:T(8,128)S(1)} %copy.20.refs_5_.pattern, f32[4,8,256]{2,1,0:T(8,128)S(1)} %get-tuple-element.65.value, f32[4,4,256,256]{3,2,1,0:T(8,128)} %inverse.17, f32[8,3,4,64,256]{4,3,2,1,0:T(8,128)} %bitcast.67, f32[8,3,4,64,256]{4,3,2,1,0:T(8,128)} %bitcast.68, ...), custom_call_target="tpu_custom_call" | custom-call | tf_op jit(solution)/shard_map/start_level/pallas_call | solution.py:309
  116.4 3.7 %solve_level.7 = (f32[256,128]{1,0:T(8,128)S(1)}, f32[4,8,256]{2,1,0:T(8,128)}) custom-call(f32[256,128]{1,0:T(8,128)S(1)} %get-tuple-element.92.full, f32[4,4,256,256]{3,2,1,0:T(8,128)} %lower.9), custom_call_target="tpu_custom_call" | custom-call | tf_op jit(solution)/shard_map/solve_level/pallas_call | solution.py:261
  122.2 2.1 %forward_out.1 = f32[4,128,4,128]{3,2,1,0:T(4,128)} custom-call(f32[256,128]{1,0:T(8,128)S(1)} %get-tuple-element.93.refs_0_, f32[256,128]{1,0:T(8,128)S(1)} %collective-permute-done.22.refs_1_, f32[256,128]{1,0:T(8,128)S(1)} %get-tuple-element.87.refs_2_, f32[256,128]{1,0:T(8,128)S(1)} %collective-permute-done.23.refs_3_, ...), custom_call_target="tpu_custom_call" | custom-call | tf_op jit(solution)/shard_map/forward_out/pallas_call | solution.py:415
  124.2 2.3 %backward_out.2.refs_2_ = f32[4,128,4,128]{3,2,1,0:T(4,128)} custom-call(f32[4,3,4,8,256]{4,3,2,1,0:T(8,128)S(1)} %pad_maximum_fusion.refs_0_, f32[4,3,4,8,256]{4,3,2,1,0:T(8,128)S(1)} %collective-permute-done.42.refs_1_), custom_call_target="tpu_custom_call" | custom-call | tf_op jit(solution)/shard_map/backward_out/pallas_call | solution.py:448
  (109 shorter events, 53.4 us)
Async XLA Ops:
  7.2 70.7 %all-gather.3.cloned.1.call-start = ((), (), s32[]{:S(2)}) async-start(), calls=%async_computation | async-start | bytes 7077888 | tf_op jit(solution)/shard_map/all_gather | solution.py:505
  12.8 8.3 %collective-permute-start.1 = (f32[64,128]{1,0:T(8,128)S(1)}, f32[64,128]{1,0:T(8,128)S(1)}, u32[]{:S(2)}, u32[]{:S(2)}) collective-permute-start(f32[64,128]{1,0:T(8,128)S(1)} %fusion.refs_0_), channel_id=1, source_target_pairs={{0,4},{4,0},{8,12},{12,8},{1,5},{5,1},{9,13},{13,9},{2,6},{6,2},{1... | collective-permute-start | bytes 98312 | tf_op jit(solution)/shard_map/ppermute | solution.py:61
  23.2 7.2 %collective-permute-start.6 = (f32[64,128]{1,0:T(8,128)S(1)}, f32[64,128]{1,0:T(8,128)S(1)}, u32[]{:S(2)}, u32[]{:S(2)}) collective-permute-start(f32[64,128]{1,0:T(8,128)S(1)} %get-tuple-element.62), channel_id=1, source_target_pairs={{0,3},{1,2},{2,1},{3,0},{4,7},{5,6},{6,5},{7,4},{8,11},{9,10},{10,... | collective-permute-start | bytes 98312 | tf_op jit(solution)/shard_map/ppermute | solution.py:61
  31.7 6.5 %collective-permute-start.7 = (f32[64,128]{1,0:T(8,128)S(1)}, f32[64,128]{1,0:T(8,128)S(1)}, u32[]{:S(2)}, u32[]{:S(2)}) collective-permute-start(f32[64,128]{1,0:T(8,128)S(1)} %fusion.3.refs_0_), channel_id=1, source_target_pairs={{0,4},{4,0},{8,12},{12,8},{1,5},{5,1},{9,13},{13,9},{2,6},{6,2},{1... | collective-permute-start | bytes 98312 | tf_op jit(solution)/shard_map/ppermute | solution.py:61
  40.3 7.3 %collective-permute-start.12 = (f32[64,128]{1,0:T(8,128)S(1)}, f32[64,128]{1,0:T(8,128)S(1)}, u32[]{:S(2)}, u32[]{:S(2)}) collective-permute-start(f32[64,128]{1,0:T(8,128)S(1)} %get-tuple-element.74), channel_id=1, source_target_pairs={{0,3},{1,2},{2,1},{3,0},{4,7},{5,6},{6,5},{7,4},{8,11},{9,10},{10,... | collective-permute-start | bytes 98312 | tf_op jit(solution)/shard_map/ppermute | solution.py:61
  47.6 6.3 %collective-permute-start.13 = (f32[64,128]{1,0:T(8,128)S(1)}, f32[64,128]{1,0:T(8,128)S(1)}, u32[]{:S(2)}, u32[]{:S(2)}) collective-permute-start(f32[64,128]{1,0:T(8,128)S(1)} %fusion.6.refs_0_), channel_id=1, source_target_pairs={{0,4},{4,0},{8,12},{12,8},{1,5},{5,1},{9,13},{13,9},{2,6},{6,2},{1... | collective-permute-start | bytes 98312 | tf_op jit(solution)/shard_map/ppermute | solution.py:61
  48.2 5.7 %collective-permute-start.14 = (f32[64,128]{1,0:T(8,128)S(1)}, f32[64,128]{1,0:T(8,128)S(1)}, u32[]{:S(2)}, u32[]{:S(2)}) collective-permute-start(f32[64,128]{1,0:T(8,128)S(1)} %fusion.6.refs_0_), channel_id=1, source_target_pairs={{0,8},{4,12},{8,0},{12,4},{1,9},{5,13},{9,1},{13,5},{2,10},{6,14},... | collective-permute-start | bytes 98312 | tf_op jit(solution)/shard_map/ppermute | solution.py:61
  49.3 5.5 %collective-permute-start.15 = (f32[64,128]{1,0:T(8,128)S(1)}, f32[64,128]{1,0:T(8,128)S(1)}, u32[]{:S(2)}, u32[]{:S(2)}) collective-permute-start(f32[64,128]{1,0:T(8,128)S(1)} %fusion.6.refs_0_), channel_id=1, source_target_pairs={{0,12},{4,8},{8,4},{12,0},{1,13},{5,9},{9,5},{13,1},{2,14},{6,10},... | collective-permute-start | bytes 98312 | tf_op jit(solution)/shard_map/ppermute | solution.py:61
  55.8 7.2 %collective-permute-start.18 = (f32[64,128]{1,0:T(8,128)S(1)}, f32[64,128]{1,0:T(8,128)S(1)}, u32[]{:S(2)}, u32[]{:S(2)}) collective-permute-start(f32[64,128]{1,0:T(8,128)S(1)} %get-tuple-element.85), channel_id=1, source_target_pairs={{0,3},{1,2},{2,1},{3,0},{4,7},{5,6},{6,5},{7,4},{8,11},{9,10},{10,... | collective-permute-start | bytes 98312 | tf_op jit(solution)/shard_map/ppermute | solution.py:61
  63.3 6.5 %collective-permute-start.19 = (f32[64,128]{1,0:T(8,128)S(1)}, f32[64,128]{1,0:T(8,128)S(1)}, u32[]{:S(2)}, u32[]{:S(2)}) collective-permute-start(f32[64,128]{1,0:T(8,128)S(1)} %fusion.9.refs_0_), channel_id=1, source_target_pairs={{0,4},{4,0},{8,12},{12,8},{1,5},{5,1},{9,13},{13,9},{2,6},{6,2},{1... | collective-permute-start | bytes 98312 | tf_op jit(solution)/shard_map/ppermute | solution.py:61
  64.2 5.6 %collective-permute-start.20 = (f32[64,128]{1,0:T(8,128)S(1)}, f32[64,128]{1,0:T(8,128)S(1)}, u32[]{:S(2)}, u32[]{:S(2)}) collective-permute-start(f32[64,128]{1,0:T(8,128)S(1)} %fusion.9.refs_0_), channel_id=1, source_target_pairs={{0,8},{4,12},{8,0},{12,4},{1,9},{5,13},{9,1},{13,5},{2,10},{6,14},... | collective-permute-start | bytes 98312 | tf_op jit(solution)/shard_map/ppermute | solution.py:61
  70.9 10.0 %collective-permute-start.26 = (f32[4,8,256]{2,1,0:T(8,128)S(1)}, f32[4,8,256]{2,1,0:T(8,128)S(1)}, u32[]{:S(2)}, u32[]{:S(2)}) collective-permute-start(f32[4,8,256]{2,1,0:T(8,128)S(1)} %get-tuple-element.95.refs_0_.refs_2_.refs_1_), channel_id=1, source_target_pairs={{0,1},{1,0},{2,3},{3,2},{4,5},{5,4},{6,7},{7,6},{8,9},{9,8},{10,11... | collective-permute-start | bytes 98312 | tf_op jit(solution)/shard_map/ppermute | solution.py:61
  73.0 8.0 %collective-permute-start.27 = (f32[4,8,256]{2,1,0:T(8,128)S(1)}, f32[4,8,256]{2,1,0:T(8,128)S(1)}, u32[]{:S(2)}, u32[]{:S(2)}) collective-permute-start(f32[4,8,256]{2,1,0:T(8,128)S(1)} %get-tuple-element.95.refs_0_.refs_2_.refs_1_), channel_id=1, source_target_pairs={{0,2},{1,3},{2,0},{3,1},{4,6},{5,7},{6,4},{7,5},{8,10},{9,11},{10,... | collective-permute-start | bytes 98312 | tf_op jit(solution)/shard_map/ppermute | solution.py:61
  73.9 7.0 %collective-permute-start.28 = (f32[4,8,256]{2,1,0:T(8,128)S(1)}, f32[4,8,256]{2,1,0:T(8,128)S(1)}, u32[]{:S(2)}, u32[]{:S(2)}) collective-permute-start(f32[4,8,256]{2,1,0:T(8,128)S(1)} %get-tuple-element.95.refs_0_.refs_2_.refs_1_), channel_id=1, source_target_pairs={{0,3},{1,2},{2,1},{3,0},{4,7},{5,6},{6,5},{7,4},{8,11},{9,10},{10,... | collective-permute-start | bytes 98312 | tf_op jit(solution)/shard_map/ppermute | solution.py:61
  82.0 10.5 %collective-permute-start.29 = (f32[4,8,256]{2,1,0:T(8,128)S(1)}, f32[4,8,256]{2,1,0:T(8,128)S(1)}, u32[]{:S(2)}, u32[]{:S(2)}) collective-permute-start(f32[4,8,256]{2,1,0:T(8,128)S(1)} %backward_level.3.refs_6_.refs_0_), channel_id=1, source_target_pairs={{0,1},{1,0},{2,3},{3,2},{4,5},{5,4},{6,7},{7,6},{8,9},{9,8},{10,11... | collective-permute-start | bytes 98312 | tf_op jit(solution)/shard_map/ppermute | solution.py:61
  83.1 9.4 %collective-permute-start.30 = (f32[4,8,256]{2,1,0:T(8,128)S(1)}, f32[4,8,256]{2,1,0:T(8,128)S(1)}, u32[]{:S(2)}, u32[]{:S(2)}) collective-permute-start(f32[4,8,256]{2,1,0:T(8,128)S(1)} %backward_level.3.refs_6_.refs_0_), channel_id=1, source_target_pairs={{0,2},{1,3},{2,0},{3,1},{4,6},{5,7},{6,4},{7,5},{8,10},{9,11},{10,... | collective-permute-start | bytes 98312 | tf_op jit(solution)/shard_map/ppermute | solution.py:61
  84.9 7.6 %collective-permute-start.31 = (f32[4,8,256]{2,1,0:T(8,128)S(1)}, f32[4,8,256]{2,1,0:T(8,128)S(1)}, u32[]{:S(2)}, u32[]{:S(2)}) collective-permute-start(f32[4,8,256]{2,1,0:T(8,128)S(1)} %backward_level.3.refs_6_.refs_0_), channel_id=1, source_target_pairs={{0,3},{1,2},{2,1},{3,0},{4,7},{5,6},{6,5},{7,4},{8,11},{9,10},{10,... | collective-permute-start | bytes 98312 | tf_op jit(solution)/shard_map/ppermute | solution.py:61
  95.3 5.5 %collective-permute-start.41 = (f32[3,4,8,256]{3,2,1,0:T(8,128)S(1)}, f32[3,4,8,256]{3,2,1,0:T(8,128)S(1)}, u32[]{:S(2)}, u32[]{:S(2)}) collective-permute-start(f32[3,4,8,256]{3,2,1,0:T(8,128)S(1)} %get-tuple-element.103), channel_id=1, source_target_pairs={{0,12},{4,8},{8,4},{12,0},{1,13},{5,9},{9,5},{13,1},{2,14},{6,10},... | collective-permute-start | bytes 294920 | tf_op jit(solution)/shard_map/ppermute | solution.py:61
  100.9 23.4 %collective-permute-start.42 = (f32[4,3,4,8,256]{4,3,2,1,0:T(8,128)S(1)}, f32[4,3,4,8,256]{4,3,2,1,0:T(8,128)S(1)}, u32[]{:S(2)}, u32[]{:S(2)}) collective-permute-start(f32[4,3,4,8,256]{4,3,2,1,0:T(8,128)S(1)} %pad_maximum_fusion.refs_0_), channel_id=1, source_target_pairs={{0,16},{16,0},{1,17},{17,1},{2,18},{18,2},{3,19},{19,3},{4,20},{20... | collective-permute-start | bytes 1179656 | tf_op jit(solution)/shard_map/ppermute | solution.py:61
  100.9 10.9 %collective-permute-start.32 = (f32[4,8,256]{2,1,0:T(8,128)S(1)}, f32[4,8,256]{2,1,0:T(8,128)S(1)}, u32[]{:S(2)}, u32[]{:S(2)}) collective-permute-start(f32[4,8,256]{2,1,0:T(8,128)S(1)} %backward_level.4.refs_0_), channel_id=1, source_target_pairs={{0,1},{1,0},{2,3},{3,2},{4,5},{5,4},{6,7},{7,6},{8,9},{9,8},{10,11... | collective-permute-start | bytes 98312 | tf_op jit(solution)/shard_map/ppermute | solution.py:61
  101.2 10.7 %collective-permute-start.33 = (f32[4,8,256]{2,1,0:T(8,128)S(1)}, f32[4,8,256]{2,1,0:T(8,128)S(1)}, u32[]{:S(2)}, u32[]{:S(2)}) collective-permute-start(f32[4,8,256]{2,1,0:T(8,128)S(1)} %backward_level.4.refs_0_), channel_id=1, source_target_pairs={{0,2},{1,3},{2,0},{3,1},{4,6},{5,7},{6,4},{7,5},{8,10},{9,11},{10,... | collective-permute-start | bytes 98312 | tf_op jit(solution)/shard_map/ppermute | solution.py:61
  103.9 8.0 %collective-permute-start.34 = (f32[4,8,256]{2,1,0:T(8,128)S(1)}, f32[4,8,256]{2,1,0:T(8,128)S(1)}, u32[]{:S(2)}, u32[]{:S(2)}) collective-permute-start(f32[4,8,256]{2,1,0:T(8,128)S(1)} %backward_level.4.refs_0_), channel_id=1, source_target_pairs={{0,3},{1,2},{2,1},{3,0},{4,7},{5,6},{6,5},{7,4},{8,11},{9,10},{10,... | collective-permute-start | bytes 98312 | tf_op jit(solution)/shard_map/ppermute | solution.py:61
  112.9 7.2 %collective-permute-start.35 = (f32[1,4,8,256]{3,2,1,0:T(8,128)S(1)}, f32[1,4,8,256]{3,2,1,0:T(8,128)S(1)}, u32[]{:S(2)}, u32[]{:S(2)}) collective-permute-start(f32[1,4,8,256]{3,2,1,0:T(8,128)S(1)} %bitcast.59), channel_id=1, source_target_pairs={{0,4},{4,0},{8,12},{12,8},{1,5},{5,1},{9,13},{13,9},{2,6},{6,2},{1... | collective-permute-start | bytes 98312 | tf_op jit(solution)/shard_map/ppermute | solution.py:61
  113.8 6.9 %collective-permute-start.36 = (f32[1,4,8,256]{3,2,1,0:T(8,128)S(1)}, f32[1,4,8,256]{3,2,1,0:T(8,128)S(1)}, u32[]{:S(2)}, u32[]{:S(2)}) collective-permute-start(f32[1,4,8,256]{3,2,1,0:T(8,128)S(1)} %bitcast.60), channel_id=1, source_target_pairs={{0,8},{4,12},{8,0},{12,4},{1,9},{5,13},{9,1},{13,5},{2,10},{6,14},... | collective-permute-start | bytes 98312 | tf_op jit(solution)/shard_map/ppermute | solution.py:61
  (25 other events, 120.0 us)
Sparse Core Ops, SparseCore 0:
  11.5 49.9 all-gather.2

commit v7 on v6

--- a/solution.py
+++ b/solution.py
@@ -131,8 +131,10 @@
     )(blocks, inverse)
 
 
-def middle_kernel(upper, lower, high_out, low_out):
-    high_out[0], low_out[0] = split(product(split(upper[0, 0]), split(lower[0, 0])))
+def middle_kernel(upper, lower, high_out, low_out, lower_high, lower_low):
+    right = split(lower[0, 0])
+    lower_high[0], lower_low[0] = right
+    high_out[0], low_out[0] = split(product(split(upper[0, 0]), right))
 
 
 def middle_step(upper, lower):
@@ -141,9 +143,9 @@
     return pl.pallas_call(
         middle_kernel,
         grid=(nodes,),
-        out_shape=[out, out],
+        out_shape=[out] * 4,
         in_specs=[pl.BlockSpec((1, 1, WIDTH, WIDTH), lambda i: (0, i, 0, 0))] * 2,
-        out_specs=[pl.BlockSpec((1, WIDTH, WIDTH), lambda i: (i, 0, 0))] * 2,
+        out_specs=[pl.BlockSpec((1, WIDTH, WIDTH), lambda i: (i, 0, 0))] * 4,
         compiler_params=STREAM_PARAMS,
         name="middle_product",
     )(upper, lower)
@@ -183,7 +185,7 @@
             where = lax.div(ancestor, nodes) ^ col
             term = product((m_high[distance - 1, node], m_low[distance - 1, node]), right)
             term = pltpu.roll(term, lax.rem(slot - node + nodes, nodes) * own, 1)
-            stored = jnp.where(pattern[place_of(height, distance), node] != 0, slot, -1)
+            stored = jnp.where(pattern[node, place_of(height, distance)] != 0, slot, -1)
             targets[level][where] += jnp.where(lane == stored, term, 0.0)
     for step in range(col_count):
         sends[step][...] = urgent[step]
@@ -216,26 +218,32 @@
 def last_kernel(sizes, *refs):
     nodes, part, own, row_count, col_count = sizes
     pieces = refs[:row_count]
-    z_high, z_low, full, out, turned = refs[row_count:]
+    z_high, z_low, lower_high, lower_low, solved_out, out, full, turned = refs[row_count:]
     assemble(pieces, full, part)
     turned[...] = full[...].T
     for node in range(nodes):
         left = split(own_rows(turned, node, own, row_count))
         out[node] = product_t(left, (z_high[node], z_low[node]))
-
-
-def last_step(pieces, z, sizes):
+    lane = lax.broadcasted_iota(jnp.int32, (1, nodes * own), 1) // own
+    right = split(full[...])
+    solved = jnp.zeros(full.shape, F32)
+    for node in range(nodes):
+        solved = jnp.where(lane == node, product((lower_high[node], lower_low[node]), right), solved)
+    solved_out[...] = solved
+
+
+def last_step(pieces, matrices, sizes):
     nodes, part, own, row_count, col_count = sizes
     lanes, rows = nodes * own, row_count * part
     return pl.pallas_call(
         functools.partial(last_kernel, sizes),
         out_shape=[shape_of(rows, lanes), shape_of(nodes, own // row_count, rows)],
-        in_specs=[VMEM] * (len(pieces) + 2),
+        in_specs=[VMEM] * (len(pieces) + len(matrices)),
         out_specs=[VMEM] * 2,
-        scratch_shapes=[pltpu.VMEM((lanes, rows), F32)],
+        scratch_shapes=[pltpu.VMEM((rows, lanes), F32), pltpu.VMEM((lanes, rows), F32)],
         compiler_params=PARAMS,
         name="forward_last",
-    )(*pieces, *z)
+    )(*pieces, *matrices)
 
 
 def solve_kernel(sizes, full, lower, out, own_out, turned):
@@ -270,11 +278,12 @@
     )(full, lower)
 
 
-def start_kernel(height, nodes, col_count, parents, pattern, value, inverse, *refs):
-    blocks, pieces, out = refs[: height - 1], refs[height - 1 : -1], refs[-1]
+def descend_kernel(height, nodes, col_count, parents, pattern, value, inverse, *refs):
+    blocks, pieces, (out, high_out, low_out) = refs[:height], refs[height:-3], refs[-3:]
     col = lax.axis_index("col")
     node = pl.program_id(0)
     rest = value[0]
+    left = split(inverse[0, 0])
     ancestor = parents[height - 1, col * nodes + node]
     for distance in range(2, height + 1):
         level = height - distance
@@ -285,14 +294,16 @@
         for step in range(1, col_count):
             piece = pieces[level * col_count + step][slot]
             chosen = jnp.where(where == step, piece, chosen)
-        block = blocks[distance - 2][:, 0, 0].reshape(WIDTH, WIDTH)
+        block = blocks[distance - 1][:, 0, 0].reshape(WIDTH, WIDTH)
         term = product_t(split(chosen), split(block))
-        stored = pattern[place_of(height, distance), node] != 0
+        stored = pattern[node, place_of(height, distance)] != 0
         rest = rest - jnp.where(stored, term, 0.0)
-    out[0] = product_t(split(rest), split(inverse[0, 0]))
-
-
-def start_step(height, parents, pattern, value, gathered, inverse, solved, row_count):
+    out[0] = product_t(split(rest), left)
+    nearest = blocks[0][:, 0, 0].reshape(WIDTH, WIDTH)
+    high_out[0], low_out[0] = split(product(left, split(nearest)))
+
+
+def descend_step(height, parents, pattern, value, gathered, inverse, solved, row_count):
     per, nodes, part = gathered.shape[1:4]
     col_count = lax.axis_size("col")
     few, rows = value.shape[1:]
@@ -306,43 +317,19 @@
 
     each = pl.BlockSpec((1, few, rows), lambda i: (i, 0, 0))
     whole = pl.BlockSpec((nodes, few, rows), lambda i: (0, 0, 0))
-    return pl.pallas_call(
-        functools.partial(start_kernel, height, nodes, col_count),
+    matrix = shape_of(nodes, WIDTH, WIDTH, dtype=BF16)
+    return pl.pallas_call(
+        functools.partial(descend_kernel, height, nodes, col_count),
         grid=(nodes,),
-        out_shape=shape_of(nodes, few, rows),
+        out_shape=[shape_of(nodes, few, rows), matrix, matrix],
         in_specs=[SMEM, SMEM, each]
         + [pl.BlockSpec((1, 1, WIDTH, WIDTH), lambda i: (height, i, 0, 0))]
-        + [block_spec(distance) for distance in range(2, height + 1)]
+        + [block_spec(distance) for distance in range(1, height + 1)]
         + [whole] * len(pieces),
-        out_specs=each,
+        out_specs=[each] + [pl.BlockSpec((1, WIDTH, WIDTH), lambda i: (i, 0, 0))] * 2,
         compiler_params=STREAM_PARAMS,
-        name="start_level",
-    )(parents, pattern, value, inverse, *([gathered] * (height - 1)), *pieces)
-
-
-def compose_kernel(gathered, inverse, high_out, low_out):
-    block = gathered[:, 0, 0].reshape(WIDTH, WIDTH)
-    high_out[0], low_out[0] = split(product(split(inverse[0, 0]), split(block)))
-
-
-def compose_step(height, gathered, inverse, row_count):
-    per, nodes, part = gathered.shape[1:4]
-    place = place_of(height, 1)
-    out = shape_of(nodes, WIDTH, WIDTH, dtype=BF16)
-    return pl.pallas_call(
-        compose_kernel,
-        grid=(nodes,),
-        out_shape=[out, out],
-        in_specs=[
-            pl.BlockSpec(
-                (row_count, 1, 1, part, WIDTH), lambda i: (place // per, place % per, i, 0, 0)
-            ),
-            pl.BlockSpec((1, 1, WIDTH, WIDTH), lambda i: (height, i, 0, 0)),
-        ],
-        out_specs=[pl.BlockSpec((1, WIDTH, WIDTH), lambda i: (i, 0, 0))] * 2,
-        compiler_params=STREAM_PARAMS,
-        name="compose_level",
-    )(gathered, inverse)
+        name="descend_level",
+    )(parents, pattern, value, inverse, *([gathered] * height), *pieces)
 
 
 def backward_kernel(height, nodes, parents, pattern, start, high, low, *refs):
@@ -355,7 +342,7 @@
         where = lax.div(ancestor, nodes) ^ col
         left = split(solved[where, lax.rem(ancestor, nodes)])
         term = product_t(left, (high[node], low[node]))
-        stored = pattern[place_of(height, 1), node] != 0
+        stored = pattern[node, place_of(height, 1)] != 0
         out[node] = start[node] - jnp.where(stored, term, 0.0)
 
 
@@ -462,10 +449,6 @@
     )(*parts, *ready)
 
 
-def layers_of(value):
-    return with_layers(jnp.stack(gather(value, "row")))
-
-
 def body(
     right_side,
     layer_sums,
@@ -503,7 +486,8 @@
     per = upper_blocks.shape[0] // gz_count
     half = lax.dynamic_slice_in_dim(after(upper_blocks, *away), gz * per, per, 0)
     upper_rows = lax.all_gather(half, ("gz", "row"))
-    others = [swap(away[step - 1], "gz", step) for step in steps_of(gz_count)]
+    others = [after(swap(away[step - 1], "gz", step), half) for step in steps_of(gz_count)]
+    pattern = pattern.T
     initial = [kept[level] + sum(other[level] for other in others) for level in range(4)]
 
     fulls = [None] * 4
@@ -523,14 +507,13 @@
         taken[-1] = after(taken[-1], *forward[height])
         mine = initial[height - 1] - sends[0] - sum(taken)
     z = middle_step(upper_diagonal_inverses, lower_inverse)
-    fulls[0], solved = last_step(gather(mine, "row"), z, sizes)
-    forward[0] = solve_step(0, fulls[0], lower_inverse, sizes)
+    solved_forward, solved = last_step(gather(mine, "row"), z, sizes)
+    forward[0] = (solved_forward,)
 
     backward = [solved]
     whole = []
     for height in (1, 2, 3):
-        composed = compose_step(height, upper_rows, upper_diagonal_inverses, row_count)
-        start = start_step(
+        start, *composed = descend_step(
             height,
             parents,
             pattern,
@@ -541,12 +524,17 @@
             row_count,
         )
         whole = whole + [gather(backward[-1], "col")]
+        if height == 3:
+            early = gather(after(jnp.stack(backward), whole[-1][-1]), "row")
         backward.append(backward_step(height, parents, pattern, start, composed, whole[-1]))
 
     forward_parts = [piece for level in forward for piece in with_layers(level[0])]
     forward_all = forward_out(forward_parts, nodes, own, gz_count)
-    backward_all = backward_out(layers_of(jnp.stack(backward[:3])), None, 0, own)
-    backward_all = backward_out(layers_of(backward[3][None]), backward_all, 3, own)
+    late = gather(backward[3][None], "row")
+    early = [after(piece, *late, forward_all) for piece in early]
+    early, late = with_layers(jnp.stack(early)), with_layers(jnp.stack(late))
+    backward_all = backward_out(early, None, 0, own)
+    backward_all = backward_out(late, backward_all, 3, own)
     return tuple(
         value.transpose(0, 2, 1, 3).reshape(4, nodes, WIDTH * COLUMNS)
         for value in (forward_all, backward_all)

time: 135 us -> 130 us (0.963)
  Pallas kernels: 55 us -> 45.7 us
  waiting for transfers between devices: 10.5 us -> 17.5 us
  starting transfers between devices: 50.6 us -> 47.7 us
    ppermute x43, waiting for transfers between devices: 10.5 us -> 17.5 us  [swap(): lax.ppermute(value, axis, [(i, i ^ step) for i in range(lax.axis_size(axi...]
    pallas_call x7 -> x4, Pallas kernels: 21 us -> 15.4 us  [the longest x3 11.9 us: descend_step(): pl.pallas_call(functools.partial(descend_kernel, height, nodes, col_count...]
    pallas_call x4 -> x3, Pallas kernels: 12.1 us -> 8.34 us  [solve_step(): pl.pallas_call(functools.partial(solve_kernel, sizes), grid=(nodes,), out...]
    ppermute x43, starting transfers between devices: 50.6 us -> 47.7 us  [swap(): lax.ppermute(value, axis, [(i, i ^ step) for i in range(lax.axis_size(axi...]
    unnamed x11 -> x14, local copies, waits for them, and re-layouts: 2.79 us -> 3.06 us
  transfers between devices with their start and end apart: 44 -> 44, of which waited for: 14 -> 13; matrix products, arithmetic and copies ran while one was open for 1% -> 0% of each run, Pallas kernels for 38% -> 34%
where the time goes in v7:
time: 130 us
  starting transfers between devices  47.7 us (37%)
  Pallas kernels  45.7 us (35%)
  waiting for transfers between devices  17.5 us (13%)
  between operations  14.4 us (11%)
  local copies, waits for them, and re-layouts  4.04 us (3%)
    ppermute x43, starting transfers between devices, swap(): lax.ppermute(value, axis, [(i, i ^ step) for i in range(lax.axis_size(axi...  47.7 us
    ppermute x43, waiting for transfers between devices, swap(): lax.ppermute(value, axis, [(i, i ^ step) for i in range(lax.axis_size(axi...  17.5 us
    pallas_call x3, Pallas kernels, descend_step(): pl.pallas_call(functools.partial(descend_kernel, height, nodes, col_count...  11.9 us
    pallas_call x3, Pallas kernels, lower_step(): pl.pallas_call(functools.partial(lower_kernel, height), grid=(nodes,), ou...  8.66 us
    pallas_call x3, Pallas kernels, solve_step(): pl.pallas_call(functools.partial(solve_kernel, sizes), grid=(nodes,), out...  8.34 us
    pallas_call x1, Pallas kernels, middle_step(): pl.pallas_call(middle_kernel, grid=(nodes,), out_shape=[out] * 4, in_spec...  3.55 us
    pallas_call x2, Pallas kernels, backward_out(): pl.pallas_call(functools.partial(backward_out_kernel, nodes, len(parts),...  3.38 us
    pallas_call x3, Pallas kernels, forward_step(): pl.pallas_call(functools.partial(forward_kernel, height, sizes), out_shap...  3.14 us
  transfers between devices with their start and end apart: 44, of which 13 were waited for; matrix products, arithmetic and copies ran while one was open for 0% of the time, Pallas kernels for 34%

profile of v7, /device:TPU:0, one launch (start us, length us, event | category | flops | bytes accessed | tf_op | source)
XLA Modules:
  0.0 129.5 jit_solution(5565499388671075420)
XLA Ops:
  12.9 2.8 %collective-permute-start.1 = (f32[64,128]{1,0:T(8,128)S(1)}, f32[64,128]{1,0:T(8,128)S(1)}, u32[]{:S(2)}, u32[]{:S(2)}) collective-permute-start(f32[64,128]{1,0:T(8,128)S(1)} %bitcast_add_fusion.refs_0_), channel_id=1, source_target_pairs={{0,4},{4,0},{8,12},{12,8},{1,5},{5,1},{9,13},{13,9},{2,6},{6,2},{1... | collective-permute-start | bytes 98312 | tf_op jit(solution)/shard_map/ppermute | solution.py:61
  17.2 3.0 %lower_products.3 = (bf16[3,4,64,256]{3,2,1,0:T(8,128)(2,1)S(1)}, bf16[3,4,64,256]{3,2,1,0:T(8,128)(2,1)S(1)}) custom-call(f32[6,4,64,256]{3,2,1,0:T(8,128)} %blocks.5, f32[4,4,256,256]{3,2,1,0:T(8,128)} %lower.7), custom_call_target="tpu_custom_call" | custom-call | tf_op jit(solution)/shard_map/lower_products/pallas_call | solution.py:120
  20.3 1.7 %collective-permute-done.3.refs_3_ = f32[64,128]{1,0:T(8,128)S(1)} collective-permute-done((f32[64,128]{1,0:T(8,128)S(1)}, f32[64,128]{1,0:T(8,128)S(1)}, u32[]{:S(2)}, u32[]{:S(2)}) %collective-permute-start.3) | collective-permute-done | bytes 32800 | tf_op jit(solution)/shard_map/ppermute | solution.py:61
  23.2 3.7 %collective-permute-start.6 = (f32[64,128]{1,0:T(8,128)S(1)}, f32[64,128]{1,0:T(8,128)S(1)}, u32[]{:S(2)}, u32[]{:S(2)}) collective-permute-start(f32[64,128]{1,0:T(8,128)S(1)} %get-tuple-element.74), channel_id=1, source_target_pairs={{0,3},{1,2},{2,1},{3,0},{4,7},{5,6},{6,5},{7,4},{8,11},{9,10},{10,... | collective-permute-start | bytes 98312 | tf_op jit(solution)/shard_map/ppermute | solution.py:61
  27.7 2.8 %solve_level.3 = (f32[256,128]{1,0:T(8,128)S(1)}, f32[4,8,256]{2,1,0:T(8,128)S(1)}) custom-call(f32[256,128]{1,0:T(8,128)S(1)} %get-tuple-element.75.full, f32[4,4,256,256]{3,2,1,0:T(8,128)} %lower.7), custom_call_target="tpu_custom_call" | custom-call | tf_op jit(solution)/shard_map/solve_level/pallas_call | solution.py:269
  35.3 2.9 %lower_products.4 = (bf16[2,4,64,256]{3,2,1,0:T(8,128)(2,1)S(1)}, bf16[2,4,64,256]{3,2,1,0:T(8,128)(2,1)S(1)}) custom-call(f32[6,4,64,256]{3,2,1,0:T(8,128)} %blocks.5, f32[4,4,256,256]{3,2,1,0:T(8,128)} %lower.7), custom_call_target="tpu_custom_call" | custom-call | tf_op jit(solution)/shard_map/lower_products/pallas_call | solution.py:120
  39.4 2.5 %collective-permute-start.12 = (f32[64,128]{1,0:T(8,128)S(1)}, f32[64,128]{1,0:T(8,128)S(1)}, u32[]{:S(2)}, u32[]{:S(2)}) collective-permute-start(f32[64,128]{1,0:T(8,128)S(1)} %get-tuple-element.86), channel_id=1, source_target_pairs={{0,3},{1,2},{2,1},{3,0},{4,7},{5,6},{6,5},{7,4},{8,11},{9,10},{10,... | collective-permute-start | bytes 98312 | tf_op jit(solution)/shard_map/ppermute | solution.py:61
  41.9 2.0 %collective-permute-start.11 = (f32[64,128]{1,0:T(8,128)S(1)}, f32[64,128]{1,0:T(8,128)S(1)}, u32[]{:S(2)}, u32[]{:S(2)}) collective-permute-start(f32[64,128]{1,0:T(8,128)S(1)} %get-tuple-element.85), channel_id=1, source_target_pairs={{0,2},{1,3},{2,0},{3,1},{4,6},{5,7},{6,4},{7,5},{8,10},{9,11},{10,... | collective-permute-start | bytes 98312 | tf_op jit(solution)/shard_map/ppermute | solution.py:61
  43.9 2.8 %solve_level.4 = (f32[256,128]{1,0:T(8,128)S(1)}, f32[4,8,256]{2,1,0:T(8,128)S(1)}) custom-call(f32[256,128]{1,0:T(8,128)S(1)} %get-tuple-element.87.full, f32[4,4,256,256]{3,2,1,0:T(8,128)} %lower.7), custom_call_target="tpu_custom_call" | custom-call | tf_op jit(solution)/shard_map/solve_level/pallas_call | solution.py:269
  50.3 2.7 %lower_products.5 = (bf16[1,4,64,256]{3,2,1,0:T(8,128)(2,1)S(1)}, bf16[1,4,64,256]{3,2,1,0:T(8,128)(2,1)S(1)}) custom-call(f32[6,4,64,256]{3,2,1,0:T(8,128)S(1)} %copy-done.1, f32[4,4,256,256]{3,2,1,0:T(8,128)} %lower.7), custom_call_target="tpu_custom_call" | custom-call | tf_op jit(solution)/shard_map/lower_products/pallas_call | solution.py:120
  55.5 2.6 %collective-permute-start.18 = (f32[64,128]{1,0:T(8,128)S(1)}, f32[64,128]{1,0:T(8,128)S(1)}, u32[]{:S(2)}, u32[]{:S(2)}) collective-permute-start(f32[64,128]{1,0:T(8,128)S(1)} %get-tuple-element.97), channel_id=1, source_target_pairs={{0,3},{1,2},{2,1},{3,0},{4,7},{5,6},{6,5},{7,4},{8,11},{9,10},{10,... | collective-permute-start | bytes 98312 | tf_op jit(solution)/shard_map/ppermute | solution.py:61
  58.1 1.8 %collective-permute-start.17 = (f32[64,128]{1,0:T(8,128)S(1)}, f32[64,128]{1,0:T(8,128)S(1)}, u32[]{:S(2)}, u32[]{:S(2)}) collective-permute-start(f32[64,128]{1,0:T(8,128)S(1)} %get-tuple-element.96), channel_id=1, source_target_pairs={{0,2},{1,3},{2,0},{3,1},{4,6},{5,7},{6,4},{7,5},{8,10},{9,11},{10,... | collective-permute-start | bytes 98312 | tf_op jit(solution)/shard_map/ppermute | solution.py:61
  60.0 2.8 %solve_level.5 = (f32[256,128]{1,0:T(8,128)S(1)}, f32[4,8,256]{2,1,0:T(8,128)S(1)}) custom-call(f32[256,128]{1,0:T(8,128)S(1)} %get-tuple-element.98.full, f32[4,4,256,256]{3,2,1,0:T(8,128)} %lower.7), custom_call_target="tpu_custom_call" | custom-call | tf_op jit(solution)/shard_map/solve_level/pallas_call | solution.py:269
  66.5 3.6 %middle_product.1 = (bf16[4,256,256]{2,1,0:T(8,128)(2,1)S(1)}, bf16[4,256,256]{2,1,0:T(8,128)(2,1)S(1)}, bf16[4,256,256]{2,1,0:T(8,128)(2,1)S(1)}, bf16[4,256,256]{2,1,0:T(8,128)(2,1)}) custom-call(f32[4,4,256,256]{3,2,1,0:T(8,128)} %inverse.11, f32[4,4,256,256]{3,2,1,0:T(8,128)} %lower.7), custom_call_target="tpu_custom_call" | custom-call | tf_op jit(solution)/shard_map/middle_product/pallas_call | solution.py:143
  71.9 2.1 %collective-permute-start.26 = (f32[4,8,256]{2,1,0:T(8,128)S(1)}, f32[4,8,256]{2,1,0:T(8,128)S(1)}, u32[]{:S(2)}, u32[]{:S(2)}) collective-permute-start(f32[4,8,256]{2,1,0:T(8,128)S(1)} %get-tuple-element.107.refs_0_.refs_3_.refs_2_), channel_id=1, source_target_pairs={{0,1},{1,0},{2,3},{3,2},{4,5},{5,4},{6,7},{7,6},{8,9},{9,8},{10,11... | collective-permute-start | bytes 98312 | tf_op jit(solution)/shard_map/ppermute | solution.py:61
  76.4 3.2 %descend_level.3 = (f32[4,8,256]{2,1,0:T(8,128)S(1)}, bf16[4,256,256]{2,1,0:T(8,128)(2,1)S(1)}, bf16[4,256,256]{2,1,0:T(8,128)(2,1)S(1)}) custom-call(s32[3,16]{1,0:T(4,128)S(1)} %copy-done.5, s32[4,6]{1,0:T(4,128)S(1)} %bitcast.54, f32[4,8,256]{2,1,0:T(8,128)S(1)} %get-tuple-element.100.value, f32[4,4,256,256]{3,2,1,0:T(8,128)} %inverse.11, ...), custom_call_target="tpu_custom_call" | custom-call | tf_op jit(solution)/shard_map/descend_level/pallas_call | solution.py:321
  81.7 2.0 %collective-permute-start.30 = (f32[4,8,256]{2,1,0:T(8,128)S(1)}, f32[4,8,256]{2,1,0:T(8,128)S(1)}, u32[]{:S(2)}, u32[]{:S(2)}) collective-permute-start(f32[4,8,256]{2,1,0:T(8,128)S(1)} %backward_level.3.refs_7_.refs_0_), channel_id=1, source_target_pairs={{0,2},{1,3},{2,0},{3,1},{4,6},{5,7},{6,4},{7,5},{8,10},{9,11},{10,... | collective-permute-start | bytes 98312 | tf_op jit(solution)/shard_map/ppermute | solution.py:61
  83.7 2.4 %collective-permute-start.31 = (f32[4,8,256]{2,1,0:T(8,128)S(1)}, f32[4,8,256]{2,1,0:T(8,128)S(1)}, u32[]{:S(2)}, u32[]{:S(2)}) collective-permute-start(f32[4,8,256]{2,1,0:T(8,128)S(1)} %backward_level.3.refs_7_.refs_0_), channel_id=1, source_target_pairs={{0,3},{1,2},{2,1},{3,0},{4,7},{5,6},{6,5},{7,4},{8,11},{9,10},{10,... | collective-permute-start | bytes 98312 | tf_op jit(solution)/shard_map/ppermute | solution.py:61
  86.0 4.2 %descend_level.5 = (f32[4,8,256]{2,1,0:T(8,128)S(1)}, bf16[4,256,256]{2,1,0:T(8,128)(2,1)S(1)}, bf16[4,256,256]{2,1,0:T(8,128)(2,1)S(1)}) custom-call(s32[3,16]{1,0:T(4,128)S(1)} %copy-done.5, s32[4,6]{1,0:T(4,128)S(1)} %bitcast.56, f32[4,8,256]{2,1,0:T(8,128)S(1)} %get-tuple-element.89.value, f32[4,4,256,256]{3,2,1,0:T(8,128)} %inverse.11, ...), custom_call_target="tpu_custom_call" | custom-call | tf_op jit(solution)/shard_map/descend_level/pallas_call | solution.py:321
  93.3 3.8 %collective-permute-done.34.refs_3_ = f32[4,8,256]{2,1,0:T(8,128)S(1)} collective-permute-done((f32[4,8,256]{2,1,0:T(8,128)S(1)}, f32[4,8,256]{2,1,0:T(8,128)S(1)}, u32[]{:S(2)}, u32[]{:S(2)}) %collective-permute-start.34) | collective-permute-done | bytes 32800 | tf_op jit(solution)/shard_map/ppermute | solution.py:61
  98.9 2.9 %collective-permute-done.33.refs_2_ = f32[4,8,256]{2,1,0:T(8,128)S(1)} collective-permute-done((f32[4,8,256]{2,1,0:T(8,128)S(1)}, f32[4,8,256]{2,1,0:T(8,128)S(1)}, u32[]{:S(2)}, u32[]{:S(2)}) %collective-permute-start.33) | collective-permute-done | bytes 32800 | tf_op jit(solution)/shard_map/ppermute | solution.py:61
  103.1 4.6 %descend_level.4 = (f32[4,8,256]{2,1,0:T(8,128)S(1)}, bf16[4,256,256]{2,1,0:T(8,128)(2,1)S(1)}, bf16[4,256,256]{2,1,0:T(8,128)(2,1)S(1)}) custom-call(s32[3,16]{1,0:T(4,128)S(1)} %copy-done.5, s32[4,6]{1,0:T(4,128)S(1)} %bitcast.58, f32[4,8,256]{2,1,0:T(8,128)S(1)} %get-tuple-element.77.value, f32[4,4,256,256]{3,2,1,0:T(8,128)} %inverse.11, ...), custom_call_target="tpu_custom_call" | custom-call | tf_op jit(solution)/shard_map/descend_level/pallas_call | solution.py:321
  114.3 2.1 %forward_out.1 = f32[4,128,4,128]{3,2,1,0:T(4,128)} custom-call(f32[256,128]{1,0:T(8,128)S(1)} %get-tuple-element.106.refs_0_, f32[256,128]{1,0:T(8,128)S(1)} %collective-permute-done.22.refs_1_, f32[256,128]{1,0:T(8,128)S(1)} %get-tuple-element.99.refs_2_, f32[256,128]{1,0:T(8,128)S(1)} %collective-permute-done.23.refs_3_, ...), custom_call_target="tpu_custom_call" | custom-call | tf_op jit(solution)/shard_map/forward_out/pallas_call | solution.py:402
  119.3 2.3 %backward_out.2.refs_2_ = f32[4,128,4,128]{3,2,1,0:T(4,128)} custom-call(f32[4,3,4,8,256]{4,3,2,1,0:T(8,128)S(1)} %pad_maximum_fusion.refs_0_, f32[4,3,4,8,256]{4,3,2,1,0:T(8,128)S(1)} %collective-permute-done.42.refs_1_), custom_call_target="tpu_custom_call" | custom-call | tf_op jit(solution)/shard_map/backward_out/pallas_call | solution.py:435
  (108 shorter events, 48.0 us)
Async XLA Ops:
  7.2 69.2 %all-gather.3.cloned.1.call-start = ((), (), s32[]{:S(2)}) async-start(), calls=%async_computation | async-start | bytes 7077888 | tf_op jit(solution)/shard_map/all_gather | solution.py:488
  12.9 7.4 %collective-permute-start.1 = (f32[64,128]{1,0:T(8,128)S(1)}, f32[64,128]{1,0:T(8,128)S(1)}, u32[]{:S(2)}, u32[]{:S(2)}) collective-permute-start(f32[64,128]{1,0:T(8,128)S(1)} %bitcast_add_fusion.refs_0_), channel_id=1, source_target_pairs={{0,4},{4,0},{8,12},{12,8},{1,5},{5,1},{9,13},{13,9},{2,6},{6,2},{1... | collective-permute-start | bytes 98312 | tf_op jit(solution)/shard_map/ppermute | solution.py:61
  23.2 7.2 %collective-permute-start.6 = (f32[64,128]{1,0:T(8,128)S(1)}, f32[64,128]{1,0:T(8,128)S(1)}, u32[]{:S(2)}, u32[]{:S(2)}) collective-permute-start(f32[64,128]{1,0:T(8,128)S(1)} %get-tuple-element.74), channel_id=1, source_target_pairs={{0,3},{1,2},{2,1},{3,0},{4,7},{5,6},{6,5},{7,4},{8,11},{9,10},{10,... | collective-permute-start | bytes 98312 | tf_op jit(solution)/shard_map/ppermute | solution.py:61
  31.7 6.5 %collective-permute-start.7 = (f32[64,128]{1,0:T(8,128)S(1)}, f32[64,128]{1,0:T(8,128)S(1)}, u32[]{:S(2)}, u32[]{:S(2)}) collective-permute-start(f32[64,128]{1,0:T(8,128)S(1)} %fusion.1.refs_0_), channel_id=1, source_target_pairs={{0,4},{4,0},{8,12},{12,8},{1,5},{5,1},{9,13},{13,9},{2,6},{6,2},{1... | collective-permute-start | bytes 98312 | tf_op jit(solution)/shard_map/ppermute | solution.py:61
  32.3 5.9 %collective-permute-start.8 = (f32[64,128]{1,0:T(8,128)S(1)}, f32[64,128]{1,0:T(8,128)S(1)}, u32[]{:S(2)}, u32[]{:S(2)}) collective-permute-start(f32[64,128]{1,0:T(8,128)S(1)} %fusion.1.refs_0_), channel_id=1, source_target_pairs={{0,8},{4,12},{8,0},{12,4},{1,9},{5,13},{9,1},{13,5},{2,10},{6,14},... | collective-permute-start | bytes 98312 | tf_op jit(solution)/shard_map/ppermute | solution.py:61
  39.4 7.2 %collective-permute-start.12 = (f32[64,128]{1,0:T(8,128)S(1)}, f32[64,128]{1,0:T(8,128)S(1)}, u32[]{:S(2)}, u32[]{:S(2)}) collective-permute-start(f32[64,128]{1,0:T(8,128)S(1)} %get-tuple-element.86), channel_id=1, source_target_pairs={{0,3},{1,2},{2,1},{3,0},{4,7},{5,6},{6,5},{7,4},{8,11},{9,10},{10,... | collective-permute-start | bytes 98312 | tf_op jit(solution)/shard_map/ppermute | solution.py:61
  46.7 6.2 %collective-permute-start.13 = (f32[64,128]{1,0:T(8,128)S(1)}, f32[64,128]{1,0:T(8,128)S(1)}, u32[]{:S(2)}, u32[]{:S(2)}) collective-permute-start(f32[64,128]{1,0:T(8,128)S(1)} %fusion.3.refs_0_), channel_id=1, source_target_pairs={{0,4},{4,0},{8,12},{12,8},{1,5},{5,1},{9,13},{13,9},{2,6},{6,2},{1... | collective-permute-start | bytes 98312 | tf_op jit(solution)/shard_map/ppermute | solution.py:61
  55.5 7.2 %collective-permute-start.18 = (f32[64,128]{1,0:T(8,128)S(1)}, f32[64,128]{1,0:T(8,128)S(1)}, u32[]{:S(2)}, u32[]{:S(2)}) collective-permute-start(f32[64,128]{1,0:T(8,128)S(1)} %get-tuple-element.97), channel_id=1, source_target_pairs={{0,3},{1,2},{2,1},{3,0},{4,7},{5,6},{6,5},{7,4},{8,11},{9,10},{10,... | collective-permute-start | bytes 98312 | tf_op jit(solution)/shard_map/ppermute | solution.py:61
  63.0 7.1 %collective-permute-start.19 = (f32[64,128]{1,0:T(8,128)S(1)}, f32[64,128]{1,0:T(8,128)S(1)}, u32[]{:S(2)}, u32[]{:S(2)}) collective-permute-start(f32[64,128]{1,0:T(8,128)S(1)} %fusion.5.refs_0_), channel_id=1, source_target_pairs={{0,4},{4,0},{8,12},{12,8},{1,5},{5,1},{9,13},{13,9},{2,6},{6,2},{1... | collective-permute-start | bytes 98312 | tf_op jit(solution)/shard_map/ppermute | solution.py:61
  63.6 6.5 %collective-permute-start.20 = (f32[64,128]{1,0:T(8,128)S(1)}, f32[64,128]{1,0:T(8,128)S(1)}, u32[]{:S(2)}, u32[]{:S(2)}) collective-permute-start(f32[64,128]{1,0:T(8,128)S(1)} %fusion.5.refs_0_), channel_id=1, source_target_pairs={{0,8},{4,12},{8,0},{12,4},{1,9},{5,13},{9,1},{13,5},{2,10},{6,14},... | collective-permute-start | bytes 98312 | tf_op jit(solution)/shard_map/ppermute | solution.py:61
  66.5 26.8 %collective-permute-start.25 = (f32[256,128]{1,0:T(8,128)S(1)}, f32[256,128]{1,0:T(8,128)S(1)}, u32[]{:S(2)}, u32[]{:S(2)}) collective-permute-start(f32[256,128]{1,0:T(8,128)S(1)} %get-tuple-element.76.refs_6_), channel_id=1, source_target_pairs={{0,16},{16,0},{1,17},{17,1},{2,18},{18,2},{3,19},{19,3},{4,20},{20... | collective-permute-start | bytes 393224 | tf_op jit(solution)/shard_map/ppermute | solution.py:61
  71.9 7.7 %collective-permute-start.26 = (f32[4,8,256]{2,1,0:T(8,128)S(1)}, f32[4,8,256]{2,1,0:T(8,128)S(1)}, u32[]{:S(2)}, u32[]{:S(2)}) collective-permute-start(f32[4,8,256]{2,1,0:T(8,128)S(1)} %get-tuple-element.107.refs_0_.refs_3_.refs_2_), channel_id=1, source_target_pairs={{0,1},{1,0},{2,3},{3,2},{4,5},{5,4},{6,7},{7,6},{8,9},{9,8},{10,11... | collective-permute-start | bytes 98312 | tf_op jit(solution)/shard_map/ppermute | solution.py:61
  74.0 5.6 %collective-permute-start.27 = (f32[4,8,256]{2,1,0:T(8,128)S(1)}, f32[4,8,256]{2,1,0:T(8,128)S(1)}, u32[]{:S(2)}, u32[]{:S(2)}) collective-permute-start(f32[4,8,256]{2,1,0:T(8,128)S(1)} %get-tuple-element.107.refs_0_.refs_3_.refs_2_), channel_id=1, source_target_pairs={{0,2},{1,3},{2,0},{3,1},{4,6},{5,7},{6,4},{7,5},{8,10},{9,11},{10,... | collective-permute-start | bytes 98312 | tf_op jit(solution)/shard_map/ppermute | solution.py:61
  75.0 5.7 %collective-permute-start.28 = (f32[4,8,256]{2,1,0:T(8,128)S(1)}, f32[4,8,256]{2,1,0:T(8,128)S(1)}, u32[]{:S(2)}, u32[]{:S(2)}) collective-permute-start(f32[4,8,256]{2,1,0:T(8,128)S(1)} %get-tuple-element.107.refs_0_.refs_3_.refs_2_), channel_id=1, source_target_pairs={{0,3},{1,2},{2,1},{3,0},{4,7},{5,6},{6,5},{7,4},{8,11},{9,10},{10,... | collective-permute-start | bytes 98312 | tf_op jit(solution)/shard_map/ppermute | solution.py:61
  81.6 8.6 %collective-permute-start.29 = (f32[4,8,256]{2,1,0:T(8,128)S(1)}, f32[4,8,256]{2,1,0:T(8,128)S(1)}, u32[]{:S(2)}, u32[]{:S(2)}) collective-permute-start(f32[4,8,256]{2,1,0:T(8,128)S(1)} %backward_level.3.refs_7_.refs_0_), channel_id=1, source_target_pairs={{0,1},{1,0},{2,3},{3,2},{4,5},{5,4},{6,7},{7,6},{8,9},{9,8},{10,11... | collective-permute-start | bytes 98312 | tf_op jit(solution)/shard_map/ppermute | solution.py:61
  81.7 8.5 %collective-permute-start.30 = (f32[4,8,256]{2,1,0:T(8,128)S(1)}, f32[4,8,256]{2,1,0:T(8,128)S(1)}, u32[]{:S(2)}, u32[]{:S(2)}) collective-permute-start(f32[4,8,256]{2,1,0:T(8,128)S(1)} %backward_level.3.refs_7_.refs_0_), channel_id=1, source_target_pairs={{0,2},{1,3},{2,0},{3,1},{4,6},{5,7},{6,4},{7,5},{8,10},{9,11},{10,... | collective-permute-start | bytes 98312 | tf_op jit(solution)/shard_map/ppermute | solution.py:61
  83.7 6.6 %collective-permute-start.31 = (f32[4,8,256]{2,1,0:T(8,128)S(1)}, f32[4,8,256]{2,1,0:T(8,128)S(1)}, u32[]{:S(2)}, u32[]{:S(2)}) collective-permute-start(f32[4,8,256]{2,1,0:T(8,128)S(1)} %backward_level.3.refs_7_.refs_0_), channel_id=1, source_target_pairs={{0,3},{1,2},{2,1},{3,0},{4,7},{5,6},{6,5},{7,4},{8,11},{9,10},{10,... | collective-permute-start | bytes 98312 | tf_op jit(solution)/shard_map/ppermute | solution.py:61
  91.2 5.8 %collective-permute-start.34 = (f32[4,8,256]{2,1,0:T(8,128)S(1)}, f32[4,8,256]{2,1,0:T(8,128)S(1)}, u32[]{:S(2)}, u32[]{:S(2)}) collective-permute-start(f32[4,8,256]{2,1,0:T(8,128)S(1)} %backward_level.4.refs_0_), channel_id=1, source_target_pairs={{0,3},{1,2},{2,1},{3,0},{4,7},{5,6},{6,5},{7,4},{8,11},{9,10},{10,... | collective-permute-start | bytes 98312 | tf_op jit(solution)/shard_map/ppermute | solution.py:61
  92.8 15.9 %collective-permute-start.23 = (f32[256,128]{1,0:T(8,128)S(1)}, f32[256,128]{1,0:T(8,128)S(1)}, u32[]{:S(2)}, u32[]{:S(2)}) collective-permute-start(f32[256,128]{1,0:T(8,128)S(1)} %get-tuple-element.99.refs_2_), channel_id=1, source_target_pairs={{0,16},{16,0},{1,17},{17,1},{2,18},{18,2},{3,19},{19,3},{4,20},{20... | collective-permute-start | bytes 393224 | tf_op jit(solution)/shard_map/ppermute | solution.py:61
  93.3 16.2 %collective-permute-start.22 = (f32[256,128]{1,0:T(8,128)S(1)}, f32[256,128]{1,0:T(8,128)S(1)}, u32[]{:S(2)}, u32[]{:S(2)}) collective-permute-start(f32[256,128]{1,0:T(8,128)S(1)} %get-tuple-element.106.refs_0_), channel_id=1, source_target_pairs={{0,16},{16,0},{1,17},{17,1},{2,18},{18,2},{3,19},{19,3},{4,20},{20... | collective-permute-start | bytes 393224 | tf_op jit(solution)/shard_map/ppermute | solution.py:61
  97.1 20.4 %collective-permute-start.39 = (f32[3,4,8,256]{3,2,1,0:T(8,128)S(1)}, f32[3,4,8,256]{3,2,1,0:T(8,128)S(1)}, u32[]{:S(2)}, u32[]{:S(2)}) collective-permute-start(f32[3,4,8,256]{3,2,1,0:T(8,128)S(1)} %pad_maximum_fusion.2), channel_id=1, source_target_pairs={{0,4},{4,0},{8,12},{12,8},{1,5},{5,1},{9,13},{13,9},{2,6},{6,2},{1... | collective-permute-start | bytes 294920 | tf_op jit(solution)/shard_map/ppermute | solution.py:61
  97.6 19.8 %collective-permute-start.40 = (f32[3,4,8,256]{3,2,1,0:T(8,128)S(1)}, f32[3,4,8,256]{3,2,1,0:T(8,128)S(1)}, u32[]{:S(2)}, u32[]{:S(2)}) collective-permute-start(f32[3,4,8,256]{3,2,1,0:T(8,128)S(1)} %pad_maximum_fusion.2), channel_id=1, source_target_pairs={{0,8},{4,12},{8,0},{12,4},{1,9},{5,13},{9,1},{13,5},{2,10},{6,14},... | collective-permute-start | bytes 294920 | tf_op jit(solution)/shard_map/ppermute | solution.py:61
  101.9 15.6 %collective-permute-start.41 = (f32[3,4,8,256]{3,2,1,0:T(8,128)S(1)}, f32[3,4,8,256]{3,2,1,0:T(8,128)S(1)}, u32[]{:S(2)}, u32[]{:S(2)}) collective-permute-start(f32[3,4,8,256]{3,2,1,0:T(8,128)S(1)} %pad_maximum_fusion.2), channel_id=1, source_target_pairs={{0,12},{4,8},{8,4},{12,0},{1,13},{5,9},{9,5},{13,1},{2,14},{6,10},... | collective-permute-start | bytes 294920 | tf_op jit(solution)/shard_map/ppermute | solution.py:61
  109.4 7.0 %collective-permute-start.36 = (f32[1,4,8,256]{3,2,1,0:T(8,128)S(1)}, f32[1,4,8,256]{3,2,1,0:T(8,128)S(1)}, u32[]{:S(2)}, u32[]{:S(2)}) collective-permute-start(f32[1,4,8,256]{3,2,1,0:T(8,128)S(1)} %bitcast.61), channel_id=1, source_target_pairs={{0,8},{4,12},{8,0},{12,4},{1,9},{5,13},{9,1},{13,5},{2,10},{6,14},... | collective-permute-start | bytes 98312 | tf_op jit(solution)/shard_map/ppermute | solution.py:61
  (27 other events, 136.0 us)
Sparse Core Ops, SparseCore 0:
  11.5 50.6 all-gather.2

commit v8 on v7

--- a/solution.py
+++ b/solution.py
@@ -16,6 +16,8 @@
 VMEM = pl.BlockSpec(memory_space=pltpu.VMEM)
 HBM = pl.BlockSpec(memory_space=pltpu.HBM)
 PARAMS = pltpu.CompilerParams(vmem_limit_bytes=16 * 2**20)
+INPUT_PARAMS = pltpu.CompilerParams(vmem_limit_bytes=54 * 2**20)
+MIDDLE_PARAMS = pltpu.CompilerParams(vmem_limit_bytes=51 * 2**20)
 STREAM_PARAMS = pltpu.CompilerParams(vmem_limit_bytes=52 * 2**20)
 
 
@@ -146,7 +148,7 @@
         out_shape=[out] * 4,
         in_specs=[pl.BlockSpec((1, 1, WIDTH, WIDTH), lambda i: (0, i, 0, 0))] * 2,
         out_specs=[pl.BlockSpec((1, WIDTH, WIDTH), lambda i: (i, 0, 0))] * 4,
-        compiler_params=STREAM_PARAMS,
+        compiler_params=MIDDLE_PARAMS,
         name="middle_product",
     )(upper, lower)
 
@@ -332,10 +334,12 @@
     )(parents, pattern, value, inverse, *([gathered] * height), *pieces)
 
 
-def backward_kernel(height, nodes, parents, pattern, start, high, low, *refs):
-    pieces, out, solved = refs[:-2], refs[-2], refs[-1]
+def backward_kernel(height, nodes, col_count, parents, pattern, start, high, low, *refs):
+    pieces, earlier, (out, solved) = refs[:col_count], refs[col_count:-2], refs[-2:]
     for step, piece in enumerate(pieces):
         solved[step] = piece[...]
+    for level, value in enumerate(earlier):
+        out[level] = value[...]
     col = lax.axis_index("col")
     for node in range(nodes):
         ancestor = parents[height - 1, col * nodes + node]
@@ -343,19 +347,24 @@
         left = split(solved[where, lax.rem(ancestor, nodes)])
         term = product_t(left, (high[node], low[node]))
         stored = pattern[node, place_of(height, 1)] != 0
-        out[node] = start[node] - jnp.where(stored, term, 0.0)
-
-
-def backward_step(height, parents, pattern, start, composed, pieces):
-    return pl.pallas_call(
-        functools.partial(backward_kernel, height, start.shape[0]),
-        out_shape=shape_of(*start.shape),
-        in_specs=[SMEM, SMEM] + [VMEM] * (3 + len(pieces)),
+        total = start[node] - jnp.where(stored, term, 0.0)
+        if earlier:
+            out[height, node] = total
+        else:
+            out[node] = total
+
+
+def backward_step(height, parents, pattern, start, composed, pieces, earlier):
+    out = ((1 + len(earlier),) if earlier else ()) + start.shape
+    return pl.pallas_call(
+        functools.partial(backward_kernel, height, start.shape[0], len(pieces)),
+        out_shape=shape_of(*out),
+        in_specs=[SMEM, SMEM] + [VMEM] * (3 + len(pieces) + len(earlier)),
         out_specs=VMEM,
         scratch_shapes=[pltpu.VMEM((len(pieces),) + start.shape, F32)],
         compiler_params=PARAMS,
         name="backward_level",
-    )(parents, pattern, start, *composed, *pieces)
+    )(parents, pattern, start, *composed, *pieces, *earlier)
 
 
 def groups_found(found, groups):
@@ -411,7 +420,7 @@
 
 
 def backward_out_kernel(nodes, gz_count, own, *refs):
-    parts, (out, columns, turned) = refs[:gz_count], refs[-3:]
+    parts, (out, columns, turned) = refs[:-3], refs[-3:]
     groups = COLUMNS // own
     per_tile = LANES // COLUMNS
     tiles = out.shape[1]
@@ -422,31 +431,29 @@
             values = groups_found([part[step, 0, node] for part in parts], groups)
             for which, value in enumerate(values):
                 index = which * row_count + (row ^ step)
-                columns[pl.ds(pl.multiple_of(index * few, few), few), :] = value
-        turned[...] = columns[...].T
-        rows = [turned[pl.ds(step, tiles, stride=per_tile), :] for step in range(per_tile)]
+                columns[node, pl.ds(pl.multiple_of(index * few, few), few), :] = value
+        turned[node] = columns[node].T
+        rows = [turned[node, pl.ds(step, tiles, stride=per_tile), :] for step in range(per_tile)]
         out[0, :, node, :] = jnp.concatenate(rows, axis=1)
 
 
-def backward_out(parts, before, first, own):
+def backward_out(parts, own):
     row_count, levels, nodes, few, rows = parts[0].shape
     tiles = rows * COLUMNS // LANES
-    ready = [before] if before is not None else []
+    part_spec = pl.BlockSpec((row_count, 1, nodes, few, rows), lambda i: (0, i, 0, 0, 0))
     return pl.pallas_call(
         functools.partial(backward_out_kernel, nodes, len(parts), own),
         grid=(levels,),
-        out_shape=shape_of(4, tiles, nodes, LANES),
-        in_specs=[
-            pl.BlockSpec((row_count, 1, nodes, few, rows), lambda i: (0, i, 0, 0, 0))
-            for part in parts
-        ]
-        + [HBM] * len(ready),
-        out_specs=pl.BlockSpec((1, tiles, nodes, LANES), lambda i: (first + i, 0, 0, 0)),
-        scratch_shapes=[pltpu.VMEM((COLUMNS, rows), F32), pltpu.VMEM((rows, COLUMNS), F32)],
-        input_output_aliases={len(parts): 0} if ready else {},
+        out_shape=shape_of(levels, tiles, nodes, LANES),
+        in_specs=[part_spec] * len(parts),
+        out_specs=pl.BlockSpec((1, tiles, nodes, LANES), lambda i: (i, 0, 0, 0)),
+        scratch_shapes=[
+            pltpu.VMEM((nodes, COLUMNS, rows), F32),
+            pltpu.VMEM((nodes, rows, COLUMNS), F32),
+        ],
         compiler_params=PARAMS,
         name="backward_out",
-    )(*parts, *ready)
+    )(*parts)
 
 
 def body(
@@ -478,7 +485,7 @@
         in_specs=[VMEM, VMEM],
         out_specs=[VMEM] * (3 + gz_count),
         scratch_shapes=[pltpu.VMEM((4, lanes // LANES, COLUMNS // own, part, LANES), F32)],
-        compiler_params=STREAM_PARAMS,
+        compiler_params=INPUT_PARAMS,
         name="input_parts",
     )(tiled(right_side), tiled(layer_sums[0]))
     kept, away = parts[:4], parts[4:]
@@ -524,17 +531,15 @@
             row_count,
         )
         whole = whole + [gather(backward[-1], "col")]
-        if height == 3:
-            early = gather(after(jnp.stack(backward), whole[-1][-1]), "row")
-        backward.append(backward_step(height, parents, pattern, start, composed, whole[-1]))
+        earlier = backward if height == 3 else []
+        results = backward_step(height, parents, pattern, start, composed, whole[-1], earlier)
+        backward.append(results)
 
     forward_parts = [piece for level in forward for piece in with_layers(level[0])]
     forward_all = forward_out(forward_parts, nodes, own, gz_count)
-    late = gather(backward[3][None], "row")
-    early = [after(piece, *late, forward_all) for piece in early]
-    early, late = with_layers(jnp.stack(early)), with_layers(jnp.stack(late))
-    backward_all = backward_out(early, None, 0, own)
-    backward_all = backward_out(late, backward_all, 3, own)
+    pieces = gather(backward[3], "row")
+    pieces[-1] = after(pieces[-1], forward_all)
+    backward_all = backward_out(with_layers(jnp.stack(pieces)), own)
     return tuple(
         value.transpose(0, 2, 1, 3).reshape(4, nodes, WIDTH * COLUMNS)
         for value in (forward_all, backward_all)

time: 130 us -> 123 us (0.946)
  waiting for transfers between devices: 17.5 us -> 12.5 us
  local copies, waits for them, and re-layouts: 4.04 us -> 1.01 us
    ppermute x43 -> x39, waiting for transfers between devices: 17.5 us -> 12.5 us  [swap(): lax.ppermute(value, axis, [(i, i ^ step) for i in range(lax.axis_size(axi...]
    unnamed x14, local copies, waits for them, and re-layouts: 3.06 us -> 0.04 us
    pallas_call x1, Pallas kernels: 1.07 us -> 2.89 us  [body(): pl.pallas_call(functools.partial(input_kernel, gz_count, nodes, own), out...]
    ppermute x43 -> x39, starting transfers between devices: 47.7 us -> 46.9 us  [swap(): lax.ppermute(value, axis, [(i, i ^ step) for i in range(lax.axis_size(axi...]
    pallas_call x2 -> x1, Pallas kernels: 3.38 us -> 2.77 us  [backward_out(): pl.pallas_call(functools.partial(backward_out_kernel, nodes, len(parts),...]
  transfers between devices with their start and end apart: 44 -> 40, of which waited for: 13 -> 12; matrix products, arithmetic and copies ran while one was open for 0% -> 1% of each run, Pallas kernels for 34% -> 33%
where the time goes in v8:
time: 123 us; the launch traced here: 122 us
  starting transfers between devices  47 us (38%)
  Pallas kernels  46.5 us (38%)
  between operations  14.4 us (12%)
  waiting for transfers between devices  12.5 us (10%)
    ppermute x39, starting transfers between devices, swap(): lax.ppermute(value, axis, [(i, i ^ step) for i in range(lax.axis_size(axi...  46.9 us
    ppermute x39, waiting for transfers between devices, swap(): lax.ppermute(value, axis, [(i, i ^ step) for i in range(lax.axis_size(axi...  12.5 us
    pallas_call x3, Pallas kernels, descend_step(): pl.pallas_call(functools.partial(descend_kernel, height, nodes, col_count...  11.9 us
    pallas_call x3, Pallas kernels, lower_step(): pl.pallas_call(functools.partial(lower_kernel, height), grid=(nodes,), ou...  8.71 us
    pallas_call x3, Pallas kernels, solve_step(): pl.pallas_call(functools.partial(solve_kernel, sizes), grid=(nodes,), out...  8.4 us
    pallas_call x3, Pallas kernels, forward_step(): pl.pallas_call(functools.partial(forward_kernel, height, sizes), out_shap...  3.14 us
    pallas_call x1, Pallas kernels, middle_step(): pl.pallas_call(middle_kernel, grid=(nodes,), out_shape=[out] * 4, in_spec...  2.98 us
    pallas_call x3, Pallas kernels, backward_step(): pl.pallas_call(functools.partial(backward_kernel, height, start.shape[0],...  2.9 us
  transfers between devices with their start and end apart: 40, of which 12 were waited for; matrix products, arithmetic and copies ran while one was open for 1% of the time, Pallas kernels for 33%

profile of v8, /device:TPU:0, one launch (start us, length us, event | category | flops | bytes accessed | tf_op | source)
XLA Modules:
  0.0 122.3 jit_solution(15892385125484883316)
XLA Ops:
  7.2 2.9 %input_parts.1 = (f32[64,128]{1,0:T(8,128)}, f32[64,128]{1,0:T(8,128)}, f32[64,128]{1,0:T(8,128)}, f32[64,128]{1,0:T(8,128)}, f32[4,64,128]{2,1,0:T(8,128)}) custom-call(f32[4,32,4,128]{3,2,1,0:T(4,128)} %bitcast.56, f32[4,32,4,128]{3,2,1,0:T(4,128)} %bitcast.57), custom_call_target="tpu_custom_call" | custom-call | tf_op jit(solution)/shard_map/input_parts/pallas_call | solution.py:482
  13.6 2.8 %collective-permute-start.1 = (f32[64,128]{1,0:T(8,128)S(1)}, f32[64,128]{1,0:T(8,128)S(1)}, u32[]{:S(2)}, u32[]{:S(2)}) collective-permute-start(f32[64,128]{1,0:T(8,128)S(1)} %bitcast_add_fusion.refs_0_), channel_id=1, source_target_pairs={{0,4},{4,0},{8,12},{12,8},{1,5},{5,1},{9,13},{13,9},{2,6},{6,2},{1... | collective-permute-start | bytes 98312 | tf_op jit(solution)/shard_map/ppermute | solution.py:63
  18.0 3.1 %lower_products.3 = (bf16[3,4,64,256]{3,2,1,0:T(8,128)(2,1)S(1)}, bf16[3,4,64,256]{3,2,1,0:T(8,128)(2,1)S(1)}) custom-call(f32[6,4,64,256]{3,2,1,0:T(8,128)} %blocks.5, f32[4,4,256,256]{3,2,1,0:T(8,128)} %lower.7), custom_call_target="tpu_custom_call" | custom-call | tf_op jit(solution)/shard_map/lower_products/pallas_call | solution.py:122
  24.0 3.7 %collective-permute-start.6 = (f32[64,128]{1,0:T(8,128)S(1)}, f32[64,128]{1,0:T(8,128)S(1)}, u32[]{:S(2)}, u32[]{:S(2)}) collective-permute-start(f32[64,128]{1,0:T(8,128)S(1)} %get-tuple-element.70), channel_id=1, source_target_pairs={{0,3},{1,2},{2,1},{3,0},{4,7},{5,6},{6,5},{7,4},{8,11},{9,10},{10,... | collective-permute-start | bytes 98312 | tf_op jit(solution)/shard_map/ppermute | solution.py:63
  28.4 2.8 %solve_level.3 = (f32[256,128]{1,0:T(8,128)S(1)}, f32[4,8,256]{2,1,0:T(8,128)S(1)}) custom-call(f32[256,128]{1,0:T(8,128)S(1)} %get-tuple-element.71.full, f32[4,4,256,256]{3,2,1,0:T(8,128)} %lower.7), custom_call_target="tpu_custom_call" | custom-call | tf_op jit(solution)/shard_map/solve_level/pallas_call | solution.py:271
  36.0 2.9 %lower_products.4 = (bf16[2,4,64,256]{3,2,1,0:T(8,128)(2,1)S(1)}, bf16[2,4,64,256]{3,2,1,0:T(8,128)(2,1)S(1)}) custom-call(f32[6,4,64,256]{3,2,1,0:T(8,128)} %blocks.5, f32[4,4,256,256]{3,2,1,0:T(8,128)} %lower.7), custom_call_target="tpu_custom_call" | custom-call | tf_op jit(solution)/shard_map/lower_products/pallas_call | solution.py:122
  40.3 2.5 %collective-permute-start.12 = (f32[64,128]{1,0:T(8,128)S(1)}, f32[64,128]{1,0:T(8,128)S(1)}, u32[]{:S(2)}, u32[]{:S(2)}) collective-permute-start(f32[64,128]{1,0:T(8,128)S(1)} %get-tuple-element.82), channel_id=1, source_target_pairs={{0,3},{1,2},{2,1},{3,0},{4,7},{5,6},{6,5},{7,4},{8,11},{9,10},{10,... | collective-permute-start | bytes 98312 | tf_op jit(solution)/shard_map/ppermute | solution.py:63
  42.7 2.0 %collective-permute-start.11 = (f32[64,128]{1,0:T(8,128)S(1)}, f32[64,128]{1,0:T(8,128)S(1)}, u32[]{:S(2)}, u32[]{:S(2)}) collective-permute-start(f32[64,128]{1,0:T(8,128)S(1)} %get-tuple-element.81), channel_id=1, source_target_pairs={{0,2},{1,3},{2,0},{3,1},{4,6},{5,7},{6,4},{7,5},{8,10},{9,11},{10,... | collective-permute-start | bytes 98312 | tf_op jit(solution)/shard_map/ppermute | solution.py:63
  44.7 2.8 %solve_level.4 = (f32[256,128]{1,0:T(8,128)S(1)}, f32[4,8,256]{2,1,0:T(8,128)S(1)}) custom-call(f32[256,128]{1,0:T(8,128)S(1)} %get-tuple-element.83.full, f32[4,4,256,256]{3,2,1,0:T(8,128)} %lower.7), custom_call_target="tpu_custom_call" | custom-call | tf_op jit(solution)/shard_map/solve_level/pallas_call | solution.py:271
  51.2 2.7 %lower_products.5 = (bf16[1,4,64,256]{3,2,1,0:T(8,128)(2,1)S(1)}, bf16[1,4,64,256]{3,2,1,0:T(8,128)(2,1)S(1)}) custom-call(f32[6,4,64,256]{3,2,1,0:T(8,128)S(1)} %copy-done.1, f32[4,4,256,256]{3,2,1,0:T(8,128)} %lower.7), custom_call_target="tpu_custom_call" | custom-call | tf_op jit(solution)/shard_map/lower_products/pallas_call | solution.py:122
  56.3 2.6 %collective-permute-start.18 = (f32[64,128]{1,0:T(8,128)S(1)}, f32[64,128]{1,0:T(8,128)S(1)}, u32[]{:S(2)}, u32[]{:S(2)}) collective-permute-start(f32[64,128]{1,0:T(8,128)S(1)} %get-tuple-element.93), channel_id=1, source_target_pairs={{0,3},{1,2},{2,1},{3,0},{4,7},{5,6},{6,5},{7,4},{8,11},{9,10},{10,... | collective-permute-start | bytes 98312 | tf_op jit(solution)/shard_map/ppermute | solution.py:63
  60.7 2.8 %solve_level.5 = (f32[256,128]{1,0:T(8,128)S(1)}, f32[4,8,256]{2,1,0:T(8,128)S(1)}) custom-call(f32[256,128]{1,0:T(8,128)S(1)} %get-tuple-element.94.full, f32[4,4,256,256]{3,2,1,0:T(8,128)} %lower.7), custom_call_target="tpu_custom_call" | custom-call | tf_op jit(solution)/shard_map/solve_level/pallas_call | solution.py:271
  67.8 3.0 %middle_product.1 = (bf16[4,256,256]{2,1,0:T(8,128)(2,1)S(1)}, bf16[4,256,256]{2,1,0:T(8,128)(2,1)S(1)}, bf16[4,256,256]{2,1,0:T(8,128)(2,1)S(1)}, bf16[4,256,256]{2,1,0:T(8,128)(2,1)S(1)}) custom-call(f32[4,4,256,256]{3,2,1,0:T(8,128)} %inverse.11, f32[4,4,256,256]{3,2,1,0:T(8,128)} %lower.7), custom_call_target="tpu_custom_call" | custom-call | tf_op jit(solution)/shard_map/middle_product/pallas_call | solution.py:145
  71.6 2.1 %collective-permute-start.26 = (f32[4,8,256]{2,1,0:T(8,128)S(1)}, f32[4,8,256]{2,1,0:T(8,128)S(1)}, u32[]{:S(2)}, u32[]{:S(2)}) collective-permute-start(f32[4,8,256]{2,1,0:T(8,128)S(1)} %get-tuple-element.103.refs_0_.refs_3_.refs_2_.refs_4_), channel_id=1, source_target_pairs={{0,1},{1,0},{2,3},{3,2},{4,5},{5,4},{6,7},{7,6},{8,9},{9,8},{10,11... | collective-permute-start | bytes 98312 | tf_op jit(solution)/shard_map/ppermute | solution.py:63
  76.1 3.2 %descend_level.3 = (f32[4,8,256]{2,1,0:T(8,128)S(1)}, bf16[4,256,256]{2,1,0:T(8,128)(2,1)S(1)}, bf16[4,256,256]{2,1,0:T(8,128)(2,1)S(1)}) custom-call(s32[3,16]{1,0:T(4,128)S(1)} %copy-done.2, s32[4,6]{1,0:T(4,128)S(1)} %bitcast.42, f32[4,8,256]{2,1,0:T(8,128)S(1)} %get-tuple-element.96.value, f32[4,4,256,256]{3,2,1,0:T(8,128)} %inverse.11, ...), custom_call_target="tpu_custom_call" | custom-call | tf_op jit(solution)/shard_map/descend_level/pallas_call | solution.py:323
  81.4 2.0 %collective-permute-start.30 = (f32[4,8,256]{2,1,0:T(8,128)S(1)}, f32[4,8,256]{2,1,0:T(8,128)S(1)}, u32[]{:S(2)}, u32[]{:S(2)}) collective-permute-start(f32[4,8,256]{2,1,0:T(8,128)S(1)} %backward_level.3.refs_7_.refs_0_.refs_5_), channel_id=1, source_target_pairs={{0,2},{1,3},{2,0},{3,1},{4,6},{5,7},{6,4},{7,5},{8,10},{9,11},{10,... | collective-permute-start | bytes 98312 | tf_op jit(solution)/shard_map/ppermute | solution.py:63
  83.4 2.4 %collective-permute-start.31 = (f32[4,8,256]{2,1,0:T(8,128)S(1)}, f32[4,8,256]{2,1,0:T(8,128)S(1)}, u32[]{:S(2)}, u32[]{:S(2)}) collective-permute-start(f32[4,8,256]{2,1,0:T(8,128)S(1)} %backward_level.3.refs_7_.refs_0_.refs_5_), channel_id=1, source_target_pairs={{0,3},{1,2},{2,1},{3,0},{4,7},{5,6},{6,5},{7,4},{8,11},{9,10},{10,... | collective-permute-start | bytes 98312 | tf_op jit(solution)/shard_map/ppermute | solution.py:63
  85.7 4.2 %descend_level.5 = (f32[4,8,256]{2,1,0:T(8,128)S(1)}, bf16[4,256,256]{2,1,0:T(8,128)(2,1)S(1)}, bf16[4,256,256]{2,1,0:T(8,128)(2,1)S(1)}) custom-call(s32[3,16]{1,0:T(4,128)S(1)} %copy-done.2, s32[4,6]{1,0:T(4,128)S(1)} %bitcast.44, f32[4,8,256]{2,1,0:T(8,128)S(1)} %get-tuple-element.85.value, f32[4,4,256,256]{3,2,1,0:T(8,128)} %inverse.11, ...), custom_call_target="tpu_custom_call" | custom-call | tf_op jit(solution)/shard_map/descend_level/pallas_call | solution.py:323
  90.9 2.1 %collective-permute-start.33 = (f32[4,8,256]{2,1,0:T(8,128)S(1)}, f32[4,8,256]{2,1,0:T(8,128)S(1)}, u32[]{:S(2)}, u32[]{:S(2)}) collective-permute-start(f32[4,8,256]{2,1,0:T(8,128)S(1)} %backward_level.4.refs_0_.refs_6_), channel_id=1, source_target_pairs={{0,2},{1,3},{2,0},{3,1},{4,6},{5,7},{6,4},{7,5},{8,10},{9,11},{10,... | collective-permute-start | bytes 98312 | tf_op jit(solution)/shard_map/ppermute | solution.py:63
  93.0 2.3 %collective-permute-start.34 = (f32[4,8,256]{2,1,0:T(8,128)S(1)}, f32[4,8,256]{2,1,0:T(8,128)S(1)}, u32[]{:S(2)}, u32[]{:S(2)}) collective-permute-start(f32[4,8,256]{2,1,0:T(8,128)S(1)} %backward_level.4.refs_0_.refs_6_), channel_id=1, source_target_pairs={{0,3},{1,2},{2,1},{3,0},{4,7},{5,6},{6,5},{7,4},{8,11},{9,10},{10,... | collective-permute-start | bytes 98312 | tf_op jit(solution)/shard_map/ppermute | solution.py:63
  95.3 4.6 %descend_level.4 = (f32[4,8,256]{2,1,0:T(8,128)S(1)}, bf16[4,256,256]{2,1,0:T(8,128)(2,1)S(1)}, bf16[4,256,256]{2,1,0:T(8,128)(2,1)S(1)}) custom-call(s32[3,16]{1,0:T(4,128)S(1)} %copy-done.2, s32[4,6]{1,0:T(4,128)S(1)} %bitcast.46, f32[4,8,256]{2,1,0:T(8,128)S(1)} %get-tuple-element.73.value, f32[4,4,256,256]{3,2,1,0:T(8,128)} %inverse.11, ...), custom_call_target="tpu_custom_call" | custom-call | tf_op jit(solution)/shard_map/descend_level/pallas_call | solution.py:323
  104.9 2.1 %forward_out.1 = f32[4,128,4,128]{3,2,1,0:T(4,128)} custom-call(f32[256,128]{1,0:T(8,128)S(1)} %get-tuple-element.102.refs_0_, f32[256,128]{1,0:T(8,128)S(1)} %collective-permute-done.22.refs_1_, f32[256,128]{1,0:T(8,128)S(1)} %get-tuple-element.95.refs_2_, f32[256,128]{1,0:T(8,128)S(1)} %collective-permute-done.23.refs_3_, ...), custom_call_target="tpu_custom_call" | custom-call | tf_op jit(solution)/shard_map/forward_out/pallas_call | solution.py:411
  110.8 1.9 %collective-permute-done.38.refs_1_ = f32[4,4,4,8,256]{4,3,2,1,0:T(8,128)S(1)} collective-permute-done((f32[4,4,4,8,256]{4,3,2,1,0:T(8,128)S(1)}, f32[4,4,4,8,256]{4,3,2,1,0:T(8,128)S(1)}, u32[]{:S(2)}, u32[]{:S(2)}) %collective-permute-start.38) | collective-permute-done | bytes 524320 | tf_op jit(solution)/shard_map/ppermute | solution.py:63
  112.7 2.8 %backward_out.1 = f32[4,128,4,128]{3,2,1,0:T(4,128)} custom-call(f32[4,4,4,8,256]{4,3,2,1,0:T(8,128)S(1)} %pad_maximum_fusion.refs_0_, f32[4,4,4,8,256]{4,3,2,1,0:T(8,128)S(1)} %collective-permute-done.38.refs_1_), custom_call_target="tpu_custom_call" | custom-call | tf_op jit(solution)/shard_map/backward_out/pallas_call | solution.py:444
  (97 shorter events, 41.9 us)
Async XLA Ops:
  7.2 68.9 %all-gather.3.cloned.1.call-start = ((), (), s32[]{:S(2)}) async-start(), calls=%async_computation | async-start | bytes 7077888 | tf_op jit(solution)/shard_map/all_gather | solution.py:495
  13.6 7.5 %collective-permute-start.1 = (f32[64,128]{1,0:T(8,128)S(1)}, f32[64,128]{1,0:T(8,128)S(1)}, u32[]{:S(2)}, u32[]{:S(2)}) collective-permute-start(f32[64,128]{1,0:T(8,128)S(1)} %bitcast_add_fusion.refs_0_), channel_id=1, source_target_pairs={{0,4},{4,0},{8,12},{12,8},{1,5},{5,1},{9,13},{13,9},{2,6},{6,2},{1... | collective-permute-start | bytes 98312 | tf_op jit(solution)/shard_map/ppermute | solution.py:63
  24.0 7.2 %collective-permute-start.6 = (f32[64,128]{1,0:T(8,128)S(1)}, f32[64,128]{1,0:T(8,128)S(1)}, u32[]{:S(2)}, u32[]{:S(2)}) collective-permute-start(f32[64,128]{1,0:T(8,128)S(1)} %get-tuple-element.70), channel_id=1, source_target_pairs={{0,3},{1,2},{2,1},{3,0},{4,7},{5,6},{6,5},{7,4},{8,11},{9,10},{10,... | collective-permute-start | bytes 98312 | tf_op jit(solution)/shard_map/ppermute | solution.py:63
  32.5 6.5 %collective-permute-start.7 = (f32[64,128]{1,0:T(8,128)S(1)}, f32[64,128]{1,0:T(8,128)S(1)}, u32[]{:S(2)}, u32[]{:S(2)}) collective-permute-start(f32[64,128]{1,0:T(8,128)S(1)} %fusion.1.refs_0_), channel_id=1, source_target_pairs={{0,4},{4,0},{8,12},{12,8},{1,5},{5,1},{9,13},{13,9},{2,6},{6,2},{1... | collective-permute-start | bytes 98312 | tf_op jit(solution)/shard_map/ppermute | solution.py:63
  33.1 5.9 %collective-permute-start.8 = (f32[64,128]{1,0:T(8,128)S(1)}, f32[64,128]{1,0:T(8,128)S(1)}, u32[]{:S(2)}, u32[]{:S(2)}) collective-permute-start(f32[64,128]{1,0:T(8,128)S(1)} %fusion.1.refs_0_), channel_id=1, source_target_pairs={{0,8},{4,12},{8,0},{12,4},{1,9},{5,13},{9,1},{13,5},{2,10},{6,14},... | collective-permute-start | bytes 98312 | tf_op jit(solution)/shard_map/ppermute | solution.py:63
  40.3 7.3 %collective-permute-start.12 = (f32[64,128]{1,0:T(8,128)S(1)}, f32[64,128]{1,0:T(8,128)S(1)}, u32[]{:S(2)}, u32[]{:S(2)}) collective-permute-start(f32[64,128]{1,0:T(8,128)S(1)} %get-tuple-element.82), channel_id=1, source_target_pairs={{0,3},{1,2},{2,1},{3,0},{4,7},{5,6},{6,5},{7,4},{8,11},{9,10},{10,... | collective-permute-start | bytes 98312 | tf_op jit(solution)/shard_map/ppermute | solution.py:63
  47.6 6.2 %collective-permute-start.13 = (f32[64,128]{1,0:T(8,128)S(1)}, f32[64,128]{1,0:T(8,128)S(1)}, u32[]{:S(2)}, u32[]{:S(2)}) collective-permute-start(f32[64,128]{1,0:T(8,128)S(1)} %fusion.3.refs_0_), channel_id=1, source_target_pairs={{0,4},{4,0},{8,12},{12,8},{1,5},{5,1},{9,13},{13,9},{2,6},{6,2},{1... | collective-permute-start | bytes 98312 | tf_op jit(solution)/shard_map/ppermute | solution.py:63
  56.3 7.2 %collective-permute-start.18 = (f32[64,128]{1,0:T(8,128)S(1)}, f32[64,128]{1,0:T(8,128)S(1)}, u32[]{:S(2)}, u32[]{:S(2)}) collective-permute-start(f32[64,128]{1,0:T(8,128)S(1)} %get-tuple-element.93), channel_id=1, source_target_pairs={{0,3},{1,2},{2,1},{3,0},{4,7},{5,6},{6,5},{7,4},{8,11},{9,10},{10,... | collective-permute-start | bytes 98312 | tf_op jit(solution)/shard_map/ppermute | solution.py:63
  63.7 7.1 %collective-permute-start.19 = (f32[64,128]{1,0:T(8,128)S(1)}, f32[64,128]{1,0:T(8,128)S(1)}, u32[]{:S(2)}, u32[]{:S(2)}) collective-permute-start(f32[64,128]{1,0:T(8,128)S(1)} %fusion.5.refs_0_), channel_id=1, source_target_pairs={{0,4},{4,0},{8,12},{12,8},{1,5},{5,1},{9,13},{13,9},{2,6},{6,2},{1... | collective-permute-start | bytes 98312 | tf_op jit(solution)/shard_map/ppermute | solution.py:63
  64.3 6.5 %collective-permute-start.20 = (f32[64,128]{1,0:T(8,128)S(1)}, f32[64,128]{1,0:T(8,128)S(1)}, u32[]{:S(2)}, u32[]{:S(2)}) collective-permute-start(f32[64,128]{1,0:T(8,128)S(1)} %fusion.5.refs_0_), channel_id=1, source_target_pairs={{0,8},{4,12},{8,0},{12,4},{1,9},{5,13},{9,1},{13,5},{2,10},{6,14},... | collective-permute-start | bytes 98312 | tf_op jit(solution)/shard_map/ppermute | solution.py:63
  67.3 35.4 %collective-permute-start.25 = (f32[256,128]{1,0:T(8,128)S(1)}, f32[256,128]{1,0:T(8,128)S(1)}, u32[]{:S(2)}, u32[]{:S(2)}) collective-permute-start(f32[256,128]{1,0:T(8,128)S(1)} %get-tuple-element.72.refs_6_), channel_id=1, source_target_pairs={{0,16},{16,0},{1,17},{17,1},{2,18},{18,2},{3,19},{19,3},{4,20},{20... | collective-permute-start | bytes 393224 | tf_op jit(solution)/shard_map/ppermute | solution.py:63
  67.3 36.1 %collective-permute-start.24 = (f32[256,128]{1,0:T(8,128)S(1)}, f32[256,128]{1,0:T(8,128)S(1)}, u32[]{:S(2)}, u32[]{:S(2)}) collective-permute-start(f32[256,128]{1,0:T(8,128)S(1)} %get-tuple-element.84.refs_4_), channel_id=1, source_target_pairs={{0,16},{16,0},{1,17},{17,1},{2,18},{18,2},{3,19},{19,3},{4,20},{20... | collective-permute-start | bytes 393224 | tf_op jit(solution)/shard_map/ppermute | solution.py:63
  71.6 7.7 %collective-permute-start.26 = (f32[4,8,256]{2,1,0:T(8,128)S(1)}, f32[4,8,256]{2,1,0:T(8,128)S(1)}, u32[]{:S(2)}, u32[]{:S(2)}) collective-permute-start(f32[4,8,256]{2,1,0:T(8,128)S(1)} %get-tuple-element.103.refs_0_.refs_3_.refs_2_.refs_4_), channel_id=1, source_target_pairs={{0,1},{1,0},{2,3},{3,2},{4,5},{5,4},{6,7},{7,6},{8,9},{9,8},{10,11... | collective-permute-start | bytes 98312 | tf_op jit(solution)/shard_map/ppermute | solution.py:63
  73.6 5.6 %collective-permute-start.27 = (f32[4,8,256]{2,1,0:T(8,128)S(1)}, f32[4,8,256]{2,1,0:T(8,128)S(1)}, u32[]{:S(2)}, u32[]{:S(2)}) collective-permute-start(f32[4,8,256]{2,1,0:T(8,128)S(1)} %get-tuple-element.103.refs_0_.refs_3_.refs_2_.refs_4_), channel_id=1, source_target_pairs={{0,2},{1,3},{2,0},{3,1},{4,6},{5,7},{6,4},{7,5},{8,10},{9,11},{10,... | collective-permute-start | bytes 98312 | tf_op jit(solution)/shard_map/ppermute | solution.py:63
  74.6 5.7 %collective-permute-start.28 = (f32[4,8,256]{2,1,0:T(8,128)S(1)}, f32[4,8,256]{2,1,0:T(8,128)S(1)}, u32[]{:S(2)}, u32[]{:S(2)}) collective-permute-start(f32[4,8,256]{2,1,0:T(8,128)S(1)} %get-tuple-element.103.refs_0_.refs_3_.refs_2_.refs_4_), channel_id=1, source_target_pairs={{0,3},{1,2},{2,1},{3,0},{4,7},{5,6},{6,5},{7,4},{8,11},{9,10},{10,... | collective-permute-start | bytes 98312 | tf_op jit(solution)/shard_map/ppermute | solution.py:63
  81.3 8.6 %collective-permute-start.29 = (f32[4,8,256]{2,1,0:T(8,128)S(1)}, f32[4,8,256]{2,1,0:T(8,128)S(1)}, u32[]{:S(2)}, u32[]{:S(2)}) collective-permute-start(f32[4,8,256]{2,1,0:T(8,128)S(1)} %backward_level.3.refs_7_.refs_0_.refs_5_), channel_id=1, source_target_pairs={{0,1},{1,0},{2,3},{3,2},{4,5},{5,4},{6,7},{7,6},{8,9},{9,8},{10,11... | collective-permute-start | bytes 98312 | tf_op jit(solution)/shard_map/ppermute | solution.py:63
  81.4 8.5 %collective-permute-start.30 = (f32[4,8,256]{2,1,0:T(8,128)S(1)}, f32[4,8,256]{2,1,0:T(8,128)S(1)}, u32[]{:S(2)}, u32[]{:S(2)}) collective-permute-start(f32[4,8,256]{2,1,0:T(8,128)S(1)} %backward_level.3.refs_7_.refs_0_.refs_5_), channel_id=1, source_target_pairs={{0,2},{1,3},{2,0},{3,1},{4,6},{5,7},{6,4},{7,5},{8,10},{9,11},{10,... | collective-permute-start | bytes 98312 | tf_op jit(solution)/shard_map/ppermute | solution.py:63
  83.4 6.5 %collective-permute-start.31 = (f32[4,8,256]{2,1,0:T(8,128)S(1)}, f32[4,8,256]{2,1,0:T(8,128)S(1)}, u32[]{:S(2)}, u32[]{:S(2)}) collective-permute-start(f32[4,8,256]{2,1,0:T(8,128)S(1)} %backward_level.3.refs_7_.refs_0_.refs_5_), channel_id=1, source_target_pairs={{0,3},{1,2},{2,1},{3,0},{4,7},{5,6},{6,5},{7,4},{8,11},{9,10},{10,... | collective-permute-start | bytes 98312 | tf_op jit(solution)/shard_map/ppermute | solution.py:63
  90.9 9.0 %collective-permute-start.32 = (f32[4,8,256]{2,1,0:T(8,128)S(1)}, f32[4,8,256]{2,1,0:T(8,128)S(1)}, u32[]{:S(2)}, u32[]{:S(2)}) collective-permute-start(f32[4,8,256]{2,1,0:T(8,128)S(1)} %backward_level.4.refs_0_.refs_6_), channel_id=1, source_target_pairs={{0,1},{1,0},{2,3},{3,2},{4,5},{5,4},{6,7},{7,6},{8,9},{9,8},{10,11... | collective-permute-start | bytes 98312 | tf_op jit(solution)/shard_map/ppermute | solution.py:63
  90.9 9.0 %collective-permute-start.33 = (f32[4,8,256]{2,1,0:T(8,128)S(1)}, f32[4,8,256]{2,1,0:T(8,128)S(1)}, u32[]{:S(2)}, u32[]{:S(2)}) collective-permute-start(f32[4,8,256]{2,1,0:T(8,128)S(1)} %backward_level.4.refs_0_.refs_6_), channel_id=1, source_target_pairs={{0,2},{1,3},{2,0},{3,1},{4,6},{5,7},{6,4},{7,5},{8,10},{9,11},{10,... | collective-permute-start | bytes 98312 | tf_op jit(solution)/shard_map/ppermute | solution.py:63
  93.0 7.5 %collective-permute-start.34 = (f32[4,8,256]{2,1,0:T(8,128)S(1)}, f32[4,8,256]{2,1,0:T(8,128)S(1)}, u32[]{:S(2)}, u32[]{:S(2)}) collective-permute-start(f32[4,8,256]{2,1,0:T(8,128)S(1)} %backward_level.4.refs_0_.refs_6_), channel_id=1, source_target_pairs={{0,3},{1,2},{2,1},{3,0},{4,7},{5,6},{6,5},{7,4},{8,11},{9,10},{10,... | collective-permute-start | bytes 98312 | tf_op jit(solution)/shard_map/ppermute | solution.py:63
  101.4 7.3 %collective-permute-start.37 = (f32[4,4,8,256]{3,2,1,0:T(8,128)S(1)}, f32[4,4,8,256]{3,2,1,0:T(8,128)S(1)}, u32[]{:S(2)}, u32[]{:S(2)}) collective-permute-start(f32[4,4,8,256]{3,2,1,0:T(8,128)S(1)} %backward_level.5), channel_id=1, source_target_pairs={{0,12},{4,8},{8,4},{12,0},{1,13},{5,9},{9,5},{13,1},{2,14},{6,10},... | collective-permute-start | bytes 393224 | tf_op jit(solution)/shard_map/ppermute | solution.py:63
  102.7 7.0 %collective-permute-start.35 = (f32[4,4,8,256]{3,2,1,0:T(8,128)S(1)}, f32[4,4,8,256]{3,2,1,0:T(8,128)S(1)}, u32[]{:S(2)}, u32[]{:S(2)}) collective-permute-start(f32[4,4,8,256]{3,2,1,0:T(8,128)S(1)} %backward_level.5), channel_id=1, source_target_pairs={{0,4},{4,0},{8,12},{12,8},{1,5},{5,1},{9,13},{13,9},{2,6},{6,2},{1... | collective-permute-start | bytes 393224 | tf_op jit(solution)/shard_map/ppermute | solution.py:63
  103.4 7.2 %collective-permute-start.36 = (f32[4,4,8,256]{3,2,1,0:T(8,128)S(1)}, f32[4,4,8,256]{3,2,1,0:T(8,128)S(1)}, u32[]{:S(2)}, u32[]{:S(2)}) collective-permute-start(f32[4,4,8,256]{3,2,1,0:T(8,128)S(1)} %backward_level.5), channel_id=1, source_target_pairs={{0,8},{4,12},{8,0},{12,4},{1,9},{5,13},{9,1},{13,5},{2,10},{6,14},... | collective-permute-start | bytes 393224 | tf_op jit(solution)/shard_map/ppermute | solution.py:63
  (23 other events, 169.2 us)
Sparse Core Ops, SparseCore 0:
  11.3 49.9 all-gather.2

commit v9 on v8

--- a/solution.py
+++ b/solution.py
@@ -16,9 +16,12 @@
 VMEM = pl.BlockSpec(memory_space=pltpu.VMEM)
 HBM = pl.BlockSpec(memory_space=pltpu.HBM)
 PARAMS = pltpu.CompilerParams(vmem_limit_bytes=16 * 2**20)
-INPUT_PARAMS = pltpu.CompilerParams(vmem_limit_bytes=54 * 2**20)
+INPUT_PARAMS = pltpu.CompilerParams(vmem_limit_bytes=53 * 2**20)
 MIDDLE_PARAMS = pltpu.CompilerParams(vmem_limit_bytes=51 * 2**20)
 STREAM_PARAMS = pltpu.CompilerParams(vmem_limit_bytes=52 * 2**20)
+
+
+STEP = 2
 
 
 def place_of(height, distance):
@@ -111,9 +114,10 @@
 def lower_kernel(height, blocks, inverse, high_out, low_out):
     first = place_of(height, 1)
     part, width = blocks.shape[2:]
-    left = blocks[first : first + height, 0].reshape(height * part, width)
-    whole = product(split(left), split(inverse[0, 0])).reshape(height, part, width)
-    high_out[:, 0], low_out[:, 0] = split(whole)
+    for node in range(blocks.shape[1]):
+        left = blocks[first : first + height, node].reshape(height * part, width)
+        whole = product(split(left), split(inverse[0, node])).reshape(height, part, width)
+        high_out[:, node], low_out[:, node] = split(whole)
 
 
 def lower_step(height, blocks, inverse):
@@ -121,22 +125,23 @@
     out = shape_of(height, nodes, part, WIDTH, dtype=BF16)
     return pl.pallas_call(
         functools.partial(lower_kernel, height),
-        grid=(nodes,),
+        grid=(nodes // STEP,),
         out_shape=[out, out],
         in_specs=[
-            pl.BlockSpec((pairs, 1, part, WIDTH), lambda i: (0, i, 0, 0)),
-            pl.BlockSpec((1, 1, WIDTH, WIDTH), lambda i: (height, i, 0, 0)),
+            pl.BlockSpec((pairs, STEP, part, WIDTH), lambda i: (0, i, 0, 0)),
+            pl.BlockSpec((1, STEP, WIDTH, WIDTH), lambda i: (height, i, 0, 0)),
         ],
-        out_specs=[pl.BlockSpec((height, 1, part, WIDTH), lambda i: (0, i, 0, 0))] * 2,
+        out_specs=[pl.BlockSpec((height, STEP, part, WIDTH), lambda i: (0, i, 0, 0))] * 2,
         compiler_params=STREAM_PARAMS,
         name="lower_products",
     )(blocks, inverse)
 
 
 def middle_kernel(upper, lower, high_out, low_out, lower_high, lower_low):
-    right = split(lower[0, 0])
-    lower_high[0], lower_low[0] = right
-    high_out[0], low_out[0] = split(product(split(upper[0, 0]), right))
+    for node in range(STEP):
+        right = split(lower[0, node])
+        lower_high[node], lower_low[node] = right
+        high_out[node], low_out[node] = split(product(split(upper[0, node]), right))
 
 
 def middle_step(upper, lower):
@@ -144,10 +149,10 @@
     out = shape_of(nodes, WIDTH, WIDTH, dtype=BF16)
     return pl.pallas_call(
         middle_kernel,
-        grid=(nodes,),
+        grid=(nodes // STEP,),
         out_shape=[out] * 4,
-        in_specs=[pl.BlockSpec((1, 1, WIDTH, WIDTH), lambda i: (0, i, 0, 0))] * 2,
-        out_specs=[pl.BlockSpec((1, WIDTH, WIDTH), lambda i: (i, 0, 0))] * 4,
+        in_specs=[pl.BlockSpec((1, STEP, WIDTH, WIDTH), lambda i: (0, i, 0, 0))] * 2,
+        out_specs=[pl.BlockSpec((STEP, WIDTH, WIDTH), lambda i: (i, 0, 0))] * 4,
         compiler_params=MIDDLE_PARAMS,
         name="middle_product",
     )(upper, lower)
@@ -178,6 +183,8 @@
         target = urgent if level == height - 1 else pending_out[level]
         target[...] = pending_in[level][...] if pending_in else jnp.zeros(target.shape, F32)
         targets.append(target)
+    rows = height * nodes * part
+    whole = product((m_high[...].reshape(rows, WIDTH), m_low[...].reshape(rows, WIDTH)), right)
     for node in range(nodes):
         ancestor = col * nodes + node
         for distance in range(1, height + 1):
@@ -185,7 +192,8 @@
             ancestor = parents[level, ancestor]
             slot = lax.rem(ancestor, nodes)
             where = lax.div(ancestor, nodes) ^ col
-            term = product((m_high[distance - 1, node], m_low[distance - 1, node]), right)
+            start = ((distance - 1) * nodes + node) * part
+            term = whole[start : start + part]
             term = pltpu.roll(term, lax.rem(slot - node + nodes, nodes) * own, 1)
             stored = jnp.where(pattern[node, place_of(height, distance)] != 0, slot, -1)
             targets[level][where] += jnp.where(lane == stored, term, 0.0)
@@ -227,10 +235,12 @@
         left = split(own_rows(turned, node, own, row_count))
         out[node] = product_t(left, (z_high[node], z_low[node]))
     lane = lax.broadcasted_iota(jnp.int32, (1, nodes * own), 1) // own
-    right = split(full[...])
-    solved = jnp.zeros(full.shape, F32)
-    for node in range(nodes):
-        solved = jnp.where(lane == node, product((lower_high[node], lower_low[node]), right), solved)
+    rows = nodes * WIDTH
+    left = (lower_high[...].reshape(rows, WIDTH), lower_low[...].reshape(rows, WIDTH))
+    whole = product(left, split(full[...]))
+    solved = whole[:WIDTH]
+    for node in range(1, nodes):
+        solved = jnp.where(lane == node, whole[node * WIDTH : (node + 1) * WIDTH], solved)
     solved_out[...] = solved
 
 
@@ -250,17 +260,23 @@
 
 def solve_kernel(sizes, full, lower, out, own_out, turned):
     nodes, part, own, row_count, col_count = sizes
-    node = pl.program_id(0)
+    first = pl.program_id(0) * STEP
     lane = lax.broadcasted_iota(jnp.int32, (1, nodes * own), 1) // own
 
-    @pl.when(node == 0)
+    @pl.when(first == 0)
     def _():
         turned[...] = full[...].T
         out[...] = jnp.zeros(out.shape, F32)
 
-    inverse = split(lower[0, 0])
-    out[...] = jnp.where(lane == node, product(inverse, split(full[...])), out[...])
-    own_out[0] = product_t(split(own_rows(turned, node, own, row_count)), inverse)
+    high, low = split(lower[0].reshape(STEP * WIDTH, WIDTH))
+    whole = product((high, low), split(full[...]))
+    solved = out[...]
+    for step in range(STEP):
+        node, rows = first + step, slice(step * WIDTH, (step + 1) * WIDTH)
+        solved = jnp.where(lane == node, whole[rows], solved)
+        left = split(own_rows(turned, node, own, row_count))
+        own_out[step] = product_t(left, (high[rows], low[rows]))
+    out[...] = solved
 
 
 def solve_step(height, full, lower, sizes):
@@ -270,10 +286,10 @@
     whole = pl.BlockSpec((rows, lanes), lambda i: (0, 0))
     return pl.pallas_call(
         functools.partial(solve_kernel, sizes),
-        grid=(nodes,),
+        grid=(nodes // STEP,),
         out_shape=[shape_of(rows, lanes), shape_of(nodes, few, rows)],
-        in_specs=[whole, pl.BlockSpec((1, 1, rows, rows), lambda i: (height, i, 0, 0))],
-        out_specs=[whole, pl.BlockSpec((1, few, rows), lambda i: (i, 0, 0))],
+        in_specs=[whole, pl.BlockSpec((1, STEP, rows, rows), lambda i: (height, i, 0, 0))],
+        out_specs=[whole, pl.BlockSpec((STEP, few, rows), lambda i: (i, 0, 0))],
         scratch_shapes=[pltpu.VMEM((lanes, rows), F32)],
         compiler_params=STREAM_PARAMS,
         name="solve_level",
@@ -283,26 +299,27 @@
 def descend_kernel(height, nodes, col_count, parents, pattern, value, inverse, *refs):
     blocks, pieces, (out, high_out, low_out) = refs[:height], refs[height:-3], refs[-3:]
     col = lax.axis_index("col")
-    node = pl.program_id(0)
-    rest = value[0]
-    left = split(inverse[0, 0])
-    ancestor = parents[height - 1, col * nodes + node]
-    for distance in range(2, height + 1):
-        level = height - distance
-        ancestor = parents[level, ancestor]
-        where = lax.div(ancestor, nodes) ^ col
-        slot = lax.rem(ancestor, nodes)
-        chosen = pieces[level * col_count][slot]
-        for step in range(1, col_count):
-            piece = pieces[level * col_count + step][slot]
-            chosen = jnp.where(where == step, piece, chosen)
-        block = blocks[distance - 1][:, 0, 0].reshape(WIDTH, WIDTH)
-        term = product_t(split(chosen), split(block))
-        stored = pattern[node, place_of(height, distance)] != 0
-        rest = rest - jnp.where(stored, term, 0.0)
-    out[0] = product_t(split(rest), left)
-    nearest = blocks[0][:, 0, 0].reshape(WIDTH, WIDTH)
-    high_out[0], low_out[0] = split(product(left, split(nearest)))
+    for index in range(STEP):
+        node = pl.program_id(0) * STEP + index
+        rest = value[index]
+        left = split(inverse[0, index])
+        ancestor = parents[height - 1, col * nodes + node]
+        for distance in range(2, height + 1):
+            level = height - distance
+            ancestor = parents[level, ancestor]
+            where = lax.div(ancestor, nodes) ^ col
+            slot = lax.rem(ancestor, nodes)
+            chosen = pieces[level * col_count][slot]
+            for step in range(1, col_count):
+                piece = pieces[level * col_count + step][slot]
+                chosen = jnp.where(where == step, piece, chosen)
+            block = blocks[distance - 1][:, 0, index].reshape(WIDTH, WIDTH)
+            term = product_t(split(chosen), split(block))
+            stored = pattern[node, place_of(height, distance)] != 0
+            rest = rest - jnp.where(stored, term, 0.0)
+        nearest = blocks[0][:, 0, index].reshape(WIDTH, WIDTH)
+        high_out[index], low_out[index] = split(product(left, split(nearest)))
+        out[index] = product_t(split(rest), left)
 
 
 def descend_step(height, parents, pattern, value, gathered, inverse, solved, row_count):
@@ -314,21 +331,21 @@
     def block_spec(distance):
         place = place_of(height, distance)
         return pl.BlockSpec(
-            (row_count, 1, 1, part, WIDTH), lambda i: (place // per, place % per, i, 0, 0)
+            (row_count, 1, STEP, part, WIDTH), lambda i: (place // per, place % per, i, 0, 0)
         )
 
-    each = pl.BlockSpec((1, few, rows), lambda i: (i, 0, 0))
+    each = pl.BlockSpec((STEP, few, rows), lambda i: (i, 0, 0))
     whole = pl.BlockSpec((nodes, few, rows), lambda i: (0, 0, 0))
     matrix = shape_of(nodes, WIDTH, WIDTH, dtype=BF16)
     return pl.pallas_call(
         functools.partial(descend_kernel, height, nodes, col_count),
-        grid=(nodes,),
+        grid=(nodes // STEP,),
         out_shape=[shape_of(nodes, few, rows), matrix, matrix],
         in_specs=[SMEM, SMEM, each]
-        + [pl.BlockSpec((1, 1, WIDTH, WIDTH), lambda i: (height, i, 0, 0))]
+        + [pl.BlockSpec((1, STEP, WIDTH, WIDTH), lambda i: (height, i, 0, 0))]
         + [block_spec(distance) for distance in range(1, height + 1)]
         + [whole] * len(pieces),
-        out_specs=[each] + [pl.BlockSpec((1, WIDTH, WIDTH), lambda i: (i, 0, 0))] * 2,
+        out_specs=[each] + [pl.BlockSpec((STEP, WIDTH, WIDTH), lambda i: (i, 0, 0))] * 2,
         compiler_params=STREAM_PARAMS,
         name="descend_level",
     )(parents, pattern, value, inverse, *([gathered] * height), *pieces)

time: 123 us -> 118 us (0.959)
  Pallas kernels: 46.5 us -> 34 us
  waiting for transfers between devices: 12.5 us -> 19.6 us
  local copies, waits for them, and re-layouts: 1.01 us -> 3 us
    ppermute x39, waiting for transfers between devices: 12.5 us -> 19.6 us  [swap(): lax.ppermute(value, axis, [(i, i ^ step) for i in range(lax.axis_size(axi...]
    pallas_call x7, Pallas kernels: 20.1 us -> 13.5 us  [the longest x3 5.77 us: lower_step(): pl.pallas_call(functools.partial(lower_kernel, height), grid=(nodes // ST...]
    pallas_call x3, Pallas kernels: 11.9 us -> 8.01 us  [descend_step(): pl.pallas_call(functools.partial(descend_kernel, height, nodes, col_count...]
    unnamed x14 -> x12, local copies, waits for them, and re-layouts: 0.04 us -> 2.03 us
    pallas_call x1, Pallas kernels: 2.89 us -> 1.07 us  [body(): pl.pallas_call(functools.partial(input_kernel, gz_count, nodes, own), out...]
  transfers between devices with their start and end apart: 40 -> 40, of which waited for: 12 -> 18; matrix products, arithmetic and copies ran while one was open for 1% -> 0% of each run, Pallas kernels for 33% -> 26%
where the time goes in v9:
time: 118 us
  starting transfers between devices  47 us (40%)
  Pallas kernels  34 us (29%)
  waiting for transfers between devices  19.6 us (17%)
  between operations  14.4 us (12%)
  local copies, waits for them, and re-layouts  3 us (3%)
    ppermute x39, starting transfers between devices, swap(): lax.ppermute(value, axis, [(i, i ^ step) for i in range(lax.axis_size(axi...  46.9 us
    ppermute x39, waiting for transfers between devices, swap(): lax.ppermute(value, axis, [(i, i ^ step) for i in range(lax.axis_size(axi...  19.6 us
    pallas_call x3, Pallas kernels, descend_step(): pl.pallas_call(functools.partial(descend_kernel, height, nodes, col_count...  8.01 us
    pallas_call x3, Pallas kernels, lower_step(): pl.pallas_call(functools.partial(lower_kernel, height), grid=(nodes // ST...  5.77 us
    pallas_call x3, Pallas kernels, solve_step(): pl.pallas_call(functools.partial(solve_kernel, sizes), grid=(nodes // STE...  5.72 us
    pallas_call x3, Pallas kernels, forward_step(): pl.pallas_call(functools.partial(forward_kernel, height, sizes), out_shap...  2.95 us
    pallas_call x3, Pallas kernels, backward_step(): pl.pallas_call(functools.partial(backward_kernel, height, start.shape[0],...  2.9 us
    pallas_call x1, Pallas kernels, backward_out(): pl.pallas_call(functools.partial(backward_out_kernel, nodes, len(parts),...  2.77 us
  transfers between devices with their start and end apart: 40, of which 18 were waited for; matrix products, arithmetic and copies ran while one was open for 0% of the time, Pallas kernels for 26%

profile of v9, /device:TPU:0, one launch (start us, length us, event | category | flops | bytes accessed | tf_op | source)
XLA Modules:
  0.0 118.1 jit_solution(90366358642289526)
XLA Ops:
  12.9 2.8 %collective-permute-start.1 = (f32[64,128]{1,0:T(8,128)S(1)}, f32[64,128]{1,0:T(8,128)S(1)}, u32[]{:S(2)}, u32[]{:S(2)}) collective-permute-start(f32[64,128]{1,0:T(8,128)S(1)} %bitcast_add_fusion.refs_0_), channel_id=1, source_target_pairs={{0,4},{4,0},{8,12},{12,8},{1,5},{5,1},{9,13},{13,9},{2,6},{6,2},{1... | collective-permute-start | bytes 98312 | tf_op jit(solution)/shard_map/ppermute | solution.py:66
  17.2 2.1 %lower_products.3 = (bf16[3,4,64,256]{3,2,1,0:T(8,128)(2,1)S(1)}, bf16[3,4,64,256]{3,2,1,0:T(8,128)(2,1)S(1)}) custom-call(f32[6,4,64,256]{3,2,1,0:T(8,128)} %blocks.5, f32[4,4,256,256]{3,2,1,0:T(8,128)} %lower.7), custom_call_target="tpu_custom_call" | custom-call | tf_op jit(solution)/shard_map/lower_products/pallas_call | solution.py:126
  19.6 2.4 %collective-permute-done.3.refs_3_ = f32[64,128]{1,0:T(8,128)S(1)} collective-permute-done((f32[64,128]{1,0:T(8,128)S(1)}, f32[64,128]{1,0:T(8,128)S(1)}, u32[]{:S(2)}, u32[]{:S(2)}) %collective-permute-start.3) | collective-permute-done | bytes 32800 | tf_op jit(solution)/shard_map/ppermute | solution.py:66
  23.1 3.7 %collective-permute-start.6 = (f32[64,128]{1,0:T(8,128)S(1)}, f32[64,128]{1,0:T(8,128)S(1)}, u32[]{:S(2)}, u32[]{:S(2)}) collective-permute-start(f32[64,128]{1,0:T(8,128)S(1)} %get-tuple-element.70), channel_id=1, source_target_pairs={{0,3},{1,2},{2,1},{3,0},{4,7},{5,6},{6,5},{7,4},{8,11},{9,10},{10,... | collective-permute-start | bytes 98312 | tf_op jit(solution)/shard_map/ppermute | solution.py:66
  32.7 2.4 %collective-permute-start.9 = (f32[64,128]{1,0:T(8,128)S(1)}, f32[64,128]{1,0:T(8,128)S(1)}, u32[]{:S(2)}, u32[]{:S(2)}) collective-permute-start(f32[64,128]{1,0:T(8,128)S(1)} %fusion.1.refs_0_), channel_id=1, source_target_pairs={{0,12},{4,8},{8,4},{12,0},{1,13},{5,9},{9,5},{13,1},{2,14},{6,10},... | collective-permute-start | bytes 98312 | tf_op jit(solution)/shard_map/ppermute | solution.py:66
  35.2 2.0 %lower_products.4 = (bf16[2,4,64,256]{3,2,1,0:T(8,128)(2,1)S(1)}, bf16[2,4,64,256]{3,2,1,0:T(8,128)(2,1)S(1)}) custom-call(f32[6,4,64,256]{3,2,1,0:T(8,128)} %blocks.5, f32[4,4,256,256]{3,2,1,0:T(8,128)} %lower.7), custom_call_target="tpu_custom_call" | custom-call | tf_op jit(solution)/shard_map/lower_products/pallas_call | solution.py:126
  40.7 2.3 %collective-permute-start.11 = (f32[64,128]{1,0:T(8,128)S(1)}, f32[64,128]{1,0:T(8,128)S(1)}, u32[]{:S(2)}, u32[]{:S(2)}) collective-permute-start(f32[64,128]{1,0:T(8,128)S(1)} %get-tuple-element.81), channel_id=1, source_target_pairs={{0,2},{1,3},{2,0},{3,1},{4,6},{5,7},{6,4},{7,5},{8,10},{9,11},{10,... | collective-permute-start | bytes 98312 | tf_op jit(solution)/shard_map/ppermute | solution.py:66
  43.0 1.9 %solve_level.4 = (f32[256,128]{1,0:T(8,128)S(1)}, f32[4,8,256]{2,1,0:T(8,128)S(1)}) custom-call(f32[256,128]{1,0:T(8,128)S(1)} %get-tuple-element.83.full, f32[4,4,256,256]{3,2,1,0:T(8,128)} %lower.7), custom_call_target="tpu_custom_call" | custom-call | tf_op jit(solution)/shard_map/solve_level/pallas_call | solution.py:287
  51.7 2.4 %collective-permute-done.15.refs_3_ = f32[64,128]{1,0:T(8,128)S(1)} collective-permute-done((f32[64,128]{1,0:T(8,128)S(1)}, f32[64,128]{1,0:T(8,128)S(1)}, u32[]{:S(2)}, u32[]{:S(2)}) %collective-permute-start.15) | collective-permute-done | bytes 32800 | tf_op jit(solution)/shard_map/ppermute | solution.py:66
  55.0 2.9 %collective-permute-start.18 = (f32[64,128]{1,0:T(8,128)S(1)}, f32[64,128]{1,0:T(8,128)S(1)}, u32[]{:S(2)}, u32[]{:S(2)}) collective-permute-start(f32[64,128]{1,0:T(8,128)S(1)} %get-tuple-element.93), channel_id=1, source_target_pairs={{0,3},{1,2},{2,1},{3,0},{4,7},{5,6},{6,5},{7,4},{8,11},{9,10},{10,... | collective-permute-start | bytes 98312 | tf_op jit(solution)/shard_map/ppermute | solution.py:66
  59.5 1.9 %solve_level.5 = (f32[256,128]{1,0:T(8,128)S(1)}, f32[4,8,256]{2,1,0:T(8,128)S(1)}) custom-call(f32[256,128]{1,0:T(8,128)S(1)} %get-tuple-element.94.full, f32[4,4,256,256]{3,2,1,0:T(8,128)} %lower.7), custom_call_target="tpu_custom_call" | custom-call | tf_op jit(solution)/shard_map/solve_level/pallas_call | solution.py:287
  63.9 2.4 %collective-permute-start.21 = (f32[64,128]{1,0:T(8,128)S(1)}, f32[64,128]{1,0:T(8,128)S(1)}, u32[]{:S(2)}, u32[]{:S(2)}) collective-permute-start(f32[64,128]{1,0:T(8,128)S(1)} %fusion.5.refs_0_), channel_id=1, source_target_pairs={{0,12},{4,8},{8,4},{12,0},{1,13},{5,9},{9,5},{13,1},{2,14},{6,10},... | collective-permute-start | bytes 98312 | tf_op jit(solution)/shard_map/ppermute | solution.py:66
  66.8 2.0 %middle_product.1 = (bf16[4,256,256]{2,1,0:T(8,128)(2,1)S(1)}, bf16[4,256,256]{2,1,0:T(8,128)(2,1)S(1)}, bf16[4,256,256]{2,1,0:T(8,128)(2,1)S(1)}, bf16[4,256,256]{2,1,0:T(8,128)(2,1)S(1)}) custom-call(f32[4,4,256,256]{3,2,1,0:T(8,128)} %inverse.11, f32[4,4,256,256]{3,2,1,0:T(8,128)} %lower.7), custom_call_target="tpu_custom_call" | custom-call | tf_op jit(solution)/shard_map/middle_product/pallas_call | solution.py:150
  69.7 2.1 %collective-permute-start.26 = (f32[4,8,256]{2,1,0:T(8,128)S(1)}, f32[4,8,256]{2,1,0:T(8,128)S(1)}, u32[]{:S(2)}, u32[]{:S(2)}) collective-permute-start(f32[4,8,256]{2,1,0:T(8,128)S(1)} %get-tuple-element.103.refs_0_.refs_3_.refs_2_.refs_4_), channel_id=1, source_target_pairs={{0,1},{1,0},{2,3},{3,2},{4,5},{5,4},{6,7},{7,6},{8,9},{9,8},{10,11... | collective-permute-start | bytes 98312 | tf_op jit(solution)/shard_map/ppermute | solution.py:66
  72.1 2.1 %collective-permute-start.28 = (f32[4,8,256]{2,1,0:T(8,128)S(1)}, f32[4,8,256]{2,1,0:T(8,128)S(1)}, u32[]{:S(2)}, u32[]{:S(2)}) collective-permute-start(f32[4,8,256]{2,1,0:T(8,128)S(1)} %get-tuple-element.103.refs_0_.refs_3_.refs_2_.refs_4_), channel_id=1, source_target_pairs={{0,3},{1,2},{2,1},{3,0},{4,7},{5,6},{6,5},{7,4},{8,11},{9,10},{10,... | collective-permute-start | bytes 98312 | tf_op jit(solution)/shard_map/ppermute | solution.py:66
  74.2 2.2 %descend_level.3 = (f32[4,8,256]{2,1,0:T(8,128)S(1)}, bf16[4,256,256]{2,1,0:T(8,128)(2,1)S(1)}, bf16[4,256,256]{2,1,0:T(8,128)(2,1)S(1)}) custom-call(s32[3,16]{1,0:T(4,128)S(1)} %copy-done.4, s32[4,6]{1,0:T(4,128)S(1)} %bitcast.44, f32[4,8,256]{2,1,0:T(8,128)S(1)} %get-tuple-element.96.value, f32[4,4,256,256]{3,2,1,0:T(8,128)} %inverse.11, ...), custom_call_target="tpu_custom_call" | custom-call | tf_op jit(solution)/shard_map/descend_level/pallas_call | solution.py:340
  78.8 2.7 %collective-permute-start.30 = (f32[4,8,256]{2,1,0:T(8,128)S(1)}, f32[4,8,256]{2,1,0:T(8,128)S(1)}, u32[]{:S(2)}, u32[]{:S(2)}) collective-permute-start(f32[4,8,256]{2,1,0:T(8,128)S(1)} %backward_level.3.refs_7_.refs_0_.refs_5_), channel_id=1, source_target_pairs={{0,2},{1,3},{2,0},{3,1},{4,6},{5,7},{6,4},{7,5},{8,10},{9,11},{10,... | collective-permute-start | bytes 98312 | tf_op jit(solution)/shard_map/ppermute | solution.py:66
  83.2 2.7 %descend_level.5 = (f32[4,8,256]{2,1,0:T(8,128)S(1)}, bf16[4,256,256]{2,1,0:T(8,128)(2,1)S(1)}, bf16[4,256,256]{2,1,0:T(8,128)(2,1)S(1)}) custom-call(s32[3,16]{1,0:T(4,128)S(1)} %copy-done.4, s32[4,6]{1,0:T(4,128)S(1)} %bitcast.46, f32[4,8,256]{2,1,0:T(8,128)S(1)} %get-tuple-element.85.value, f32[4,4,256,256]{3,2,1,0:T(8,128)} %inverse.11, ...), custom_call_target="tpu_custom_call" | custom-call | tf_op jit(solution)/shard_map/descend_level/pallas_call | solution.py:340
  88.2 2.3 %collective-permute-start.33 = (f32[4,8,256]{2,1,0:T(8,128)S(1)}, f32[4,8,256]{2,1,0:T(8,128)S(1)}, u32[]{:S(2)}, u32[]{:S(2)}) collective-permute-start(f32[4,8,256]{2,1,0:T(8,128)S(1)} %backward_level.4.refs_0_.refs_6_), channel_id=1, source_target_pairs={{0,2},{1,3},{2,0},{3,1},{4,6},{5,7},{6,4},{7,5},{8,10},{9,11},{10,... | collective-permute-start | bytes 98312 | tf_op jit(solution)/shard_map/ppermute | solution.py:66
  90.5 2.1 %collective-permute-start.34 = (f32[4,8,256]{2,1,0:T(8,128)S(1)}, f32[4,8,256]{2,1,0:T(8,128)S(1)}, u32[]{:S(2)}, u32[]{:S(2)}) collective-permute-start(f32[4,8,256]{2,1,0:T(8,128)S(1)} %backward_level.4.refs_0_.refs_6_), channel_id=1, source_target_pairs={{0,3},{1,2},{2,1},{3,0},{4,7},{5,6},{6,5},{7,4},{8,11},{9,10},{10,... | collective-permute-start | bytes 98312 | tf_op jit(solution)/shard_map/ppermute | solution.py:66
  92.6 3.1 %descend_level.4 = (f32[4,8,256]{2,1,0:T(8,128)S(1)}, bf16[4,256,256]{2,1,0:T(8,128)(2,1)S(1)}, bf16[4,256,256]{2,1,0:T(8,128)(2,1)S(1)}) custom-call(s32[3,16]{1,0:T(4,128)S(1)} %copy-done.4, s32[4,6]{1,0:T(4,128)S(1)} %bitcast.48, f32[4,8,256]{2,1,0:T(8,128)S(1)} %get-tuple-element.73.value, f32[4,4,256,256]{3,2,1,0:T(8,128)} %inverse.11, ...), custom_call_target="tpu_custom_call" | custom-call | tf_op jit(solution)/shard_map/descend_level/pallas_call | solution.py:340
  97.2 2.3 %collective-permute-start.37 = (f32[4,4,8,256]{3,2,1,0:T(8,128)S(1)}, f32[4,4,8,256]{3,2,1,0:T(8,128)S(1)}, u32[]{:S(2)}, u32[]{:S(2)}) collective-permute-start(f32[4,4,8,256]{3,2,1,0:T(8,128)S(1)} %backward_level.5), channel_id=1, source_target_pairs={{0,12},{4,8},{8,4},{12,0},{1,13},{5,9},{9,5},{13,1},{2,14},{6,10},... | collective-permute-start | bytes 393224 | tf_op jit(solution)/shard_map/ppermute | solution.py:66
  100.8 2.1 %forward_out.1 = f32[4,128,4,128]{3,2,1,0:T(4,128)} custom-call(f32[256,128]{1,0:T(8,128)S(1)} %get-tuple-element.102.refs_0_, f32[256,128]{1,0:T(8,128)S(1)} %collective-permute-done.22.refs_1_, f32[256,128]{1,0:T(8,128)S(1)} %get-tuple-element.95.refs_2_, f32[256,128]{1,0:T(8,128)S(1)} %collective-permute-done.23.refs_3_, ...), custom_call_target="tpu_custom_call" | custom-call | tf_op jit(solution)/shard_map/forward_out/pallas_call | solution.py:428
  108.5 2.8 %backward_out.1 = f32[4,128,4,128]{3,2,1,0:T(4,128)} custom-call(f32[4,4,4,8,256]{4,3,2,1,0:T(8,128)S(1)} %pad_maximum_fusion.refs_0_, f32[4,4,4,8,256]{4,3,2,1,0:T(8,128)S(1)} %collective-permute-done.38.refs_1_), custom_call_target="tpu_custom_call" | custom-call | tf_op jit(solution)/shard_map/backward_out/pallas_call | solution.py:461
  (95 shorter events, 46.0 us)
Async XLA Ops:
  7.2 67.0 %all-gather.3.cloned.1.call-start = ((), (), s32[]{:S(2)}) async-start(), calls=%async_computation | async-start | bytes 7077888 | tf_op jit(solution)/shard_map/all_gather | solution.py:512
  12.9 6.5 %collective-permute-start.1 = (f32[64,128]{1,0:T(8,128)S(1)}, f32[64,128]{1,0:T(8,128)S(1)}, u32[]{:S(2)}, u32[]{:S(2)}) collective-permute-start(f32[64,128]{1,0:T(8,128)S(1)} %bitcast_add_fusion.refs_0_), channel_id=1, source_target_pairs={{0,4},{4,0},{8,12},{12,8},{1,5},{5,1},{9,13},{13,9},{2,6},{6,2},{1... | collective-permute-start | bytes 98312 | tf_op jit(solution)/shard_map/ppermute | solution.py:66
  23.1 6.4 %collective-permute-start.6 = (f32[64,128]{1,0:T(8,128)S(1)}, f32[64,128]{1,0:T(8,128)S(1)}, u32[]{:S(2)}, u32[]{:S(2)}) collective-permute-start(f32[64,128]{1,0:T(8,128)S(1)} %get-tuple-element.70), channel_id=1, source_target_pairs={{0,3},{1,2},{2,1},{3,0},{4,7},{5,6},{6,5},{7,4},{8,11},{9,10},{10,... | collective-permute-start | bytes 98312 | tf_op jit(solution)/shard_map/ppermute | solution.py:66
  31.6 5.6 %collective-permute-start.7 = (f32[64,128]{1,0:T(8,128)S(1)}, f32[64,128]{1,0:T(8,128)S(1)}, u32[]{:S(2)}, u32[]{:S(2)}) collective-permute-start(f32[64,128]{1,0:T(8,128)S(1)} %fusion.1.refs_0_), channel_id=1, source_target_pairs={{0,4},{4,0},{8,12},{12,8},{1,5},{5,1},{9,13},{13,9},{2,6},{6,2},{1... | collective-permute-start | bytes 98312 | tf_op jit(solution)/shard_map/ppermute | solution.py:66
  38.5 6.4 %collective-permute-start.12 = (f32[64,128]{1,0:T(8,128)S(1)}, f32[64,128]{1,0:T(8,128)S(1)}, u32[]{:S(2)}, u32[]{:S(2)}) collective-permute-start(f32[64,128]{1,0:T(8,128)S(1)} %get-tuple-element.82), channel_id=1, source_target_pairs={{0,3},{1,2},{2,1},{3,0},{4,7},{5,6},{6,5},{7,4},{8,11},{9,10},{10,... | collective-permute-start | bytes 98312 | tf_op jit(solution)/shard_map/ppermute | solution.py:66
  45.5 5.3 %collective-permute-start.13 = (f32[64,128]{1,0:T(8,128)S(1)}, f32[64,128]{1,0:T(8,128)S(1)}, u32[]{:S(2)}, u32[]{:S(2)}) collective-permute-start(f32[64,128]{1,0:T(8,128)S(1)} %fusion.3.refs_0_), channel_id=1, source_target_pairs={{0,4},{4,0},{8,12},{12,8},{1,5},{5,1},{9,13},{13,9},{2,6},{6,2},{1... | collective-permute-start | bytes 98312 | tf_op jit(solution)/shard_map/ppermute | solution.py:66
  48.6 5.5 %collective-permute-start.15 = (f32[64,128]{1,0:T(8,128)S(1)}, f32[64,128]{1,0:T(8,128)S(1)}, u32[]{:S(2)}, u32[]{:S(2)}) collective-permute-start(f32[64,128]{1,0:T(8,128)S(1)} %fusion.3.refs_0_), channel_id=1, source_target_pairs={{0,12},{4,8},{8,4},{12,0},{1,13},{5,9},{9,5},{13,1},{2,14},{6,10},... | collective-permute-start | bytes 98312 | tf_op jit(solution)/shard_map/ppermute | solution.py:66
  55.0 6.4 %collective-permute-start.18 = (f32[64,128]{1,0:T(8,128)S(1)}, f32[64,128]{1,0:T(8,128)S(1)}, u32[]{:S(2)}, u32[]{:S(2)}) collective-permute-start(f32[64,128]{1,0:T(8,128)S(1)} %get-tuple-element.93), channel_id=1, source_target_pairs={{0,3},{1,2},{2,1},{3,0},{4,7},{5,6},{6,5},{7,4},{8,11},{9,10},{10,... | collective-permute-start | bytes 98312 | tf_op jit(solution)/shard_map/ppermute | solution.py:66
  62.8 6.1 %collective-permute-start.19 = (f32[64,128]{1,0:T(8,128)S(1)}, f32[64,128]{1,0:T(8,128)S(1)}, u32[]{:S(2)}, u32[]{:S(2)}) collective-permute-start(f32[64,128]{1,0:T(8,128)S(1)} %fusion.5.refs_0_), channel_id=1, source_target_pairs={{0,4},{4,0},{8,12},{12,8},{1,5},{5,1},{9,13},{13,9},{2,6},{6,2},{1... | collective-permute-start | bytes 98312 | tf_op jit(solution)/shard_map/ppermute | solution.py:66
  63.4 5.5 %collective-permute-start.20 = (f32[64,128]{1,0:T(8,128)S(1)}, f32[64,128]{1,0:T(8,128)S(1)}, u32[]{:S(2)}, u32[]{:S(2)}) collective-permute-start(f32[64,128]{1,0:T(8,128)S(1)} %fusion.5.refs_0_), channel_id=1, source_target_pairs={{0,8},{4,12},{8,0},{12,4},{1,9},{5,13},{9,1},{13,5},{2,10},{6,14},... | collective-permute-start | bytes 98312 | tf_op jit(solution)/shard_map/ppermute | solution.py:66
  66.3 33.2 %collective-permute-start.25 = (f32[256,128]{1,0:T(8,128)S(1)}, f32[256,128]{1,0:T(8,128)S(1)}, u32[]{:S(2)}, u32[]{:S(2)}) collective-permute-start(f32[256,128]{1,0:T(8,128)S(1)} %get-tuple-element.72.refs_6_), channel_id=1, source_target_pairs={{0,16},{16,0},{1,17},{17,1},{2,18},{18,2},{3,19},{19,3},{4,20},{20... | collective-permute-start | bytes 393224 | tf_op jit(solution)/shard_map/ppermute | solution.py:66
  66.3 33.7 %collective-permute-start.24 = (f32[256,128]{1,0:T(8,128)S(1)}, f32[256,128]{1,0:T(8,128)S(1)}, u32[]{:S(2)}, u32[]{:S(2)}) collective-permute-start(f32[256,128]{1,0:T(8,128)S(1)} %get-tuple-element.84.refs_4_), channel_id=1, source_target_pairs={{0,16},{16,0},{1,17},{17,1},{2,18},{18,2},{3,19},{19,3},{4,20},{20... | collective-permute-start | bytes 393224 | tf_op jit(solution)/shard_map/ppermute | solution.py:66
  69.7 6.8 %collective-permute-start.26 = (f32[4,8,256]{2,1,0:T(8,128)S(1)}, f32[4,8,256]{2,1,0:T(8,128)S(1)}, u32[]{:S(2)}, u32[]{:S(2)}) collective-permute-start(f32[4,8,256]{2,1,0:T(8,128)S(1)} %get-tuple-element.103.refs_0_.refs_3_.refs_2_.refs_4_), channel_id=1, source_target_pairs={{0,1},{1,0},{2,3},{3,2},{4,5},{5,4},{6,7},{7,6},{8,9},{9,8},{10,11... | collective-permute-start | bytes 98312 | tf_op jit(solution)/shard_map/ppermute | solution.py:66
  71.8 5.1 %collective-permute-start.27 = (f32[4,8,256]{2,1,0:T(8,128)S(1)}, f32[4,8,256]{2,1,0:T(8,128)S(1)}, u32[]{:S(2)}, u32[]{:S(2)}) collective-permute-start(f32[4,8,256]{2,1,0:T(8,128)S(1)} %get-tuple-element.103.refs_0_.refs_3_.refs_2_.refs_4_), channel_id=1, source_target_pairs={{0,2},{1,3},{2,0},{3,1},{4,6},{5,7},{6,4},{7,5},{8,10},{9,11},{10,... | collective-permute-start | bytes 98312 | tf_op jit(solution)/shard_map/ppermute | solution.py:66
  72.1 5.7 %collective-permute-start.28 = (f32[4,8,256]{2,1,0:T(8,128)S(1)}, f32[4,8,256]{2,1,0:T(8,128)S(1)}, u32[]{:S(2)}, u32[]{:S(2)}) collective-permute-start(f32[4,8,256]{2,1,0:T(8,128)S(1)} %get-tuple-element.103.refs_0_.refs_3_.refs_2_.refs_4_), channel_id=1, source_target_pairs={{0,3},{1,2},{2,1},{3,0},{4,7},{5,6},{6,5},{7,4},{8,11},{9,10},{10,... | collective-permute-start | bytes 98312 | tf_op jit(solution)/shard_map/ppermute | solution.py:66
  78.8 7.1 %collective-permute-start.29 = (f32[4,8,256]{2,1,0:T(8,128)S(1)}, f32[4,8,256]{2,1,0:T(8,128)S(1)}, u32[]{:S(2)}, u32[]{:S(2)}) collective-permute-start(f32[4,8,256]{2,1,0:T(8,128)S(1)} %backward_level.3.refs_7_.refs_0_.refs_5_), channel_id=1, source_target_pairs={{0,1},{1,0},{2,3},{3,2},{4,5},{5,4},{6,7},{7,6},{8,9},{9,8},{10,11... | collective-permute-start | bytes 98312 | tf_op jit(solution)/shard_map/ppermute | solution.py:66
  78.8 7.1 %collective-permute-start.30 = (f32[4,8,256]{2,1,0:T(8,128)S(1)}, f32[4,8,256]{2,1,0:T(8,128)S(1)}, u32[]{:S(2)}, u32[]{:S(2)}) collective-permute-start(f32[4,8,256]{2,1,0:T(8,128)S(1)} %backward_level.3.refs_7_.refs_0_.refs_5_), channel_id=1, source_target_pairs={{0,2},{1,3},{2,0},{3,1},{4,6},{5,7},{6,4},{7,5},{8,10},{9,11},{10,... | collective-permute-start | bytes 98312 | tf_op jit(solution)/shard_map/ppermute | solution.py:66
  81.5 5.7 %collective-permute-start.31 = (f32[4,8,256]{2,1,0:T(8,128)S(1)}, f32[4,8,256]{2,1,0:T(8,128)S(1)}, u32[]{:S(2)}, u32[]{:S(2)}) collective-permute-start(f32[4,8,256]{2,1,0:T(8,128)S(1)} %backward_level.3.refs_7_.refs_0_.refs_5_), channel_id=1, source_target_pairs={{0,3},{1,2},{2,1},{3,0},{4,7},{5,6},{6,5},{7,4},{8,11},{9,10},{10,... | collective-permute-start | bytes 98312 | tf_op jit(solution)/shard_map/ppermute | solution.py:66
  88.2 7.5 %collective-permute-start.32 = (f32[4,8,256]{2,1,0:T(8,128)S(1)}, f32[4,8,256]{2,1,0:T(8,128)S(1)}, u32[]{:S(2)}, u32[]{:S(2)}) collective-permute-start(f32[4,8,256]{2,1,0:T(8,128)S(1)} %backward_level.4.refs_0_.refs_6_), channel_id=1, source_target_pairs={{0,1},{1,0},{2,3},{3,2},{4,5},{5,4},{6,7},{7,6},{8,9},{9,8},{10,11... | collective-permute-start | bytes 98312 | tf_op jit(solution)/shard_map/ppermute | solution.py:66
  88.2 7.6 %collective-permute-start.33 = (f32[4,8,256]{2,1,0:T(8,128)S(1)}, f32[4,8,256]{2,1,0:T(8,128)S(1)}, u32[]{:S(2)}, u32[]{:S(2)}) collective-permute-start(f32[4,8,256]{2,1,0:T(8,128)S(1)} %backward_level.4.refs_0_.refs_6_), channel_id=1, source_target_pairs={{0,2},{1,3},{2,0},{3,1},{4,6},{5,7},{6,4},{7,5},{8,10},{9,11},{10,... | collective-permute-start | bytes 98312 | tf_op jit(solution)/shard_map/ppermute | solution.py:66
  90.5 5.8 %collective-permute-start.34 = (f32[4,8,256]{2,1,0:T(8,128)S(1)}, f32[4,8,256]{2,1,0:T(8,128)S(1)}, u32[]{:S(2)}, u32[]{:S(2)}) collective-permute-start(f32[4,8,256]{2,1,0:T(8,128)S(1)} %backward_level.4.refs_0_.refs_6_), channel_id=1, source_target_pairs={{0,3},{1,2},{2,1},{3,0},{4,7},{5,6},{6,5},{7,4},{8,11},{9,10},{10,... | collective-permute-start | bytes 98312 | tf_op jit(solution)/shard_map/ppermute | solution.py:66
  97.2 7.3 %collective-permute-start.37 = (f32[4,4,8,256]{3,2,1,0:T(8,128)S(1)}, f32[4,4,8,256]{3,2,1,0:T(8,128)S(1)}, u32[]{:S(2)}, u32[]{:S(2)}) collective-permute-start(f32[4,4,8,256]{3,2,1,0:T(8,128)S(1)} %backward_level.5), channel_id=1, source_target_pairs={{0,12},{4,8},{8,4},{12,0},{1,13},{5,9},{9,5},{13,1},{2,14},{6,10},... | collective-permute-start | bytes 393224 | tf_op jit(solution)/shard_map/ppermute | solution.py:66
  99.5 6.8 %collective-permute-start.35 = (f32[4,4,8,256]{3,2,1,0:T(8,128)S(1)}, f32[4,4,8,256]{3,2,1,0:T(8,128)S(1)}, u32[]{:S(2)}, u32[]{:S(2)}) collective-permute-start(f32[4,4,8,256]{3,2,1,0:T(8,128)S(1)} %backward_level.5), channel_id=1, source_target_pairs={{0,4},{4,0},{8,12},{12,8},{1,5},{5,1},{9,13},{13,9},{2,6},{6,2},{1... | collective-permute-start | bytes 393224 | tf_op jit(solution)/shard_map/ppermute | solution.py:66
  100.1 6.4 %collective-permute-start.36 = (f32[4,4,8,256]{3,2,1,0:T(8,128)S(1)}, f32[4,4,8,256]{3,2,1,0:T(8,128)S(1)}, u32[]{:S(2)}, u32[]{:S(2)}) collective-permute-start(f32[4,4,8,256]{3,2,1,0:T(8,128)S(1)} %backward_level.5), channel_id=1, source_target_pairs={{0,8},{4,12},{8,0},{12,4},{1,9},{5,13},{9,1},{13,5},{2,10},{6,14},... | collective-permute-start | bytes 393224 | tf_op jit(solution)/shard_map/ppermute | solution.py:66
  (22 other events, 114.6 us)
Sparse Core Ops, SparseCore 0:
  11.5 51.0 all-gather.2

commit v10 on v9

--- a/solution.py
+++ b/solution.py
@@ -16,7 +16,7 @@
 VMEM = pl.BlockSpec(memory_space=pltpu.VMEM)
 HBM = pl.BlockSpec(memory_space=pltpu.HBM)
 PARAMS = pltpu.CompilerParams(vmem_limit_bytes=16 * 2**20)
-INPUT_PARAMS = pltpu.CompilerParams(vmem_limit_bytes=53 * 2**20)
+INPUT_PARAMS = pltpu.CompilerParams(vmem_limit_bytes=107 * 2**19)
 MIDDLE_PARAMS = pltpu.CompilerParams(vmem_limit_bytes=51 * 2**20)
 STREAM_PARAMS = pltpu.CompilerParams(vmem_limit_bytes=52 * 2**20)
 
@@ -297,13 +297,18 @@
 
 
 def descend_kernel(height, nodes, col_count, parents, pattern, value, inverse, *refs):
-    blocks, pieces, (out, high_out, low_out) = refs[:height], refs[height:-3], refs[-3:]
+    blocks, pieces, outs = refs[:height], refs[height:-4], refs[-4:]
+    out, high_out, low_out, choice = outs
     col = lax.axis_index("col")
+    places = lax.broadcasted_iota(jnp.int32, choice.shape[1:], 0)
     for index in range(STEP):
         node = pl.program_id(0) * STEP + index
         rest = value[index]
         left = split(inverse[0, index])
         ancestor = parents[height - 1, col * nodes + node]
+        place = (lax.div(ancestor, nodes) ^ col) * nodes + lax.rem(ancestor, nodes)
+        place = jnp.where(pattern[node, place_of(height, 1)] != 0, place, -1)
+        choice[index] = jnp.where(places == place, 1.0, 0.0)
         for distance in range(2, height + 1):
             level = height - distance
             ancestor = parents[level, ancestor]
@@ -340,48 +345,51 @@
     return pl.pallas_call(
         functools.partial(descend_kernel, height, nodes, col_count),
         grid=(nodes // STEP,),
-        out_shape=[shape_of(nodes, few, rows), matrix, matrix],
+        out_shape=[
+            shape_of(nodes, few, rows),
+            matrix,
+            matrix,
+            shape_of(nodes, col_count * nodes, rows),
+        ],
         in_specs=[SMEM, SMEM, each]
         + [pl.BlockSpec((1, STEP, WIDTH, WIDTH), lambda i: (height, i, 0, 0))]
         + [block_spec(distance) for distance in range(1, height + 1)]
         + [whole] * len(pieces),
-        out_specs=[each] + [pl.BlockSpec((STEP, WIDTH, WIDTH), lambda i: (i, 0, 0))] * 2,
+        out_specs=[each]
+        + [pl.BlockSpec((STEP, WIDTH, WIDTH), lambda i: (i, 0, 0))] * 2
+        + [pl.BlockSpec((STEP, col_count * nodes, rows), lambda i: (i, 0, 0))],
         compiler_params=STREAM_PARAMS,
         name="descend_level",
     )(parents, pattern, value, inverse, *([gathered] * height), *pieces)
 
 
-def backward_kernel(height, nodes, col_count, parents, pattern, start, high, low, *refs):
-    pieces, earlier, (out, solved) = refs[:col_count], refs[col_count:-2], refs[-2:]
-    for step, piece in enumerate(pieces):
-        solved[step] = piece[...]
+def backward_kernel(height, start, high, low, choice, *refs):
+    nodes, count = choice.shape[0], choice.shape[1] // choice.shape[0]
+    pieces, earlier, out = refs[:count], refs[count:-1], refs[-1]
     for level, value in enumerate(earlier):
         out[level] = value[...]
-    col = lax.axis_index("col")
     for node in range(nodes):
-        ancestor = parents[height - 1, col * nodes + node]
-        where = lax.div(ancestor, nodes) ^ col
-        left = split(solved[where, lax.rem(ancestor, nodes)])
-        term = product_t(left, (high[node], low[node]))
-        stored = pattern[node, place_of(height, 1)] != 0
-        total = start[node] - jnp.where(stored, term, 0.0)
+        chosen = jnp.zeros(start.shape[1:], F32)
+        for place in range(count * nodes):
+            weight = choice[node, place : place + 1, :]
+            chosen = chosen + weight * pieces[place // nodes][place % nodes]
+        total = start[node] - product_t(split(chosen), (high[node], low[node]))
         if earlier:
             out[height, node] = total
         else:
             out[node] = total
 
 
-def backward_step(height, parents, pattern, start, composed, pieces, earlier):
-    out = ((1 + len(earlier),) if earlier else ()) + start.shape
-    return pl.pallas_call(
-        functools.partial(backward_kernel, height, start.shape[0], len(pieces)),
-        out_shape=shape_of(*out),
-        in_specs=[SMEM, SMEM] + [VMEM] * (3 + len(pieces) + len(earlier)),
+def backward_step(height, parts, pieces, earlier):
+    start = parts[0].shape
+    return pl.pallas_call(
+        functools.partial(backward_kernel, height),
+        out_shape=shape_of(*(((1 + len(earlier),) if earlier else ()) + start)),
+        in_specs=[VMEM] * (len(parts) + len(pieces) + len(earlier)),
         out_specs=VMEM,
-        scratch_shapes=[pltpu.VMEM((len(pieces),) + start.shape, F32)],
         compiler_params=PARAMS,
         name="backward_level",
-    )(parents, pattern, start, *composed, *pieces, *earlier)
+    )(*parts, *pieces, *earlier)
 
 
 def groups_found(found, groups):
@@ -537,7 +545,7 @@
     backward = [solved]
     whole = []
     for height in (1, 2, 3):
-        start, *composed = descend_step(
+        parts = descend_step(
             height,
             parents,
             pattern,
@@ -549,8 +557,7 @@
         )
         whole = whole + [gather(backward[-1], "col")]
         earlier = backward if height == 3 else []
-        results = backward_step(height, parents, pattern, start, composed, whole[-1], earlier)
-        backward.append(results)
+        backward.append(backward_step(height, parts, whole[-1], earlier))
 
     forward_parts = [piece for level in forward for piece in with_layers(level[0])]
     forward_all = forward_out(forward_parts, nodes, own, gz_count)

time: 118 us -> 116 us (0.983)
  local copies, waits for them, and re-layouts: 3 us -> 1 us
    unnamed x12 -> x8, local copies, waits for them, and re-layouts: 2.03 us -> 0.03 us
    pallas_call x3, Pallas kernels: 2.9 us -> 1.13 us  [backward_step(): pl.pallas_call(functools.partial(backward_kernel, height), out_shape=shap...]
  transfers between devices with their start and end apart: 40 -> 40, of which waited for: 18 -> 18; matrix products, arithmetic and copies ran while one was open for 0% -> 0% of each run, Pallas kernels for 26% -> 25%
where the time goes in v10:
time: 116 us
  starting transfers between devices  47 us (41%)
  Pallas kernels  33.4 us (29%)
  waiting for transfers between devices  19.7 us (17%)
  between operations  14.4 us (12%)
    ppermute x39, starting transfers between devices, swap(): lax.ppermute(value, axis, [(i, i ^ step) for i in range(lax.axis_size(axi...  46.9 us
    ppermute x39, waiting for transfers between devices, swap(): lax.ppermute(value, axis, [(i, i ^ step) for i in range(lax.axis_size(axi...  19.7 us
    pallas_call x3, Pallas kernels, descend_step(): pl.pallas_call(functools.partial(descend_kernel, height, nodes, col_count...  8.03 us
    pallas_call x3, Pallas kernels, lower_step(): pl.pallas_call(functools.partial(lower_kernel, height), grid=(nodes // ST...  5.77 us
    pallas_call x3, Pallas kernels, solve_step(): pl.pallas_call(functools.partial(solve_kernel, sizes), grid=(nodes // STE...  5.72 us
    pallas_call x3, Pallas kernels, forward_step(): pl.pallas_call(functools.partial(forward_kernel, height, sizes), out_shap...  2.95 us
    pallas_call x1, Pallas kernels, backward_out(): pl.pallas_call(functools.partial(backward_out_kernel, nodes, len(parts),...  2.77 us
  transfers between devices with their start and end apart: 40, of which 18 were waited for; matrix products, arithmetic and copies ran while one was open for 0% of the time, Pallas kernels for 25%

profile of v10, /device:TPU:0, one launch (start us, length us, event | category | flops | bytes accessed | tf_op | source)
XLA Modules:
  0.0 115.5 jit_solution(11993116108104057297)
XLA Ops:
  7.2 2.2 %input_parts.1 = (f32[64,128]{1,0:T(8,128)S(1)}, f32[64,128]{1,0:T(8,128)S(1)}, f32[64,128]{1,0:T(8,128)S(1)}, f32[64,128]{1,0:T(8,128)S(1)}, f32[4,64,128]{2,1,0:T(8,128)S(1)}) custom-call(f32[4,32,4,128]{3,2,1,0:T(4,128)} %bitcast.53, f32[4,32,4,128]{3,2,1,0:T(4,128)} %bitcast.54), custom_call_target="tpu_custom_call" | custom-call | tf_op jit(solution)/shard_map/input_parts/pallas_call | solution.py:507
  12.0 2.8 %collective-permute-start.1 = (f32[64,128]{1,0:T(8,128)S(1)}, f32[64,128]{1,0:T(8,128)S(1)}, u32[]{:S(2)}, u32[]{:S(2)}) collective-permute-start(f32[64,128]{1,0:T(8,128)S(1)} %bitcast_add_fusion.refs_0_), channel_id=1, source_target_pairs={{0,4},{4,0},{8,12},{12,8},{1,5},{5,1},{9,13},{13,9},{2,6},{6,2},{1... | collective-permute-start | bytes 98312 | tf_op jit(solution)/shard_map/ppermute | solution.py:66
  16.4 2.1 %lower_products.3 = (bf16[3,4,64,256]{3,2,1,0:T(8,128)(2,1)S(1)}, bf16[3,4,64,256]{3,2,1,0:T(8,128)(2,1)S(1)}) custom-call(f32[6,4,64,256]{3,2,1,0:T(8,128)} %blocks.5, f32[4,4,256,256]{3,2,1,0:T(8,128)} %lower.7), custom_call_target="tpu_custom_call" | custom-call | tf_op jit(solution)/shard_map/lower_products/pallas_call | solution.py:126
  18.7 2.4 %collective-permute-done.3.refs_3_ = f32[64,128]{1,0:T(8,128)S(1)} collective-permute-done((f32[64,128]{1,0:T(8,128)S(1)}, f32[64,128]{1,0:T(8,128)S(1)}, u32[]{:S(2)}, u32[]{:S(2)}) %collective-permute-start.3) | collective-permute-done | bytes 32800 | tf_op jit(solution)/shard_map/ppermute | solution.py:66
  22.2 3.7 %collective-permute-start.6 = (f32[64,128]{1,0:T(8,128)S(1)}, f32[64,128]{1,0:T(8,128)S(1)}, u32[]{:S(2)}, u32[]{:S(2)}) collective-permute-start(f32[64,128]{1,0:T(8,128)S(1)} %get-tuple-element.73), channel_id=1, source_target_pairs={{0,3},{1,2},{2,1},{3,0},{4,7},{5,6},{6,5},{7,4},{8,11},{9,10},{10,... | collective-permute-start | bytes 98312 | tf_op jit(solution)/shard_map/ppermute | solution.py:66
  31.8 2.4 %collective-permute-start.9 = (f32[64,128]{1,0:T(8,128)S(1)}, f32[64,128]{1,0:T(8,128)S(1)}, u32[]{:S(2)}, u32[]{:S(2)}) collective-permute-start(f32[64,128]{1,0:T(8,128)S(1)} %fusion.1.refs_0_), channel_id=1, source_target_pairs={{0,12},{4,8},{8,4},{12,0},{1,13},{5,9},{9,5},{13,1},{2,14},{6,10},... | collective-permute-start | bytes 98312 | tf_op jit(solution)/shard_map/ppermute | solution.py:66
  34.3 2.0 %lower_products.4 = (bf16[2,4,64,256]{3,2,1,0:T(8,128)(2,1)S(1)}, bf16[2,4,64,256]{3,2,1,0:T(8,128)(2,1)S(1)}) custom-call(f32[6,4,64,256]{3,2,1,0:T(8,128)} %blocks.5, f32[4,4,256,256]{3,2,1,0:T(8,128)} %lower.7), custom_call_target="tpu_custom_call" | custom-call | tf_op jit(solution)/shard_map/lower_products/pallas_call | solution.py:126
  39.8 2.3 %collective-permute-start.11 = (f32[64,128]{1,0:T(8,128)S(1)}, f32[64,128]{1,0:T(8,128)S(1)}, u32[]{:S(2)}, u32[]{:S(2)}) collective-permute-start(f32[64,128]{1,0:T(8,128)S(1)} %get-tuple-element.84), channel_id=1, source_target_pairs={{0,2},{1,3},{2,0},{3,1},{4,6},{5,7},{6,4},{7,5},{8,10},{9,11},{10,... | collective-permute-start | bytes 98312 | tf_op jit(solution)/shard_map/ppermute | solution.py:66
  50.8 2.4 %collective-permute-done.15.refs_3_ = f32[64,128]{1,0:T(8,128)S(1)} collective-permute-done((f32[64,128]{1,0:T(8,128)S(1)}, f32[64,128]{1,0:T(8,128)S(1)}, u32[]{:S(2)}, u32[]{:S(2)}) %collective-permute-start.15) | collective-permute-done | bytes 32800 | tf_op jit(solution)/shard_map/ppermute | solution.py:66
  54.1 2.9 %collective-permute-start.18 = (f32[64,128]{1,0:T(8,128)S(1)}, f32[64,128]{1,0:T(8,128)S(1)}, u32[]{:S(2)}, u32[]{:S(2)}) collective-permute-start(f32[64,128]{1,0:T(8,128)S(1)} %get-tuple-element.96), channel_id=1, source_target_pairs={{0,3},{1,2},{2,1},{3,0},{4,7},{5,6},{6,5},{7,4},{8,11},{9,10},{10,... | collective-permute-start | bytes 98312 | tf_op jit(solution)/shard_map/ppermute | solution.py:66
  58.6 1.9 %solve_level.5 = (f32[256,128]{1,0:T(8,128)S(1)}, f32[4,8,256]{2,1,0:T(8,128)S(1)}) custom-call(f32[256,128]{1,0:T(8,128)S(1)} %get-tuple-element.97.full, f32[4,4,256,256]{3,2,1,0:T(8,128)} %lower.7), custom_call_target="tpu_custom_call" | custom-call | tf_op jit(solution)/shard_map/solve_level/pallas_call | solution.py:287
  63.0 2.4 %collective-permute-start.21 = (f32[64,128]{1,0:T(8,128)S(1)}, f32[64,128]{1,0:T(8,128)S(1)}, u32[]{:S(2)}, u32[]{:S(2)}) collective-permute-start(f32[64,128]{1,0:T(8,128)S(1)} %fusion.5.refs_0_), channel_id=1, source_target_pairs={{0,12},{4,8},{8,4},{12,0},{1,13},{5,9},{9,5},{13,1},{2,14},{6,10},... | collective-permute-start | bytes 98312 | tf_op jit(solution)/shard_map/ppermute | solution.py:66
  66.0 2.0 %middle_product.1 = (bf16[4,256,256]{2,1,0:T(8,128)(2,1)S(1)}, bf16[4,256,256]{2,1,0:T(8,128)(2,1)S(1)}, bf16[4,256,256]{2,1,0:T(8,128)(2,1)S(1)}, bf16[4,256,256]{2,1,0:T(8,128)(2,1)S(1)}) custom-call(f32[4,4,256,256]{3,2,1,0:T(8,128)} %inverse.11, f32[4,4,256,256]{3,2,1,0:T(8,128)} %lower.7), custom_call_target="tpu_custom_call" | custom-call | tf_op jit(solution)/shard_map/middle_product/pallas_call | solution.py:150
  68.8 2.1 %collective-permute-start.26 = (f32[4,8,256]{2,1,0:T(8,128)S(1)}, f32[4,8,256]{2,1,0:T(8,128)S(1)}, u32[]{:S(2)}, u32[]{:S(2)}) collective-permute-start(f32[4,8,256]{2,1,0:T(8,128)S(1)} %get-tuple-element.106.refs_0_.refs_3_.refs_2_.refs_4_), channel_id=1, source_target_pairs={{0,1},{1,0},{2,3},{3,2},{4,5},{5,4},{6,7},{7,6},{8,9},{9,8},{10,11... | collective-permute-start | bytes 98312 | tf_op jit(solution)/shard_map/ppermute | solution.py:66
  71.2 2.1 %collective-permute-start.28 = (f32[4,8,256]{2,1,0:T(8,128)S(1)}, f32[4,8,256]{2,1,0:T(8,128)S(1)}, u32[]{:S(2)}, u32[]{:S(2)}) collective-permute-start(f32[4,8,256]{2,1,0:T(8,128)S(1)} %get-tuple-element.106.refs_0_.refs_3_.refs_2_.refs_4_), channel_id=1, source_target_pairs={{0,3},{1,2},{2,1},{3,0},{4,7},{5,6},{6,5},{7,4},{8,11},{9,10},{10,... | collective-permute-start | bytes 98312 | tf_op jit(solution)/shard_map/ppermute | solution.py:66
  73.3 2.2 %descend_level.3 = (f32[4,8,256]{2,1,0:T(8,128)S(1)}, bf16[4,256,256]{2,1,0:T(8,128)(2,1)S(1)}, bf16[4,256,256]{2,1,0:T(8,128)(2,1)S(1)}, f32[4,16,256]{2,1,0:T(8,128)S(1)}) custom-call(s32[3,16]{1,0:T(4,128)S(1)} %copy-done.2, s32[4,6]{1,0:T(4,128)S(1)} %bitcast.42, f32[4,8,256]{2,1,0:T(8,128)S(1)} %get-tuple-element.99.value, f32[4,4,256,256]{3,2,1,0:T(8,128)} %inverse.11, ...), custom_call_target="tpu_custom_call" | custom-call | tf_op jit(solution)/shard_map/descend_level/pallas_call | solution.py:345
  77.3 2.7 %collective-permute-start.30 = (f32[4,8,256]{2,1,0:T(8,128)S(1)}, f32[4,8,256]{2,1,0:T(8,128)S(1)}, u32[]{:S(2)}, u32[]{:S(2)}) collective-permute-start(f32[4,8,256]{2,1,0:T(8,128)S(1)} %backward_level.3.refs_7_.refs_0_.refs_5_), channel_id=1, source_target_pairs={{0,2},{1,3},{2,0},{3,1},{4,6},{5,7},{6,4},{7,5},{8,10},{9,11},{10,... | collective-permute-start | bytes 98312 | tf_op jit(solution)/shard_map/ppermute | solution.py:66
  81.7 2.7 %descend_level.5 = (f32[4,8,256]{2,1,0:T(8,128)S(1)}, bf16[4,256,256]{2,1,0:T(8,128)(2,1)S(1)}, bf16[4,256,256]{2,1,0:T(8,128)(2,1)S(1)}, f32[4,16,256]{2,1,0:T(8,128)S(1)}) custom-call(s32[3,16]{1,0:T(4,128)S(1)} %copy-done.2, s32[4,6]{1,0:T(4,128)S(1)} %bitcast.43, f32[4,8,256]{2,1,0:T(8,128)S(1)} %get-tuple-element.88.value, f32[4,4,256,256]{3,2,1,0:T(8,128)} %inverse.11, ...), custom_call_target="tpu_custom_call" | custom-call | tf_op jit(solution)/shard_map/descend_level/pallas_call | solution.py:345
  86.2 2.2 %collective-permute-start.33 = (f32[4,8,256]{2,1,0:T(8,128)S(1)}, f32[4,8,256]{2,1,0:T(8,128)S(1)}, u32[]{:S(2)}, u32[]{:S(2)}) collective-permute-start(f32[4,8,256]{2,1,0:T(8,128)S(1)} %backward_level.4.refs_0_.refs_6_), channel_id=1, source_target_pairs={{0,2},{1,3},{2,0},{3,1},{4,6},{5,7},{6,4},{7,5},{8,10},{9,11},{10,... | collective-permute-start | bytes 98312 | tf_op jit(solution)/shard_map/ppermute | solution.py:66
  88.4 2.2 %collective-permute-start.34 = (f32[4,8,256]{2,1,0:T(8,128)S(1)}, f32[4,8,256]{2,1,0:T(8,128)S(1)}, u32[]{:S(2)}, u32[]{:S(2)}) collective-permute-start(f32[4,8,256]{2,1,0:T(8,128)S(1)} %backward_level.4.refs_0_.refs_6_), channel_id=1, source_target_pairs={{0,3},{1,2},{2,1},{3,0},{4,7},{5,6},{6,5},{7,4},{8,11},{9,10},{10,... | collective-permute-start | bytes 98312 | tf_op jit(solution)/shard_map/ppermute | solution.py:66
  90.6 3.1 %descend_level.4 = (f32[4,8,256]{2,1,0:T(8,128)S(1)}, bf16[4,256,256]{2,1,0:T(8,128)(2,1)S(1)}, bf16[4,256,256]{2,1,0:T(8,128)(2,1)S(1)}, f32[4,16,256]{2,1,0:T(8,128)S(1)}) custom-call(s32[3,16]{1,0:T(4,128)S(1)} %copy-done.2, s32[4,6]{1,0:T(4,128)S(1)} %bitcast.44, f32[4,8,256]{2,1,0:T(8,128)S(1)} %get-tuple-element.76.value, f32[4,4,256,256]{3,2,1,0:T(8,128)} %inverse.11, ...), custom_call_target="tpu_custom_call" | custom-call | tf_op jit(solution)/shard_map/descend_level/pallas_call | solution.py:345
  94.7 2.4 %collective-permute-start.37 = (f32[4,4,8,256]{3,2,1,0:T(8,128)S(1)}, f32[4,4,8,256]{3,2,1,0:T(8,128)S(1)}, u32[]{:S(2)}, u32[]{:S(2)}) collective-permute-start(f32[4,4,8,256]{3,2,1,0:T(8,128)S(1)} %backward_level.5), channel_id=1, source_target_pairs={{0,12},{4,8},{8,4},{12,0},{1,13},{5,9},{9,5},{13,1},{2,14},{6,10},... | collective-permute-start | bytes 393224 | tf_op jit(solution)/shard_map/ppermute | solution.py:66
  98.2 2.0 %forward_out.1 = f32[4,128,4,128]{3,2,1,0:T(4,128)} custom-call(f32[256,128]{1,0:T(8,128)S(1)} %get-tuple-element.105.refs_0_, f32[256,128]{1,0:T(8,128)S(1)} %collective-permute-done.22.refs_1_, f32[256,128]{1,0:T(8,128)S(1)} %get-tuple-element.98.refs_2_, f32[256,128]{1,0:T(8,128)S(1)} %collective-permute-done.23.refs_3_, ...), custom_call_target="tpu_custom_call" | custom-call | tf_op jit(solution)/shard_map/forward_out/pallas_call | solution.py:436
  105.9 2.8 %backward_out.1 = f32[4,128,4,128]{3,2,1,0:T(4,128)} custom-call(f32[4,4,4,8,256]{4,3,2,1,0:T(8,128)S(1)} %pad_maximum_fusion.refs_0_, f32[4,4,4,8,256]{4,3,2,1,0:T(8,128)S(1)} %collective-permute-done.38.refs_1_), custom_call_target="tpu_custom_call" | custom-call | tf_op jit(solution)/shard_map/backward_out/pallas_call | solution.py:469
  (91 shorter events, 43.0 us)
Async XLA Ops:
  7.2 66.1 %all-gather.3.cloned.1.call-start = ((), (), s32[]{:S(2)}) async-start(), calls=%async_computation | async-start | bytes 7077888 | tf_op jit(solution)/shard_map/all_gather | solution.py:520
  12.0 6.5 %collective-permute-start.1 = (f32[64,128]{1,0:T(8,128)S(1)}, f32[64,128]{1,0:T(8,128)S(1)}, u32[]{:S(2)}, u32[]{:S(2)}) collective-permute-start(f32[64,128]{1,0:T(8,128)S(1)} %bitcast_add_fusion.refs_0_), channel_id=1, source_target_pairs={{0,4},{4,0},{8,12},{12,8},{1,5},{5,1},{9,13},{13,9},{2,6},{6,2},{1... | collective-permute-start | bytes 98312 | tf_op jit(solution)/shard_map/ppermute | solution.py:66
  22.2 6.4 %collective-permute-start.6 = (f32[64,128]{1,0:T(8,128)S(1)}, f32[64,128]{1,0:T(8,128)S(1)}, u32[]{:S(2)}, u32[]{:S(2)}) collective-permute-start(f32[64,128]{1,0:T(8,128)S(1)} %get-tuple-element.73), channel_id=1, source_target_pairs={{0,3},{1,2},{2,1},{3,0},{4,7},{5,6},{6,5},{7,4},{8,11},{9,10},{10,... | collective-permute-start | bytes 98312 | tf_op jit(solution)/shard_map/ppermute | solution.py:66
  30.7 5.6 %collective-permute-start.7 = (f32[64,128]{1,0:T(8,128)S(1)}, f32[64,128]{1,0:T(8,128)S(1)}, u32[]{:S(2)}, u32[]{:S(2)}) collective-permute-start(f32[64,128]{1,0:T(8,128)S(1)} %fusion.1.refs_0_), channel_id=1, source_target_pairs={{0,4},{4,0},{8,12},{12,8},{1,5},{5,1},{9,13},{13,9},{2,6},{6,2},{1... | collective-permute-start | bytes 98312 | tf_op jit(solution)/shard_map/ppermute | solution.py:66
  37.6 6.4 %collective-permute-start.12 = (f32[64,128]{1,0:T(8,128)S(1)}, f32[64,128]{1,0:T(8,128)S(1)}, u32[]{:S(2)}, u32[]{:S(2)}) collective-permute-start(f32[64,128]{1,0:T(8,128)S(1)} %get-tuple-element.85), channel_id=1, source_target_pairs={{0,3},{1,2},{2,1},{3,0},{4,7},{5,6},{6,5},{7,4},{8,11},{9,10},{10,... | collective-permute-start | bytes 98312 | tf_op jit(solution)/shard_map/ppermute | solution.py:66
  44.6 5.3 %collective-permute-start.13 = (f32[64,128]{1,0:T(8,128)S(1)}, f32[64,128]{1,0:T(8,128)S(1)}, u32[]{:S(2)}, u32[]{:S(2)}) collective-permute-start(f32[64,128]{1,0:T(8,128)S(1)} %fusion.3.refs_0_), channel_id=1, source_target_pairs={{0,4},{4,0},{8,12},{12,8},{1,5},{5,1},{9,13},{13,9},{2,6},{6,2},{1... | collective-permute-start | bytes 98312 | tf_op jit(solution)/shard_map/ppermute | solution.py:66
  47.7 5.5 %collective-permute-start.15 = (f32[64,128]{1,0:T(8,128)S(1)}, f32[64,128]{1,0:T(8,128)S(1)}, u32[]{:S(2)}, u32[]{:S(2)}) collective-permute-start(f32[64,128]{1,0:T(8,128)S(1)} %fusion.3.refs_0_), channel_id=1, source_target_pairs={{0,12},{4,8},{8,4},{12,0},{1,13},{5,9},{9,5},{13,1},{2,14},{6,10},... | collective-permute-start | bytes 98312 | tf_op jit(solution)/shard_map/ppermute | solution.py:66
  54.1 6.4 %collective-permute-start.18 = (f32[64,128]{1,0:T(8,128)S(1)}, f32[64,128]{1,0:T(8,128)S(1)}, u32[]{:S(2)}, u32[]{:S(2)}) collective-permute-start(f32[64,128]{1,0:T(8,128)S(1)} %get-tuple-element.96), channel_id=1, source_target_pairs={{0,3},{1,2},{2,1},{3,0},{4,7},{5,6},{6,5},{7,4},{8,11},{9,10},{10,... | collective-permute-start | bytes 98312 | tf_op jit(solution)/shard_map/ppermute | solution.py:66
  61.9 6.1 %collective-permute-start.19 = (f32[64,128]{1,0:T(8,128)S(1)}, f32[64,128]{1,0:T(8,128)S(1)}, u32[]{:S(2)}, u32[]{:S(2)}) collective-permute-start(f32[64,128]{1,0:T(8,128)S(1)} %fusion.5.refs_0_), channel_id=1, source_target_pairs={{0,4},{4,0},{8,12},{12,8},{1,5},{5,1},{9,13},{13,9},{2,6},{6,2},{1... | collective-permute-start | bytes 98312 | tf_op jit(solution)/shard_map/ppermute | solution.py:66
  62.5 5.5 %collective-permute-start.20 = (f32[64,128]{1,0:T(8,128)S(1)}, f32[64,128]{1,0:T(8,128)S(1)}, u32[]{:S(2)}, u32[]{:S(2)}) collective-permute-start(f32[64,128]{1,0:T(8,128)S(1)} %fusion.5.refs_0_), channel_id=1, source_target_pairs={{0,8},{4,12},{8,0},{12,4},{1,9},{5,13},{9,1},{13,5},{2,10},{6,14},... | collective-permute-start | bytes 98312 | tf_op jit(solution)/shard_map/ppermute | solution.py:66
  65.4 31.7 %collective-permute-start.25 = (f32[256,128]{1,0:T(8,128)S(1)}, f32[256,128]{1,0:T(8,128)S(1)}, u32[]{:S(2)}, u32[]{:S(2)}) collective-permute-start(f32[256,128]{1,0:T(8,128)S(1)} %get-tuple-element.75.refs_6_), channel_id=1, source_target_pairs={{0,16},{16,0},{1,17},{17,1},{2,18},{18,2},{3,19},{19,3},{4,20},{20... | collective-permute-start | bytes 393224 | tf_op jit(solution)/shard_map/ppermute | solution.py:66
  65.5 32.1 %collective-permute-start.24 = (f32[256,128]{1,0:T(8,128)S(1)}, f32[256,128]{1,0:T(8,128)S(1)}, u32[]{:S(2)}, u32[]{:S(2)}) collective-permute-start(f32[256,128]{1,0:T(8,128)S(1)} %get-tuple-element.87.refs_4_), channel_id=1, source_target_pairs={{0,16},{16,0},{1,17},{17,1},{2,18},{18,2},{3,19},{19,3},{4,20},{20... | collective-permute-start | bytes 393224 | tf_op jit(solution)/shard_map/ppermute | solution.py:66
  68.8 6.8 %collective-permute-start.26 = (f32[4,8,256]{2,1,0:T(8,128)S(1)}, f32[4,8,256]{2,1,0:T(8,128)S(1)}, u32[]{:S(2)}, u32[]{:S(2)}) collective-permute-start(f32[4,8,256]{2,1,0:T(8,128)S(1)} %get-tuple-element.106.refs_0_.refs_3_.refs_2_.refs_4_), channel_id=1, source_target_pairs={{0,1},{1,0},{2,3},{3,2},{4,5},{5,4},{6,7},{7,6},{8,9},{9,8},{10,11... | collective-permute-start | bytes 98312 | tf_op jit(solution)/shard_map/ppermute | solution.py:66
  70.9 5.1 %collective-permute-start.27 = (f32[4,8,256]{2,1,0:T(8,128)S(1)}, f32[4,8,256]{2,1,0:T(8,128)S(1)}, u32[]{:S(2)}, u32[]{:S(2)}) collective-permute-start(f32[4,8,256]{2,1,0:T(8,128)S(1)} %get-tuple-element.106.refs_0_.refs_3_.refs_2_.refs_4_), channel_id=1, source_target_pairs={{0,2},{1,3},{2,0},{3,1},{4,6},{5,7},{6,4},{7,5},{8,10},{9,11},{10,... | collective-permute-start | bytes 98312 | tf_op jit(solution)/shard_map/ppermute | solution.py:66
  71.2 5.7 %collective-permute-start.28 = (f32[4,8,256]{2,1,0:T(8,128)S(1)}, f32[4,8,256]{2,1,0:T(8,128)S(1)}, u32[]{:S(2)}, u32[]{:S(2)}) collective-permute-start(f32[4,8,256]{2,1,0:T(8,128)S(1)} %get-tuple-element.106.refs_0_.refs_3_.refs_2_.refs_4_), channel_id=1, source_target_pairs={{0,3},{1,2},{2,1},{3,0},{4,7},{5,6},{6,5},{7,4},{8,11},{9,10},{10,... | collective-permute-start | bytes 98312 | tf_op jit(solution)/shard_map/ppermute | solution.py:66
  77.3 7.1 %collective-permute-start.29 = (f32[4,8,256]{2,1,0:T(8,128)S(1)}, f32[4,8,256]{2,1,0:T(8,128)S(1)}, u32[]{:S(2)}, u32[]{:S(2)}) collective-permute-start(f32[4,8,256]{2,1,0:T(8,128)S(1)} %backward_level.3.refs_7_.refs_0_.refs_5_), channel_id=1, source_target_pairs={{0,1},{1,0},{2,3},{3,2},{4,5},{5,4},{6,7},{7,6},{8,9},{9,8},{10,11... | collective-permute-start | bytes 98312 | tf_op jit(solution)/shard_map/ppermute | solution.py:66
  77.3 7.1 %collective-permute-start.30 = (f32[4,8,256]{2,1,0:T(8,128)S(1)}, f32[4,8,256]{2,1,0:T(8,128)S(1)}, u32[]{:S(2)}, u32[]{:S(2)}) collective-permute-start(f32[4,8,256]{2,1,0:T(8,128)S(1)} %backward_level.3.refs_7_.refs_0_.refs_5_), channel_id=1, source_target_pairs={{0,2},{1,3},{2,0},{3,1},{4,6},{5,7},{6,4},{7,5},{8,10},{9,11},{10,... | collective-permute-start | bytes 98312 | tf_op jit(solution)/shard_map/ppermute | solution.py:66
  80.0 5.8 %collective-permute-start.31 = (f32[4,8,256]{2,1,0:T(8,128)S(1)}, f32[4,8,256]{2,1,0:T(8,128)S(1)}, u32[]{:S(2)}, u32[]{:S(2)}) collective-permute-start(f32[4,8,256]{2,1,0:T(8,128)S(1)} %backward_level.3.refs_7_.refs_0_.refs_5_), channel_id=1, source_target_pairs={{0,3},{1,2},{2,1},{3,0},{4,7},{5,6},{6,5},{7,4},{8,11},{9,10},{10,... | collective-permute-start | bytes 98312 | tf_op jit(solution)/shard_map/ppermute | solution.py:66
  86.2 7.5 %collective-permute-start.32 = (f32[4,8,256]{2,1,0:T(8,128)S(1)}, f32[4,8,256]{2,1,0:T(8,128)S(1)}, u32[]{:S(2)}, u32[]{:S(2)}) collective-permute-start(f32[4,8,256]{2,1,0:T(8,128)S(1)} %backward_level.4.refs_0_.refs_6_), channel_id=1, source_target_pairs={{0,1},{1,0},{2,3},{3,2},{4,5},{5,4},{6,7},{7,6},{8,9},{9,8},{10,11... | collective-permute-start | bytes 98312 | tf_op jit(solution)/shard_map/ppermute | solution.py:66
  86.2 7.6 %collective-permute-start.33 = (f32[4,8,256]{2,1,0:T(8,128)S(1)}, f32[4,8,256]{2,1,0:T(8,128)S(1)}, u32[]{:S(2)}, u32[]{:S(2)}) collective-permute-start(f32[4,8,256]{2,1,0:T(8,128)S(1)} %backward_level.4.refs_0_.refs_6_), channel_id=1, source_target_pairs={{0,2},{1,3},{2,0},{3,1},{4,6},{5,7},{6,4},{7,5},{8,10},{9,11},{10,... | collective-permute-start | bytes 98312 | tf_op jit(solution)/shard_map/ppermute | solution.py:66
  88.4 5.9 %collective-permute-start.34 = (f32[4,8,256]{2,1,0:T(8,128)S(1)}, f32[4,8,256]{2,1,0:T(8,128)S(1)}, u32[]{:S(2)}, u32[]{:S(2)}) collective-permute-start(f32[4,8,256]{2,1,0:T(8,128)S(1)} %backward_level.4.refs_0_.refs_6_), channel_id=1, source_target_pairs={{0,3},{1,2},{2,1},{3,0},{4,7},{5,6},{6,5},{7,4},{8,11},{9,10},{10,... | collective-permute-start | bytes 98312 | tf_op jit(solution)/shard_map/ppermute | solution.py:66
  94.7 7.3 %collective-permute-start.37 = (f32[4,4,8,256]{3,2,1,0:T(8,128)S(1)}, f32[4,4,8,256]{3,2,1,0:T(8,128)S(1)}, u32[]{:S(2)}, u32[]{:S(2)}) collective-permute-start(f32[4,4,8,256]{3,2,1,0:T(8,128)S(1)} %backward_level.5), channel_id=1, source_target_pairs={{0,12},{4,8},{8,4},{12,0},{1,13},{5,9},{9,5},{13,1},{2,14},{6,10},... | collective-permute-start | bytes 393224 | tf_op jit(solution)/shard_map/ppermute | solution.py:66
  97.1 6.7 %collective-permute-start.35 = (f32[4,4,8,256]{3,2,1,0:T(8,128)S(1)}, f32[4,4,8,256]{3,2,1,0:T(8,128)S(1)}, u32[]{:S(2)}, u32[]{:S(2)}) collective-permute-start(f32[4,4,8,256]{3,2,1,0:T(8,128)S(1)} %backward_level.5), channel_id=1, source_target_pairs={{0,4},{4,0},{8,12},{12,8},{1,5},{5,1},{9,13},{13,9},{2,6},{6,2},{1... | collective-permute-start | bytes 393224 | tf_op jit(solution)/shard_map/ppermute | solution.py:66
  97.5 6.4 %collective-permute-start.36 = (f32[4,4,8,256]{3,2,1,0:T(8,128)S(1)}, f32[4,4,8,256]{3,2,1,0:T(8,128)S(1)}, u32[]{:S(2)}, u32[]{:S(2)}) collective-permute-start(f32[4,4,8,256]{3,2,1,0:T(8,128)S(1)} %backward_level.5), channel_id=1, source_target_pairs={{0,8},{4,12},{8,0},{12,4},{1,9},{5,13},{9,1},{13,5},{2,10},{6,14},... | collective-permute-start | bytes 393224 | tf_op jit(solution)/shard_map/ppermute | solution.py:66
  (20 other events, 110.5 us)
Sparse Core Ops, SparseCore 0:
  10.6 51.0 all-gather.2

commit v11 on v10

--- a/solution.py
+++ b/solution.py
@@ -111,30 +111,46 @@
                     away[step - 1][level, :, lanes] = chosen
 
 
-def lower_kernel(height, blocks, inverse, high_out, low_out):
+def lower_kernel(height, nodes, own, parents, pattern, blocks, inverse, high_out, low_out, route):
     first = place_of(height, 1)
     part, width = blocks.shape[2:]
-    for node in range(blocks.shape[1]):
-        left = blocks[first : first + height, node].reshape(height * part, width)
-        whole = product(split(left), split(inverse[0, node])).reshape(height, part, width)
-        high_out[:, node], low_out[:, node] = split(whole)
-
-
-def lower_step(height, blocks, inverse):
+    col = lax.axis_index("col")
+    columns = lax.broadcasted_iota(jnp.int32, route.shape[2:], 0)
+    slots = lax.broadcasted_iota(jnp.int32, route.shape[2:], 1) // own
+    for index in range(STEP):
+        node = pl.program_id(0) * STEP + index
+        left = blocks[first : first + height, index].reshape(height * part, width)
+        whole = product(split(left), split(inverse[0, index])).reshape(height, part, width)
+        high_out[:, index], low_out[:, index] = split(whole)
+        ancestor = col * nodes + node
+        for distance in range(1, height + 1):
+            ancestor = parents[height - distance, ancestor]
+            stored = pattern[node, place_of(height, distance)] != 0
+            slot = jnp.where(stored, lax.rem(ancestor, nodes), -1)
+            here = (columns == (lax.div(ancestor, nodes) ^ col)) & (slots == slot)
+            route[distance - 1, index] = jnp.where(here, 1.0, 0.0)
+
+
+def lower_step(height, parents, pattern, blocks, inverse, sizes):
     pairs, nodes, part = blocks.shape[:3]
+    own, col_count = sizes[2], sizes[4]
     out = shape_of(height, nodes, part, WIDTH, dtype=BF16)
-    return pl.pallas_call(
-        functools.partial(lower_kernel, height),
+    route = shape_of(height, nodes, col_count, nodes * own)
+    return pl.pallas_call(
+        functools.partial(lower_kernel, height, nodes, own),
         grid=(nodes // STEP,),
-        out_shape=[out, out],
+        out_shape=[out, out, route],
         in_specs=[
+            SMEM,
+            SMEM,
             pl.BlockSpec((pairs, STEP, part, WIDTH), lambda i: (0, i, 0, 0)),
             pl.BlockSpec((1, STEP, WIDTH, WIDTH), lambda i: (height, i, 0, 0)),
         ],
-        out_specs=[pl.BlockSpec((height, STEP, part, WIDTH), lambda i: (0, i, 0, 0))] * 2,
+        out_specs=[pl.BlockSpec((height, STEP, part, WIDTH), lambda i: (0, i, 0, 0))] * 2
+        + [pl.BlockSpec((height, STEP) + route.shape[2:], lambda i: (0, i, 0, 0))],
         compiler_params=STREAM_PARAMS,
         name="lower_products",
-    )(blocks, inverse)
+    )(parents, pattern, blocks, inverse)
 
 
 def middle_kernel(upper, lower, high_out, low_out, lower_high, lower_low):
@@ -168,40 +184,38 @@
     nodes, part, own, row_count, col_count = sizes
     lanes = nodes * own
     pieces, refs = refs[:row_count], refs[row_count:]
-    parents, pattern, m_high, m_low = refs[:4]
-    pending_in = refs[4 : 4 + height] if height < 3 else ()
-    refs = refs[4 + len(pending_in) :]
-    full, sends = refs[0], refs[1 : 1 + col_count]
-    pending_out = refs[1 + col_count : col_count + height]
-    urgent = refs[-1]
+    m_high, m_low, route = refs[:3]
+    pending_in = refs[3 : 3 + height] if height < 3 else ()
+    refs = refs[3 + len(pending_in) :]
+    full, sends, pending_out = refs[0], refs[1 : 1 + col_count], refs[1 + col_count :]
     assemble(pieces, full, part)
     lane = lax.broadcasted_iota(jnp.int32, (1, lanes), 1) // own
-    col = lax.axis_index("col")
     right = split(full[...])
-    targets = []
-    for level in range(height):
-        target = urgent if level == height - 1 else pending_out[level]
-        target[...] = pending_in[level][...] if pending_in else jnp.zeros(target.shape, F32)
-        targets.append(target)
     rows = height * nodes * part
     whole = product((m_high[...].reshape(rows, WIDTH), m_low[...].reshape(rows, WIDTH)), right)
-    for node in range(nodes):
-        ancestor = col * nodes + node
-        for distance in range(1, height + 1):
-            level = height - distance
-            ancestor = parents[level, ancestor]
-            slot = lax.rem(ancestor, nodes)
-            where = lax.div(ancestor, nodes) ^ col
+    for distance in range(1, height + 1):
+        level = height - distance
+        terms = []
+        for node in range(nodes):
             start = ((distance - 1) * nodes + node) * part
             term = whole[start : start + part]
-            term = pltpu.roll(term, lax.rem(slot - node + nodes, nodes) * own, 1)
-            stored = jnp.where(pattern[node, place_of(height, distance)] != 0, slot, -1)
-            targets[level][where] += jnp.where(lane == stored, term, 0.0)
-    for step in range(col_count):
-        sends[step][...] = urgent[step]
-
-
-def forward_step(height, pieces, parents, pattern, m, pending, sizes):
+            spread = term
+            for slot in range(nodes):
+                if slot != node:
+                    turned = pltpu.roll(term, (slot - node) * own % lanes, 1)
+                    spread = jnp.where(lane == slot, turned, spread)
+            terms.append(spread)
+        for where in range(col_count):
+            total = pending_in[level][where] if pending_in else jnp.zeros((part, lanes), F32)
+            for node in range(nodes):
+                total = total + route[distance - 1, node, where : where + 1, :] * terms[node]
+            if distance == 1:
+                sends[where][...] = total
+            else:
+                pending_out[level][where] = total
+
+
+def forward_step(height, pieces, m, pending, sizes):
     nodes, part, own, row_count, col_count = sizes
     lanes = nodes * own
     piece = shape_of(part, lanes)
@@ -210,12 +224,11 @@
     results = pl.pallas_call(
         functools.partial(forward_kernel, height, sizes),
         out_shape=out_shape,
-        in_specs=[VMEM] * len(pieces) + [SMEM, SMEM] + [VMEM] * (2 + len(pending)),
+        in_specs=[VMEM] * (len(pieces) + len(m) + len(pending)),
         out_specs=[VMEM] * len(out_shape),
-        scratch_shapes=[pltpu.VMEM(stack.shape, F32)],
         compiler_params=PARAMS,
         name="forward_level",
-    )(*pieces, parents, pattern, *m, *pending)
+    )(*pieces, *m, *pending)
     return results[0], results[1 : 1 + col_count], results[1 + col_count :]
 
 
@@ -526,13 +539,13 @@
     forward = [None] * 4
     pending = []
     mine = initial[3]
-    m = lower_step(3, lower_blocks, lower_inverse)
+    m = lower_step(3, parents, pattern, lower_blocks, lower_inverse, sizes)
     for height in (3, 2, 1):
         pieces = gather(mine, "row")
         if height < 3:
-            m = lower_step(height, lower_blocks, lower_inverse)
+            m = lower_step(height, parents, pattern, lower_blocks, lower_inverse, sizes)
         fulls[height], sends, pending = forward_step(
-            height, pieces, parents, pattern, m, pending, sizes
+            height, pieces, m, pending, sizes
         )
         forward[height] = solve_step(height, fulls[height], lower_inverse, sizes)
         taken = [swap(sends[step], "col", step) for step in steps_of(col_count)]

time: 116 us -> 115 us (level)
  Pallas kernels: 33.4 us -> 31.9 us
  local copies, waits for them, and re-layouts: 1 us -> 2.36 us
    pallas_call x3, Pallas kernels: 2.95 us -> 1.37 us  [forward_step(): pl.pallas_call(functools.partial(forward_kernel, height, sizes), out_shap...]
    unnamed x8 -> x12, local copies, waits for them, and re-layouts: 0.03 us -> 1.39 us
  transfers between devices with their start and end apart: 40 -> 40, of which waited for: 18 -> 18; matrix products, arithmetic and copies ran while one was open for 0% -> 0% of each run, Pallas kernels for 25% -> 23%
where the time goes in v11:
time: 115 us
  starting transfers between devices  47 us (41%)
  Pallas kernels  31.9 us (28%)
  waiting for transfers between devices  19.2 us (17%)
  between operations  14.4 us (13%)
  local copies, waits for them, and re-layouts  2.36 us (2%)
    ppermute x39, starting transfers between devices, swap(): lax.ppermute(value, axis, [(i, i ^ step) for i in range(lax.axis_size(axi...  46.9 us
    ppermute x39, waiting for transfers between devices, swap(): lax.ppermute(value, axis, [(i, i ^ step) for i in range(lax.axis_size(axi...  19.1 us
    pallas_call x3, Pallas kernels, descend_step(): pl.pallas_call(functools.partial(descend_kernel, height, nodes, col_count...  8.04 us
    pallas_call x3, Pallas kernels, lower_step(): pl.pallas_call(functools.partial(lower_kernel, height, nodes, own), grid=...  5.87 us
    pallas_call x3, Pallas kernels, solve_step(): pl.pallas_call(functools.partial(solve_kernel, sizes), grid=(nodes // STE...  5.73 us
    pallas_call x1, Pallas kernels, backward_out(): pl.pallas_call(functools.partial(backward_out_kernel, nodes, len(parts),...  2.77 us
  transfers between devices with their start and end apart: 40, of which 18 were waited for; matrix products, arithmetic and copies ran while one was open for 0% of the time, Pallas kernels for 23%

profile of v11, /device:TPU:0, one launch (start us, length us, event | category | flops | bytes accessed | tf_op | source)
XLA Modules:
  0.0 114.9 jit_solution(11019840689167229244)
XLA Ops:
  7.2 2.2 %input_parts.1 = (f32[64,128]{1,0:T(8,128)S(1)}, f32[64,128]{1,0:T(8,128)S(1)}, f32[64,128]{1,0:T(8,128)S(1)}, f32[64,128]{1,0:T(8,128)S(1)}, f32[4,64,128]{2,1,0:T(8,128)S(1)}) custom-call(f32[4,32,4,128]{3,2,1,0:T(4,128)} %bitcast.53, f32[4,32,4,128]{3,2,1,0:T(4,128)} %bitcast.54), custom_call_target="tpu_custom_call" | custom-call | tf_op jit(solution)/shard_map/input_parts/pallas_call | solution.py:520
  12.0 2.8 %collective-permute-start.1 = (f32[64,128]{1,0:T(8,128)S(1)}, f32[64,128]{1,0:T(8,128)S(1)}, u32[]{:S(2)}, u32[]{:S(2)}) collective-permute-start(f32[64,128]{1,0:T(8,128)S(1)} %bitcast_add_fusion.refs_0_), channel_id=1, source_target_pairs={{0,4},{4,0},{8,12},{12,8},{1,5},{5,1},{9,13},{13,9},{2,6},{6,2},{1... | collective-permute-start | bytes 98312 | tf_op jit(solution)/shard_map/ppermute | solution.py:66
  17.7 2.1 %lower_products.3 = (bf16[3,4,64,256]{3,2,1,0:T(8,128)(2,1)S(1)}, bf16[3,4,64,256]{3,2,1,0:T(8,128)(2,1)S(1)}, f32[3,4,4,128]{3,2,1,0:T(4,128)S(1)}) custom-call(s32[3,16]{1,0:T(4,128)S(1)} %copy-done.2, s32[4,6]{1,0:T(4,128)S(1)} %bitcast.39, f32[6,4,64,256]{3,2,1,0:T(8,128)} %blocks.5, f32[4,4,256,256]{3,2,1,0:T(8,128)} %lower.7), custom_call_target="tpu_custom_call" | custom-call | tf_op jit(solution)/shard_map/lower_products/pallas_call | solution.py:139
  21.7 3.7 %collective-permute-start.6 = (f32[64,128]{1,0:T(8,128)S(1)}, f32[64,128]{1,0:T(8,128)S(1)}, u32[]{:S(2)}, u32[]{:S(2)}) collective-permute-start(f32[64,128]{1,0:T(8,128)S(1)} %get-tuple-element.77), channel_id=1, source_target_pairs={{0,3},{1,2},{2,1},{3,0},{4,7},{5,6},{6,5},{7,4},{8,11},{9,10},{10,... | collective-permute-start | bytes 98312 | tf_op jit(solution)/shard_map/ppermute | solution.py:66
  26.2 1.9 %solve_level.3 = (f32[256,128]{1,0:T(8,128)S(1)}, f32[4,8,256]{2,1,0:T(8,128)S(1)}) custom-call(f32[256,128]{1,0:T(8,128)S(1)} %get-tuple-element.78.full, f32[4,4,256,256]{3,2,1,0:T(8,128)} %lower.7), custom_call_target="tpu_custom_call" | custom-call | tf_op jit(solution)/shard_map/solve_level/pallas_call | solution.py:300
  33.8 2.0 %lower_products.4 = (bf16[2,4,64,256]{3,2,1,0:T(8,128)(2,1)S(1)}, bf16[2,4,64,256]{3,2,1,0:T(8,128)(2,1)S(1)}, f32[2,4,4,128]{3,2,1,0:T(4,128)S(1)}) custom-call(s32[3,16]{1,0:T(4,128)S(1)} %copy-done.2, s32[4,6]{1,0:T(4,128)S(1)} %bitcast.40, f32[6,4,64,256]{3,2,1,0:T(8,128)} %blocks.5, f32[4,4,256,256]{3,2,1,0:T(8,128)} %lower.7), custom_call_target="tpu_custom_call" | custom-call | tf_op jit(solution)/shard_map/lower_products/pallas_call | solution.py:139
  37.8 1.9 %collective-permute-start.12 = (f32[64,128]{1,0:T(8,128)S(1)}, f32[64,128]{1,0:T(8,128)S(1)}, u32[]{:S(2)}, u32[]{:S(2)}) collective-permute-start(f32[64,128]{1,0:T(8,128)S(1)} %get-tuple-element.90), channel_id=1, source_target_pairs={{0,3},{1,2},{2,1},{3,0},{4,7},{5,6},{6,5},{7,4},{8,11},{9,10},{10,... | collective-permute-start | bytes 98312 | tf_op jit(solution)/shard_map/ppermute | solution.py:66
  40.0 2.3 %collective-permute-start.11 = (f32[64,128]{1,0:T(8,128)S(1)}, f32[64,128]{1,0:T(8,128)S(1)}, u32[]{:S(2)}, u32[]{:S(2)}) collective-permute-start(f32[64,128]{1,0:T(8,128)S(1)} %get-tuple-element.89), channel_id=1, source_target_pairs={{0,2},{1,3},{2,0},{3,1},{4,6},{5,7},{6,4},{7,5},{8,10},{9,11},{10,... | collective-permute-start | bytes 98312 | tf_op jit(solution)/shard_map/ppermute | solution.py:66
  42.3 1.9 %solve_level.4 = (f32[256,128]{1,0:T(8,128)S(1)}, f32[4,8,256]{2,1,0:T(8,128)S(1)}) custom-call(f32[256,128]{1,0:T(8,128)S(1)} %get-tuple-element.91.full, f32[4,4,256,256]{3,2,1,0:T(8,128)} %lower.7), custom_call_target="tpu_custom_call" | custom-call | tf_op jit(solution)/shard_map/solve_level/pallas_call | solution.py:300
  50.1 2.1 %collective-permute-done.15.refs_3_ = f32[64,128]{1,0:T(8,128)S(1)} collective-permute-done((f32[64,128]{1,0:T(8,128)S(1)}, f32[64,128]{1,0:T(8,128)S(1)}, u32[]{:S(2)}, u32[]{:S(2)}) %collective-permute-start.15) | collective-permute-done | bytes 32800 | tf_op jit(solution)/shard_map/ppermute | solution.py:66
  52.5 2.9 %collective-permute-start.18 = (f32[64,128]{1,0:T(8,128)S(1)}, f32[64,128]{1,0:T(8,128)S(1)}, u32[]{:S(2)}, u32[]{:S(2)}) collective-permute-start(f32[64,128]{1,0:T(8,128)S(1)} %get-tuple-element.102), channel_id=1, source_target_pairs={{0,3},{1,2},{2,1},{3,0},{4,7},{5,6},{6,5},{7,4},{8,11},{9,10},{10,... | collective-permute-start | bytes 98312 | tf_op jit(solution)/shard_map/ppermute | solution.py:66
  57.0 1.9 %solve_level.5 = (f32[256,128]{1,0:T(8,128)S(1)}, f32[4,8,256]{2,1,0:T(8,128)S(1)}) custom-call(f32[256,128]{1,0:T(8,128)S(1)} %get-tuple-element.103.full, f32[4,4,256,256]{3,2,1,0:T(8,128)} %lower.7), custom_call_target="tpu_custom_call" | custom-call | tf_op jit(solution)/shard_map/solve_level/pallas_call | solution.py:300
  64.4 2.0 %middle_product.1 = (bf16[4,256,256]{2,1,0:T(8,128)(2,1)S(1)}, bf16[4,256,256]{2,1,0:T(8,128)(2,1)S(1)}, bf16[4,256,256]{2,1,0:T(8,128)(2,1)S(1)}, bf16[4,256,256]{2,1,0:T(8,128)(2,1)S(1)}) custom-call(f32[4,4,256,256]{3,2,1,0:T(8,128)} %inverse.11, f32[4,4,256,256]{3,2,1,0:T(8,128)} %lower.7), custom_call_target="tpu_custom_call" | custom-call | tf_op jit(solution)/shard_map/middle_product/pallas_call | solution.py:166
  68.2 2.1 %collective-permute-start.26 = (f32[4,8,256]{2,1,0:T(8,128)S(1)}, f32[4,8,256]{2,1,0:T(8,128)S(1)}, u32[]{:S(2)}, u32[]{:S(2)}) collective-permute-start(f32[4,8,256]{2,1,0:T(8,128)S(1)} %get-tuple-element.112.refs_0_.refs_3_.refs_2_.refs_4_), channel_id=1, source_target_pairs={{0,1},{1,0},{2,3},{3,2},{4,5},{5,4},{6,7},{7,6},{8,9},{9,8},{10,11... | collective-permute-start | bytes 98312 | tf_op jit(solution)/shard_map/ppermute | solution.py:66
  70.6 2.1 %collective-permute-start.28 = (f32[4,8,256]{2,1,0:T(8,128)S(1)}, f32[4,8,256]{2,1,0:T(8,128)S(1)}, u32[]{:S(2)}, u32[]{:S(2)}) collective-permute-start(f32[4,8,256]{2,1,0:T(8,128)S(1)} %get-tuple-element.112.refs_0_.refs_3_.refs_2_.refs_4_), channel_id=1, source_target_pairs={{0,3},{1,2},{2,1},{3,0},{4,7},{5,6},{6,5},{7,4},{8,11},{9,10},{10,... | collective-permute-start | bytes 98312 | tf_op jit(solution)/shard_map/ppermute | solution.py:66
  72.7 2.3 %descend_level.3 = (f32[4,8,256]{2,1,0:T(8,128)S(1)}, bf16[4,256,256]{2,1,0:T(8,128)(2,1)S(1)}, bf16[4,256,256]{2,1,0:T(8,128)(2,1)S(1)}, f32[4,16,256]{2,1,0:T(8,128)S(1)}) custom-call(s32[3,16]{1,0:T(4,128)S(1)} %copy-done.3, s32[4,6]{1,0:T(4,128)S(1)} %bitcast.42, f32[4,8,256]{2,1,0:T(8,128)S(1)} %get-tuple-element.105.value, ...), custom_call_target="tpu_custom_call" | custom-call | tf_op jit(solution)/shard_map/descend_level/pallas_call | solution.py:358
  76.7 2.6 %collective-permute-start.30 = (f32[4,8,256]{2,1,0:T(8,128)S(1)}, f32[4,8,256]{2,1,0:T(8,128)S(1)}, u32[]{:S(2)}, u32[]{:S(2)}) collective-permute-start(f32[4,8,256]{2,1,0:T(8,128)S(1)} %backward_level.3.refs_7_.refs_0_.refs_5_), channel_id=1, source_target_pairs={{0,2},{1,3},{2,0},{3,1},{4,6},{5,7},{6,4},{7,5},{8,10},{9,11},{10,... | collective-permute-start | bytes 98312 | tf_op jit(solution)/shard_map/ppermute | solution.py:66
  81.1 2.7 %descend_level.5 = (f32[4,8,256]{2,1,0:T(8,128)S(1)}, bf16[4,256,256]{2,1,0:T(8,128)(2,1)S(1)}, bf16[4,256,256]{2,1,0:T(8,128)(2,1)S(1)}, f32[4,16,256]{2,1,0:T(8,128)S(1)}) custom-call(s32[3,16]{1,0:T(4,128)S(1)} %copy-done.3, s32[4,6]{1,0:T(4,128)S(1)} %bitcast.43, f32[4,8,256]{2,1,0:T(8,128)S(1)} %get-tuple-element.93.value, f32[4,4,256,256]{3,2,1,0:T(8,128)} %inverse.11, ...), custom_call_target="tpu_custom_call" | custom-call | tf_op jit(solution)/shard_map/descend_level/pallas_call | solution.py:358
  85.6 2.5 %collective-permute-start.33 = (f32[4,8,256]{2,1,0:T(8,128)S(1)}, f32[4,8,256]{2,1,0:T(8,128)S(1)}, u32[]{:S(2)}, u32[]{:S(2)}) collective-permute-start(f32[4,8,256]{2,1,0:T(8,128)S(1)} %backward_level.4.refs_0_.refs_6_), channel_id=1, source_target_pairs={{0,2},{1,3},{2,0},{3,1},{4,6},{5,7},{6,4},{7,5},{8,10},{9,11},{10,... | collective-permute-start | bytes 98312 | tf_op jit(solution)/shard_map/ppermute | solution.py:66
  88.1 1.8 %collective-permute-start.34 = (f32[4,8,256]{2,1,0:T(8,128)S(1)}, f32[4,8,256]{2,1,0:T(8,128)S(1)}, u32[]{:S(2)}, u32[]{:S(2)}) collective-permute-start(f32[4,8,256]{2,1,0:T(8,128)S(1)} %backward_level.4.refs_0_.refs_6_), channel_id=1, source_target_pairs={{0,3},{1,2},{2,1},{3,0},{4,7},{5,6},{6,5},{7,4},{8,11},{9,10},{10,... | collective-permute-start | bytes 98312 | tf_op jit(solution)/shard_map/ppermute | solution.py:66
  89.9 3.1 %descend_level.4 = (f32[4,8,256]{2,1,0:T(8,128)S(1)}, bf16[4,256,256]{2,1,0:T(8,128)(2,1)S(1)}, bf16[4,256,256]{2,1,0:T(8,128)(2,1)S(1)}, f32[4,16,256]{2,1,0:T(8,128)S(1)}) custom-call(s32[3,16]{1,0:T(4,128)S(1)} %copy-done.3, s32[4,6]{1,0:T(4,128)S(1)} %bitcast.44, f32[4,8,256]{2,1,0:T(8,128)S(1)} %get-tuple-element.80.value, f32[4,4,256,256]{3,2,1,0:T(8,128)} %inverse.11, ...), custom_call_target="tpu_custom_call" | custom-call | tf_op jit(solution)/shard_map/descend_level/pallas_call | solution.py:358
  97.7 2.0 %forward_out.1 = f32[4,128,4,128]{3,2,1,0:T(4,128)} custom-call(f32[256,128]{1,0:T(8,128)S(1)} %get-tuple-element.111.refs_0_, f32[256,128]{1,0:T(8,128)S(1)} %collective-permute-done.22.refs_1_, f32[256,128]{1,0:T(8,128)S(1)} %get-tuple-element.104.refs_2_, f32[256,128]{1,0:T(8,128)S(1)} %collective-permute-done.23.refs_3_, ...), custom_call_target="tpu_custom_call" | custom-call | tf_op jit(solution)/shard_map/forward_out/pallas_call | solution.py:449
  103.4 1.9 %collective-permute-done.38.refs_1_ = f32[4,4,4,8,256]{4,3,2,1,0:T(8,128)S(1)} collective-permute-done((f32[4,4,4,8,256]{4,3,2,1,0:T(8,128)S(1)}, f32[4,4,4,8,256]{4,3,2,1,0:T(8,128)S(1)}, u32[]{:S(2)}, u32[]{:S(2)}) %collective-permute-start.38) | collective-permute-done | bytes 524320 | tf_op jit(solution)/shard_map/ppermute | solution.py:66
  105.3 2.8 %backward_out.1 = f32[4,128,4,128]{3,2,1,0:T(4,128)} custom-call(f32[4,4,4,8,256]{4,3,2,1,0:T(8,128)S(1)} %pad_maximum_fusion.refs_0_, f32[4,4,4,8,256]{4,3,2,1,0:T(8,128)S(1)} %collective-permute-done.38.refs_1_), custom_call_target="tpu_custom_call" | custom-call | tf_op jit(solution)/shard_map/backward_out/pallas_call | solution.py:482
  (95 shorter events, 44.8 us)
Async XLA Ops:
  7.2 65.5 %all-gather.3.cloned.1.call-start = ((), (), s32[]{:S(2)}) async-start(), calls=%async_computation | async-start | bytes 7077888 | tf_op jit(solution)/shard_map/all_gather | solution.py:533
  12.0 7.9 %collective-permute-start.1 = (f32[64,128]{1,0:T(8,128)S(1)}, f32[64,128]{1,0:T(8,128)S(1)}, u32[]{:S(2)}, u32[]{:S(2)}) collective-permute-start(f32[64,128]{1,0:T(8,128)S(1)} %bitcast_add_fusion.refs_0_), channel_id=1, source_target_pairs={{0,4},{4,0},{8,12},{12,8},{1,5},{5,1},{9,13},{13,9},{2,6},{6,2},{1... | collective-permute-start | bytes 98312 | tf_op jit(solution)/shard_map/ppermute | solution.py:66
  14.8 5.0 %collective-permute-start.2 = (f32[64,128]{1,0:T(8,128)S(1)}, f32[64,128]{1,0:T(8,128)S(1)}, u32[]{:S(2)}, u32[]{:S(2)}) collective-permute-start(f32[64,128]{1,0:T(8,128)S(1)} %bitcast_add_fusion.refs_0_), channel_id=1, source_target_pairs={{0,8},{4,12},{8,0},{12,4},{1,9},{5,13},{9,1},{13,5},{2,10},{6,14},... | collective-permute-start | bytes 98312 | tf_op jit(solution)/shard_map/ppermute | solution.py:66
  21.7 6.4 %collective-permute-start.6 = (f32[64,128]{1,0:T(8,128)S(1)}, f32[64,128]{1,0:T(8,128)S(1)}, u32[]{:S(2)}, u32[]{:S(2)}) collective-permute-start(f32[64,128]{1,0:T(8,128)S(1)} %get-tuple-element.77), channel_id=1, source_target_pairs={{0,3},{1,2},{2,1},{3,0},{4,7},{5,6},{6,5},{7,4},{8,11},{9,10},{10,... | collective-permute-start | bytes 98312 | tf_op jit(solution)/shard_map/ppermute | solution.py:66
  30.2 5.6 %collective-permute-start.7 = (f32[64,128]{1,0:T(8,128)S(1)}, f32[64,128]{1,0:T(8,128)S(1)}, u32[]{:S(2)}, u32[]{:S(2)}) collective-permute-start(f32[64,128]{1,0:T(8,128)S(1)} %fusion.1.refs_0_), channel_id=1, source_target_pairs={{0,4},{4,0},{8,12},{12,8},{1,5},{5,1},{9,13},{13,9},{2,6},{6,2},{1... | collective-permute-start | bytes 98312 | tf_op jit(solution)/shard_map/ppermute | solution.py:66
  37.8 6.4 %collective-permute-start.12 = (f32[64,128]{1,0:T(8,128)S(1)}, f32[64,128]{1,0:T(8,128)S(1)}, u32[]{:S(2)}, u32[]{:S(2)}) collective-permute-start(f32[64,128]{1,0:T(8,128)S(1)} %get-tuple-element.90), channel_id=1, source_target_pairs={{0,3},{1,2},{2,1},{3,0},{4,7},{5,6},{6,5},{7,4},{8,11},{9,10},{10,... | collective-permute-start | bytes 98312 | tf_op jit(solution)/shard_map/ppermute | solution.py:66
  44.8 5.3 %collective-permute-start.13 = (f32[64,128]{1,0:T(8,128)S(1)}, f32[64,128]{1,0:T(8,128)S(1)}, u32[]{:S(2)}, u32[]{:S(2)}) collective-permute-start(f32[64,128]{1,0:T(8,128)S(1)} %fusion.3.refs_0_), channel_id=1, source_target_pairs={{0,4},{4,0},{8,12},{12,8},{1,5},{5,1},{9,13},{13,9},{2,6},{6,2},{1... | collective-permute-start | bytes 98312 | tf_op jit(solution)/shard_map/ppermute | solution.py:66
  46.7 5.5 %collective-permute-start.15 = (f32[64,128]{1,0:T(8,128)S(1)}, f32[64,128]{1,0:T(8,128)S(1)}, u32[]{:S(2)}, u32[]{:S(2)}) collective-permute-start(f32[64,128]{1,0:T(8,128)S(1)} %fusion.3.refs_0_), channel_id=1, source_target_pairs={{0,12},{4,8},{8,4},{12,0},{1,13},{5,9},{9,5},{13,1},{2,14},{6,10},... | collective-permute-start | bytes 98312 | tf_op jit(solution)/shard_map/ppermute | solution.py:66
  52.5 6.4 %collective-permute-start.18 = (f32[64,128]{1,0:T(8,128)S(1)}, f32[64,128]{1,0:T(8,128)S(1)}, u32[]{:S(2)}, u32[]{:S(2)}) collective-permute-start(f32[64,128]{1,0:T(8,128)S(1)} %get-tuple-element.102), channel_id=1, source_target_pairs={{0,3},{1,2},{2,1},{3,0},{4,7},{5,6},{6,5},{7,4},{8,11},{9,10},{10,... | collective-permute-start | bytes 98312 | tf_op jit(solution)/shard_map/ppermute | solution.py:66
  60.3 6.1 %collective-permute-start.19 = (f32[64,128]{1,0:T(8,128)S(1)}, f32[64,128]{1,0:T(8,128)S(1)}, u32[]{:S(2)}, u32[]{:S(2)}) collective-permute-start(f32[64,128]{1,0:T(8,128)S(1)} %fusion.5.refs_0_), channel_id=1, source_target_pairs={{0,4},{4,0},{8,12},{12,8},{1,5},{5,1},{9,13},{13,9},{2,6},{6,2},{1... | collective-permute-start | bytes 98312 | tf_op jit(solution)/shard_map/ppermute | solution.py:66
  61.1 5.3 %collective-permute-start.20 = (f32[64,128]{1,0:T(8,128)S(1)}, f32[64,128]{1,0:T(8,128)S(1)}, u32[]{:S(2)}, u32[]{:S(2)}) collective-permute-start(f32[64,128]{1,0:T(8,128)S(1)} %fusion.5.refs_0_), channel_id=1, source_target_pairs={{0,8},{4,12},{8,0},{12,4},{1,9},{5,13},{9,1},{13,5},{2,10},{6,14},... | collective-permute-start | bytes 98312 | tf_op jit(solution)/shard_map/ppermute | solution.py:66
  63.9 31.6 %collective-permute-start.25 = (f32[256,128]{1,0:T(8,128)S(1)}, f32[256,128]{1,0:T(8,128)S(1)}, u32[]{:S(2)}, u32[]{:S(2)}) collective-permute-start(f32[256,128]{1,0:T(8,128)S(1)} %get-tuple-element.79.refs_6_), channel_id=1, source_target_pairs={{0,16},{16,0},{1,17},{17,1},{2,18},{18,2},{3,19},{19,3},{4,20},{20... | collective-permute-start | bytes 393224 | tf_op jit(solution)/shard_map/ppermute | solution.py:66
  63.9 32.3 %collective-permute-start.24 = (f32[256,128]{1,0:T(8,128)S(1)}, f32[256,128]{1,0:T(8,128)S(1)}, u32[]{:S(2)}, u32[]{:S(2)}) collective-permute-start(f32[256,128]{1,0:T(8,128)S(1)} %get-tuple-element.92.refs_4_), channel_id=1, source_target_pairs={{0,16},{16,0},{1,17},{17,1},{2,18},{18,2},{3,19},{19,3},{4,20},{20... | collective-permute-start | bytes 393224 | tf_op jit(solution)/shard_map/ppermute | solution.py:66
  68.2 6.8 %collective-permute-start.26 = (f32[4,8,256]{2,1,0:T(8,128)S(1)}, f32[4,8,256]{2,1,0:T(8,128)S(1)}, u32[]{:S(2)}, u32[]{:S(2)}) collective-permute-start(f32[4,8,256]{2,1,0:T(8,128)S(1)} %get-tuple-element.112.refs_0_.refs_3_.refs_2_.refs_4_), channel_id=1, source_target_pairs={{0,1},{1,0},{2,3},{3,2},{4,5},{5,4},{6,7},{7,6},{8,9},{9,8},{10,11... | collective-permute-start | bytes 98312 | tf_op jit(solution)/shard_map/ppermute | solution.py:66
  70.6 5.7 %collective-permute-start.28 = (f32[4,8,256]{2,1,0:T(8,128)S(1)}, f32[4,8,256]{2,1,0:T(8,128)S(1)}, u32[]{:S(2)}, u32[]{:S(2)}) collective-permute-start(f32[4,8,256]{2,1,0:T(8,128)S(1)} %get-tuple-element.112.refs_0_.refs_3_.refs_2_.refs_4_), channel_id=1, source_target_pairs={{0,3},{1,2},{2,1},{3,0},{4,7},{5,6},{6,5},{7,4},{8,11},{9,10},{10,... | collective-permute-start | bytes 98312 | tf_op jit(solution)/shard_map/ppermute | solution.py:66
  76.7 7.1 %collective-permute-start.29 = (f32[4,8,256]{2,1,0:T(8,128)S(1)}, f32[4,8,256]{2,1,0:T(8,128)S(1)}, u32[]{:S(2)}, u32[]{:S(2)}) collective-permute-start(f32[4,8,256]{2,1,0:T(8,128)S(1)} %backward_level.3.refs_7_.refs_0_.refs_5_), channel_id=1, source_target_pairs={{0,1},{1,0},{2,3},{3,2},{4,5},{5,4},{6,7},{7,6},{8,9},{9,8},{10,11... | collective-permute-start | bytes 98312 | tf_op jit(solution)/shard_map/ppermute | solution.py:66
  76.7 7.1 %collective-permute-start.30 = (f32[4,8,256]{2,1,0:T(8,128)S(1)}, f32[4,8,256]{2,1,0:T(8,128)S(1)}, u32[]{:S(2)}, u32[]{:S(2)}) collective-permute-start(f32[4,8,256]{2,1,0:T(8,128)S(1)} %backward_level.3.refs_7_.refs_0_.refs_5_), channel_id=1, source_target_pairs={{0,2},{1,3},{2,0},{3,1},{4,6},{5,7},{6,4},{7,5},{8,10},{9,11},{10,... | collective-permute-start | bytes 98312 | tf_op jit(solution)/shard_map/ppermute | solution.py:66
  79.4 5.8 %collective-permute-start.31 = (f32[4,8,256]{2,1,0:T(8,128)S(1)}, f32[4,8,256]{2,1,0:T(8,128)S(1)}, u32[]{:S(2)}, u32[]{:S(2)}) collective-permute-start(f32[4,8,256]{2,1,0:T(8,128)S(1)} %backward_level.3.refs_7_.refs_0_.refs_5_), channel_id=1, source_target_pairs={{0,3},{1,2},{2,1},{3,0},{4,7},{5,6},{6,5},{7,4},{8,11},{9,10},{10,... | collective-permute-start | bytes 98312 | tf_op jit(solution)/shard_map/ppermute | solution.py:66
  85.5 7.5 %collective-permute-start.32 = (f32[4,8,256]{2,1,0:T(8,128)S(1)}, f32[4,8,256]{2,1,0:T(8,128)S(1)}, u32[]{:S(2)}, u32[]{:S(2)}) collective-permute-start(f32[4,8,256]{2,1,0:T(8,128)S(1)} %backward_level.4.refs_0_.refs_6_), channel_id=1, source_target_pairs={{0,1},{1,0},{2,3},{3,2},{4,5},{5,4},{6,7},{7,6},{8,9},{9,8},{10,11... | collective-permute-start | bytes 98312 | tf_op jit(solution)/shard_map/ppermute | solution.py:66
  85.6 7.6 %collective-permute-start.33 = (f32[4,8,256]{2,1,0:T(8,128)S(1)}, f32[4,8,256]{2,1,0:T(8,128)S(1)}, u32[]{:S(2)}, u32[]{:S(2)}) collective-permute-start(f32[4,8,256]{2,1,0:T(8,128)S(1)} %backward_level.4.refs_0_.refs_6_), channel_id=1, source_target_pairs={{0,2},{1,3},{2,0},{3,1},{4,6},{5,7},{6,4},{7,5},{8,10},{9,11},{10,... | collective-permute-start | bytes 98312 | tf_op jit(solution)/shard_map/ppermute | solution.py:66
  88.1 5.7 %collective-permute-start.34 = (f32[4,8,256]{2,1,0:T(8,128)S(1)}, f32[4,8,256]{2,1,0:T(8,128)S(1)}, u32[]{:S(2)}, u32[]{:S(2)}) collective-permute-start(f32[4,8,256]{2,1,0:T(8,128)S(1)} %backward_level.4.refs_0_.refs_6_), channel_id=1, source_target_pairs={{0,3},{1,2},{2,1},{3,0},{4,7},{5,6},{6,5},{7,4},{8,11},{9,10},{10,... | collective-permute-start | bytes 98312 | tf_op jit(solution)/shard_map/ppermute | solution.py:66
  94.2 7.3 %collective-permute-start.37 = (f32[4,4,8,256]{3,2,1,0:T(8,128)S(1)}, f32[4,4,8,256]{3,2,1,0:T(8,128)S(1)}, u32[]{:S(2)}, u32[]{:S(2)}) collective-permute-start(f32[4,4,8,256]{3,2,1,0:T(8,128)S(1)} %backward_level.5), channel_id=1, source_target_pairs={{0,12},{4,8},{8,4},{12,0},{1,13},{5,9},{9,5},{13,1},{2,14},{6,10},... | collective-permute-start | bytes 393224 | tf_op jit(solution)/shard_map/ppermute | solution.py:66
  95.5 7.0 %collective-permute-start.35 = (f32[4,4,8,256]{3,2,1,0:T(8,128)S(1)}, f32[4,4,8,256]{3,2,1,0:T(8,128)S(1)}, u32[]{:S(2)}, u32[]{:S(2)}) collective-permute-start(f32[4,4,8,256]{3,2,1,0:T(8,128)S(1)} %backward_level.5), channel_id=1, source_target_pairs={{0,4},{4,0},{8,12},{12,8},{1,5},{5,1},{9,13},{13,9},{2,6},{6,2},{1... | collective-permute-start | bytes 393224 | tf_op jit(solution)/shard_map/ppermute | solution.py:66
  96.2 7.0 %collective-permute-start.36 = (f32[4,4,8,256]{3,2,1,0:T(8,128)S(1)}, f32[4,4,8,256]{3,2,1,0:T(8,128)S(1)}, u32[]{:S(2)}, u32[]{:S(2)}) collective-permute-start(f32[4,4,8,256]{3,2,1,0:T(8,128)S(1)} %backward_level.5), channel_id=1, source_target_pairs={{0,8},{4,12},{8,0},{12,4},{1,9},{5,13},{9,1},{13,5},{2,10},{6,14},... | collective-permute-start | bytes 393224 | tf_op jit(solution)/shard_map/ppermute | solution.py:66
  (22 other events, 109.3 us)
Sparse Core Ops, SparseCore 0:
  10.6 51.2 all-gather.2

commit v12 on v11

--- a/solution.py
+++ b/solution.py
@@ -464,30 +464,35 @@
     tiles = out.shape[1]
     row_count, _, _, few, _ = parts[0].shape
     row = lax.axis_index("row")
-    for node in range(nodes):
-        for step in range(row_count):
-            values = groups_found([part[step, 0, node] for part in parts], groups)
-            for which, value in enumerate(values):
-                index = which * row_count + (row ^ step)
-                columns[node, pl.ds(pl.multiple_of(index * few, few), few), :] = value
-        turned[node] = columns[node].T
-        rows = [turned[node, pl.ds(step, tiles, stride=per_tile), :] for step in range(per_tile)]
-        out[0, :, node, :] = jnp.concatenate(rows, axis=1)
+    for level in range(STEP):
+        for node in range(nodes):
+            for step in range(row_count):
+                values = groups_found([part[step, level, node] for part in parts], groups)
+                for which, value in enumerate(values):
+                    index = which * row_count + (row ^ step)
+                    place = pl.ds(pl.multiple_of(index * few, few), few)
+                    columns[level, node, place, :] = value
+            turned[level, node] = columns[level, node].T
+            rows = [
+                turned[level, node, pl.ds(step, tiles, stride=per_tile), :]
+                for step in range(per_tile)
+            ]
+            out[level, :, node, :] = jnp.concatenate(rows, axis=1)
 
 
 def backward_out(parts, own):
     row_count, levels, nodes, few, rows = parts[0].shape
     tiles = rows * COLUMNS // LANES
-    part_spec = pl.BlockSpec((row_count, 1, nodes, few, rows), lambda i: (0, i, 0, 0, 0))
+    part_spec = pl.BlockSpec((row_count, STEP, nodes, few, rows), lambda i: (0, i, 0, 0, 0))
     return pl.pallas_call(
         functools.partial(backward_out_kernel, nodes, len(parts), own),
-        grid=(levels,),
+        grid=(levels // STEP,),
         out_shape=shape_of(levels, tiles, nodes, LANES),
         in_specs=[part_spec] * len(parts),
-        out_specs=pl.BlockSpec((1, tiles, nodes, LANES), lambda i: (i, 0, 0, 0)),
+        out_specs=pl.BlockSpec((STEP, tiles, nodes, LANES), lambda i: (i, 0, 0, 0)),
         scratch_shapes=[
-            pltpu.VMEM((nodes, COLUMNS, rows), F32),
-            pltpu.VMEM((nodes, rows, COLUMNS), F32),
+            pltpu.VMEM((STEP, nodes, COLUMNS, rows), F32),
+            pltpu.VMEM((STEP, nodes, rows, COLUMNS), F32),
         ],
         compiler_params=PARAMS,
         name="backward_out",

time: 115 us -> 115 us (level)
  transfers between devices with their start and end apart: 40 -> 40, of which waited for: 18 -> 18; matrix products, arithmetic and copies ran while one was open for 0% -> 0% of each run, Pallas kernels for 23% -> 24%
where the time goes in v12:
time: 115 us; the launch traced here: 114 us
  starting transfers between devices  47 us (41%)
  Pallas kernels  31.5 us (27%)
  waiting for transfers between devices  19.2 us (17%)
  between operations  14.4 us (13%)
  local copies, waits for them, and re-layouts  2.36 us (2%)
    ppermute x39, starting transfers between devices, swap(): lax.ppermute(value, axis, [(i, i ^ step) for i in range(lax.axis_size(axi...  46.9 us
    ppermute x39, waiting for transfers between devices, swap(): lax.ppermute(value, axis, [(i, i ^ step) for i in range(lax.axis_size(axi...  19.1 us
    pallas_call x3, Pallas kernels, descend_step(): pl.pallas_call(functools.partial(descend_kernel, height, nodes, col_count...  8.04 us
    pallas_call x3, Pallas kernels, lower_step(): pl.pallas_call(functools.partial(lower_kernel, height, nodes, own), grid=...  5.87 us
    pallas_call x3, Pallas kernels, solve_step(): pl.pallas_call(functools.partial(solve_kernel, sizes), grid=(nodes // STE...  5.73 us
  transfers between devices with their start and end apart: 40, of which 18 were waited for; matrix products, arithmetic and copies ran while one was open for 0% of the time, Pallas kernels for 24%

profile of v12, /device:TPU:0, one launch (start us, length us, event | category | flops | bytes accessed | tf_op | source)
XLA Modules:
  0.0 114.4 jit_solution(18045940222368044978)
XLA Ops:
  7.2 2.2 %input_parts.1 = (f32[64,128]{1,0:T(8,128)S(1)}, f32[64,128]{1,0:T(8,128)S(1)}, f32[64,128]{1,0:T(8,128)S(1)}, f32[64,128]{1,0:T(8,128)S(1)}, f32[4,64,128]{2,1,0:T(8,128)S(1)}) custom-call(f32[4,32,4,128]{3,2,1,0:T(4,128)} %bitcast.53, f32[4,32,4,128]{3,2,1,0:T(4,128)} %bitcast.54), custom_call_target="tpu_custom_call" | custom-call | tf_op jit(solution)/shard_map/input_parts/pallas_call | solution.py:525
  12.0 2.8 %collective-permute-start.1 = (f32[64,128]{1,0:T(8,128)S(1)}, f32[64,128]{1,0:T(8,128)S(1)}, u32[]{:S(2)}, u32[]{:S(2)}) collective-permute-start(f32[64,128]{1,0:T(8,128)S(1)} %bitcast_add_fusion.refs_0_), channel_id=1, source_target_pairs={{0,4},{4,0},{8,12},{12,8},{1,5},{5,1},{9,13},{13,9},{2,6},{6,2},{1... | collective-permute-start | bytes 98312 | tf_op jit(solution)/shard_map/ppermute | solution.py:66
  17.7 2.1 %lower_products.3 = (bf16[3,4,64,256]{3,2,1,0:T(8,128)(2,1)S(1)}, bf16[3,4,64,256]{3,2,1,0:T(8,128)(2,1)S(1)}, f32[3,4,4,128]{3,2,1,0:T(4,128)S(1)}) custom-call(s32[3,16]{1,0:T(4,128)S(1)} %copy-done.2, s32[4,6]{1,0:T(4,128)S(1)} %bitcast.39, f32[6,4,64,256]{3,2,1,0:T(8,128)} %blocks.5, f32[4,4,256,256]{3,2,1,0:T(8,128)} %lower.7), custom_call_target="tpu_custom_call" | custom-call | tf_op jit(solution)/shard_map/lower_products/pallas_call | solution.py:139
  21.7 3.7 %collective-permute-start.6 = (f32[64,128]{1,0:T(8,128)S(1)}, f32[64,128]{1,0:T(8,128)S(1)}, u32[]{:S(2)}, u32[]{:S(2)}) collective-permute-start(f32[64,128]{1,0:T(8,128)S(1)} %get-tuple-element.77), channel_id=1, source_target_pairs={{0,3},{1,2},{2,1},{3,0},{4,7},{5,6},{6,5},{7,4},{8,11},{9,10},{10,... | collective-permute-start | bytes 98312 | tf_op jit(solution)/shard_map/ppermute | solution.py:66
  26.2 1.9 %solve_level.3 = (f32[256,128]{1,0:T(8,128)S(1)}, f32[4,8,256]{2,1,0:T(8,128)S(1)}) custom-call(f32[256,128]{1,0:T(8,128)S(1)} %get-tuple-element.78.full, f32[4,4,256,256]{3,2,1,0:T(8,128)} %lower.7), custom_call_target="tpu_custom_call" | custom-call | tf_op jit(solution)/shard_map/solve_level/pallas_call | solution.py:300
  33.8 2.0 %lower_products.4 = (bf16[2,4,64,256]{3,2,1,0:T(8,128)(2,1)S(1)}, bf16[2,4,64,256]{3,2,1,0:T(8,128)(2,1)S(1)}, f32[2,4,4,128]{3,2,1,0:T(4,128)S(1)}) custom-call(s32[3,16]{1,0:T(4,128)S(1)} %copy-done.2, s32[4,6]{1,0:T(4,128)S(1)} %bitcast.40, f32[6,4,64,256]{3,2,1,0:T(8,128)} %blocks.5, f32[4,4,256,256]{3,2,1,0:T(8,128)} %lower.7), custom_call_target="tpu_custom_call" | custom-call | tf_op jit(solution)/shard_map/lower_products/pallas_call | solution.py:139
  37.8 1.9 %collective-permute-start.12 = (f32[64,128]{1,0:T(8,128)S(1)}, f32[64,128]{1,0:T(8,128)S(1)}, u32[]{:S(2)}, u32[]{:S(2)}) collective-permute-start(f32[64,128]{1,0:T(8,128)S(1)} %get-tuple-element.90), channel_id=1, source_target_pairs={{0,3},{1,2},{2,1},{3,0},{4,7},{5,6},{6,5},{7,4},{8,11},{9,10},{10,... | collective-permute-start | bytes 98312 | tf_op jit(solution)/shard_map/ppermute | solution.py:66
  40.0 2.3 %collective-permute-start.11 = (f32[64,128]{1,0:T(8,128)S(1)}, f32[64,128]{1,0:T(8,128)S(1)}, u32[]{:S(2)}, u32[]{:S(2)}) collective-permute-start(f32[64,128]{1,0:T(8,128)S(1)} %get-tuple-element.89), channel_id=1, source_target_pairs={{0,2},{1,3},{2,0},{3,1},{4,6},{5,7},{6,4},{7,5},{8,10},{9,11},{10,... | collective-permute-start | bytes 98312 | tf_op jit(solution)/shard_map/ppermute | solution.py:66
  42.3 1.9 %solve_level.4 = (f32[256,128]{1,0:T(8,128)S(1)}, f32[4,8,256]{2,1,0:T(8,128)S(1)}) custom-call(f32[256,128]{1,0:T(8,128)S(1)} %get-tuple-element.91.full, f32[4,4,256,256]{3,2,1,0:T(8,128)} %lower.7), custom_call_target="tpu_custom_call" | custom-call | tf_op jit(solution)/shard_map/solve_level/pallas_call | solution.py:300
  50.1 2.1 %collective-permute-done.15.refs_3_ = f32[64,128]{1,0:T(8,128)S(1)} collective-permute-done((f32[64,128]{1,0:T(8,128)S(1)}, f32[64,128]{1,0:T(8,128)S(1)}, u32[]{:S(2)}, u32[]{:S(2)}) %collective-permute-start.15) | collective-permute-done | bytes 32800 | tf_op jit(solution)/shard_map/ppermute | solution.py:66
  52.5 2.9 %collective-permute-start.18 = (f32[64,128]{1,0:T(8,128)S(1)}, f32[64,128]{1,0:T(8,128)S(1)}, u32[]{:S(2)}, u32[]{:S(2)}) collective-permute-start(f32[64,128]{1,0:T(8,128)S(1)} %get-tuple-element.102), channel_id=1, source_target_pairs={{0,3},{1,2},{2,1},{3,0},{4,7},{5,6},{6,5},{7,4},{8,11},{9,10},{10,... | collective-permute-start | bytes 98312 | tf_op jit(solution)/shard_map/ppermute | solution.py:66
  57.0 1.9 %solve_level.5 = (f32[256,128]{1,0:T(8,128)S(1)}, f32[4,8,256]{2,1,0:T(8,128)S(1)}) custom-call(f32[256,128]{1,0:T(8,128)S(1)} %get-tuple-element.103.full, f32[4,4,256,256]{3,2,1,0:T(8,128)} %lower.7), custom_call_target="tpu_custom_call" | custom-call | tf_op jit(solution)/shard_map/solve_level/pallas_call | solution.py:300
  64.4 2.0 %middle_product.1 = (bf16[4,256,256]{2,1,0:T(8,128)(2,1)S(1)}, bf16[4,256,256]{2,1,0:T(8,128)(2,1)S(1)}, bf16[4,256,256]{2,1,0:T(8,128)(2,1)S(1)}, bf16[4,256,256]{2,1,0:T(8,128)(2,1)S(1)}) custom-call(f32[4,4,256,256]{3,2,1,0:T(8,128)} %inverse.11, f32[4,4,256,256]{3,2,1,0:T(8,128)} %lower.7), custom_call_target="tpu_custom_call" | custom-call | tf_op jit(solution)/shard_map/middle_product/pallas_call | solution.py:166
  68.2 2.1 %collective-permute-start.26 = (f32[4,8,256]{2,1,0:T(8,128)S(1)}, f32[4,8,256]{2,1,0:T(8,128)S(1)}, u32[]{:S(2)}, u32[]{:S(2)}) collective-permute-start(f32[4,8,256]{2,1,0:T(8,128)S(1)} %get-tuple-element.112.refs_0_.refs_3_.refs_2_.refs_4_), channel_id=1, source_target_pairs={{0,1},{1,0},{2,3},{3,2},{4,5},{5,4},{6,7},{7,6},{8,9},{9,8},{10,11... | collective-permute-start | bytes 98312 | tf_op jit(solution)/shard_map/ppermute | solution.py:66
  70.6 2.1 %collective-permute-start.28 = (f32[4,8,256]{2,1,0:T(8,128)S(1)}, f32[4,8,256]{2,1,0:T(8,128)S(1)}, u32[]{:S(2)}, u32[]{:S(2)}) collective-permute-start(f32[4,8,256]{2,1,0:T(8,128)S(1)} %get-tuple-element.112.refs_0_.refs_3_.refs_2_.refs_4_), channel_id=1, source_target_pairs={{0,3},{1,2},{2,1},{3,0},{4,7},{5,6},{6,5},{7,4},{8,11},{9,10},{10,... | collective-permute-start | bytes 98312 | tf_op jit(solution)/shard_map/ppermute | solution.py:66
  72.7 2.3 %descend_level.3 = (f32[4,8,256]{2,1,0:T(8,128)S(1)}, bf16[4,256,256]{2,1,0:T(8,128)(2,1)S(1)}, bf16[4,256,256]{2,1,0:T(8,128)(2,1)S(1)}, f32[4,16,256]{2,1,0:T(8,128)S(1)}) custom-call(s32[3,16]{1,0:T(4,128)S(1)} %copy-done.3, s32[4,6]{1,0:T(4,128)S(1)} %bitcast.42, f32[4,8,256]{2,1,0:T(8,128)S(1)} %get-tuple-element.105.value, ...), custom_call_target="tpu_custom_call" | custom-call | tf_op jit(solution)/shard_map/descend_level/pallas_call | solution.py:358
  76.7 2.6 %collective-permute-start.30 = (f32[4,8,256]{2,1,0:T(8,128)S(1)}, f32[4,8,256]{2,1,0:T(8,128)S(1)}, u32[]{:S(2)}, u32[]{:S(2)}) collective-permute-start(f32[4,8,256]{2,1,0:T(8,128)S(1)} %backward_level.3.refs_7_.refs_0_.refs_5_), channel_id=1, source_target_pairs={{0,2},{1,3},{2,0},{3,1},{4,6},{5,7},{6,4},{7,5},{8,10},{9,11},{10,... | collective-permute-start | bytes 98312 | tf_op jit(solution)/shard_map/ppermute | solution.py:66
  81.1 2.7 %descend_level.5 = (f32[4,8,256]{2,1,0:T(8,128)S(1)}, bf16[4,256,256]{2,1,0:T(8,128)(2,1)S(1)}, bf16[4,256,256]{2,1,0:T(8,128)(2,1)S(1)}, f32[4,16,256]{2,1,0:T(8,128)S(1)}) custom-call(s32[3,16]{1,0:T(4,128)S(1)} %copy-done.3, s32[4,6]{1,0:T(4,128)S(1)} %bitcast.43, f32[4,8,256]{2,1,0:T(8,128)S(1)} %get-tuple-element.93.value, f32[4,4,256,256]{3,2,1,0:T(8,128)} %inverse.11, ...), custom_call_target="tpu_custom_call" | custom-call | tf_op jit(solution)/shard_map/descend_level/pallas_call | solution.py:358
  85.6 2.5 %collective-permute-start.33 = (f32[4,8,256]{2,1,0:T(8,128)S(1)}, f32[4,8,256]{2,1,0:T(8,128)S(1)}, u32[]{:S(2)}, u32[]{:S(2)}) collective-permute-start(f32[4,8,256]{2,1,0:T(8,128)S(1)} %backward_level.4.refs_0_.refs_6_), channel_id=1, source_target_pairs={{0,2},{1,3},{2,0},{3,1},{4,6},{5,7},{6,4},{7,5},{8,10},{9,11},{10,... | collective-permute-start | bytes 98312 | tf_op jit(solution)/shard_map/ppermute | solution.py:66
  88.1 1.8 %collective-permute-start.34 = (f32[4,8,256]{2,1,0:T(8,128)S(1)}, f32[4,8,256]{2,1,0:T(8,128)S(1)}, u32[]{:S(2)}, u32[]{:S(2)}) collective-permute-start(f32[4,8,256]{2,1,0:T(8,128)S(1)} %backward_level.4.refs_0_.refs_6_), channel_id=1, source_target_pairs={{0,3},{1,2},{2,1},{3,0},{4,7},{5,6},{6,5},{7,4},{8,11},{9,10},{10,... | collective-permute-start | bytes 98312 | tf_op jit(solution)/shard_map/ppermute | solution.py:66
  89.9 3.1 %descend_level.4 = (f32[4,8,256]{2,1,0:T(8,128)S(1)}, bf16[4,256,256]{2,1,0:T(8,128)(2,1)S(1)}, bf16[4,256,256]{2,1,0:T(8,128)(2,1)S(1)}, f32[4,16,256]{2,1,0:T(8,128)S(1)}) custom-call(s32[3,16]{1,0:T(4,128)S(1)} %copy-done.3, s32[4,6]{1,0:T(4,128)S(1)} %bitcast.44, f32[4,8,256]{2,1,0:T(8,128)S(1)} %get-tuple-element.80.value, f32[4,4,256,256]{3,2,1,0:T(8,128)} %inverse.11, ...), custom_call_target="tpu_custom_call" | custom-call | tf_op jit(solution)/shard_map/descend_level/pallas_call | solution.py:358
  97.7 2.0 %forward_out.1 = f32[4,128,4,128]{3,2,1,0:T(4,128)} custom-call(f32[256,128]{1,0:T(8,128)S(1)} %get-tuple-element.111.refs_0_, f32[256,128]{1,0:T(8,128)S(1)} %collective-permute-done.22.refs_1_, f32[256,128]{1,0:T(8,128)S(1)} %get-tuple-element.104.refs_2_, f32[256,128]{1,0:T(8,128)S(1)} %collective-permute-done.23.refs_3_, ...), custom_call_target="tpu_custom_call" | custom-call | tf_op jit(solution)/shard_map/forward_out/pallas_call | solution.py:449
  103.4 1.9 %collective-permute-done.38.refs_1_ = f32[4,4,4,8,256]{4,3,2,1,0:T(8,128)S(1)} collective-permute-done((f32[4,4,4,8,256]{4,3,2,1,0:T(8,128)S(1)}, f32[4,4,4,8,256]{4,3,2,1,0:T(8,128)S(1)}, u32[]{:S(2)}, u32[]{:S(2)}) %collective-permute-start.38) | collective-permute-done | bytes 524320 | tf_op jit(solution)/shard_map/ppermute | solution.py:66
  105.3 2.3 %backward_out.1 = f32[4,128,4,128]{3,2,1,0:T(4,128)} custom-call(f32[4,4,4,8,256]{4,3,2,1,0:T(8,128)S(1)} %pad_maximum_fusion.refs_0_, f32[4,4,4,8,256]{4,3,2,1,0:T(8,128)S(1)} %collective-permute-done.38.refs_1_), custom_call_target="tpu_custom_call" | custom-call | tf_op jit(solution)/shard_map/backward_out/pallas_call | solution.py:487
  (95 shorter events, 44.8 us)
Async XLA Ops:
  7.2 65.5 %all-gather.3.cloned.1.call-start = ((), (), s32[]{:S(2)}) async-start(), calls=%async_computation | async-start | bytes 7077888 | tf_op jit(solution)/shard_map/all_gather | solution.py:538
  12.0 7.9 %collective-permute-start.1 = (f32[64,128]{1,0:T(8,128)S(1)}, f32[64,128]{1,0:T(8,128)S(1)}, u32[]{:S(2)}, u32[]{:S(2)}) collective-permute-start(f32[64,128]{1,0:T(8,128)S(1)} %bitcast_add_fusion.refs_0_), channel_id=1, source_target_pairs={{0,4},{4,0},{8,12},{12,8},{1,5},{5,1},{9,13},{13,9},{2,6},{6,2},{1... | collective-permute-start | bytes 98312 | tf_op jit(solution)/shard_map/ppermute | solution.py:66
  14.8 5.0 %collective-permute-start.2 = (f32[64,128]{1,0:T(8,128)S(1)}, f32[64,128]{1,0:T(8,128)S(1)}, u32[]{:S(2)}, u32[]{:S(2)}) collective-permute-start(f32[64,128]{1,0:T(8,128)S(1)} %bitcast_add_fusion.refs_0_), channel_id=1, source_target_pairs={{0,8},{4,12},{8,0},{12,4},{1,9},{5,13},{9,1},{13,5},{2,10},{6,14},... | collective-permute-start | bytes 98312 | tf_op jit(solution)/shard_map/ppermute | solution.py:66
  21.7 6.4 %collective-permute-start.6 = (f32[64,128]{1,0:T(8,128)S(1)}, f32[64,128]{1,0:T(8,128)S(1)}, u32[]{:S(2)}, u32[]{:S(2)}) collective-permute-start(f32[64,128]{1,0:T(8,128)S(1)} %get-tuple-element.77), channel_id=1, source_target_pairs={{0,3},{1,2},{2,1},{3,0},{4,7},{5,6},{6,5},{7,4},{8,11},{9,10},{10,... | collective-permute-start | bytes 98312 | tf_op jit(solution)/shard_map/ppermute | solution.py:66
  30.2 5.6 %collective-permute-start.7 = (f32[64,128]{1,0:T(8,128)S(1)}, f32[64,128]{1,0:T(8,128)S(1)}, u32[]{:S(2)}, u32[]{:S(2)}) collective-permute-start(f32[64,128]{1,0:T(8,128)S(1)} %fusion.1.refs_0_), channel_id=1, source_target_pairs={{0,4},{4,0},{8,12},{12,8},{1,5},{5,1},{9,13},{13,9},{2,6},{6,2},{1... | collective-permute-start | bytes 98312 | tf_op jit(solution)/shard_map/ppermute | solution.py:66
  37.8 6.4 %collective-permute-start.12 = (f32[64,128]{1,0:T(8,128)S(1)}, f32[64,128]{1,0:T(8,128)S(1)}, u32[]{:S(2)}, u32[]{:S(2)}) collective-permute-start(f32[64,128]{1,0:T(8,128)S(1)} %get-tuple-element.90), channel_id=1, source_target_pairs={{0,3},{1,2},{2,1},{3,0},{4,7},{5,6},{6,5},{7,4},{8,11},{9,10},{10,... | collective-permute-start | bytes 98312 | tf_op jit(solution)/shard_map/ppermute | solution.py:66
  44.8 5.3 %collective-permute-start.13 = (f32[64,128]{1,0:T(8,128)S(1)}, f32[64,128]{1,0:T(8,128)S(1)}, u32[]{:S(2)}, u32[]{:S(2)}) collective-permute-start(f32[64,128]{1,0:T(8,128)S(1)} %fusion.3.refs_0_), channel_id=1, source_target_pairs={{0,4},{4,0},{8,12},{12,8},{1,5},{5,1},{9,13},{13,9},{2,6},{6,2},{1... | collective-permute-start | bytes 98312 | tf_op jit(solution)/shard_map/ppermute | solution.py:66
  46.7 5.5 %collective-permute-start.15 = (f32[64,128]{1,0:T(8,128)S(1)}, f32[64,128]{1,0:T(8,128)S(1)}, u32[]{:S(2)}, u32[]{:S(2)}) collective-permute-start(f32[64,128]{1,0:T(8,128)S(1)} %fusion.3.refs_0_), channel_id=1, source_target_pairs={{0,12},{4,8},{8,4},{12,0},{1,13},{5,9},{9,5},{13,1},{2,14},{6,10},... | collective-permute-start | bytes 98312 | tf_op jit(solution)/shard_map/ppermute | solution.py:66
  52.5 6.4 %collective-permute-start.18 = (f32[64,128]{1,0:T(8,128)S(1)}, f32[64,128]{1,0:T(8,128)S(1)}, u32[]{:S(2)}, u32[]{:S(2)}) collective-permute-start(f32[64,128]{1,0:T(8,128)S(1)} %get-tuple-element.102), channel_id=1, source_target_pairs={{0,3},{1,2},{2,1},{3,0},{4,7},{5,6},{6,5},{7,4},{8,11},{9,10},{10,... | collective-permute-start | bytes 98312 | tf_op jit(solution)/shard_map/ppermute | solution.py:66
  60.3 6.1 %collective-permute-start.19 = (f32[64,128]{1,0:T(8,128)S(1)}, f32[64,128]{1,0:T(8,128)S(1)}, u32[]{:S(2)}, u32[]{:S(2)}) collective-permute-start(f32[64,128]{1,0:T(8,128)S(1)} %fusion.5.refs_0_), channel_id=1, source_target_pairs={{0,4},{4,0},{8,12},{12,8},{1,5},{5,1},{9,13},{13,9},{2,6},{6,2},{1... | collective-permute-start | bytes 98312 | tf_op jit(solution)/shard_map/ppermute | solution.py:66
  61.1 5.3 %collective-permute-start.20 = (f32[64,128]{1,0:T(8,128)S(1)}, f32[64,128]{1,0:T(8,128)S(1)}, u32[]{:S(2)}, u32[]{:S(2)}) collective-permute-start(f32[64,128]{1,0:T(8,128)S(1)} %fusion.5.refs_0_), channel_id=1, source_target_pairs={{0,8},{4,12},{8,0},{12,4},{1,9},{5,13},{9,1},{13,5},{2,10},{6,14},... | collective-permute-start | bytes 98312 | tf_op jit(solution)/shard_map/ppermute | solution.py:66
  63.9 31.6 %collective-permute-start.25 = (f32[256,128]{1,0:T(8,128)S(1)}, f32[256,128]{1,0:T(8,128)S(1)}, u32[]{:S(2)}, u32[]{:S(2)}) collective-permute-start(f32[256,128]{1,0:T(8,128)S(1)} %get-tuple-element.79.refs_6_), channel_id=1, source_target_pairs={{0,16},{16,0},{1,17},{17,1},{2,18},{18,2},{3,19},{19,3},{4,20},{20... | collective-permute-start | bytes 393224 | tf_op jit(solution)/shard_map/ppermute | solution.py:66
  63.9 32.3 %collective-permute-start.24 = (f32[256,128]{1,0:T(8,128)S(1)}, f32[256,128]{1,0:T(8,128)S(1)}, u32[]{:S(2)}, u32[]{:S(2)}) collective-permute-start(f32[256,128]{1,0:T(8,128)S(1)} %get-tuple-element.92.refs_4_), channel_id=1, source_target_pairs={{0,16},{16,0},{1,17},{17,1},{2,18},{18,2},{3,19},{19,3},{4,20},{20... | collective-permute-start | bytes 393224 | tf_op jit(solution)/shard_map/ppermute | solution.py:66
  68.2 6.8 %collective-permute-start.26 = (f32[4,8,256]{2,1,0:T(8,128)S(1)}, f32[4,8,256]{2,1,0:T(8,128)S(1)}, u32[]{:S(2)}, u32[]{:S(2)}) collective-permute-start(f32[4,8,256]{2,1,0:T(8,128)S(1)} %get-tuple-element.112.refs_0_.refs_3_.refs_2_.refs_4_), channel_id=1, source_target_pairs={{0,1},{1,0},{2,3},{3,2},{4,5},{5,4},{6,7},{7,6},{8,9},{9,8},{10,11... | collective-permute-start | bytes 98312 | tf_op jit(solution)/shard_map/ppermute | solution.py:66
  70.6 5.7 %collective-permute-start.28 = (f32[4,8,256]{2,1,0:T(8,128)S(1)}, f32[4,8,256]{2,1,0:T(8,128)S(1)}, u32[]{:S(2)}, u32[]{:S(2)}) collective-permute-start(f32[4,8,256]{2,1,0:T(8,128)S(1)} %get-tuple-element.112.refs_0_.refs_3_.refs_2_.refs_4_), channel_id=1, source_target_pairs={{0,3},{1,2},{2,1},{3,0},{4,7},{5,6},{6,5},{7,4},{8,11},{9,10},{10,... | collective-permute-start | bytes 98312 | tf_op jit(solution)/shard_map/ppermute | solution.py:66
  76.7 7.1 %collective-permute-start.29 = (f32[4,8,256]{2,1,0:T(8,128)S(1)}, f32[4,8,256]{2,1,0:T(8,128)S(1)}, u32[]{:S(2)}, u32[]{:S(2)}) collective-permute-start(f32[4,8,256]{2,1,0:T(8,128)S(1)} %backward_level.3.refs_7_.refs_0_.refs_5_), channel_id=1, source_target_pairs={{0,1},{1,0},{2,3},{3,2},{4,5},{5,4},{6,7},{7,6},{8,9},{9,8},{10,11... | collective-permute-start | bytes 98312 | tf_op jit(solution)/shard_map/ppermute | solution.py:66
  76.7 7.1 %collective-permute-start.30 = (f32[4,8,256]{2,1,0:T(8,128)S(1)}, f32[4,8,256]{2,1,0:T(8,128)S(1)}, u32[]{:S(2)}, u32[]{:S(2)}) collective-permute-start(f32[4,8,256]{2,1,0:T(8,128)S(1)} %backward_level.3.refs_7_.refs_0_.refs_5_), channel_id=1, source_target_pairs={{0,2},{1,3},{2,0},{3,1},{4,6},{5,7},{6,4},{7,5},{8,10},{9,11},{10,... | collective-permute-start | bytes 98312 | tf_op jit(solution)/shard_map/ppermute | solution.py:66
  79.4 5.8 %collective-permute-start.31 = (f32[4,8,256]{2,1,0:T(8,128)S(1)}, f32[4,8,256]{2,1,0:T(8,128)S(1)}, u32[]{:S(2)}, u32[]{:S(2)}) collective-permute-start(f32[4,8,256]{2,1,0:T(8,128)S(1)} %backward_level.3.refs_7_.refs_0_.refs_5_), channel_id=1, source_target_pairs={{0,3},{1,2},{2,1},{3,0},{4,7},{5,6},{6,5},{7,4},{8,11},{9,10},{10,... | collective-permute-start | bytes 98312 | tf_op jit(solution)/shard_map/ppermute | solution.py:66
  85.5 7.5 %collective-permute-start.32 = (f32[4,8,256]{2,1,0:T(8,128)S(1)}, f32[4,8,256]{2,1,0:T(8,128)S(1)}, u32[]{:S(2)}, u32[]{:S(2)}) collective-permute-start(f32[4,8,256]{2,1,0:T(8,128)S(1)} %backward_level.4.refs_0_.refs_6_), channel_id=1, source_target_pairs={{0,1},{1,0},{2,3},{3,2},{4,5},{5,4},{6,7},{7,6},{8,9},{9,8},{10,11... | collective-permute-start | bytes 98312 | tf_op jit(solution)/shard_map/ppermute | solution.py:66
  85.6 7.6 %collective-permute-start.33 = (f32[4,8,256]{2,1,0:T(8,128)S(1)}, f32[4,8,256]{2,1,0:T(8,128)S(1)}, u32[]{:S(2)}, u32[]{:S(2)}) collective-permute-start(f32[4,8,256]{2,1,0:T(8,128)S(1)} %backward_level.4.refs_0_.refs_6_), channel_id=1, source_target_pairs={{0,2},{1,3},{2,0},{3,1},{4,6},{5,7},{6,4},{7,5},{8,10},{9,11},{10,... | collective-permute-start | bytes 98312 | tf_op jit(solution)/shard_map/ppermute | solution.py:66
  88.1 5.7 %collective-permute-start.34 = (f32[4,8,256]{2,1,0:T(8,128)S(1)}, f32[4,8,256]{2,1,0:T(8,128)S(1)}, u32[]{:S(2)}, u32[]{:S(2)}) collective-permute-start(f32[4,8,256]{2,1,0:T(8,128)S(1)} %backward_level.4.refs_0_.refs_6_), channel_id=1, source_target_pairs={{0,3},{1,2},{2,1},{3,0},{4,7},{5,6},{6,5},{7,4},{8,11},{9,10},{10,... | collective-permute-start | bytes 98312 | tf_op jit(solution)/shard_map/ppermute | solution.py:66
  94.2 7.3 %collective-permute-start.37 = (f32[4,4,8,256]{3,2,1,0:T(8,128)S(1)}, f32[4,4,8,256]{3,2,1,0:T(8,128)S(1)}, u32[]{:S(2)}, u32[]{:S(2)}) collective-permute-start(f32[4,4,8,256]{3,2,1,0:T(8,128)S(1)} %backward_level.5), channel_id=1, source_target_pairs={{0,12},{4,8},{8,4},{12,0},{1,13},{5,9},{9,5},{13,1},{2,14},{6,10},... | collective-permute-start | bytes 393224 | tf_op jit(solution)/shard_map/ppermute | solution.py:66
  95.5 7.0 %collective-permute-start.35 = (f32[4,4,8,256]{3,2,1,0:T(8,128)S(1)}, f32[4,4,8,256]{3,2,1,0:T(8,128)S(1)}, u32[]{:S(2)}, u32[]{:S(2)}) collective-permute-start(f32[4,4,8,256]{3,2,1,0:T(8,128)S(1)} %backward_level.5), channel_id=1, source_target_pairs={{0,4},{4,0},{8,12},{12,8},{1,5},{5,1},{9,13},{13,9},{2,6},{6,2},{1... | collective-permute-start | bytes 393224 | tf_op jit(solution)/shard_map/ppermute | solution.py:66
  96.2 7.0 %collective-permute-start.36 = (f32[4,4,8,256]{3,2,1,0:T(8,128)S(1)}, f32[4,4,8,256]{3,2,1,0:T(8,128)S(1)}, u32[]{:S(2)}, u32[]{:S(2)}) collective-permute-start(f32[4,4,8,256]{3,2,1,0:T(8,128)S(1)} %backward_level.5), channel_id=1, source_target_pairs={{0,8},{4,12},{8,0},{12,4},{1,9},{5,13},{9,1},{13,5},{2,10},{6,14},... | collective-permute-start | bytes 393224 | tf_op jit(solution)/shard_map/ppermute | solution.py:66
  (22 other events, 109.3 us)
Sparse Core Ops, SparseCore 0:
  10.6 51.2 all-gather.2
